TPU v7x, 256 devices: a whole 4x4x8 slice. The times are simulated.
256 devices in a mesh: space: 16 (over z, x_lo), tracer: 16 (over x_hi, y, core).
Axes of the slice: x: 4 (x_hi: 2, x_lo: 2; x = x_hi * 2 + x_lo), y: 4, z: 8, core: 2. Of those that a mesh axis runs over, the one named last changes fastest.
Arguments:
- tracer_mass: float32 [288, 3, 32, 2048], P('tracer', None, None, 'space'), may hold values from -6 to 6
- thickness: float32 [16, 3, 32, 2048], P('tracer', None, None, 'space'), may hold values from 0.6 to 1.8
- flux_east: float32 [16, 3, 32, 2048], P('tracer', None, None, 'space'), may hold values from -0.08 to 0.08
- flux_north: float32 [16, 3, 32, 2048], P('tracer', None, None, 'space'), may hold values from -0.08 to 0.08
- courant_east: float32 [16, 3, 32, 2048], P('tracer', None, None, 'space'), may hold values from -0.95 to 0.95
- courant_north: float32 [16, 3, 32, 2048], P('tracer', None, None, 'space'), may hold values from -0.9 to 0.9
- whole_east: int32 [16, 3, 32, 2048], P('tracer', None, None, 'space'), may hold values from 0 to 2
- dynamics_owner: int32 [16], P('space'), may hold values from 0 to 15
Outputs:
- mixing_ratio: float32 [288, 3, 32, 2048], P('tracer', None, None, 'space')
Inputs may be any that keep to these rules, and one draw needn't show every extreme that they name: `whole_east`: whole cells counts, 0 to 2.
All inputs are finite; a program needn't handle non-finite values.
Results may differ from a plain program's by a relative error of at most 0.0003.
Values sent between devices are 32-bit elements; how exact they have to be, the bound alone decides.
No kernel may reach another device: no remote copies, remote signals or barrier semaphores. Data moves between devices by JAX's collectives and lax.ppermute only.
A program may use at most 64 MiB of HBM per device.

v0:
```python
import jax
import jax.numpy as jnp
from jax import lax
from jax.sharding import PartitionSpec as P

NS = 2


def from_root(x, axis, root):
    mine = lax.axis_index(axis) == root
    return lax.psum(jnp.where(mine, x, jnp.zeros_like(x)), axis)


def passed_along(x, axis, by):
    size = lax.axis_size(axis)
    return lax.ppermute(x, axis, [(i, (i + by) % size) for i in range(size)])


def extended_2(cells, sides, width):
    for axis, dim in sides:
        count = lax.axis_size(axis)
        head = lax.slice_in_dim(cells, 0, width, axis=dim)
        tail = lax.slice_in_dim(cells, cells.shape[dim] - width, cells.shape[dim], axis=dim)
        cells = jnp.concatenate(
            [
                lax.ppermute(tail, axis, [(i, (i + 1) % count) for i in range(count)]),
                cells,
                lax.ppermute(head, axis, [((i + 1) % count, i) for i in range(count)]),
            ],
            axis=dim,
        )
    return cells


def take_slice(values_in, start_at, stop_at, along):
    return lax.slice_in_dim(values_in, start_at, stop_at, axis=along)


def parabola_parts(extended, along):
    length = extended.shape[along]
    edge_values = (
        7.0
        * (take_slice(extended, 1, length - 2, along) + take_slice(extended, 2, length - 1, along))
        - (take_slice(extended, 0, length - 3, along) + take_slice(extended, 3, length, along))
    ) / 12.0
    left_edge = take_slice(edge_values, 0, length - 4, along)
    right_edge = take_slice(edge_values, 1, length - 3, along)
    cell_mean = take_slice(extended, 2, length - 2, along)
    curvature = 6.0 * cell_mean - 3.0 * (left_edge + right_edge)
    return (left_edge, right_edge, right_edge - left_edge, curvature)


def face_flux(extended, parabola, courant, whole_cells, most_cells, margin, face_count, along):
    left_edge, right_edge, edge_slope, curvature = parabola
    fraction = jnp.abs(courant)
    forward = courant >= 0.0
    shape_term = 1.0 - 2.0 / 3.0 * fraction
    whole_forward = 0.0
    whole_backward = 0.0
    flux_total = None
    for shift_count in range(most_cells + 1):
        if shift_count > 0:
            whole_forward = whole_forward + take_slice(
                extended, margin - shift_count, margin - shift_count + face_count, along
            )
            whole_backward = whole_backward + take_slice(
                extended, margin + shift_count - 1, margin + shift_count - 1 + face_count, along
            )
        upwind_left = margin - shift_count - 3
        upwind_right = margin + shift_count - 2
        from_left = take_slice(
            right_edge, upwind_left, upwind_left + face_count, along
        ) - 0.5 * fraction * (
            take_slice(edge_slope, upwind_left, upwind_left + face_count, along)
            - shape_term * take_slice(curvature, upwind_left, upwind_left + face_count, along)
        )
        from_right = take_slice(
            left_edge, upwind_right, upwind_right + face_count, along
        ) + 0.5 * fraction * (
            take_slice(edge_slope, upwind_right, upwind_right + face_count, along)
            + shape_term * take_slice(curvature, upwind_right, upwind_right + face_count, along)
        )
        candidate = jnp.where(
            forward, whole_forward + fraction * from_left, -(whole_backward + fraction * from_right)
        )
        if shift_count == 0:
            flux_total = candidate
        else:
            flux_total = jnp.where(whole_cells == shift_count, candidate, flux_total)
    return flux_total


def row_flux(quantity, courant):
    row_count = quantity.shape[2]
    padded = jnp.pad(quantity, ((0, 0), (0, 0), (2, 2), (0, 0)))
    parabola = parabola_parts(padded, 2)
    inner_faces = face_flux(
        padded, parabola, take_slice(courant, 1, row_count, 1), None, 0, 3, row_count - 1, 2
    )
    zero_row = jnp.zeros_like(take_slice(inner_faces, 0, 1, 2))
    return jnp.concatenate([zero_row, inner_faces, zero_row], axis=2)


def row_update(quantity, face_fluxes, factor):
    row_count = quantity.shape[2]
    return quantity + factor * (
        take_slice(face_fluxes, 0, row_count, 2) - take_slice(face_fluxes, 1, row_count + 1, 2)
    )


def column_flux(extended, courant_faces, whole_faces):
    parabola = parabola_parts(extended, 3)
    return face_flux(
        extended, parabola, courant_faces, whole_faces, NS, NS + 3, courant_faces.shape[3], 3
    )


def column_update(quantity, face_fluxes, factor):
    column_count = quantity.shape[3]
    return quantity + factor * (
        take_slice(face_fluxes, 0, column_count, 3)
        - take_slice(face_fluxes, 1, column_count + 1, 3)
    )


def north_differences(north_mass):
    row_count = north_mass.shape[1]
    zero_row = jnp.zeros_like(north_mass[:, :1, :])
    north_faces = jnp.concatenate([zero_row, north_mass[:, 1:row_count, :], zero_row], axis=1)
    return north_faces[:, :-1, :] - north_faces[:, 1:, :]


def shards(
    tracer_mass,
    thickness,
    flux_east,
    flux_north,
    courant_east,
    courant_north,
    whole_east,
    dynamics_owner,
):
    margin = NS + 3
    source = dynamics_owner[0]
    counts_float = whole_east[0].astype(jnp.float32)
    courant_pack = jnp.stack([courant_east[0], courant_north[0], counts_float])
    thick_here, east_mass, north_mass, courant_here = (
        from_root(thickness[0], "tracer", source),
        from_root(flux_east[0], "tracer", source),
        from_root(flux_north[0], "tracer", source),
        from_root(courant_pack, "tracer", source),
    )
    first_mass = east_mass[:, :, :1]
    north_frac = courant_here[1]
    east_frac = courant_here[0]
    whole_float = courant_here[2]
    edge_frac, edge_whole, edge_mass = passed_along(
        (east_frac[:, :, :1], whole_float[:, :, :1], first_mass), "space", -1
    )
    east_faces = jnp.concatenate([east_frac, edge_frac], axis=2)
    whole_faces = jnp.concatenate([whole_float, edge_whole], axis=2).astype(jnp.int32)
    wide_mass = extended_2(tracer_mass, (("space", 3),), margin)
    inner_north = row_update(tracer_mass, row_flux(tracer_mass, north_frac), 0.5)
    wide_inner = extended_2(inner_north, (("space", 3),), margin)
    east_first = column_flux(wide_mass, east_faces[None], whole_faces[None])
    inner_east = column_update(tracer_mass, east_first, 0.5)
    east_final = column_flux(wide_inner, east_faces[None], whole_faces[None])
    north_final = row_flux(inner_east, north_frac)
    new_mass = row_update(column_update(tracer_mass, east_final, 1.0), north_final, 1.0)
    mass_faces = jnp.concatenate([east_mass, edge_mass], axis=2)
    new_thickness = (
        thick_here + (mass_faces[:, :, :-1] - mass_faces[:, :, 1:]) + north_differences(north_mass)
    )
    return new_mass / new_thickness[None]


def solution(mesh):
    in_specs = (
        P("tracer", None, None, "space"),
        P("tracer", None, None, "space"),
        P("tracer", None, None, "space"),
        P("tracer", None, None, "space"),
        P("tracer", None, None, "space"),
        P("tracer", None, None, "space"),
        P("tracer", None, None, "space"),
        P("space"),
    )
    out_specs = P("tracer", None, None, "space")
    return jax.shard_map(shards, mesh=mesh, in_specs=in_specs, out_specs=out_specs, check_vma=False)
```

profile of v0, /device:TPU:1, one launch (start us, length us, event | category | flops | bytes accessed | tf_op | source)
XLA Modules:
  0.0 341.4 jit_solution(5290984685331895111)
XLA Ops:
  7.2 0.8 convert_element_type.17
  8.0 1.5 maximum_select_fusion
  9.6 1.8 fusion.126
  11.4 0.5 copy.113
  11.9 2.1 collective-permute-start.4
  14.0 0.5 copy.114
  14.6 5.4 %collective-permute-start.5 = (f32[18,3,32,5]{2,0,3,1:T(8,128)S(1)}, f32[18,3,32,5]{2,0,3,1:T(8,128)S(1)}, u32[]{:S(2)}, u32[]{:S(2)}) collective-permute-start(f32[18,3,32,5]{2,0,3,1:T(8,128)S(1)} %copy.114), channel_id=1, source_target_pairs={{16,0},{32,16},{48,32},{64,48},{80,64},{96,80},{112,96},{128,112},... | collective-permute-start | bytes 103688 | tf_op jit(solution)/shard_map/ppermute | solution.py:28
  19.9 0.6 select_bitcast_fusion
  20.6 0.6 select_bitcast_fusion.2
  21.2 1.4 fusion.87
  22.6 1.1 collective-permute-done.4
  23.7 0.4 copy.108
  24.2 0.4 copy.111
  24.6 0.5 copy-done.4
  25.0 0.7 pad_maximum_fusion.5
  25.9 1.4 fusion.39
  27.4 2.2 slice_subtract_fusion
  29.6 117.4 %all-reduce.12.cloned.1.call-done = f32[3,3,32,128]{3,2,1,0:T(8,128)} async-done(((f32[3,3,32,128]{3,2,1,0:T(8,128)}), f32[3,3,32,128]{3,2,1,0:T(8,128)}) %all-reduce.12.cloned.1.call-update) | async-done | bytes 147472 | tf_op jit(solution)/shard_map/psum | solution.py:11
  147.0 1.5 slice_bitcast_fusion.2
  148.5 3.0 collective-permute-start.1
  151.5 0.7 slice_abs_fusion
  152.2 1.3 collective-permute-start
  153.5 130.4 %all-reduce.14.cloned.1.call-done = (f32[3,32,128]{2,1,0:T(8,128)}, f32[3,32,128]{2,1,0:T(8,128)}, f32[3,32,128]{2,1,0:T(8,128)}) async-done(((f32[3,32,128]{2,1,0:T(8,128)}, f32[3,32,128]{2,1,0:T(8,128)}, f32[3,32,128]{2,1,0:T(8,128)}), (f32[3,32,128]{2,1,0:T(8,128)}, f32[3,32,128]{2,1,0:T(8,128)}, f32[3,32,128]{2,1,0:T(8,128)})) %all-reduce.14.cloned.1.call-update) | async-done | bytes 147472 | tf_op jit(solution)/shard_map/psum | solution.py:11
  283.9 3.0 collective-permute-start.6
  286.9 1.4 slice.506
  288.4 0.8 fusion.119
  289.2 0.9 fusion.120
  290.2 0.9 fusion.122
  291.1 13.5 %fusion.7 = f32[18,3,32,129]{3,2,1,0:T(8,128)S(1)} fusion(f32[18,3,32,134]{3,2,1,0:T(8,128)} %get-tuple-element.9, f32[18,3,32,134]{3,2,1,0:T(8,128)S(1)} %get-tuple-element.8, f32[18,3,32,135]{3,2,1,0:T(8,128)S(1)} %fusion.39, f32[18,3,32,5]{3,2,1,0:T(8,128)} %copy-done.5, f32[18,3,32,128]{3,2,1,0:T(8,128)} %param.8, f32[18,3,32,5]{3,2,1,0:T(8,128)} %copy-done.4, ...), kind=kLoop, calls=%fused_computation.8 | loop fusion | flops 10699776 | bytes 17189280 | tf_op jit(solution)/shard_map/jit(_where)/select_n | solution.py:89
  304.7 0.5 slice_subtract_fusion.5
  305.2 0.4 fusion.92
  305.7 0.3 slice_subtract_fusion.4
  306.0 0.5 copy-done.18
  306.5 1.2 fusion.99
  307.9 0.3 fusion.127
  308.2 1.2 copy.101
  309.4 0.5 copy.103
  310.0 3.9 %collective-permute-start.3 = (f32[18,3,32,5]{2,0,3,1:T(8,128)S(1)}, f32[18,3,32,5]{2,0,3,1:T(8,128)}, u32[]{:S(2)}, u32[]{:S(2)}) collective-permute-start(f32[18,3,32,5]{2,0,3,1:T(8,128)S(1)} %copy.103), channel_id=1, source_target_pairs={{16,0},{32,16},{48,32},{64,48},{80,64},{96,80},{112,96},{128,112},... | collective-permute-start | bytes 103688 | tf_op jit(solution)/shard_map/ppermute | solution.py:28
  313.8 1.6 fusion.125
  315.5 1.4 collective-permute-done.2
  316.9 0.4 copy.102
  317.3 2.0 collective-permute-done.3
  319.3 1.3 copy.105
  320.6 0.7 pad_maximum_fusion.4
  321.4 1.4 fusion.81
  322.9 1.0 slice_subtract_fusion.1
  324.0 9.2 %fusion.49 = f32[18,3,32,129]{3,2,1,0:T(8,128)S(1)} fusion(f32[18,3,32,134]{3,2,1,0:T(8,128)S(1)} %get-tuple-element.11, f32[18,3,32,134]{3,2,1,0:T(8,128)S(1)} %get-tuple-element.10, f32[18,3,32,135]{3,2,1,0:T(8,128)S(1)} %fusion.81, f32[18,3,32,5]{3,2,1,0:T(8,128)S(1)} %copy.105, f32[18,3,32,128]{3,2,1,0:T(8,128)S(1)} %multiply_add_fusion, ...), kind=kLoop, calls=%fused_computation.61 | loop fusion | flops 10699776 | bytes 17189280 | tf_op jit(solution)/shard_map/jit(_where)/select_n | solution.py:89
  333.2 1.3 fusion.108
  (59 shorter events, 0.6 us)
Async XLA Ops:
  6.5 140.4 %all-reduce.12.cloned.1.call-start = ((), (), s32[]{:S(2)}) async-start(), calls=%async_computation | async-start | bytes 294912 | tf_op jit(solution)/shard_map/psum | solution.py:11
  9.5 274.4 %all-reduce.14.cloned.1.call-start = ((), (), s32[]{:S(2)}) async-start(), calls=%async_computation.1 | async-start | bytes 294912 | tf_op jit(solution)/shard_map/psum | solution.py:11
  11.3 8.6 %copy-start.23 = (f32[1,3,32,128]{3,2,1,0:T(8,128)S(1)}, f32[1,3,32,128]{3,2,1,0:T(8,128)}, u32[]{:S(2)}) copy-start(f32[1,3,32,128]{3,2,1,0:T(8,128)} %param.11) | copy-start | bytes 147460
  11.4 8.6 %copy-start.24 = (f32[1,3,32,128]{3,2,1,0:T(8,128)S(1)}, f32[1,3,32,128]{3,2,1,0:T(8,128)}, u32[]{:S(2)}) copy-start(f32[1,3,32,128]{3,2,1,0:T(8,128)} %param.10) | copy-start | bytes 147460
  11.4 9.2 %copy-start.22 = (f32[1,3,32,128]{3,2,1,0:T(8,128)S(1)}, f32[1,3,32,128]{3,2,1,0:T(8,128)}, u32[]{:S(2)}) copy-start(f32[1,3,32,128]{3,2,1,0:T(8,128)} %param.9) | copy-start | bytes 147460
  11.4 9.9 %copy-start = (f32[18,3,32,128]{3,2,1,0:T(8,128)S(1)}, f32[18,3,32,128]{3,2,1,0:T(8,128)}, u32[]{:S(2)}) copy-start(f32[18,3,32,128]{3,2,1,0:T(8,128)} %param.8) | copy-start | bytes 2654212
  11.9 11.8 %collective-permute-start.4 = (f32[18,3,32,5]{2,0,3,1:T(8,128)S(1)}, f32[18,3,32,5]{2,0,3,1:T(8,128)S(1)}, u32[]{:S(2)}, u32[]{:S(2)}) collective-permute-start(f32[18,3,32,5]{2,0,3,1:T(8,128)S(1)} %copy.113), channel_id=1, source_target_pairs={{0,16},{16,32},{32,48},{48,64},{64,80},{80,96},{96,112},{112,128},... | collective-permute-start | bytes 103688 | tf_op jit(solution)/shard_map/ppermute | solution.py:26
  14.6 9.6 %collective-permute-start.5 = (f32[18,3,32,5]{2,0,3,1:T(8,128)S(1)}, f32[18,3,32,5]{2,0,3,1:T(8,128)S(1)}, u32[]{:S(2)}, u32[]{:S(2)}) collective-permute-start(f32[18,3,32,5]{2,0,3,1:T(8,128)S(1)} %copy.114), channel_id=1, source_target_pairs={{16,0},{32,16},{48,32},{64,48},{80,64},{96,80},{112,96},{128,112},... | collective-permute-start | bytes 103688 | tf_op jit(solution)/shard_map/ppermute | solution.py:28
  24.1 0.9 copy-start.4
  25.0 0.9 copy-start.5
  148.5 139.9 %collective-permute-start.1 = (f32[3,32,1]{2,1,0:T(8,128)}, f32[3,32,1]{2,1,0:T(8,128)}, u32[]{:S(2)}, u32[]{:S(2)}) collective-permute-start(f32[3,32,1]{2,1,0:T(8,128)} %bitcast.13), channel_id=1, source_target_pairs={{0,240},{16,0},{32,16},{48,32},{64,48},{80,64},{96,80},{112,96},{1... | collective-permute-start | bytes 1160 | tf_op jit(solution)/shard_map/ppermute | solution.py:16
  152.2 138.0 %collective-permute-start = (f32[3,32,1]{2,1,0:T(8,128)}, f32[3,32,1]{2,1,0:T(8,128)}, u32[]{:S(2)}, u32[]{:S(2)}) collective-permute-start(f32[3,32,1]{2,1,0:T(8,128)} %bitcast.14), channel_id=1, source_target_pairs={{0,240},{16,0},{32,16},{48,32},{64,48},{80,64},{96,80},{112,96},{1... | collective-permute-start | bytes 1160 | tf_op jit(solution)/shard_map/ppermute | solution.py:16
  283.9 29.9 %collective-permute-start.6 = (f32[3,32,1]{2,1,0:T(8,128)}, f32[3,32,1]{2,1,0:T(8,128)}, u32[]{:S(2)}, u32[]{:S(2)}) collective-permute-start(f32[3,32,1]{2,1,0:T(8,128)} %bitcast.17), channel_id=1, source_target_pairs={{0,240},{16,0},{32,16},{48,32},{64,48},{80,64},{96,80},{112,96},{1... | collective-permute-start | bytes 1160 | tf_op jit(solution)/shard_map/ppermute | solution.py:16
  289.2 15.4 %copy-start.6 = (f32[3,32,129]{2,1,0:T(8,128)}, f32[3,32,129]{2,1,0:T(8,128)S(1)}, u32[]{:S(2)}) copy-start(f32[3,32,129]{2,1,0:T(8,128)S(1)} %get-tuple-element.28) | copy-start | bytes 148612
  289.2 15.4 %copy-start.8 = (f32[3,32,129]{2,1,0:T(8,128)}, f32[3,32,129]{2,1,0:T(8,128)S(1)}, u32[]{:S(2)}) copy-start(f32[3,32,129]{2,1,0:T(8,128)S(1)} %get-tuple-element.29) | copy-start | bytes 148612
  289.2 15.4 %copy-start.10 = (f32[3,32,129]{2,1,0:T(8,128)}, f32[3,32,129]{2,1,0:T(8,128)S(1)}, u32[]{:S(2)}) copy-start(f32[3,32,129]{2,1,0:T(8,128)S(1)} %get-tuple-element.30) | copy-start | bytes 148612
  290.2 14.5 %copy-start.16 = (pred[3,32,129]{2,1,0:T(8,128)(4,1)}, pred[3,32,129]{2,1,0:T(8,128)(4,1)S(1)}, u32[]{:S(2)}) copy-start(pred[3,32,129]{2,1,0:T(8,128)(4,1)S(1)} %fusion.120) | copy-start | bytes 37156
  291.1 13.6 %copy-start.12 = (pred[3,32,129]{2,1,0:T(8,128)(4,1)}, pred[3,32,129]{2,1,0:T(8,128)(4,1)S(1)}, u32[]{:S(2)}) copy-start(pred[3,32,129]{2,1,0:T(8,128)(4,1)S(1)} %get-tuple-element.26) | copy-start | bytes 37156
  291.1 13.6 %copy-start.14 = (pred[3,32,129]{2,1,0:T(8,128)(4,1)}, pred[3,32,129]{2,1,0:T(8,128)(4,1)S(1)}, u32[]{:S(2)}) copy-start(pred[3,32,129]{2,1,0:T(8,128)(4,1)S(1)} %get-tuple-element.27) | copy-start | bytes 37156
  291.1 13.6 %copy-start.1 = (f32[18,3,32,128]{3,2,1,0:T(8,128)S(1)}, f32[18,3,32,128]{3,2,1,0:T(8,128)}, u32[]{:S(2)}) copy-start(f32[18,3,32,128]{3,2,1,0:T(8,128)} %param.8) | copy-start | bytes 2654212
  291.1 13.6 %copy-start.3 = (f32[18,3,33,128]{3,2,1,0:T(8,128)S(1)}, f32[18,3,33,128]{3,2,1,0:T(8,128)}, u32[]{:S(2)}) copy-start(f32[18,3,33,128]{3,2,1,0:T(8,128)} %fusion.87) | copy-start | bytes 2737156
  305.6 0.8 copy-start.18
  305.6 0.8 copy-start.19
  305.6 0.8 copy-start.20
  309.4 7.4 %collective-permute-start.2 = (f32[18,3,32,5]{2,0,3,1:T(8,128)}, f32[18,3,32,5]{2,0,3,1:T(8,128)S(1)}, u32[]{:S(2)}, u32[]{:S(2)}) collective-permute-start(f32[18,3,32,5]{2,0,3,1:T(8,128)} %copy.101), channel_id=1, source_target_pairs={{0,16},{16,32},{32,48},{48,64},{64,80},{80,96},{96,112},{112,128},... | collective-permute-start | bytes 103688 | tf_op jit(solution)/shard_map/ppermute | solution.py:26
  310.0 9.3 %collective-permute-start.3 = (f32[18,3,32,5]{2,0,3,1:T(8,128)S(1)}, f32[18,3,32,5]{2,0,3,1:T(8,128)}, u32[]{:S(2)}, u32[]{:S(2)}) collective-permute-start(f32[18,3,32,5]{2,0,3,1:T(8,128)S(1)} %copy.103), channel_id=1, source_target_pairs={{16,0},{32,16},{48,32},{64,48},{80,64},{96,80},{112,96},{128,112},... | collective-permute-start | bytes 103688 | tf_op jit(solution)/shard_map/ppermute | solution.py:28
  322.8 1.1 copy-start.7
  322.8 1.1 copy-start.9
  322.8 1.1 copy-start.11
  322.8 1.1 copy-start.13
  322.8 1.1 copy-start.15
  322.9 1.1 copy-start.17
  323.9 9.3 %copy-start.2 = (f32[18,3,32,128]{3,2,1,0:T(8,128)S(1)}, f32[18,3,32,128]{3,2,1,0:T(8,128)}, u32[]{:S(2)}) copy-start(f32[18,3,32,128]{3,2,1,0:T(8,128)} %param.8) | copy-start | bytes 2654212
  323.9 9.3 %copy-start.21 = (f32[3,32,128]{2,1,0:T(8,128)S(1)}, f32[3,32,128]{2,1,0:T(8,128)}, u32[]{:S(2)}) copy-start(f32[3,32,128]{2,1,0:T(8,128)} %fusion.125) | copy-start | bytes 147460
Sparse Core Ops, SparseCore 0:
  10.0 136.9 all-reduce.11
  150.0 133.8 all-reduce.13
where the time goes:
time: 342 us; the launch traced here: 341 us
  waiting for transfers between devices  252 us (74%)
  other arithmetic  44.1 us (13%)
  starting transfers between devices  18.7 us (5%)
  between operations  14.5 us (4%)
  local copies, waits for them, and re-layouts  11.6 us (3%)
    psum x2, waiting for transfers between devices, from_root(): return lax.psum(jnp.where(mine, x, jnp.zeros_like(x)), axis)  248 us
    select_n x2, other arithmetic, face_flux(): flux_total = jnp.where(whole_cells == shift_count, candidate, flux_total)  22.8 us
    ppermute x2, starting transfers between devices, extended_2(): lax.ppermute(head, axis, [((i + 1) % count, i) for i in range(count)])  9.24 us
    ppermute x3, starting transfers between devices, passed_along(): return lax.ppermute(x, axis, [(i, (i + by) % size) for i in range(size)])  7.33 us
  transfers between devices with their start and end apart: 9, of which 5 were waited for; matrix products, arithmetic and copies ran while one was open for 11% of the time, Pallas kernels for 0%

commit v1 on v0

v1 whole, which is shorter than its diff:
```python
import functools

import jax
import jax.numpy as jnp
from jax import lax
from jax.experimental import pallas as pl
from jax.experimental.pallas import tpu as pltpu
from jax.sharding import PartitionSpec as P

NS = 2
EDGE = NS + 3
SEG = 2 * EDGE
PACK = 9
GROUP = 3
MET_SEG = 16


def lane_index(shape):
    return lax.broadcasted_iota(jnp.int32, shape, len(shape) - 1)


def row_index(shape):
    return lax.broadcasted_iota(jnp.int32, shape, len(shape) - 2)


def lanes(x, shift):
    return pltpu.roll(x, shift % x.shape[-1], x.ndim - 1)


def rows(x, shift):
    return pltpu.roll(x, shift % x.shape[-2], x.ndim - 2)


def face_weights(courant):
    fraction = jnp.abs(courant)
    ramp = 1.5 * fraction * (1.0 - 2.0 / 3.0 * fraction)
    near = 0.5 * courant * (1.0 - 0.5 * fraction - ramp)
    far = 0.5 * courant * (0.5 * fraction - ramp)
    mean = courant * ramp
    far_outer = far * (1.0 / 12.0)
    near_outer = near * (1.0 / 12.0)
    return (
        -near_outer,
        7.0 * near_outer - far_outer,
        7.0 * (near_outer + far_outer) + mean,
        7.0 * far_outer - near_outer,
        -far_outer,
    )


def north_taps(courant):
    down1, up0, up1, up2, up3 = (w for w in face_weights(courant))
    forward = courant >= 0.0
    zero = jnp.zeros_like(courant)
    f = {1: down1, 0: up0, -1: up1, -2: up2, -3: up3}
    b = {-2: down1, -1: up0, 0: up1, 1: up2, 2: up3}
    return {m: jnp.where(forward, f.get(m, zero), b.get(m, zero)) for m in range(-3, 3)}


def east_taps(courant, whole):
    weights = face_weights(courant)
    forward = courant >= 0.0
    zero = jnp.zeros_like(courant)
    one = whole == 1.0
    two = whole == 2.0
    some = whole > 0.5
    taps = {}
    for m in range(-EDGE, EDGE):
        ahead = []
        behind = []
        for n in range(NS + 1):
            place = 1 - n - m
            ahead.append(weights[place] if 0 <= place < 5 else zero)
            place = m + 2 - n
            behind.append(weights[place] if 0 <= place < 5 else zero)
        f = jnp.where(two, ahead[2], jnp.where(one, ahead[1], ahead[0]))
        b = jnp.where(two, behind[2], jnp.where(one, behind[1], behind[0]))
        if m == -1:
            f = f + jnp.where(some, 0.5, 0.0)
        if m == -2:
            f = f + jnp.where(two, 0.5, 0.0)
        if m == 0:
            b = b - jnp.where(some, 0.5, 0.0)
        if m == 1:
            b = b - jnp.where(two, 0.5, 0.0)
        taps[m] = jnp.where(forward, f, b)
    return taps


def difference_taps(here, ahead, reach):
    out = {}
    for m in range(-reach, reach + 1):
        if m in here and m - 1 in ahead:
            out[m] = here[m] - ahead[m - 1]
        elif m in here:
            out[m] = here[m]
        else:
            out[m] = -ahead[m - 1]
    return out


def north_coefficients(courant):
    count = courant.shape[0]
    row = row_index(courant.shape)
    here = jnp.where(row == 0, 0.0, courant)
    ahead = rows(here, -1)
    taps = difference_taps(north_taps(here), north_taps(ahead), 3)
    return [
        jnp.where((row + m >= 0) & (row + m < count), taps[m], 0.0) for m in range(-3, 4)
    ]


def repeated(x):
    one = jnp.where(lane_index(x.shape) < SEG, x, 0.0)
    two = one + lanes(one, SEG)
    four = two + lanes(two, 2 * SEG)
    eight = four + lanes(four, 4 * SEG)
    return eight + lanes(one, 8 * SEG)


def prepare_kernel(ids, thick, fe, fn, ce, cn, ne, mass, parts, cells):
    owned = ids[0] == ids[1]
    core = ids[1] % 2
    levels, count, width = thick.shape[1:]
    lane = lane_index((count, width))
    row = row_index((count, width))
    edge_rows = jnp.zeros((count, width), jnp.float32)
    for l in range(levels):
        east_mass = fe[0, l]
        north_mass = jnp.where(row == 0, 0.0, fn[0, l])
        thickness = (
            thick[0, l]
            + (east_mass - jnp.where(lane == width - 1, 0.0, lanes(east_mass, -1)))
            + (north_mass - rows(north_mass, -1))
        )
        whole = ne[0, l].astype(jnp.float32)
        first = (thickness, ce[0, l])
        second = (cn[0, l], whole)
        for half, pair in enumerate((first, second)):
            for k, value in enumerate(pair):
                start = (k * levels + l) * count
                parts[(half + core) % 2, start : start + count, :] = jnp.where(owned, value, 0.0)
        edges = jnp.where(lane < SEG, lanes(cn[0, l], EDGE), 0.0)
        for k, value in enumerate((ce[0, l], whole, east_mass)):
            edges = jnp.where(lane == SEG + k, lanes(value, SEG + k), edges)
        edge_rows = edge_rows + lanes(jnp.where(lane < MET_SEG, edges, 0.0), MET_SEG * l)
    edge_rows = jnp.where(owned, edge_rows, 0.0)
    base = 2 * levels * count
    parts[0, base : base + count, :] = edge_rows
    parts[1, base : base + count, :] = edge_rows
    for half in range(2):
        for l in range(levels):
            packed = jnp.zeros((count, width), jnp.float32)
            for k in range(PACK):
                value = lanes(mass[half * PACK + k, l], EDGE + SEG * k)
                inside = (lane >= SEG * k) & (lane < SEG * (k + 1))
                packed = jnp.where(inside, value, packed)
            cells[half, l] = packed


def prepare(ids, thick, fe, fn, ce, cn, ne, mass):
    tracers, levels, count, width = mass.shape
    vmem = pl.BlockSpec(memory_space=pltpu.VMEM)
    return pl.pallas_call(
        prepare_kernel,
        out_shape=(
            jax.ShapeDtypeStruct((2, 2 * levels * count + count, width), jnp.float32),
            jax.ShapeDtypeStruct((2, levels, count, width), jnp.float32),
        ),
        in_specs=[pl.BlockSpec(memory_space=pltpu.SMEM)] + [vmem] * 7,
        out_specs=(vmem, vmem),
        name="prepare",
    )(ids, thick, fe, fn, ce, cn, ne, mass)


PAD = 8


def transport_kernel(
    ids, mine, other, met_west, met_east, cells_west, cells_east, mass, out,
    east_c, north_c, inverse, packed_first, packed_final, padded, middle,
):
    levels, count, width = mass.shape[1:]
    lane = lane_index((count, width))
    row = row_index((count, width))
    low = ids[1] % 2 == 0
    in_segment = lane % SEG
    packed_lane = lane < SEG * PACK
    zero_rows = jnp.zeros((PAD, width), jnp.float32)
    for buffer in (padded, middle):
        for g in range(2 * GROUP):
            if g < buffer.shape[0]:
                buffer[g, :PAD, :] = zero_rows
                buffer[g, PAD + count :, :] = zero_rows
    for l in range(levels):
        fields = []
        for half in range(2):
            for k in range(2):
                start = (k * levels + l) * count
                a = mine[start : start + count, :]
                b = other[start : start + count, :]
                fields.append(jnp.where(low, a, b) if half == 0 else jnp.where(low, b, a))
        thickness, east, north, whole = fields
        from_west = lanes(met_west[:, :], -MET_SEG * l)
        from_east = lanes(met_east[:, :], -MET_SEG * l)

        def next_face(value, k):
            return jnp.where(
                lane == width - 1, lanes(from_east, width - 1 - SEG - k), lanes(value, -1)
            )

        next_east = next_face(east, 0)
        next_whole = next_face(whole, 1)
        edge_mass = jnp.where(lane == width - 1, lanes(from_east, width - 1 - SEG - 2), 0.0)
        inverse[l] = 2.0 / (thickness - edge_mass)
        taps = difference_taps(east_taps(east, whole), east_taps(next_east, next_whole), EDGE)
        for m in range(-EDGE, EDGE + 1):
            value = taps[m]
            if m < 0:
                value = jnp.where(lane >= -m, value, 0.0)
            if m > 0:
                value = jnp.where(lane < width - m, value, 0.0)
            east_c[m + EDGE, l] = value
        for m, value in enumerate(north_coefficients(north)):
            north_c[m, l] = value

        packed_north = repeated(jnp.where(lane < EDGE, from_west, from_east))
        packed_east = [
            repeated(lanes(v, EDGE)) for v in (east, whole, next_east, next_whole)
        ]
        taps = difference_taps(
            east_taps(packed_east[0], packed_east[1]),
            east_taps(packed_east[2], packed_east[3]),
            EDGE,
        )
        outer = {}
        for m in range(-EDGE, EDGE + 1):
            if m != 0:
                crosses = ((in_segment < EDGE) != (in_segment + m < EDGE)) & packed_lane
                outer[m] = jnp.where(crosses, taps[m], 0.0)
        packed_taps = north_coefficients(packed_north)
        for half in range(2):
            cells = jnp.where(in_segment < EDGE, cells_west[half, l], cells_east[half, l])
            inner = cells
            for m in range(-3, 4):
                inner = inner + packed_taps[m + 3] * rows(cells, -m)
            first = jnp.zeros_like(cells)
            final = jnp.zeros_like(cells)
            for m in outer:
                first = first + outer[m] * lanes(cells, -m)
                final = final + outer[m] * lanes(inner, -m)
            packed_first[half, l] = first
            packed_final[half, l] = final

    at_edge = (lane < EDGE) | (lane >= width - EDGE)

    def group(step, carry):
        l = step % levels
        tg = step // levels
        t0 = tg * GROUP
        half = t0 // PACK
        zero = jnp.zeros((GROUP, count, width), jnp.float32)
        value = mass[pl.ds(t0, GROUP), pl.ds(l, 1)].reshape(GROUP, count, width)
        for j in range(GROUP):
            padded[j, PAD : PAD + count, :] = value[j]

        def edges(ref):
            parts = []
            for j in range(GROUP):
                k = t0 + j - half * PACK
                moved = pltpu.roll(ref[half, l], width - EDGE - SEG * k, 1)
                parts.append(jnp.where(at_edge, moved, 0.0))
            return jnp.stack(parts)

        def east_sum(start, x):
            flat = x.reshape(GROUP * count, width)
            total = start
            for m in range(-EDGE, EDGE + 1):
                moved = x if m == 0 else lanes(flat, -m).reshape(GROUP, count, width)
                total = total + east_c[m + EDGE, l][None] * moved
            return total

        def north_sum(start, ref):
            total = start
            for m in range(-3, 4):
                total = total + north_c[m + 3, l][None] * ref[:, PAD + m : PAD + m + count, :]
            return total

        inner_east = east_sum(value + edges(packed_first), value)
        middle[:, PAD : PAD + count, :] = inner_east
        inner_north = north_sum(value, padded)
        total = east_sum(0.5 * value + edges(packed_final), inner_north)
        total = north_sum(total, middle)
        result = total * inverse[l][None]
        out[pl.ds(t0, GROUP), pl.ds(l, 1)] = result.reshape(GROUP, 1, count, width)
        return carry

    lax.fori_loop(0, levels * (mass.shape[0] // GROUP), group, 0)


def transport(ids, mine, other, met_west, met_east, cells_west, cells_east, mass):
    tracers, levels, count, width = mass.shape
    vmem = pl.BlockSpec(memory_space=pltpu.VMEM)
    return pl.pallas_call(
        transport_kernel,
        out_shape=jax.ShapeDtypeStruct(mass.shape, jnp.float32),
        in_specs=[pl.BlockSpec(memory_space=pltpu.SMEM)] + [vmem] * 7,
        out_specs=vmem,
        scratch_shapes=[
            pltpu.VMEM((2 * EDGE + 1, levels, count, width), jnp.float32),
            pltpu.VMEM((7, levels, count, width), jnp.float32),
            pltpu.VMEM((levels, count, width), jnp.float32),
            pltpu.VMEM((2, levels, count, width), jnp.float32),
            pltpu.VMEM((2, levels, count, width), jnp.float32),
            pltpu.VMEM((GROUP, count + 2 * PAD, width), jnp.float32),
            pltpu.VMEM((GROUP, count + 2 * PAD, width), jnp.float32),
        ],
        compiler_params=pltpu.CompilerParams(vmem_limit_bytes=32 * 1024 * 1024),
        name="transport",
    )(ids, mine, other, met_west, met_east, cells_west, cells_east, mass)


def ring(x, by):
    size = lax.axis_size("space")
    return lax.ppermute(x, "space", [(i, (i + by) % size) for i in range(size)])


def exchange(x, flip):
    size = lax.axis_size("tracer")
    return lax.ppermute(x, "tracer", [(i, i ^ flip) for i in range(size)])


def shards(thickness_args, mass, dynamics_owner):
    thick, fe, fn, ce, cn, ne = thickness_args
    me = lax.axis_index("tracer")
    ids = jnp.stack([dynamics_owner[0], me]).astype(jnp.int32)
    parts, cells = prepare(ids, thick, fe, fn, ce, cn, ne, mass)
    main = 2 * mass.shape[1] * mass.shape[2]
    total = parts[0] + exchange(parts[1], 1)
    for flip in (2, 6, 8):
        total = total + exchange(total, flip)
    cells_west = ring(cells, 1)
    cells_east = ring(cells, -1)
    mine = total[:main]
    edges = total[main:]
    met_west = ring(edges, 1)
    met_east = ring(edges, -1)
    other = exchange(mine, 1)
    return transport(ids, mine, other, met_west, met_east, cells_west, cells_east, mass)


def solution(mesh):
    spec = P("tracer", None, None, "space")

    def run(mass, thick, fe, fn, ce, cn, ne, owner):
        return shards((thick, fe, fn, ce, cn, ne), mass, owner)

    return jax.shard_map(
        run, mesh=mesh, in_specs=(spec,) * 7 + (P("space"),), out_specs=spec, check_vma=False
    )
```

time: 342 us -> 49.3 us (0.14)
  waiting for transfers between devices: 252 us -> 13.9 us
  other arithmetic: 44.1 us -> 0.72 us
  Pallas kernels: 0 us -> 13.8 us
  between operations: 14.5 us -> 0.72 us
  local copies, waits for them, and re-layouts: 11.6 us -> 1.02 us
    psum x2 -> x0, waiting for transfers between devices: 248 us -> none  [from_root(): return lax.psum(jnp.where(mine, x, jnp.zeros_like(x)), axis)]
    select_n x6 -> x0, other arithmetic: 26.7 us -> none  [the longest x2 22.8 us: face_flux(): flux_total = jnp.where(whole_cells == shift_count, candidate, flux_total)]
    pallas_call x0 -> x2, Pallas kernels: none -> 13.8 us  [the longest x1 11.4 us: transport(): pl.pallas_call(transport_kernel, out_shape=jax.ShapeDtypeStruct(mass.shap...]
    ppermute x7 -> x9, waiting for transfers between devices: 4.55 us -> 13.9 us  [the longest x5 9.18 us: exchange(): return lax.ppermute(x, 'tracer', [(i, i ^ flip) for i in range(size)])]
    div x5 -> x0, other arithmetic: 5.95 us -> none  [the longest x4 4.62 us: parabola_parts(): (7.0 * (take_slice(extended, 1, length - 2, along) + take_slice(extended,...]
    slice x5 -> x2, local copies, waits for them, and re-layouts: 5.26 us -> 0.01 us  [the longest x1 0.01 us: shards(): mine = total[:main]]
    sub x4 -> x0, other arithmetic: 3.98 us -> none  [parabola_parts(): return (left_edge, right_edge, right_edge - left_edge, curvature)]
    ppermute x7 -> x9, starting transfers between devices: 18.7 us -> 19.1 us  [the longest x4 10.6 us: ring(): return lax.ppermute(x, 'space', [(i, (i + by) % size) for i in range(size)])]
  transfers between devices with their start and end apart: 9 -> 9, of which waited for: 5 -> 5; matrix products, arithmetic and copies ran while one was open for 11% -> 0% of each run, Pallas kernels for 0% -> 0%
where the time goes in v1:
time: 49.3 us; the launch traced here: 49.1 us
  starting transfers between devices  19.1 us (39%)
  waiting for transfers between devices  13.9 us (28%)
  Pallas kernels  13.8 us (28%)
  local copies, waits for them, and re-layouts  1.02 us (2%)
  other arithmetic  0.72 us (1%)
  between operations  0.72 us (1%)
    pallas_call x1, Pallas kernels, transport(): pl.pallas_call(transport_kernel, out_shape=jax.ShapeDtypeStruct(mass.shap...  11.4 us
    ppermute x4, starting transfers between devices, ring(): return lax.ppermute(x, 'space', [(i, (i + by) % size) for i in range(size)])  10.6 us
    ppermute x5, waiting for transfers between devices, exchange(): return lax.ppermute(x, 'tracer', [(i, i ^ flip) for i in range(size)])  9.18 us
    ppermute x5, starting transfers between devices, exchange(): return lax.ppermute(x, 'tracer', [(i, i ^ flip) for i in range(size)])  8.5 us
    ppermute x4, waiting for transfers between devices, ring(): return lax.ppermute(x, 'space', [(i, (i + by) % size) for i in range(size)])  4.69 us
    pallas_call x1, Pallas kernels, prepare(): pl.pallas_call(prepare_kernel, out_shape=(jax.ShapeDtypeStruct((2, 2 * le...  2.4 us
    squeeze x1, local copies, waits for them, and re-layouts, shards(): total = parts[0] + exchange(parts[1], 1)  1 us
  transfers between devices with their start and end apart: 9, of which 5 were waited for; matrix products, arithmetic and copies ran while one was open for 0% of the time, Pallas kernels for 0%

profile of v1, /device:TPU:1, one launch (start us, length us, event | category | flops | bytes accessed | tf_op | source)
XLA Modules:
  0.0 49.1 jit_solution(591852371085572646)
XLA Ops:
  0.7 0.7 %pad_add_fusion.ids = s32[2]{0:T(128)} fusion(s32[1]{0:T(128)} %bitcast, s32[1]{0:T(128)S(6)} %copy.9), kind=kLoop, calls=%fused_computation.2 | loop fusion | flops 2 | bytes 16 | tf_op jit(solution)/shard_map/stack | solution.py:336
  1.3 2.4 %prepare.1 = (f32[2,224,128]{2,1,0:T(8,128)}, f32[2,3,32,128]{3,2,1,0:T(8,128)}) custom-call(s32[2]{0:T(128)} %pad_add_fusion.ids, f32[1,3,32,128]{3,2,1,0:T(8,128)} %thick.1, f32[1,3,32,128]{3,2,1,0:T(8,128)} %fe.1, f32[1,3,32,128]{3,2,1,0:T(8,128)} %fn.1, f32[1,3,32,128]{3,2,1,0:T(8,128)} %ce.1, f32[1,3,32,128]{3,2,1,0:T(8,128)} %cn.1, ...), custom_call_target="tpu_custom_call" | custom-call | tf_op jit(solution)/shard_map/prepare/pallas_call | solution.py:164
  3.7 0.0 copy-start.2
  3.7 0.0 copy-start
  3.7 1.0 %slice_bitcast_fusion = f32[224,128]{1,0:T(8,128)S(1)} fusion(f32[2,224,128]{2,1,0:T(8,128)} %get-tuple-element.7), kind=kLoop, calls=%fused_computation.1 | loop fusion | bytes 229376 | tf_op jit(solution)/shard_map/squeeze | solution.py:339
  4.7 3.2 %collective-permute-start = (f32[224,128]{1,0:T(8,128)S(1)}, f32[224,128]{1,0:T(8,128)S(1)}, u32[]{:S(2)}, u32[]{:S(2)}) collective-permute-start(f32[224,128]{1,0:T(8,128)S(1)} %slice_bitcast_fusion), channel_id=1, source_target_pairs={{0,1},{1,0},{2,3},{3,2},{4,5},{5,4},{6,7},{7,6},{8,9},{9,8},{10,11... | collective-permute-start | bytes 344072 | tf_op jit(solution)/shard_map/ppermute | solution.py:330
  8.0 1.0 %collective-permute-done = f32[224,128]{1,0:T(8,128)S(1)} collective-permute-done((f32[224,128]{1,0:T(8,128)S(1)}, f32[224,128]{1,0:T(8,128)S(1)}, u32[]{:S(2)}, u32[]{:S(2)}) %collective-permute-start) | collective-permute-done | bytes 114720 | tf_op jit(solution)/shard_map/ppermute | solution.py:330
  8.9 0.0 copy-done.2
  8.9 0.1 collective-permute-start.1
  9.0 4.4 %collective-permute-done.1 = f32[224,128]{1,0:T(8,128)S(1)} collective-permute-done((f32[224,128]{1,0:T(8,128)S(1)}, f32[224,128]{1,0:T(8,128)S(1)}, u32[]{:S(2)}, u32[]{:S(2)}) %collective-permute-start.1) | collective-permute-done | bytes 114720 | tf_op jit(solution)/shard_map/ppermute | solution.py:330
  13.4 0.0 copy-start.3
  13.4 1.1 %collective-permute-start.2 = (f32[224,128]{1,0:T(8,128)S(1)}, f32[224,128]{1,0:T(8,128)S(1)}, u32[]{:S(2)}, u32[]{:S(2)}) collective-permute-start(f32[224,128]{1,0:T(8,128)S(1)} %add.13), channel_id=1, source_target_pairs={{0,6},{1,7},{2,4},{3,5},{4,2},{5,3},{6,0},{7,1},{8,14},{9,15},{10,... | collective-permute-start | bytes 344072 | tf_op jit(solution)/shard_map/ppermute | solution.py:330
  14.5 3.9 %collective-permute-done.2 = f32[224,128]{1,0:T(8,128)S(1)} collective-permute-done((f32[224,128]{1,0:T(8,128)S(1)}, f32[224,128]{1,0:T(8,128)S(1)}, u32[]{:S(2)}, u32[]{:S(2)}) %collective-permute-start.2) | collective-permute-done | bytes 114720 | tf_op jit(solution)/shard_map/ppermute | solution.py:330
  18.4 1.2 %collective-permute-start.3 = (f32[224,128]{1,0:T(8,128)S(1)}, f32[224,128]{1,0:T(8,128)S(1)}, u32[]{:S(2)}, u32[]{:S(2)}) collective-permute-start(f32[224,128]{1,0:T(8,128)S(1)} %add.14), channel_id=1, source_target_pairs={{0,8},{1,9},{2,10},{3,11},{4,12},{5,13},{6,14},{7,15},{8,0},{9,1},... | collective-permute-start | bytes 344072 | tf_op jit(solution)/shard_map/ppermute | solution.py:330
  19.5 0.0 copy-done.3
  19.6 5.6 %collective-permute-start.8 = (f32[2,3,32,128]{3,2,1,0:T(8,128)S(1)}, f32[2,3,32,128]{3,2,1,0:T(8,128)S(1)}, u32[]{:S(2)}, u32[]{:S(2)}) collective-permute-start(f32[2,3,32,128]{3,2,1,0:T(8,128)S(1)} %copy-done.3), channel_id=1, source_target_pairs={{0,240},{16,0},{32,16},{48,32},{64,48},{80,64},{96,80},{112,96},{1... | collective-permute-start | bytes 294920 | tf_op jit(solution)/shard_map/ppermute | solution.py:325
  25.2 0.0 collective-permute-start.7
  25.2 0.0 collective-permute-done.3
  25.2 0.0 copy-start.1
  25.2 2.9 %collective-permute-start.4 = (f32[192,128]{1,0:T(8,128)S(1)}, f32[192,128]{1,0:T(8,128)S(1)}, u32[]{:S(2)}, u32[]{:S(2)}) collective-permute-start(f32[192,128]{1,0:T(8,128)S(1)} %slice.16.mine), channel_id=1, source_target_pairs={{0,1},{1,0},{2,3},{3,2},{4,5},{5,4},{6,7},{7,6},{8,9},{9,8},{10,11... | collective-permute-start | bytes 294920 | tf_op jit(solution)/shard_map/ppermute | solution.py:330
  28.1 5.0 %collective-permute-start.6 = (f32[32,128]{1,0:T(8,128)S(1)}, f32[32,128]{1,0:T(8,128)S(1)}, u32[]{:S(2)}, u32[]{:S(2)}) collective-permute-start(f32[32,128]{1,0:T(8,128)S(1)} %slice.17), channel_id=1, source_target_pairs={{0,240},{16,0},{32,16},{48,32},{64,48},{80,64},{96,80},{112,96},{1... | collective-permute-start | bytes 49160 | tf_op jit(solution)/shard_map/ppermute | solution.py:325
  33.1 0.0 collective-permute-start.5
  33.1 0.0 collective-permute-done.8.cells_east
  33.1 0.0 collective-permute-done.7.cells_west
  33.1 0.9 %collective-permute-done.6.met_east = f32[32,128]{1,0:T(8,128)S(1)} collective-permute-done((f32[32,128]{1,0:T(8,128)S(1)}, f32[32,128]{1,0:T(8,128)S(1)}, u32[]{:S(2)}, u32[]{:S(2)}) %collective-permute-start.6) | collective-permute-done | bytes 16416 | tf_op jit(solution)/shard_map/ppermute | solution.py:325
  34.0 3.8 %collective-permute-done.5.met_west = f32[32,128]{1,0:T(8,128)S(1)} collective-permute-done((f32[32,128]{1,0:T(8,128)S(1)}, f32[32,128]{1,0:T(8,128)S(1)}, u32[]{:S(2)}, u32[]{:S(2)}) %collective-permute-start.5) | collective-permute-done | bytes 16416 | tf_op jit(solution)/shard_map/ppermute | solution.py:325
  37.8 0.0 collective-permute-done.4.other
  37.8 0.0 copy-done
  37.8 0.0 copy-done.1
  37.8 11.4 %transport.1 = f32[18,3,32,128]{3,2,1,0:T(8,128)} custom-call(s32[2]{0:T(128)S(1)} %copy-done.1, f32[192,128]{1,0:T(8,128)S(1)} %slice.16.mine, f32[192,128]{1,0:T(8,128)S(1)} %collective-permute-done.4.other, f32[32,128]{1,0:T(8,128)S(1)} %collective-permute-done.5.met_west, f32[32,128]{1,0:T(8,128)S(1)} %collective-permute-done.6.met_east, ...), custom_call_target="tpu_custom_call" | custom-call | tf_op jit(solution)/shard_map/transport/pallas_call | solution.py:304
  (6 shorter events, 0.1 us)
Async XLA Ops:
  3.7 5.2 %copy-start.2 = (f32[2,224,128]{2,1,0:T(8,128)S(1)}, f32[2,224,128]{2,1,0:T(8,128)}, u32[]{:S(2)}) copy-start(f32[2,224,128]{2,1,0:T(8,128)} %get-tuple-element.7) | copy-start | bytes 688132
  3.7 34.1 %copy-start = (f32[18,3,32,128]{3,2,1,0:T(8,128)S(1)}, f32[18,3,32,128]{3,2,1,0:T(8,128)}, u32[]{:S(2)}) copy-start(f32[18,3,32,128]{3,2,1,0:T(8,128)} %mass.3) | copy-start | bytes 2654212
  4.7 4.2 %collective-permute-start = (f32[224,128]{1,0:T(8,128)S(1)}, f32[224,128]{1,0:T(8,128)S(1)}, u32[]{:S(2)}, u32[]{:S(2)}) collective-permute-start(f32[224,128]{1,0:T(8,128)S(1)} %slice_bitcast_fusion), channel_id=1, source_target_pairs={{0,1},{1,0},{2,3},{3,2},{4,5},{5,4},{6,7},{7,6},{8,9},{9,8},{10,11... | collective-permute-start | bytes 344072 | tf_op jit(solution)/shard_map/ppermute | solution.py:330
  8.9 4.5 %collective-permute-start.1 = (f32[224,128]{1,0:T(8,128)S(1)}, f32[224,128]{1,0:T(8,128)S(1)}, u32[]{:S(2)}, u32[]{:S(2)}) collective-permute-start(f32[224,128]{1,0:T(8,128)S(1)} %bitcast_add_fusion), channel_id=1, source_target_pairs={{0,2},{1,3},{2,0},{3,1},{4,6},{5,7},{6,4},{7,5},{8,10},{9,11},{10,... | collective-permute-start | bytes 344072 | tf_op jit(solution)/shard_map/ppermute | solution.py:330
  13.4 6.1 %copy-start.3 = (f32[2,3,32,128]{3,2,1,0:T(8,128)S(1)}, f32[2,3,32,128]{3,2,1,0:T(8,128)}, u32[]{:S(2)}) copy-start(f32[2,3,32,128]{3,2,1,0:T(8,128)} %get-tuple-element.8) | copy-start | bytes 294916
  13.4 4.9 %collective-permute-start.2 = (f32[224,128]{1,0:T(8,128)S(1)}, f32[224,128]{1,0:T(8,128)S(1)}, u32[]{:S(2)}, u32[]{:S(2)}) collective-permute-start(f32[224,128]{1,0:T(8,128)S(1)} %add.13), channel_id=1, source_target_pairs={{0,6},{1,7},{2,4},{3,5},{4,2},{5,3},{6,0},{7,1},{8,14},{9,15},{10,... | collective-permute-start | bytes 344072 | tf_op jit(solution)/shard_map/ppermute | solution.py:330
  18.4 6.8 %collective-permute-start.3 = (f32[224,128]{1,0:T(8,128)S(1)}, f32[224,128]{1,0:T(8,128)S(1)}, u32[]{:S(2)}, u32[]{:S(2)}) collective-permute-start(f32[224,128]{1,0:T(8,128)S(1)} %add.14), channel_id=1, source_target_pairs={{0,8},{1,9},{2,10},{3,11},{4,12},{5,13},{6,14},{7,15},{8,0},{9,1},... | collective-permute-start | bytes 344072 | tf_op jit(solution)/shard_map/ppermute | solution.py:330
  19.6 13.5 %collective-permute-start.8 = (f32[2,3,32,128]{3,2,1,0:T(8,128)S(1)}, f32[2,3,32,128]{3,2,1,0:T(8,128)S(1)}, u32[]{:S(2)}, u32[]{:S(2)}) collective-permute-start(f32[2,3,32,128]{3,2,1,0:T(8,128)S(1)} %copy-done.3), channel_id=1, source_target_pairs={{0,240},{16,0},{32,16},{48,32},{64,48},{80,64},{96,80},{112,96},{1... | collective-permute-start | bytes 294920 | tf_op jit(solution)/shard_map/ppermute | solution.py:325
  25.2 7.9 %collective-permute-start.7 = (f32[2,3,32,128]{3,2,1,0:T(8,128)S(1)}, f32[2,3,32,128]{3,2,1,0:T(8,128)S(1)}, u32[]{:S(2)}, u32[]{:S(2)}) collective-permute-start(f32[2,3,32,128]{3,2,1,0:T(8,128)S(1)} %copy-done.3), channel_id=1, source_target_pairs={{0,16},{16,32},{32,48},{48,64},{64,80},{80,96},{96,112},{112,128},... | collective-permute-start | bytes 294920 | tf_op jit(solution)/shard_map/ppermute | solution.py:325
  25.2 12.6 %copy-start.1 = (s32[2]{0:T(128)S(1)}, s32[2]{0:T(128)}, u32[]{:S(2)}) copy-start(s32[2]{0:T(128)} %pad_add_fusion.ids) | copy-start | bytes 28
  25.2 12.6 %collective-permute-start.4 = (f32[192,128]{1,0:T(8,128)S(1)}, f32[192,128]{1,0:T(8,128)S(1)}, u32[]{:S(2)}, u32[]{:S(2)}) collective-permute-start(f32[192,128]{1,0:T(8,128)S(1)} %slice.16.mine), channel_id=1, source_target_pairs={{0,1},{1,0},{2,3},{3,2},{4,5},{5,4},{6,7},{7,6},{8,9},{9,8},{10,11... | collective-permute-start | bytes 294920 | tf_op jit(solution)/shard_map/ppermute | solution.py:330
  28.1 5.8 %collective-permute-start.6 = (f32[32,128]{1,0:T(8,128)S(1)}, f32[32,128]{1,0:T(8,128)S(1)}, u32[]{:S(2)}, u32[]{:S(2)}) collective-permute-start(f32[32,128]{1,0:T(8,128)S(1)} %slice.17), channel_id=1, source_target_pairs={{0,240},{16,0},{32,16},{48,32},{64,48},{80,64},{96,80},{112,96},{1... | collective-permute-start | bytes 49160 | tf_op jit(solution)/shard_map/ppermute | solution.py:325
  33.1 4.7 %collective-permute-start.5 = (f32[32,128]{1,0:T(8,128)S(1)}, f32[32,128]{1,0:T(8,128)S(1)}, u32[]{:S(2)}, u32[]{:S(2)}) collective-permute-start(f32[32,128]{1,0:T(8,128)S(1)} %slice.17), channel_id=1, source_target_pairs={{0,16},{16,32},{32,48},{48,64},{64,80},{80,96},{96,112},{112,128},... | collective-permute-start | bytes 49160 | tf_op jit(solution)/shard_map/ppermute | solution.py:325

commit v2 on v1

v2 whole, which is shorter than its diff:
```python
import jax
import jax.numpy as jnp
from jax import lax
from jax.experimental import pallas as pl
from jax.experimental.pallas import tpu as pltpu
from jax.sharding import PartitionSpec as P

NS = 2
EDGE = NS + 3
SEG = 2 * EDGE
PACK = 9
STEP = 4
GROUP = 3
PAD = 8
BLOCK = 8
MET_SEG = 16


def lane_index(shape):
    return lax.broadcasted_iota(jnp.int32, shape, len(shape) - 1)


def row_index(shape):
    return lax.broadcasted_iota(jnp.int32, shape, len(shape) - 2)


def lanes(x, shift):
    return pltpu.roll(x, shift % x.shape[-1], x.ndim - 1)


def rows(x, shift):
    return pltpu.roll(x, shift % x.shape[-2], x.ndim - 2)


def face_weights(courant):
    fraction = jnp.abs(courant)
    ramp = 1.5 * fraction * (1.0 - 2.0 / 3.0 * fraction)
    near = 0.5 * courant * (1.0 - 0.5 * fraction - ramp)
    far = 0.5 * courant * (0.5 * fraction - ramp)
    mean = courant * ramp
    far_outer = far * (1.0 / 12.0)
    near_outer = near * (1.0 / 12.0)
    return (
        -near_outer,
        7.0 * near_outer - far_outer,
        7.0 * (near_outer + far_outer) + mean,
        7.0 * far_outer - near_outer,
        -far_outer,
    )


def north_taps(courant):
    down1, up0, up1, up2, up3 = (w for w in face_weights(courant))
    forward = courant >= 0.0
    zero = jnp.zeros_like(courant)
    f = {1: down1, 0: up0, -1: up1, -2: up2, -3: up3}
    b = {-2: down1, -1: up0, 0: up1, 1: up2, 2: up3}
    return {m: jnp.where(forward, f.get(m, zero), b.get(m, zero)) for m in range(-3, 3)}


def east_taps(courant, whole):
    weights = face_weights(courant)
    forward = courant >= 0.0
    zero = jnp.zeros_like(courant)
    one = whole == 1.0
    two = whole == 2.0
    some = whole > 0.5
    taps = {}
    for m in range(-EDGE, EDGE):
        ahead = []
        behind = []
        for n in range(NS + 1):
            place = 1 - n - m
            ahead.append(weights[place] if 0 <= place < 5 else zero)
            place = m + 2 - n
            behind.append(weights[place] if 0 <= place < 5 else zero)
        f = jnp.where(two, ahead[2], jnp.where(one, ahead[1], ahead[0]))
        b = jnp.where(two, behind[2], jnp.where(one, behind[1], behind[0]))
        if m == -1:
            f = f + jnp.where(some, 0.5, 0.0)
        if m == -2:
            f = f + jnp.where(two, 0.5, 0.0)
        if m == 0:
            b = b - jnp.where(some, 0.5, 0.0)
        if m == 1:
            b = b - jnp.where(two, 0.5, 0.0)
        taps[m] = jnp.where(forward, f, b)
    return taps


def difference_taps(here, ahead, reach):
    out = {}
    for m in range(-reach, reach + 1):
        if m in here and m - 1 in ahead:
            out[m] = here[m] - ahead[m - 1]
        elif m in here:
            out[m] = here[m]
        else:
            out[m] = -ahead[m - 1]
    return out


def north_coefficients(courant):
    count = courant.shape[0]
    row = row_index(courant.shape)
    here = north_taps(jnp.where(row == 0, 0.0, courant))
    taps = difference_taps(here, {m: rows(here[m], -1) for m in here}, 3)
    return [
        jnp.where((row + m >= 0) & (row + m < count), taps[m], 0.0) for m in range(-3, 4)
    ]


def pick(x, index):
    return jnp.take_along_axis(x, index, axis=1, mode="promise_in_bounds")


def position():
    return lax.axis_index("tracer")


def prepare_kernel(owner, thick, fe, fn, ce, cn, ne, keep, send):
    me = position()
    owned = owner[0] == me
    core = me % 2
    levels, count, width = thick.shape[1:]
    lane = lane_index((count, width))
    row = row_index((count, width))
    edge_rows = jnp.zeros((count, width), jnp.float32)
    for l in range(levels):
        east_mass = fe[0, l]
        north_mass = jnp.where(row == 0, 0.0, fn[0, l])
        thickness = (
            thick[0, l]
            + (east_mass - jnp.where(lane == width - 1, 0.0, lanes(east_mass, -1)))
            + (north_mass - rows(north_mass, -1))
        )
        whole = ne[0, l].astype(jnp.float32)
        first = (thickness, ce[0, l])
        second = (cn[0, l], whole)
        for k in range(2):
            start = (k * levels + l) * count
            a = jnp.where(owned, first[k], 0.0)
            b = jnp.where(owned, second[k], 0.0)
            keep[start : start + count, :] = jnp.where(core == 0, a, b)
            send[start : start + count, :] = jnp.where(core == 0, b, a)
        edges = jnp.where(lane < SEG, lanes(cn[0, l], EDGE), 0.0)
        for k, value in enumerate((ce[0, l], whole, east_mass)):
            edges = jnp.where(lane == SEG + k, lanes(value, SEG + k), edges)
        edge_rows = edge_rows + lanes(jnp.where(lane < MET_SEG, edges, 0.0), MET_SEG * l)
    edge_rows = jnp.where(owned, edge_rows, 0.0)
    base = 2 * levels * count
    keep[base : base + count, :] = edge_rows
    send[base : base + count, :] = edge_rows


def prepare(owner, thick, fe, fn, ce, cn, ne):
    levels, count, width = thick.shape[1:]
    vmem = pl.BlockSpec(memory_space=pltpu.VMEM)
    half = pltpu.VMEM(((2 * levels + 1) * count, width), jnp.float32)
    return pl.pallas_call(
        prepare_kernel,
        out_shape=(half, half),
        in_specs=[pl.BlockSpec(memory_space=pltpu.SMEM)] + [vmem] * 6,
        out_specs=(vmem, vmem),
        name="prepare",
    )(owner, thick, fe, fn, ce, cn, ne)


def pack_kernel(mass, last, first):
    tracers, levels, count, width = mass.shape
    lane = lane_index((count, width))
    for l in range(levels):
        a = jnp.zeros((count, width), jnp.float32)
        b = a
        for t in range(tracers):
            value = mass[t, l]
            inside = (lane >= EDGE * t) & (lane < EDGE * (t + 1))
            a = jnp.where(inside, lanes(value, EDGE * (t + 1)), a)
            b = jnp.where(inside, lanes(value, EDGE * t), b)
        last[l * count : (l + 1) * count, :] = a
        first[l * count : (l + 1) * count, :] = b


def pack(mass):
    tracers, levels, count, width = mass.shape
    vmem = pl.BlockSpec(memory_space=pltpu.VMEM)
    packed = pltpu.VMEM((levels * count, width), jnp.float32)
    return pl.pallas_call(
        pack_kernel,
        out_shape=(packed, packed),
        in_specs=[vmem],
        out_specs=(vmem, vmem),
        cost_estimate=pl.CostEstimate(flops=2000000, bytes_accessed=1000000, transcendentals=0),
        name="pack",
    )(mass)


def transport_kernel(
    owner, mine, other, west, east, mass, out,
    east_c, north_c, inverse, packed_first, packed_final, padded, middle, stage, sems,
):
    tracers, levels, count, width = mass.shape
    shape = (count, width)
    lane = lane_index(shape)
    low = position() % 2 == 0
    segment = sum(((lane >= SEG * k).astype(jnp.int32) for k in range(1, PACK)), jnp.zeros(shape, jnp.int32))
    in_segment = lane - SEG * segment
    packed_lane = lane < SEG * PACK
    from_west_lane = in_segment < EDGE
    zero_rows = jnp.zeros((PAD, width), jnp.float32)
    for buffer in (padded, middle):
        for g in range(GROUP):
            buffer[g, :PAD, :] = zero_rows
            buffer[g, PAD + count :, :] = zero_rows

    base = levels * count
    met_east = east[base : base + count, :]
    met_lane = sum((jnp.where(lane >= MET_SEG * l, MET_SEG, 0) for l in range(1, levels)), jnp.zeros(shape, jnp.int32))
    met = jnp.where(lane - met_lane < EDGE, west[base : base + count, :], met_east)
    beyond = east_taps(met_east, lanes(met_east, -1))
    edge_index = jnp.where(packed_lane, in_segment + (width - EDGE), 0)
    edge_index = jnp.where(edge_index >= width, edge_index - width, edge_index)

    for l in range(levels):
        fields = []
        for half in range(2):
            for k in range(2):
                start = (k * levels + l) * count
                a = mine[start : start + count, :]
                b = other[start : start + count, :]
                fields.append(jnp.where(low, a, b) if half == 0 else jnp.where(low, b, a))
        thickness, east_courant, north_courant, whole = fields
        last = width - 1 - MET_SEG * l - SEG
        edge_mass = jnp.where(lane == width - 1, lanes(met_east, last - 2), 0.0)
        inverse[l] = 2.0 / (thickness - edge_mass)
        here = east_taps(east_courant, whole)
        ahead = {
            m: jnp.where(lane == width - 1, lanes(beyond[m], last), lanes(here[m], -1)) for m in here
        }
        taps = difference_taps(here, ahead, EDGE)
        outer = {}
        for m in range(-EDGE, EDGE + 1):
            value = taps[m]
            if m != 0:
                crosses = (from_west_lane != (in_segment + m < EDGE)) & packed_lane
                outer[m] = jnp.where(crosses, pick(value, edge_index), 0.0)
            if m < 0:
                value = jnp.where(lane >= -m, value, 0.0)
            if m > 0:
                value = jnp.where(lane < width - m, value, 0.0)
            shift = east_group(m)
            east_c[m + EDGE, l] = lanes(value, shift) if shift else value
        for m, value in enumerate(north_coefficients(north_courant)):
            north_c[m, l] = value

        packed_taps = north_coefficients(pick(met, jnp.where(packed_lane, in_segment + MET_SEG * l, 0)))
        for half in range(2):
            west_index = jnp.where(
                packed_lane, in_segment + EDGE * (segment + PACK * half), 0
            )
            east_index = west_index - EDGE
            cells = jnp.where(
                from_west_lane,
                pick(west[l * count : (l + 1) * count, :], jnp.where(from_west_lane, west_index, 0)),
                pick(east[l * count : (l + 1) * count, :], jnp.where(from_west_lane, 0, jnp.maximum(east_index, 0))),
            )
            inner = cells
            for m in range(-3, 4):
                inner = inner + packed_taps[m + 3] * rows(cells, -m)
            first = jnp.zeros_like(cells)
            final = jnp.zeros_like(cells)
            for m in outer:
                first = first + outer[m] * lanes(cells, -m)
                final = final + outer[m] * lanes(inner, -m)
            packed_first[half, l] = first
            packed_final[half, l] = final

    block_lane = lane_index((BLOCK, width))
    at_edge = (block_lane < EDGE) | (block_lane >= width - EDGE)

    def east_sum(start, taps, x):
        near = {-1: lanes(x, 1), 0: x, 1: lanes(x, -1), 2: lanes(x, -2)}
        parts = {}
        for m in range(-EDGE, EDGE + 1):
            shift = east_group(m)
            term = taps[m + EDGE] * near[m - shift]
            parts[shift] = parts[shift] + term if shift in parts else term
        return start + parts[0] + (lanes(parts[-STEP], STEP) + lanes(parts[STEP], -STEP))

    def group(step, carry):
        l = step % levels
        t0 = (step // levels) * GROUP
        half = t0 // PACK
        first_place = t0 - half * PACK

        def block(b):
            return slice(b * BLOCK, (b + 1) * BLOCK)

        def edges(ref, j, b):
            moved = pltpu.roll(ref[half, l, block(b), :], width - EDGE - SEG * (j + first_place), 1)
            return jnp.where(at_edge, moved, 0.0)

        for b in range(count // BLOCK):
            taps = [east_c[m, l, block(b), :] for m in range(2 * EDGE + 1)]
            for j in range(GROUP):
                x = mass[t0 + j, l, block(b), :]
                place = slice(PAD + b * BLOCK, PAD + (b + 1) * BLOCK)
                padded[j, place, :] = x
                middle[j, place, :] = east_sum(x + edges(packed_first, j, b), taps, x)
        for b in range(count // BLOCK):
            taps = [east_c[m, l, block(b), :] for m in range(2 * EDGE + 1)]
            north = [north_c[m, l, block(b), :] for m in range(7)]
            scale = inverse[l, block(b), :]
            for j in range(GROUP):
                x = mass[t0 + j, l, block(b), :]
                inner = x
                total = 0.5 * x + edges(packed_final, j, b)
                for m in range(-3, 4):
                    start = PAD + b * BLOCK + m
                    inner = inner + north[m + 3] * padded[j, start : start + BLOCK, :]
                    total = total + north[m + 3] * middle[j, start : start + BLOCK, :]
                stage[t0 + j, l, block(b), :] = east_sum(total, taps, inner) * scale
        copy(step).start()
        return carry

    def copy(step):
        l = step % levels
        place = pl.ds((step // levels) * GROUP, GROUP)
        return pltpu.make_async_copy(stage.at[place, l], out.at[place, l], sems.at[step])

    steps = levels * (tracers // GROUP)
    lax.fori_loop(0, steps, group, 0)
    for step in range(steps):
        copy(step).wait()


def east_group(m):
    return -STEP if m < -1 else (STEP if m > 2 else 0)


def transport(owner, mine, other, west, east, mass):
    tracers, levels, count, width = mass.shape
    vmem = pl.BlockSpec(memory_space=pltpu.VMEM)
    return pl.pallas_call(
        transport_kernel,
        out_shape=jax.ShapeDtypeStruct(mass.shape, jnp.float32),
        in_specs=[pl.BlockSpec(memory_space=pltpu.SMEM)] + [vmem] * 5,
        out_specs=pl.BlockSpec(memory_space=pl.ANY),
        scratch_shapes=[
            pltpu.VMEM((2 * EDGE + 1, levels, count, width), jnp.float32),
            pltpu.VMEM((7, levels, count, width), jnp.float32),
            pltpu.VMEM((levels, count, width), jnp.float32),
            pltpu.VMEM((2, levels, count, width), jnp.float32),
            pltpu.VMEM((2, levels, count, width), jnp.float32),
            pltpu.VMEM((GROUP, count + 2 * PAD, width), jnp.float32),
            pltpu.VMEM((GROUP, count + 2 * PAD, width), jnp.float32),
            pltpu.VMEM(mass.shape, jnp.float32),
            pltpu.SemaphoreType.DMA((levels * (tracers // GROUP),)),
        ],
        compiler_params=pltpu.CompilerParams(vmem_limit_bytes=24 * 1024 * 1024),
        name="transport",
    )(owner, mine, other, west, east, mass)


def ring(x, by):
    size = lax.axis_size("space")
    return lax.ppermute(x, "space", [(i, (i + by) % size) for i in range(size)])


def exchange(x, flip):
    size = lax.axis_size("tracer")
    return lax.ppermute(x, "tracer", [(i, i ^ flip) for i in range(size)])


def shards(mass, thick, fe, fn, ce, cn, ne, owner):
    keep, send = prepare(owner, thick, fe, fn, ce, cn, ne)
    last, first = pack(mass)
    total = keep + exchange(send, 1)
    for flip in (2, 6, 8):
        total = total + exchange(total, flip)
    main = 2 * mass.shape[1] * mass.shape[2]
    mine = total[:main]
    edges = total[main:]
    other = exchange(mine, 1)
    west = ring(jnp.concatenate([last, edges]), 1)
    east = ring(jnp.concatenate([first, edges]), -1)
    return transport(owner, mine, other, west, east, mass)


def solution(mesh):
    spec = P("tracer", None, None, "space")
    return jax.shard_map(
        shards, mesh=mesh, in_specs=(spec,) * 7 + (P("space"),), out_specs=spec, check_vma=False
    )
```

time: 49.3 us -> 43.1 us (0.87)
  starting transfers between devices: 19.1 us -> 14.1 us
  waiting for transfers between devices: 13.9 us -> 16.8 us
  Pallas kernels: 13.8 us -> 11.3 us
  local copies, waits for them, and re-layouts: 1.02 us -> 0.02 us
  other arithmetic: 0.72 us -> 0.07 us
    ppermute x4 -> x2, starting transfers between devices: 10.6 us -> 4.84 us  [ring(): return lax.ppermute(x, 'space', [(i, (i + by) % size) for i in range(size)])]
    pallas_call x1, Pallas kernels: 11.4 us -> 8.51 us  [transport(): pl.pallas_call(transport_kernel, out_shape=jax.ShapeDtypeStruct(mass.shap...]
    ppermute x5, waiting for transfers between devices: 9.18 us -> 11.6 us  [exchange(): return lax.ppermute(x, 'tracer', [(i, i ^ flip) for i in range(size)])]
    squeeze x1 -> x0, local copies, waits for them, and re-layouts: 1 us -> none  [shards(): total = parts[0] + exchange(parts[1], 1)]
    ppermute x5, starting transfers between devices: 8.5 us -> 9.24 us  [exchange(): return lax.ppermute(x, 'tracer', [(i, i ^ flip) for i in range(size)])]
    another operation x1 -> x0, other arithmetic: 0.66 us -> none  [shards(): ids = jnp.stack([dynamics_owner[0], me]).astype(jnp.int32)]
    ppermute x4 -> x2, waiting for transfers between devices: 4.69 us -> 5.22 us  [ring(): return lax.ppermute(x, 'space', [(i, (i + by) % size) for i in range(size)])]
    pallas_call x1 -> x2, Pallas kernels: 2.4 us -> 2.75 us  [the longest x1 1.67 us: pack(): pl.pallas_call(pack_kernel, out_shape=(packed, packed), in_specs=[vmem],...]
  transfers between devices with their start and end apart: 9 -> 7, of which waited for: 5 -> 6; matrix products, arithmetic and copies ran while one was open for 0% -> 0% of each run, Pallas kernels for 0% -> 4%
where the time goes in v2:
time: 43.1 us; the launch traced here: 42.9 us
  waiting for transfers between devices  16.8 us (39%)
  starting transfers between devices  14.1 us (33%)
  Pallas kernels  11.3 us (26%)
  between operations  0.71 us (2%)
    ppermute x5, waiting for transfers between devices, exchange(): return lax.ppermute(x, 'tracer', [(i, i ^ flip) for i in range(size)])  11.6 us
    ppermute x5, starting transfers between devices, exchange(): return lax.ppermute(x, 'tracer', [(i, i ^ flip) for i in range(size)])  9.24 us
    pallas_call x1, Pallas kernels, transport(): pl.pallas_call(transport_kernel, out_shape=jax.ShapeDtypeStruct(mass.shap...  8.51 us
    ppermute x2, waiting for transfers between devices, ring(): return lax.ppermute(x, 'space', [(i, (i + by) % size) for i in range(size)])  5.22 us
    ppermute x2, starting transfers between devices, ring(): return lax.ppermute(x, 'space', [(i, (i + by) % size) for i in range(size)])  4.84 us
    pallas_call x1, Pallas kernels, pack(): pl.pallas_call(pack_kernel, out_shape=(packed, packed), in_specs=[vmem],...  1.67 us
    pallas_call x1, Pallas kernels, prepare(): pl.pallas_call(prepare_kernel, out_shape=(half, half), in_specs=[pl.Block...  1.09 us
  transfers between devices with their start and end apart: 7, of which 6 were waited for; matrix products, arithmetic and copies ran while one was open for 0% of the time, Pallas kernels for 4%

profile of v2, /device:TPU:1, one launch (start us, length us, event | category | flops | bytes accessed | tf_op | source)
XLA Modules:
  0.0 42.9 jit_solution(12624825419816802034)
XLA Ops:
  0.7 1.1 %prepare.1 = (f32[224,128]{1,0:T(8,128)S(1)}, f32[224,128]{1,0:T(8,128)S(1)}) custom-call(s32[1]{0:T(128)S(6)} %copy.9.owner, f32[1,3,32,128]{3,2,1,0:T(8,128)} %thick.1, f32[1,3,32,128]{3,2,1,0:T(8,128)} %fe.1, f32[1,3,32,128]{3,2,1,0:T(8,128)} %fn.1, f32[1,3,32,128]{3,2,1,0:T(8,128)} %ce.1, f32[1,3,32,128]{3,2,1,0:T(8,128)} %cn.1, s32[1,3,32,128]{3,2,1,0:T(8,128)} %ne.1), custom_call_target="tpu_custom_call" | custom-call | tf_op jit(solution)/shard_map/prepare/pallas_call | solution.py:160
  1.7 3.3 %collective-permute-start = (f32[224,128]{1,0:T(8,128)S(1)}, f32[224,128]{1,0:T(8,128)S(1)}, u32[]{:S(2)}, u32[]{:S(2)}) collective-permute-start(f32[224,128]{1,0:T(8,128)S(1)} %get-tuple-element.10), channel_id=1, source_target_pairs={{0,1},{1,0},{2,3},{3,2},{4,5},{5,4},{6,7},{7,6},{8,9},{9,8},{10,11... | collective-permute-start | bytes 344072 | tf_op jit(solution)/shard_map/ppermute | solution.py:372
  5.1 1.0 %collective-permute-done = f32[224,128]{1,0:T(8,128)S(1)} collective-permute-done((f32[224,128]{1,0:T(8,128)S(1)}, f32[224,128]{1,0:T(8,128)S(1)}, u32[]{:S(2)}, u32[]{:S(2)}) %collective-permute-start) | collective-permute-done | bytes 114720 | tf_op jit(solution)/shard_map/ppermute | solution.py:372
  6.0 0.1 collective-permute-start.1
  6.1 4.4 %collective-permute-done.1 = f32[224,128]{1,0:T(8,128)S(1)} collective-permute-done((f32[224,128]{1,0:T(8,128)S(1)}, f32[224,128]{1,0:T(8,128)S(1)}, u32[]{:S(2)}, u32[]{:S(2)}) %collective-permute-start.1) | collective-permute-done | bytes 114720 | tf_op jit(solution)/shard_map/ppermute | solution.py:372
  10.5 1.1 %collective-permute-start.2 = (f32[224,128]{1,0:T(8,128)S(1)}, f32[224,128]{1,0:T(8,128)S(1)}, u32[]{:S(2)}, u32[]{:S(2)}) collective-permute-start(f32[224,128]{1,0:T(8,128)S(1)} %add.13), channel_id=1, source_target_pairs={{0,6},{1,7},{2,4},{3,5},{4,2},{5,3},{6,0},{7,1},{8,14},{9,15},{10,... | collective-permute-start | bytes 344072 | tf_op jit(solution)/shard_map/ppermute | solution.py:372
  11.6 3.9 %collective-permute-done.2 = f32[224,128]{1,0:T(8,128)S(1)} collective-permute-done((f32[224,128]{1,0:T(8,128)S(1)}, f32[224,128]{1,0:T(8,128)S(1)}, u32[]{:S(2)}, u32[]{:S(2)}) %collective-permute-start.2) | collective-permute-done | bytes 114720 | tf_op jit(solution)/shard_map/ppermute | solution.py:372
  15.5 0.0 copy-start
  15.5 1.2 %collective-permute-start.3 = (f32[224,128]{1,0:T(8,128)S(1)}, f32[224,128]{1,0:T(8,128)S(1)}, u32[]{:S(2)}, u32[]{:S(2)}) collective-permute-start(f32[224,128]{1,0:T(8,128)S(1)} %add.14), channel_id=1, source_target_pairs={{0,8},{1,9},{2,10},{3,11},{4,12},{5,13},{6,14},{7,15},{8,0},{9,1},... | collective-permute-start | bytes 344072 | tf_op jit(solution)/shard_map/ppermute | solution.py:372
  16.7 1.7 %pack.1 = (f32[96,128]{1,0:T(8,128)S(1)}, f32[96,128]{1,0:T(8,128)S(1)}) custom-call(f32[18,3,32,128]{3,2,1,0:T(8,128)} %mass.3), custom_call_target="tpu_custom_call" | custom-call | flops 2000000 | bytes 1000000 | tf_op jit(solution)/shard_map/pack/pallas_call | solution.py:188
  18.3 2.4 %collective-permute-done.3 = f32[224,128]{1,0:T(8,128)S(1)} collective-permute-done((f32[224,128]{1,0:T(8,128)S(1)}, f32[224,128]{1,0:T(8,128)S(1)}, u32[]{:S(2)}, u32[]{:S(2)}) %collective-permute-start.3) | collective-permute-done | bytes 114720 | tf_op jit(solution)/shard_map/ppermute | solution.py:372
  20.8 3.6 %collective-permute-start.4 = (f32[192,128]{1,0:T(8,128)S(1)}, f32[192,128]{1,0:T(8,128)S(1)}, u32[]{:S(2)}, u32[]{:S(2)}) collective-permute-start(f32[192,128]{1,0:T(8,128)S(1)} %slice.8.mine), channel_id=1, source_target_pairs={{0,1},{1,0},{2,3},{3,2},{4,5},{5,4},{6,7},{7,6},{8,9},{9,8},{10,11... | collective-permute-start | bytes 294920 | tf_op jit(solution)/shard_map/ppermute | solution.py:372
  24.4 4.8 %collective-permute-start.6 = (f32[128,128]{1,0:T(8,128)S(1)}, f32[128,128]{1,0:T(8,128)S(1)}, u32[]{:S(2)}, u32[]{:S(2)}) collective-permute-start(f32[128,128]{1,0:T(8,128)S(1)} %get-tuple-element.13), channel_id=1, source_target_pairs={{0,240},{16,0},{32,16},{48,32},{64,48},{80,64},{96,80},{112,96},{1... | collective-permute-start | bytes 196616 | tf_op jit(solution)/shard_map/ppermute | solution.py:367
  29.2 0.0 collective-permute-start.5
  29.2 1.5 %collective-permute-done.6.east = f32[128,128]{1,0:T(8,128)S(1)} collective-permute-done((f32[128,128]{1,0:T(8,128)S(1)}, f32[128,128]{1,0:T(8,128)S(1)}, u32[]{:S(2)}, u32[]{:S(2)}) %collective-permute-start.6) | collective-permute-done | bytes 65568 | tf_op jit(solution)/shard_map/ppermute | solution.py:367
  30.7 3.7 %collective-permute-done.5.west = f32[128,128]{1,0:T(8,128)S(1)} collective-permute-done((f32[128,128]{1,0:T(8,128)S(1)}, f32[128,128]{1,0:T(8,128)S(1)}, u32[]{:S(2)}, u32[]{:S(2)}) %collective-permute-start.5) | collective-permute-done | bytes 65568 | tf_op jit(solution)/shard_map/ppermute | solution.py:367
  34.4 0.0 collective-permute-done.4.other
  34.4 0.0 copy-done
  34.4 8.5 %transport.1 = f32[18,3,32,128]{3,2,1,0:T(8,128)} custom-call(s32[1]{0:T(128)S(6)} %copy.9.owner, f32[192,128]{1,0:T(8,128)S(1)} %slice.8.mine, f32[192,128]{1,0:T(8,128)S(1)} %collective-permute-done.4.other, f32[128,128]{1,0:T(8,128)S(1)} %collective-permute-done.5.west, f32[128,128]{1,0:T(8,128)S(1)} %collective-permute-done.6.east, ...), custom_call_target="tpu_custom_call" | custom-call | tf_op jit(solution)/shard_map/transport/pallas_call | solution.py:344
  (7 shorter events, 0.1 us)
Async XLA Ops:
  1.7 4.3 %collective-permute-start = (f32[224,128]{1,0:T(8,128)S(1)}, f32[224,128]{1,0:T(8,128)S(1)}, u32[]{:S(2)}, u32[]{:S(2)}) collective-permute-start(f32[224,128]{1,0:T(8,128)S(1)} %get-tuple-element.10), channel_id=1, source_target_pairs={{0,1},{1,0},{2,3},{3,2},{4,5},{5,4},{6,7},{7,6},{8,9},{9,8},{10,11... | collective-permute-start | bytes 344072 | tf_op jit(solution)/shard_map/ppermute | solution.py:372
  6.0 4.5 %collective-permute-start.1 = (f32[224,128]{1,0:T(8,128)S(1)}, f32[224,128]{1,0:T(8,128)S(1)}, u32[]{:S(2)}, u32[]{:S(2)}) collective-permute-start(f32[224,128]{1,0:T(8,128)S(1)} %add.12), channel_id=1, source_target_pairs={{0,2},{1,3},{2,0},{3,1},{4,6},{5,7},{6,4},{7,5},{8,10},{9,11},{10,... | collective-permute-start | bytes 344072 | tf_op jit(solution)/shard_map/ppermute | solution.py:372
  10.5 4.9 %collective-permute-start.2 = (f32[224,128]{1,0:T(8,128)S(1)}, f32[224,128]{1,0:T(8,128)S(1)}, u32[]{:S(2)}, u32[]{:S(2)}) collective-permute-start(f32[224,128]{1,0:T(8,128)S(1)} %add.13), channel_id=1, source_target_pairs={{0,6},{1,7},{2,4},{3,5},{4,2},{5,3},{6,0},{7,1},{8,14},{9,15},{10,... | collective-permute-start | bytes 344072 | tf_op jit(solution)/shard_map/ppermute | solution.py:372
  15.5 19.0 %copy-start = (f32[18,3,32,128]{3,2,1,0:T(8,128)S(1)}, f32[18,3,32,128]{3,2,1,0:T(8,128)}, u32[]{:S(2)}) copy-start(f32[18,3,32,128]{3,2,1,0:T(8,128)} %mass.3) | copy-start | bytes 2654212
  15.5 5.2 %collective-permute-start.3 = (f32[224,128]{1,0:T(8,128)S(1)}, f32[224,128]{1,0:T(8,128)S(1)}, u32[]{:S(2)}, u32[]{:S(2)}) collective-permute-start(f32[224,128]{1,0:T(8,128)S(1)} %add.14), channel_id=1, source_target_pairs={{0,8},{1,9},{2,10},{3,11},{4,12},{5,13},{6,14},{7,15},{8,0},{9,1},... | collective-permute-start | bytes 344072 | tf_op jit(solution)/shard_map/ppermute | solution.py:372
  20.8 13.7 %collective-permute-start.4 = (f32[192,128]{1,0:T(8,128)S(1)}, f32[192,128]{1,0:T(8,128)S(1)}, u32[]{:S(2)}, u32[]{:S(2)}) collective-permute-start(f32[192,128]{1,0:T(8,128)S(1)} %slice.8.mine), channel_id=1, source_target_pairs={{0,1},{1,0},{2,3},{3,2},{4,5},{5,4},{6,7},{7,6},{8,9},{9,8},{10,11... | collective-permute-start | bytes 294920 | tf_op jit(solution)/shard_map/ppermute | solution.py:372
  24.4 6.3 %collective-permute-start.6 = (f32[128,128]{1,0:T(8,128)S(1)}, f32[128,128]{1,0:T(8,128)S(1)}, u32[]{:S(2)}, u32[]{:S(2)}) collective-permute-start(f32[128,128]{1,0:T(8,128)S(1)} %get-tuple-element.13), channel_id=1, source_target_pairs={{0,240},{16,0},{32,16},{48,32},{64,48},{80,64},{96,80},{112,96},{1... | collective-permute-start | bytes 196616 | tf_op jit(solution)/shard_map/ppermute | solution.py:367
  29.2 5.2 %collective-permute-start.5 = (f32[128,128]{1,0:T(8,128)S(1)}, f32[128,128]{1,0:T(8,128)S(1)}, u32[]{:S(2)}, u32[]{:S(2)}) collective-permute-start(f32[128,128]{1,0:T(8,128)S(1)} %get-tuple-element.14), channel_id=1, source_target_pairs={{0,16},{16,32},{32,48},{48,64},{64,80},{80,96},{96,112},{112,128},... | collective-permute-start | bytes 196616 | tf_op jit(solution)/shard_map/ppermute | solution.py:367

commit v3 on v2

--- a/solution.py
+++ b/solution.py
@@ -13,6 +13,7 @@
 GROUP = 3
 PAD = 8
 BLOCK = 8
+NEAR = (-1, 1, 2)
 MET_SEG = 16
 
 
@@ -118,7 +119,17 @@
     return lax.axis_index("tracer")
 
 
-def prepare_kernel(owner, thick, fe, fn, ce, cn, ne, keep, send):
+def prepare_kernel(*refs):
+    sources, (keep, send, owner, *fields, sems) = refs[:7], refs[7:]
+    copies = [
+        pltpu.make_async_copy(source, place, sems.at[k])
+        for k, (source, place) in enumerate(zip(sources, (owner, *fields)))
+    ]
+    for copy in copies:
+        copy.start()
+    for copy in copies:
+        copy.wait()
+    thick, fe, fn, ce, cn, ne = fields
     me = position()
     owned = owner[0] == me
     core = me % 2
@@ -160,16 +171,21 @@
     return pl.pallas_call(
         prepare_kernel,
         out_shape=(half, half),
-        in_specs=[pl.BlockSpec(memory_space=pltpu.SMEM)] + [vmem] * 6,
+        in_specs=[pl.BlockSpec(memory_space=pl.ANY)] * 7,
         out_specs=(vmem, vmem),
+        scratch_shapes=[pltpu.SMEM((1,), jnp.int32)]
+        + [pltpu.VMEM(thick.shape, jnp.float32)] * 5
+        + [pltpu.VMEM(ne.shape, jnp.int32), pltpu.SemaphoreType.DMA((7,))],
         name="prepare",
     )(owner, thick, fe, fn, ce, cn, ne)
 
 
-def pack_kernel(mass, last, first):
+def pack_kernel(mass, last, first, padded, moved):
     tracers, levels, count, width = mass.shape
     lane = lane_index((count, width))
-    for l in range(levels):
+    zero_rows = jnp.zeros((PAD, width), jnp.float32)
+
+    def level(l, carry):
         a = jnp.zeros((count, width), jnp.float32)
         b = a
         for t in range(tracers):
@@ -177,41 +193,58 @@
             inside = (lane >= EDGE * t) & (lane < EDGE * (t + 1))
             a = jnp.where(inside, lanes(value, EDGE * (t + 1)), a)
             b = jnp.where(inside, lanes(value, EDGE * t), b)
-        last[l * count : (l + 1) * count, :] = a
-        first[l * count : (l + 1) * count, :] = b
+            padded[t, l, :PAD, :] = zero_rows
+            padded[t, l, PAD : PAD + count, :] = value
+            padded[t, l, PAD + count :, :] = zero_rows
+            for k, shift in enumerate(NEAR):
+                moved[k, t, l] = lanes(value, -shift)
+        last[l] = a
+        first[l] = b
+        return carry
+
+    lax.fori_loop(0, levels, level, 0)
 
 
 def pack(mass):
     tracers, levels, count, width = mass.shape
     vmem = pl.BlockSpec(memory_space=pltpu.VMEM)
-    packed = pltpu.VMEM((levels * count, width), jnp.float32)
-    return pl.pallas_call(
+    packed = pltpu.VMEM((levels, count, width), jnp.float32)
+    last, first, padded, moved = pl.pallas_call(
         pack_kernel,
-        out_shape=(packed, packed),
+        out_shape=(
+            packed,
+            packed,
+            pltpu.VMEM((tracers, levels, count + 2 * PAD, width), jnp.float32),
+            pltpu.VMEM((len(NEAR),) + mass.shape, jnp.float32),
+        ),
         in_specs=[vmem],
-        out_specs=(vmem, vmem),
+        out_specs=(vmem,) * 4,
+        compiler_params=pltpu.CompilerParams(vmem_limit_bytes=24 * 1024 * 1024),
         cost_estimate=pl.CostEstimate(flops=2000000, bytes_accessed=1000000, transcendentals=0),
         name="pack",
     )(mass)
+    rows_flat = (levels * count, width)
+    return last.reshape(rows_flat), first.reshape(rows_flat), padded, moved
 
 
 def transport_kernel(
-    owner, mine, other, west, east, mass, out,
-    east_c, north_c, inverse, packed_first, packed_final, padded, middle, stage, sems,
+    mine, other, west, east, padded, shifted, out,
+    east_c, north_c, inverse, corrections, inners, middle, partial, stage, sems,
 ):
-    tracers, levels, count, width = mass.shape
+    tracers, levels, count, width = out.shape
     shape = (count, width)
     lane = lane_index(shape)
     low = position() % 2 == 0
     segment = sum(((lane >= SEG * k).astype(jnp.int32) for k in range(1, PACK)), jnp.zeros(shape, jnp.int32))
     in_segment = lane - SEG * segment
     packed_lane = lane < SEG * PACK
+    at_edge = (lane < EDGE) | (lane >= width - EDGE)
     from_west_lane = in_segment < EDGE
     zero_rows = jnp.zeros((PAD, width), jnp.float32)
-    for buffer in (padded, middle):
-        for g in range(GROUP):
-            buffer[g, :PAD, :] = zero_rows
-            buffer[g, PAD + count :, :] = zero_rows
+    for slot in range(2):
+        for j in range(GROUP):
+            middle[slot, j, :PAD, :] = zero_rows
+            middle[slot, j, PAD + count :, :] = zero_rows
 
     base = levels * count
     met_east = east[base : base + count, :]
@@ -220,30 +253,45 @@
     beyond = east_taps(met_east, lanes(met_east, -1))
     edge_index = jnp.where(packed_lane, in_segment + (width - EDGE), 0)
     edge_index = jnp.where(edge_index >= width, edge_index - width, edge_index)
-
-    for l in range(levels):
+    moved_index = {0: edge_index, -STEP: lanes(edge_index, -STEP), STEP: lanes(edge_index, STEP)}
+    held = jnp.where(packed_lane, in_segment, -2 * SEG)
+    moved_segment = {0: held, -STEP: lanes(held, -STEP), STEP: lanes(held, STEP)}
+
+    def outer_sum(outer, cells):
+        near = {shift: lanes(cells, -shift) for shift in NEAR}
+        near[0] = cells
+        parts = {}
+        for m in outer:
+            shift = east_group(m)
+            term = outer[m] * near[m - shift]
+            parts[shift] = parts[shift] + term if shift in parts else term
+        return parts[0] + (lanes(parts[-STEP], STEP) + lanes(parts[STEP], -STEP))
+
+    def level(l, carry):
+        level_rows = pl.ds(pl.multiple_of(l * count, count), count)
         fields = []
         for half in range(2):
             for k in range(2):
-                start = (k * levels + l) * count
-                a = mine[start : start + count, :]
-                b = other[start : start + count, :]
+                place = pl.ds(pl.multiple_of((k * levels + l) * count, count), count)
+                a = mine[place, :]
+                b = other[place, :]
                 fields.append(jnp.where(low, a, b) if half == 0 else jnp.where(low, b, a))
         thickness, east_courant, north_courant, whole = fields
         last = width - 1 - MET_SEG * l - SEG
-        edge_mass = jnp.where(lane == width - 1, lanes(met_east, last - 2), 0.0)
+        edge_mass = jnp.where(lane == width - 1, pltpu.roll(met_east, last - 2, 1), 0.0)
         inverse[l] = 2.0 / (thickness - edge_mass)
         here = east_taps(east_courant, whole)
         ahead = {
-            m: jnp.where(lane == width - 1, lanes(beyond[m], last), lanes(here[m], -1)) for m in here
+            m: jnp.where(lane == width - 1, pltpu.roll(beyond[m], last, 1), lanes(here[m], -1)) for m in here
         }
         taps = difference_taps(here, ahead, EDGE)
         outer = {}
         for m in range(-EDGE, EDGE + 1):
             value = taps[m]
             if m != 0:
-                crosses = (from_west_lane != (in_segment + m < EDGE)) & packed_lane
-                outer[m] = jnp.where(crosses, pick(value, edge_index), 0.0)
+                q = moved_segment[east_group(m)]
+                crosses = ((q < EDGE) != (q + m < EDGE)) & (q >= 0)
+                outer[m] = jnp.where(crosses, pick(value, moved_index[east_group(m)]), 0.0)
             if m < 0:
                 value = jnp.where(lane >= -m, value, 0.0)
             if m > 0:
@@ -253,6 +301,7 @@
         for m, value in enumerate(north_coefficients(north_courant)):
             north_c[m, l] = value
 
+        edge_taps = north_coefficients(pick(north_courant, edge_index))
         packed_taps = north_coefficients(pick(met, jnp.where(packed_lane, in_segment + MET_SEG * l, 0)))
         for half in range(2):
             west_index = jnp.where(
@@ -261,75 +310,111 @@
             east_index = west_index - EDGE
             cells = jnp.where(
                 from_west_lane,
-                pick(west[l * count : (l + 1) * count, :], jnp.where(from_west_lane, west_index, 0)),
-                pick(east[l * count : (l + 1) * count, :], jnp.where(from_west_lane, 0, jnp.maximum(east_index, 0))),
+                pick(west[level_rows, :], jnp.where(from_west_lane, west_index, 0)),
+                pick(east[level_rows, :], jnp.where(from_west_lane, 0, jnp.maximum(east_index, 0))),
             )
             inner = cells
             for m in range(-3, 4):
                 inner = inner + packed_taps[m + 3] * rows(cells, -m)
-            first = jnp.zeros_like(cells)
-            final = jnp.zeros_like(cells)
-            for m in outer:
-                first = first + outer[m] * lanes(cells, -m)
-                final = final + outer[m] * lanes(inner, -m)
-            packed_first[half, l] = first
-            packed_final[half, l] = final
-
-    block_lane = lane_index((BLOCK, width))
-    at_edge = (block_lane < EDGE) | (block_lane >= width - EDGE)
-
-    def east_sum(start, taps, x):
-        near = {-1: lanes(x, 1), 0: x, 1: lanes(x, -1), 2: lanes(x, -2)}
+            first = outer_sum(outer, cells)
+            total = outer_sum(outer, inner)
+            for m in range(-3, 4):
+                total = total + edge_taps[m + 3] * rows(first, -m)
+            for k in range(PACK):
+                moved = lanes(total, width - EDGE - SEG * k)
+                corrections[half * PACK + k, l] = jnp.where(at_edge, moved, 0.0)
+        return carry
+
+    lax.fori_loop(0, levels, level, 0)
+
+    def east_parts(taps, near):
         parts = {}
         for m in range(-EDGE, EDGE + 1):
             shift = east_group(m)
             term = taps[m + EDGE] * near[m - shift]
             parts[shift] = parts[shift] + term if shift in parts else term
-        return start + parts[0] + (lanes(parts[-STEP], STEP) + lanes(parts[STEP], -STEP))
-
-    def group(step, carry):
-        l = step % levels
-        t0 = (step // levels) * GROUP
-        half = t0 // PACK
-        first_place = t0 - half * PACK
-
-        def block(b):
-            return slice(b * BLOCK, (b + 1) * BLOCK)
-
-        def edges(ref, j, b):
-            moved = pltpu.roll(ref[half, l, block(b), :], width - EDGE - SEG * (j + first_place), 1)
-            return jnp.where(at_edge, moved, 0.0)
-
-        for b in range(count // BLOCK):
-            taps = [east_c[m, l, block(b), :] for m in range(2 * EDGE + 1)]
-            for j in range(GROUP):
-                x = mass[t0 + j, l, block(b), :]
-                place = slice(PAD + b * BLOCK, PAD + (b + 1) * BLOCK)
-                padded[j, place, :] = x
-                middle[j, place, :] = east_sum(x + edges(packed_first, j, b), taps, x)
+        return parts
+
+    steps = levels * (tracers // GROUP)
+
+    def block(b):
+        return slice(b * BLOCK, (b + 1) * BLOCK)
+
+    def padded_block(b, m=0):
+        return slice(PAD + b * BLOCK + m, PAD + (b + 1) * BLOCK + m)
+
+    def place(step):
+        step = jnp.clip(step, 0, steps - 1)
+        return step % levels, (step // levels) * GROUP
+
+    def copy(step):
+        l, t0 = place(step)
+        where = pl.ds(t0, GROUP)
+        return pltpu.make_async_copy(stage.at[where, l], out.at[where, l], sems.at[step])
+
+    def front(step):
+        l, t0 = place(step)
+        slot = (step + 2) % 2
         for b in range(count // BLOCK):
             taps = [east_c[m, l, block(b), :] for m in range(2 * EDGE + 1)]
             north = [north_c[m, l, block(b), :] for m in range(7)]
+            for j in range(GROUP):
+                x = padded[t0 + j, l, padded_block(b), :]
+                inner = x + north[3] * x
+                for m in (-3, -2, -1, 1, 2, 3):
+                    inner = inner + north[m + 3] * padded[t0 + j, l, padded_block(b, m), :]
+                inners[slot, j, block(b), :] = inner
+                near = {0: x}
+                for k, shift in enumerate(NEAR):
+                    near[shift] = shifted[k, t0 + j, l, block(b), :]
+                parts = east_parts(taps, near)
+                middle[slot, j, padded_block(b), :] = (x + parts[0]) + (
+                    lanes(parts[-STEP], STEP) + lanes(parts[STEP], -STEP)
+                )
+
+    def back(step):
+        l, t0 = place(step)
+        slot = (step + 2) % 2
+        for b in range(count // BLOCK):
+            taps = [east_c[m, l, block(b), :] for m in range(2 * EDGE + 1)]
+            north = [north_c[m, l, block(b), :] for m in range(7)]
+            for j in range(GROUP):
+                inner = inners[slot, j, block(b), :]
+                near = {0: inner}
+                for shift in NEAR:
+                    near[shift] = lanes(inner, -shift)
+                parts = east_parts(taps, near)
+                total = 0.5 * padded[t0 + j, l, padded_block(b), :] + parts[0]
+                for m in range(-3, 4):
+                    total = total + north[m + 3] * middle[slot, j, padded_block(b, m), :]
+                partial[slot, 0, j, block(b), :] = total
+                partial[slot, 1, j, block(b), :] = parts[-STEP]
+                partial[slot, 2, j, block(b), :] = parts[STEP]
+
+    def finish(step):
+        l, t0 = place(step)
+        slot = (step + 2) % 2
+        for b in range(count // BLOCK):
             scale = inverse[l, block(b), :]
             for j in range(GROUP):
-                x = mass[t0 + j, l, block(b), :]
-                inner = x
-                total = 0.5 * x + edges(packed_final, j, b)
-                for m in range(-3, 4):
-                    start = PAD + b * BLOCK + m
-                    inner = inner + north[m + 3] * padded[j, start : start + BLOCK, :]
-                    total = total + north[m + 3] * middle[j, start : start + BLOCK, :]
-                stage[t0 + j, l, block(b), :] = east_sum(total, taps, inner) * scale
-        copy(step).start()
+                total = partial[slot, 0, j, block(b), :] + (
+                    lanes(partial[slot, 1, j, block(b), :], STEP)
+                    + lanes(partial[slot, 2, j, block(b), :], -STEP)
+                )
+                stage[t0 + j, l, block(b), :] = (total + corrections[t0 + j, l, block(b), :]) * scale
+
+    def step_of_three(step, carry):
+        finish(step - 1)
+        back(step)
+        front(step + 1)
+
+        @pl.when(step >= 1)
+        def _():
+            copy(step - 1).start()
+
         return carry
 
-    def copy(step):
-        l = step % levels
-        place = pl.ds((step // levels) * GROUP, GROUP)
-        return pltpu.make_async_copy(stage.at[place, l], out.at[place, l], sems.at[step])
-
-    steps = levels * (tracers // GROUP)
-    lax.fori_loop(0, steps, group, 0)
+    lax.fori_loop(-1, steps + 1, step_of_three, 0)
     for step in range(steps):
         copy(step).wait()
 
@@ -338,28 +423,28 @@
     return -STEP if m < -1 else (STEP if m > 2 else 0)
 
 
-def transport(owner, mine, other, west, east, mass):
-    tracers, levels, count, width = mass.shape
+def transport(mine, other, west, east, padded, shifted):
+    tracers, levels, count, width = shifted.shape[1:]
     vmem = pl.BlockSpec(memory_space=pltpu.VMEM)
     return pl.pallas_call(
         transport_kernel,
-        out_shape=jax.ShapeDtypeStruct(mass.shape, jnp.float32),
-        in_specs=[pl.BlockSpec(memory_space=pltpu.SMEM)] + [vmem] * 5,
+        out_shape=jax.ShapeDtypeStruct(shifted.shape[1:], jnp.float32),
+        in_specs=[vmem] * 6,
         out_specs=pl.BlockSpec(memory_space=pl.ANY),
         scratch_shapes=[
             pltpu.VMEM((2 * EDGE + 1, levels, count, width), jnp.float32),
             pltpu.VMEM((7, levels, count, width), jnp.float32),
             pltpu.VMEM((levels, count, width), jnp.float32),
-            pltpu.VMEM((2, levels, count, width), jnp.float32),
-            pltpu.VMEM((2, levels, count, width), jnp.float32),
-            pltpu.VMEM((GROUP, count + 2 * PAD, width), jnp.float32),
-            pltpu.VMEM((GROUP, count + 2 * PAD, width), jnp.float32),
-            pltpu.VMEM(mass.shape, jnp.float32),
+            pltpu.VMEM((tracers, levels, count, width), jnp.float32),
+            pltpu.VMEM((2, GROUP, count, width), jnp.float32),
+            pltpu.VMEM((2, GROUP, count + 2 * PAD, width), jnp.float32),
+            pltpu.VMEM((2, 3, GROUP, count, width), jnp.float32),
+            pltpu.VMEM((tracers, levels, count, width), jnp.float32),
             pltpu.SemaphoreType.DMA((levels * (tracers // GROUP),)),
         ],
         compiler_params=pltpu.CompilerParams(vmem_limit_bytes=24 * 1024 * 1024),
         name="transport",
-    )(owner, mine, other, west, east, mass)
+    )(mine, other, west, east, padded, shifted)
 
 
 def ring(x, by):
@@ -372,19 +457,24 @@
     return lax.ppermute(x, "tracer", [(i, i ^ flip) for i in range(size)])
 
 
+def turn(x, by):
+    size = lax.axis_size("tracer")
+    return lax.ppermute(x, "tracer", [(i, i // 8 * 8 + (i + 2 * by) % 8) for i in range(size)])
+
+
 def shards(mass, thick, fe, fn, ce, cn, ne, owner):
     keep, send = prepare(owner, thick, fe, fn, ce, cn, ne)
-    last, first = pack(mass)
+    last, first, padded, shifted = pack(mass)
     total = keep + exchange(send, 1)
-    for flip in (2, 6, 8):
-        total = total + exchange(total, flip)
+    total = total + (turn(total, 1) + turn(total, -1) + turn(total, 2))
+    total = total + exchange(total, 8)
     main = 2 * mass.shape[1] * mass.shape[2]
     mine = total[:main]
     edges = total[main:]
     other = exchange(mine, 1)
     west = ring(jnp.concatenate([last, edges]), 1)
     east = ring(jnp.concatenate([first, edges]), -1)
-    return transport(owner, mine, other, west, east, mass)
+    return transport(mine, other, west, east, padded, shifted)
 
 
 def solution(mesh):

time: 43.1 us -> 40.5 us (0.940)
  waiting for transfers between devices: 16.8 us -> 13.3 us
  Pallas kernels: 11.3 us -> 9.33 us
  starting transfers between devices: 14.1 us -> 15.7 us
  local copies, waits for them, and re-layouts: 0.02 us -> 1.18 us
    ppermute x5 -> x3, waiting for transfers between devices: 11.6 us -> 2.32 us  [exchange(): return lax.ppermute(x, 'tracer', [(i, i ^ flip) for i in range(size)])]
    ppermute x0 -> x3, waiting for transfers between devices: none -> 5.74 us  [turn(): lax.ppermute(x, 'tracer', [(i, i // 8 * 8 + (i + 2 * by) % 8) for i in ra...]
    ppermute x0 -> x3, starting transfers between devices: none -> 2.73 us  [turn(): lax.ppermute(x, 'tracer', [(i, i // 8 * 8 + (i + 2 * by) % 8) for i in ra...]
    ppermute x5 -> x3, starting transfers between devices: 9.24 us -> 7.08 us  [exchange(): return lax.ppermute(x, 'tracer', [(i, i ^ flip) for i in range(size)])]
    pallas_call x2, Pallas kernels: 10.2 us -> 8.18 us  [the longest x1 6.85 us: transport(): pl.pallas_call(transport_kernel, out_shape=jax.ShapeDtypeStruct(shifted.s...]
    unnamed x2, local copies, waits for them, and re-layouts: 0.01 us -> 1.17 us
    ppermute x2, starting transfers between devices: 4.84 us -> 5.93 us  [ring(): return lax.ppermute(x, 'space', [(i, (i + by) % size) for i in range(size)])]
  transfers between devices with their start and end apart: 7 -> 8, of which waited for: 6 -> 7; matrix products, arithmetic and copies ran while one was open for 0% -> 0% of each run, Pallas kernels for 4% -> 3%
where the time goes in v3:
time: 40.5 us; the launch traced here: 40.3 us
  starting transfers between devices  15.7 us (39%)
  waiting for transfers between devices  13.3 us (33%)
  Pallas kernels  9.33 us (23%)
  local copies, waits for them, and re-layouts  1.18 us (3%)
  between operations  0.7 us (2%)
    ppermute x3, starting transfers between devices, exchange(): return lax.ppermute(x, 'tracer', [(i, i ^ flip) for i in range(size)])  7.08 us
    pallas_call x1, Pallas kernels, transport(): pl.pallas_call(transport_kernel, out_shape=jax.ShapeDtypeStruct(shifted.s...  6.85 us
    ppermute x2, starting transfers between devices, ring(): return lax.ppermute(x, 'space', [(i, (i + by) % size) for i in range(size)])  5.93 us
    ppermute x3, waiting for transfers between devices, turn(): lax.ppermute(x, 'tracer', [(i, i // 8 * 8 + (i + 2 * by) % 8) for i in ra...  5.74 us
    ppermute x2, waiting for transfers between devices, ring(): return lax.ppermute(x, 'space', [(i, (i + by) % size) for i in range(size)])  5.22 us
    ppermute x3, starting transfers between devices, turn(): lax.ppermute(x, 'tracer', [(i, i // 8 * 8 + (i + 2 * by) % 8) for i in ra...  2.73 us
    ppermute x3, waiting for transfers between devices, exchange(): return lax.ppermute(x, 'tracer', [(i, i ^ flip) for i in range(size)])  2.32 us
    pallas_call x1, Pallas kernels, pack(): pl.pallas_call(pack_kernel, out_shape=(packed, packed, pltpu.VMEM((tracer...  1.32 us
  transfers between devices with their start and end apart: 8, of which 7 were waited for; matrix products, arithmetic and copies ran while one was open for 0% of the time, Pallas kernels for 3%

profile of v3, /device:TPU:1, one launch (start us, length us, event | category | flops | bytes accessed | tf_op | source)
XLA Modules:
  0.0 40.3 jit_solution(4131661908010157550)
XLA Ops:
  0.7 1.1 %prepare.1 = (f32[224,128]{1,0:T(8,128)S(1)}, f32[224,128]{1,0:T(8,128)S(1)}) custom-call(s32[1]{0:T(128)S(6)} %copy.9.refs_0_, f32[1,3,32,128]{3,2,1,0:T(8,128)} %refs_1_.1, f32[1,3,32,128]{3,2,1,0:T(8,128)} %refs_2_.1, f32[1,3,32,128]{3,2,1,0:T(8,128)} %refs_3_.1, f32[1,3,32,128]{3,2,1,0:T(8,128)} %refs_4_.1, f32[1,3,32,128]{3,2,1,0:T(8,128)} %refs_5_.1, ...), custom_call_target="tpu_custom_call" | custom-call | tf_op jit(solution)/shard_map/prepare/pallas_call | solution.py:171
  1.8 3.3 %collective-permute-start = (f32[224,128]{1,0:T(8,128)S(1)}, f32[224,128]{1,0:T(8,128)S(1)}, u32[]{:S(2)}, u32[]{:S(2)}) collective-permute-start(f32[224,128]{1,0:T(8,128)S(1)} %get-tuple-element.12), channel_id=1, source_target_pairs={{0,1},{1,0},{2,3},{3,2},{4,5},{5,4},{6,7},{7,6},{8,9},{9,8},{10,11... | collective-permute-start | bytes 344072 | tf_op jit(solution)/shard_map/ppermute | solution.py:457
  5.1 1.0 %collective-permute-done = f32[224,128]{1,0:T(8,128)S(1)} collective-permute-done((f32[224,128]{1,0:T(8,128)S(1)}, f32[224,128]{1,0:T(8,128)S(1)}, u32[]{:S(2)}, u32[]{:S(2)}) %collective-permute-start) | collective-permute-done | bytes 114720 | tf_op jit(solution)/shard_map/ppermute | solution.py:457
  6.1 1.3 %collective-permute-start.3 = (f32[224,128]{1,0:T(8,128)S(1)}, f32[224,128]{1,0:T(8,128)S(1)}, u32[]{:S(2)}, u32[]{:S(2)}) collective-permute-start(f32[224,128]{1,0:T(8,128)S(1)} %add.15), channel_id=1, source_target_pairs={{0,4},{1,5},{2,6},{3,7},{4,0},{5,1},{6,2},{7,3},{8,12},{9,13},{10,... | collective-permute-start | bytes 344072 | tf_op jit(solution)/shard_map/ppermute | solution.py:462
  7.4 0.8 %collective-permute-start.2 = (f32[224,128]{1,0:T(8,128)S(1)}, f32[224,128]{1,0:T(8,128)S(1)}, u32[]{:S(2)}, u32[]{:S(2)}) collective-permute-start(f32[224,128]{1,0:T(8,128)S(1)} %add.15), channel_id=1, source_target_pairs={{0,6},{1,7},{2,0},{3,1},{4,2},{5,3},{6,4},{7,5},{8,14},{9,15},{10,... | collective-permute-start | bytes 344072 | tf_op jit(solution)/shard_map/ppermute | solution.py:462
  8.2 0.7 %collective-permute-start.1 = (f32[224,128]{1,0:T(8,128)S(1)}, f32[224,128]{1,0:T(8,128)S(1)}, u32[]{:S(2)}, u32[]{:S(2)}) collective-permute-start(f32[224,128]{1,0:T(8,128)S(1)} %add.15), channel_id=1, source_target_pairs={{0,2},{1,3},{2,4},{3,5},{4,6},{5,7},{6,0},{7,1},{8,10},{9,11},{10,... | collective-permute-start | bytes 344072 | tf_op jit(solution)/shard_map/ppermute | solution.py:462
  8.9 3.2 %collective-permute-done.3 = f32[224,128]{1,0:T(8,128)S(1)} collective-permute-done((f32[224,128]{1,0:T(8,128)S(1)}, f32[224,128]{1,0:T(8,128)S(1)}, u32[]{:S(2)}, u32[]{:S(2)}) %collective-permute-start.3) | collective-permute-done | bytes 114720 | tf_op jit(solution)/shard_map/ppermute | solution.py:462
  12.1 1.1 %collective-permute-done.2 = f32[224,128]{1,0:T(8,128)S(1)} collective-permute-done((f32[224,128]{1,0:T(8,128)S(1)}, f32[224,128]{1,0:T(8,128)S(1)}, u32[]{:S(2)}, u32[]{:S(2)}) %collective-permute-start.2) | collective-permute-done | bytes 114720 | tf_op jit(solution)/shard_map/ppermute | solution.py:462
  13.1 1.4 %collective-permute-done.1 = f32[224,128]{1,0:T(8,128)S(1)} collective-permute-done((f32[224,128]{1,0:T(8,128)S(1)}, f32[224,128]{1,0:T(8,128)S(1)}, u32[]{:S(2)}, u32[]{:S(2)}) %collective-permute-start.1) | collective-permute-done | bytes 114720 | tf_op jit(solution)/shard_map/ppermute | solution.py:462
  14.6 1.4 %collective-permute-start.4 = (f32[224,128]{1,0:T(8,128)S(1)}, f32[224,128]{1,0:T(8,128)S(1)}, u32[]{:S(2)}, u32[]{:S(2)}) collective-permute-start(f32[224,128]{1,0:T(8,128)S(1)} %add_add_fusion), channel_id=1, source_target_pairs={{0,8},{1,9},{2,10},{3,11},{4,12},{5,13},{6,14},{7,15},{8,0},{9,1},... | collective-permute-start | bytes 344072 | tf_op jit(solution)/shard_map/ppermute | solution.py:457
  16.0 0.0 copy-start
  16.0 1.2 %copy-done = f32[18,3,32,128]{3,2,1,0:T(8,128)S(1)} copy-done((f32[18,3,32,128]{3,2,1,0:T(8,128)S(1)}, f32[18,3,32,128]{3,2,1,0:T(8,128)}, u32[]{:S(2)}) %copy-start) | copy-done | bytes 884760
  17.2 1.3 %pack.1 = (f32[3,32,128]{2,1,0:T(8,128)S(1)}, f32[3,32,128]{2,1,0:T(8,128)S(1)}, f32[18,3,48,128]{3,2,1,0:T(8,128)S(1)}, f32[3,18,3,32,128]{4,3,2,1,0:T(8,128)S(1)}) custom-call(f32[18,3,32,128]{3,2,1,0:T(8,128)S(1)} %copy-done), custom_call_target="tpu_custom_call" | custom-call | flops 2000000 | bytes 1000000 | tf_op jit(solution)/shard_map/pack/pallas_call | solution.py:212
  18.5 1.4 %collective-permute-done.4 = f32[224,128]{1,0:T(8,128)S(1)} collective-permute-done((f32[224,128]{1,0:T(8,128)S(1)}, f32[224,128]{1,0:T(8,128)S(1)}, u32[]{:S(2)}, u32[]{:S(2)}) %collective-permute-start.4) | collective-permute-done | bytes 114720 | tf_op jit(solution)/shard_map/ppermute | solution.py:457
  19.9 2.4 %collective-permute-start.5 = (f32[192,128]{1,0:T(8,128)S(1)}, f32[192,128]{1,0:T(8,128)S(1)}, u32[]{:S(2)}, u32[]{:S(2)}) collective-permute-start(f32[192,128]{1,0:T(8,128)S(1)} %slice.8.mine), channel_id=1, source_target_pairs={{0,1},{1,0},{2,3},{3,2},{4,5},{5,4},{6,7},{7,6},{8,9},{9,8},{10,11... | collective-permute-start | bytes 294920 | tf_op jit(solution)/shard_map/ppermute | solution.py:457
  22.3 5.9 %collective-permute-start.7 = (f32[128,128]{1,0:T(8,128)S(1)}, f32[128,128]{1,0:T(8,128)S(1)}, u32[]{:S(2)}, u32[]{:S(2)}) collective-permute-start(f32[128,128]{1,0:T(8,128)S(1)} %get-tuple-element.17), channel_id=1, source_target_pairs={{0,240},{16,0},{32,16},{48,32},{64,48},{80,64},{96,80},{112,96},{1... | collective-permute-start | bytes 196616 | tf_op jit(solution)/shard_map/ppermute | solution.py:452
  28.2 0.0 collective-permute-start.6
  28.2 1.5 %collective-permute-done.7.east = f32[128,128]{1,0:T(8,128)S(1)} collective-permute-done((f32[128,128]{1,0:T(8,128)S(1)}, f32[128,128]{1,0:T(8,128)S(1)}, u32[]{:S(2)}, u32[]{:S(2)}) %collective-permute-start.7) | collective-permute-done | bytes 65568 | tf_op jit(solution)/shard_map/ppermute | solution.py:452
  29.7 3.7 %collective-permute-done.6.west = f32[128,128]{1,0:T(8,128)S(1)} collective-permute-done((f32[128,128]{1,0:T(8,128)S(1)}, f32[128,128]{1,0:T(8,128)S(1)}, u32[]{:S(2)}, u32[]{:S(2)}) %collective-permute-start.6) | collective-permute-done | bytes 65568 | tf_op jit(solution)/shard_map/ppermute | solution.py:452
  33.4 0.0 collective-permute-done.5.other
  33.4 6.9 %transport.1 = f32[18,3,32,128]{3,2,1,0:T(8,128)} custom-call(f32[192,128]{1,0:T(8,128)S(1)} %slice.8.mine, f32[192,128]{1,0:T(8,128)S(1)} %collective-permute-done.5.other, f32[128,128]{1,0:T(8,128)S(1)} %collective-permute-done.6.west, f32[128,128]{1,0:T(8,128)S(1)} %collective-permute-done.7.east, f32[18,3,48,128]{3,2,1,0:T(8,128)S(1)} %get-tuple-element.15.padded, ...), custom_call_target="tpu_custom_call" | custom-call | tf_op jit(solution)/shard_map/transport/pallas_call | solution.py:429
  (6 shorter events, 0.1 us)
Async XLA Ops:
  1.8 4.3 %collective-permute-start = (f32[224,128]{1,0:T(8,128)S(1)}, f32[224,128]{1,0:T(8,128)S(1)}, u32[]{:S(2)}, u32[]{:S(2)}) collective-permute-start(f32[224,128]{1,0:T(8,128)S(1)} %get-tuple-element.12), channel_id=1, source_target_pairs={{0,1},{1,0},{2,3},{3,2},{4,5},{5,4},{6,7},{7,6},{8,9},{9,8},{10,11... | collective-permute-start | bytes 344072 | tf_op jit(solution)/shard_map/ppermute | solution.py:457
  6.1 6.0 %collective-permute-start.3 = (f32[224,128]{1,0:T(8,128)S(1)}, f32[224,128]{1,0:T(8,128)S(1)}, u32[]{:S(2)}, u32[]{:S(2)}) collective-permute-start(f32[224,128]{1,0:T(8,128)S(1)} %add.15), channel_id=1, source_target_pairs={{0,4},{1,5},{2,6},{3,7},{4,0},{5,1},{6,2},{7,3},{8,12},{9,13},{10,... | collective-permute-start | bytes 344072 | tf_op jit(solution)/shard_map/ppermute | solution.py:462
  7.4 5.8 %collective-permute-start.2 = (f32[224,128]{1,0:T(8,128)S(1)}, f32[224,128]{1,0:T(8,128)S(1)}, u32[]{:S(2)}, u32[]{:S(2)}) collective-permute-start(f32[224,128]{1,0:T(8,128)S(1)} %add.15), channel_id=1, source_target_pairs={{0,6},{1,7},{2,0},{3,1},{4,2},{5,3},{6,4},{7,5},{8,14},{9,15},{10,... | collective-permute-start | bytes 344072 | tf_op jit(solution)/shard_map/ppermute | solution.py:462
  8.2 6.4 %collective-permute-start.1 = (f32[224,128]{1,0:T(8,128)S(1)}, f32[224,128]{1,0:T(8,128)S(1)}, u32[]{:S(2)}, u32[]{:S(2)}) collective-permute-start(f32[224,128]{1,0:T(8,128)S(1)} %add.15), channel_id=1, source_target_pairs={{0,2},{1,3},{2,4},{3,5},{4,6},{5,7},{6,0},{7,1},{8,10},{9,11},{10,... | collective-permute-start | bytes 344072 | tf_op jit(solution)/shard_map/ppermute | solution.py:462
  14.6 5.2 %collective-permute-start.4 = (f32[224,128]{1,0:T(8,128)S(1)}, f32[224,128]{1,0:T(8,128)S(1)}, u32[]{:S(2)}, u32[]{:S(2)}) collective-permute-start(f32[224,128]{1,0:T(8,128)S(1)} %add_add_fusion), channel_id=1, source_target_pairs={{0,8},{1,9},{2,10},{3,11},{4,12},{5,13},{6,14},{7,15},{8,0},{9,1},... | collective-permute-start | bytes 344072 | tf_op jit(solution)/shard_map/ppermute | solution.py:457
  16.0 1.2 %copy-start = (f32[18,3,32,128]{3,2,1,0:T(8,128)S(1)}, f32[18,3,32,128]{3,2,1,0:T(8,128)}, u32[]{:S(2)}) copy-start(f32[18,3,32,128]{3,2,1,0:T(8,128)} %mass.1) | copy-start | bytes 2654212
  19.9 13.5 %collective-permute-start.5 = (f32[192,128]{1,0:T(8,128)S(1)}, f32[192,128]{1,0:T(8,128)S(1)}, u32[]{:S(2)}, u32[]{:S(2)}) collective-permute-start(f32[192,128]{1,0:T(8,128)S(1)} %slice.8.mine), channel_id=1, source_target_pairs={{0,1},{1,0},{2,3},{3,2},{4,5},{5,4},{6,7},{7,6},{8,9},{9,8},{10,11... | collective-permute-start | bytes 294920 | tf_op jit(solution)/shard_map/ppermute | solution.py:457
  22.3 7.4 %collective-permute-start.7 = (f32[128,128]{1,0:T(8,128)S(1)}, f32[128,128]{1,0:T(8,128)S(1)}, u32[]{:S(2)}, u32[]{:S(2)}) collective-permute-start(f32[128,128]{1,0:T(8,128)S(1)} %get-tuple-element.17), channel_id=1, source_target_pairs={{0,240},{16,0},{32,16},{48,32},{64,48},{80,64},{96,80},{112,96},{1... | collective-permute-start | bytes 196616 | tf_op jit(solution)/shard_map/ppermute | solution.py:452
  28.2 5.2 %collective-permute-start.6 = (f32[128,128]{1,0:T(8,128)S(1)}, f32[128,128]{1,0:T(8,128)S(1)}, u32[]{:S(2)}, u32[]{:S(2)}) collective-permute-start(f32[128,128]{1,0:T(8,128)S(1)} %get-tuple-element.18), channel_id=1, source_target_pairs={{0,16},{16,32},{32,48},{48,64},{64,80},{80,96},{96,112},{112,128},... | collective-permute-start | bytes 196616 | tf_op jit(solution)/shard_map/ppermute | solution.py:452

commit v4 on v3

v4 whole, which is shorter than its diff:
```python
import jax
import jax.numpy as jnp
from jax import lax
from jax.experimental import pallas as pl
from jax.experimental.pallas import tpu as pltpu
from jax.sharding import PartitionSpec as P

NS = 2
EDGE = NS + 3
SEG = 2 * EDGE
PACK = 9
STEP = 4
GROUP = 3
PAD = 8
BLOCK = 8
NEAR = (-1, 1, 2)
MET_SEG = 16


def lane_index(shape):
    return lax.broadcasted_iota(jnp.int32, shape, len(shape) - 1)


def row_index(shape):
    return lax.broadcasted_iota(jnp.int32, shape, len(shape) - 2)


def lanes(x, shift):
    return pltpu.roll(x, shift % x.shape[-1], x.ndim - 1)


def rows(x, shift):
    return pltpu.roll(x, shift % x.shape[-2], x.ndim - 2)


def face_weights(courant):
    fraction = jnp.abs(courant)
    ramp = 1.5 * fraction * (1.0 - 2.0 / 3.0 * fraction)
    near = 0.5 * courant * (1.0 - 0.5 * fraction - ramp)
    far = 0.5 * courant * (0.5 * fraction - ramp)
    mean = courant * ramp
    far_outer = far * (1.0 / 12.0)
    near_outer = near * (1.0 / 12.0)
    return (
        -near_outer,
        7.0 * near_outer - far_outer,
        7.0 * (near_outer + far_outer) + mean,
        7.0 * far_outer - near_outer,
        -far_outer,
    )


def north_taps(courant):
    down1, up0, up1, up2, up3 = (w for w in face_weights(courant))
    forward = courant >= 0.0
    zero = jnp.zeros_like(courant)
    f = {1: down1, 0: up0, -1: up1, -2: up2, -3: up3}
    b = {-2: down1, -1: up0, 0: up1, 1: up2, 2: up3}
    return {m: jnp.where(forward, f.get(m, zero), b.get(m, zero)) for m in range(-3, 3)}


def east_taps(courant, whole):
    weights = face_weights(courant)
    forward = courant >= 0.0
    zero = jnp.zeros_like(courant)
    one = whole == 1.0
    two = whole == 2.0
    some = whole > 0.5
    taps = {}
    for m in range(-EDGE, EDGE):
        ahead = []
        behind = []
        for n in range(NS + 1):
            place = 1 - n - m
            ahead.append(weights[place] if 0 <= place < 5 else zero)
            place = m + 2 - n
            behind.append(weights[place] if 0 <= place < 5 else zero)
        f = jnp.where(two, ahead[2], jnp.where(one, ahead[1], ahead[0]))
        b = jnp.where(two, behind[2], jnp.where(one, behind[1], behind[0]))
        if m == -1:
            f = f + jnp.where(some, 0.5, 0.0)
        if m == -2:
            f = f + jnp.where(two, 0.5, 0.0)
        if m == 0:
            b = b - jnp.where(some, 0.5, 0.0)
        if m == 1:
            b = b - jnp.where(two, 0.5, 0.0)
        taps[m] = jnp.where(forward, f, b)
    return taps


def difference_taps(here, ahead, reach):
    out = {}
    for m in range(-reach, reach + 1):
        if m in here and m - 1 in ahead:
            out[m] = here[m] - ahead[m - 1]
        elif m in here:
            out[m] = here[m]
        else:
            out[m] = -ahead[m - 1]
    return out


def north_coefficients(courant):
    count = courant.shape[0]
    row = row_index(courant.shape)
    here = north_taps(jnp.where(row == 0, 0.0, courant))
    taps = difference_taps(here, {m: rows(here[m], -1) for m in here}, 3)
    return [
        jnp.where((row + m >= 0) & (row + m < count), taps[m], 0.0) for m in range(-3, 4)
    ]


def pick(x, index):
    return jnp.take_along_axis(x, index, axis=1, mode="promise_in_bounds")


def position():
    return lax.axis_index("tracer")


def prepare_kernel(*refs):
    sources, (keep, send, *fields, sems) = refs[:6], refs[6:]
    copies = [
        pltpu.make_async_copy(source, place, sems.at[k])
        for k, (source, place) in enumerate(zip(sources, fields))
    ]
    for copy in copies:
        copy.start()
    for copy in copies:
        copy.wait()
    thick, fe, fn, ce, cn, ne = fields
    core = position() % 2
    levels, count, width = thick.shape[1:]
    lane = lane_index((count, width))
    row = row_index((count, width))
    edge_rows = jnp.zeros((count, width), jnp.float32)
    for l in range(levels):
        east_mass = fe[0, l]
        north_mass = jnp.where(row == 0, 0.0, fn[0, l])
        thickness = (
            thick[0, l]
            + (east_mass - jnp.where(lane == width - 1, 0.0, lanes(east_mass, -1)))
            + (north_mass - rows(north_mass, -1))
        )
        whole = ne[0, l].astype(jnp.float32)
        first = (thickness, ce[0, l])
        second = (cn[0, l], whole)
        for k in range(2):
            start = (k * levels + l) * count
            keep[start : start + count, :] = jnp.where(core == 0, first[k], second[k])
            send[start : start + count, :] = jnp.where(core == 0, second[k], first[k])
        edges = jnp.where(lane < SEG, lanes(cn[0, l], EDGE), 0.0)
        for k, value in enumerate((ce[0, l], whole, east_mass)):
            edges = jnp.where(lane == SEG + k, lanes(value, SEG + k), edges)
        edge_rows = edge_rows + lanes(jnp.where(lane < MET_SEG, edges, 0.0), MET_SEG * l)
    base = 2 * levels * count
    keep[base : base + count, :] = edge_rows
    send[base : base + count, :] = edge_rows


def prepare(thick, fe, fn, ce, cn, ne):
    levels, count, width = thick.shape[1:]
    vmem = pl.BlockSpec(memory_space=pltpu.VMEM)
    half = pltpu.VMEM(((2 * levels + 1) * count, width), jnp.float32)
    return pl.pallas_call(
        prepare_kernel,
        out_shape=(half, half),
        in_specs=[pl.BlockSpec(memory_space=pl.ANY)] * 6,
        out_specs=(vmem, vmem),
        scratch_shapes=[pltpu.VMEM(thick.shape, jnp.float32)] * 5
        + [pltpu.VMEM(ne.shape, jnp.int32), pltpu.SemaphoreType.DMA((6,))],
        name="prepare",
    )(thick, fe, fn, ce, cn, ne)


def pack_kernel(mass, last, first, padded, moved):
    tracers, levels, count, width = mass.shape
    lane = lane_index((count, width))
    zero_rows = jnp.zeros((PAD, width), jnp.float32)

    def level(l, carry):
        a = jnp.zeros((count, width), jnp.float32)
        b = a
        for t in range(tracers):
            value = mass[t, l]
            inside = (lane >= EDGE * t) & (lane < EDGE * (t + 1))
            a = jnp.where(inside, lanes(value, EDGE * (t + 1)), a)
            b = jnp.where(inside, lanes(value, EDGE * t), b)
            padded[t, l, :PAD, :] = zero_rows
            padded[t, l, PAD : PAD + count, :] = value
            padded[t, l, PAD + count :, :] = zero_rows
            for k, shift in enumerate(NEAR):
                moved[k, t, l] = lanes(value, -shift)
        last[l] = a
        first[l] = b
        return carry

    lax.fori_loop(0, levels, level, 0)


def pack(mass):
    tracers, levels, count, width = mass.shape
    vmem = pl.BlockSpec(memory_space=pltpu.VMEM)
    packed = pltpu.VMEM((levels, count, width), jnp.float32)
    last, first, padded, moved = pl.pallas_call(
        pack_kernel,
        out_shape=(
            packed,
            packed,
            pltpu.VMEM((tracers, levels, count + 2 * PAD, width), jnp.float32),
            pltpu.VMEM((len(NEAR),) + mass.shape, jnp.float32),
        ),
        in_specs=[vmem],
        out_specs=(vmem,) * 4,
        compiler_params=pltpu.CompilerParams(vmem_limit_bytes=24 * 1024 * 1024),
        cost_estimate=pl.CostEstimate(flops=2000000, bytes_accessed=1000000, transcendentals=0),
        name="pack",
    )(mass)
    rows_flat = (levels * count, width)
    return last.reshape(rows_flat), first.reshape(rows_flat), padded, moved


def segments(shape):
    lane = lane_index(shape)
    segment = sum(
        ((lane >= SEG * k).astype(jnp.int32) for k in range(1, PACK)), jnp.zeros(shape, jnp.int32)
    )
    return segment, lane - SEG * segment, lane < SEG * PACK


def moved_places(held):
    return {shift: lanes(held, shift) if shift else held for shift in (-STEP, 0, STEP)}


def east_parts(taps, near, parts=None):
    parts = dict(parts or {})
    for m in taps:
        shift = east_group(m)
        term = taps[m] * near[m - shift]
        parts[shift] = parts[shift] + term if shift in parts else term
    return parts


def moved_sum(parts):
    return parts[0] + (lanes(parts[-STEP], STEP) + lanes(parts[STEP], -STEP))


def near_cells(x):
    return {0: x, **{shift: lanes(x, -shift) for shift in NEAR}}


def inner_kernel(
    mine, other, padded, shifted, sums, outer_c, edge_c, thickness,
    east_c, north_c, inners, middle, partial,
):
    tracers, levels, count, width = sums.shape
    shape = (count, width)
    lane = lane_index(shape)
    low = position() % 2 == 0
    _, in_segment, packed_lane = segments(shape)
    zero_rows = jnp.zeros((PAD, width), jnp.float32)
    for slot in range(2):
        for j in range(GROUP):
            middle[slot, j, :PAD, :] = zero_rows
            middle[slot, j, PAD + count :, :] = zero_rows
    edge_index = jnp.where(packed_lane, in_segment + (width - EDGE), 0)
    edge_index = jnp.where(edge_index >= width, edge_index - width, edge_index)
    moved_index = moved_places(edge_index)
    moved_segment = moved_places(jnp.where(packed_lane, in_segment, -2 * SEG))

    def level(l, carry):
        fields = []
        for half in range(2):
            for k in range(2):
                place = pl.ds(pl.multiple_of((k * levels + l) * count, count), count)
                a = mine[place, :]
                b = other[place, :]
                fields.append(jnp.where(low, a, b) if half == 0 else jnp.where(low, b, a))
        thick, east_courant, north_courant, whole = fields
        thickness[l] = thick
        here = east_taps(east_courant, whole)
        ahead = {m: jnp.where(lane == width - 1, 0.0, lanes(here[m], -1)) for m in here}
        taps = difference_taps(here, ahead, EDGE)
        for m in range(-EDGE, EDGE + 1):
            value = taps[m]
            if m != 0:
                q = moved_segment[east_group(m)]
                crosses = ((q < EDGE) != (q + m < EDGE)) & (q >= 0)
                outer_c[m + EDGE, l] = jnp.where(crosses, pick(value, moved_index[east_group(m)]), 0.0)
            if m < 0:
                value = jnp.where(lane >= -m, value, 0.0)
            if m > 0:
                value = jnp.where(lane < width - m, value, 0.0)
            shift = east_group(m)
            east_c[m + EDGE, l] = lanes(value, shift) if shift else value
        for m, value in enumerate(north_coefficients(north_courant)):
            north_c[m, l] = value
        for m, value in enumerate(north_coefficients(pick(north_courant, edge_index))):
            edge_c[m, l] = value
        return carry

    lax.fori_loop(0, levels, level, 0)
    steps = levels * (tracers // GROUP)

    def block(b):
        return slice(b * BLOCK, (b + 1) * BLOCK)

    def padded_block(b, m=0):
        return slice(PAD + b * BLOCK + m, PAD + (b + 1) * BLOCK + m)

    def place(step):
        step = jnp.clip(step, 0, steps - 1)
        return step % levels, (step // levels) * GROUP

    def weights(ref, l, b, reach):
        return {m: ref[m + reach, l, block(b), :] for m in range(-reach, reach + 1)}

    def front(step):
        l, t0 = place(step)
        slot = (step + 2) % 2
        for b in range(count // BLOCK):
            taps = weights(east_c, l, b, EDGE)
            north = weights(north_c, l, b, 3)
            for j in range(GROUP):
                x = padded[t0 + j, l, padded_block(b), :]
                inner = x + north[0] * x
                for m in (-3, -2, -1, 1, 2, 3):
                    inner = inner + north[m] * padded[t0 + j, l, padded_block(b, m), :]
                inners[slot, j, block(b), :] = inner
                near = {0: x}
                for k, shift in enumerate(NEAR):
                    near[shift] = shifted[k, t0 + j, l, block(b), :]
                middle[slot, j, padded_block(b), :] = x + moved_sum(east_parts(taps, near))

    def back(step):
        l, t0 = place(step)
        slot = (step + 2) % 2
        for b in range(count // BLOCK):
            taps = weights(east_c, l, b, EDGE)
            north = weights(north_c, l, b, 3)
            for j in range(GROUP):
                parts = east_parts(taps, near_cells(inners[slot, j, block(b), :]))
                total = 0.5 * padded[t0 + j, l, padded_block(b), :] + parts[0]
                for m in range(-3, 4):
                    total = total + north[m] * middle[slot, j, padded_block(b, m), :]
                partial[slot, 0, j, block(b), :] = total
                partial[slot, 1, j, block(b), :] = parts[-STEP]
                partial[slot, 2, j, block(b), :] = parts[STEP]

    def finish(step):
        l, t0 = place(step)
        slot = (step + 2) % 2
        for b in range(count // BLOCK):
            for j in range(GROUP):
                sums[t0 + j, l, block(b), :] = partial[slot, 0, j, block(b), :] + (
                    lanes(partial[slot, 1, j, block(b), :], STEP)
                    + lanes(partial[slot, 2, j, block(b), :], -STEP)
                )

    def step_of_three(step, carry):
        finish(step - 1)
        back(step)
        front(step + 1)
        return carry

    lax.fori_loop(-1, steps + 1, step_of_three, 0)


def inner_update(mine, other, padded, shifted):
    tracers, levels, count, width = shifted.shape[1:]
    vmem = pl.BlockSpec(memory_space=pltpu.VMEM)
    level = (levels, count, width)
    return pl.pallas_call(
        inner_kernel,
        out_shape=(
            pltpu.VMEM((tracers,) + level, jnp.float32),
            pltpu.VMEM((2 * EDGE + 1,) + level, jnp.float32),
            pltpu.VMEM((7,) + level, jnp.float32),
            pltpu.VMEM(level, jnp.float32),
        ),
        in_specs=[vmem] * 4,
        out_specs=(vmem,) * 4,
        scratch_shapes=[
            pltpu.VMEM((2 * EDGE + 1,) + level, jnp.float32),
            pltpu.VMEM((7,) + level, jnp.float32),
            pltpu.VMEM((2, GROUP, count, width), jnp.float32),
            pltpu.VMEM((2, GROUP, count + 2 * PAD, width), jnp.float32),
            pltpu.VMEM((2, 3, GROUP, count, width), jnp.float32),
        ],
        compiler_params=pltpu.CompilerParams(vmem_limit_bytes=24 * 1024 * 1024),
        cost_estimate=pl.CostEstimate(flops=20000000, bytes_accessed=6000000, transcendentals=0),
        name="inner",
    )(mine, other, padded, shifted)


def edge_kernel(west, east, own, sums, outer_c, edge_c, thickness, out, stage, sems):
    tracers, levels, count, width = sums.shape
    shape = (count, width)
    lane = lane_index(shape)
    segment, in_segment, packed_lane = segments(shape)
    from_west_lane = in_segment < EDGE
    at_edge = (lane < EDGE) | (lane >= width - EDGE)
    last_face = {
        shift: q == EDGE - 1
        for shift, q in moved_places(jnp.where(packed_lane, in_segment, -2 * SEG)).items()
    }
    base = levels * count
    met_east = east[base : base + count, :]
    met_west = west[base : base + count, :]

    def copy(l):
        return pltpu.make_async_copy(stage.at[:, l], out.at[:, l], sems.at[l])

    def level(l, carry):
        level_rows = pl.ds(pl.multiple_of(l * count, count), count)
        met_lane = jnp.where(packed_lane, in_segment + MET_SEG * l, 0)
        met = jnp.where(lane - MET_SEG * l < EDGE, met_west, met_east)
        beyond = east_taps(
            pick(met_east, jnp.full(shape, SEG, jnp.int32) + MET_SEG * l),
            pick(met_east, jnp.full(shape, SEG + 1, jnp.int32) + MET_SEG * l),
        )
        mass_flux = pick(met_east, jnp.full(shape, SEG + 2, jnp.int32) + MET_SEG * l)
        inverse = 2.0 / (thickness[l] - jnp.where(lane == width - 1, mass_flux, 0.0))
        face = {
            m: jnp.where(last_face[east_group(m)], -beyond[m - 1], 0.0)
            for m in range(1 - EDGE, EDGE + 1)
        }
        outer = {m: outer_c[m + EDGE, l] for m in range(-EDGE, EDGE + 1) if m != 0}
        for m in range(1, EDGE + 1):
            outer[m] = outer[m] + face[m]
        inside = {m: face[m] for m in range(1 - EDGE, 1)}
        edge_taps = [edge_c[m, l] for m in range(7)]
        packed_taps = north_coefficients(pick(met, met_lane))
        for half in range(2):
            first_lane = EDGE * (segment + PACK * half) + in_segment
            west_index = jnp.where(packed_lane & from_west_lane, first_lane, 0)
            east_index = jnp.where(packed_lane & ~from_west_lane, first_lane - EDGE, 0)
            own_cells = pick(own[level_rows, :], west_index)
            cells = jnp.where(
                from_west_lane,
                pick(west[level_rows, :], west_index),
                pick(east[level_rows, :], east_index),
            )
            inner = cells
            own_inner = own_cells
            for m in range(-3, 4):
                inner = inner + packed_taps[m + 3] * rows(cells, -m)
                own_inner = own_inner + edge_taps[m + 3] * rows(own_cells, -m)
            first = moved_sum(
                east_parts(inside, near_cells(own_cells), east_parts(outer, near_cells(cells)))
            )
            total = moved_sum(
                east_parts(inside, near_cells(own_inner), east_parts(outer, near_cells(inner)))
            )
            for m in range(-3, 4):
                total = total + edge_taps[m + 3] * rows(first, -m)
            for k in range(PACK):
                t = half * PACK + k
                moved = jnp.where(at_edge, lanes(total, width - EDGE - SEG * k), 0.0)
                stage[t, l] = (sums[t, l] + moved) * inverse
        copy(l).start()
        return carry

    lax.fori_loop(0, levels, level, 0)
    for l in range(levels):
        copy(l).wait()


def edge_update(west, east, own, sums, outer_c, edge_c, thickness):
    tracers, levels, count, width = sums.shape
    vmem = pl.BlockSpec(memory_space=pltpu.VMEM)
    return pl.pallas_call(
        edge_kernel,
        out_shape=jax.ShapeDtypeStruct(sums.shape, jnp.float32),
        in_specs=[vmem] * 7,
        out_specs=pl.BlockSpec(memory_space=pl.ANY),
        scratch_shapes=[pltpu.VMEM(sums.shape, jnp.float32), pltpu.SemaphoreType.DMA((levels,))],
        compiler_params=pltpu.CompilerParams(vmem_limit_bytes=24 * 1024 * 1024),
        name="edges",
    )(west, east, own, sums, outer_c, edge_c, thickness)


def east_group(m):
    return -STEP if m < -1 else (STEP if m > 2 else 0)


def ring(x, by):
    size = lax.axis_size("space")
    return lax.ppermute(x, "space", [(i, (i + by) % size) for i in range(size)])


def exchange(x, flip):
    size = lax.axis_size("tracer")
    return lax.ppermute(x, "tracer", [(i, i ^ flip) for i in range(size)])


def turn(x, by):
    size = lax.axis_size("tracer")
    return lax.ppermute(x, "tracer", [(i, i // 8 * 8 + (i + 2 * by) % 8) for i in range(size)])


def shards(mass, thick, fe, fn, ce, cn, ne, owner):
    keep, send = prepare(thick, fe, fn, ce, cn, ne)
    last, first, padded, shifted = pack(mass)
    me, chosen = position(), owner[0]
    other_core = exchange(send, 1)
    total = jnp.where(chosen == me, keep, jnp.where(chosen == me ^ 1, other_core, 0.0))
    total = total + (turn(total, 1) + turn(total, -1) + turn(total, 2))
    total = total + exchange(total, 8)
    main = 2 * mass.shape[1] * mass.shape[2]
    mine = total[:main]
    edges = total[main:]
    other = exchange(mine, 1)
    west = ring(jnp.concatenate([last, edges]), 1)
    east = ring(jnp.concatenate([first, edges]), -1)
    return edge_update(west, east, last, *inner_update(mine, other, padded, shifted))


def solution(mesh):
    spec = P("tracer", None, None, "space")
    return jax.shard_map(
        shards, mesh=mesh, in_specs=(spec,) * 7 + (P("space"),), out_specs=spec, check_vma=False
    )
```

time: 40.5 us -> 35.5 us (0.88)
  waiting for transfers between devices: 13.3 us -> 8.14 us
    ppermute x2, waiting for transfers between devices: 5.22 us -> 0.74 us  [ring(): return lax.ppermute(x, 'space', [(i, (i + by) % size) for i in range(size)])]
    ppermute x3, waiting for transfers between devices: 2.32 us -> 1.67 us  [exchange(): return lax.ppermute(x, 'tracer', [(i, i ^ flip) for i in range(size)])]
    pallas_call x1 -> x2, Pallas kernels: 6.85 us -> 6.99 us  [the longest x1 4.47 us: inner_update(): pl.pallas_call(inner_kernel, out_shape=(pltpu.VMEM((tracers,) + level, jn...]
  transfers between devices with their start and end apart: 8 -> 8, of which waited for: 7 -> 6; matrix products, arithmetic and copies ran while one was open for 0% -> 0% of each run, Pallas kernels for 3% -> 16%
where the time goes in v4:
time: 35.5 us; the launch traced here: 35.3 us
  starting transfers between devices  15.7 us (44%)
  Pallas kernels  9.45 us (27%)
  waiting for transfers between devices  8.14 us (23%)
  local copies, waits for them, and re-layouts  1.18 us (3%)
  between operations  0.71 us (2%)
    ppermute x3, starting transfers between devices, exchange(): return lax.ppermute(x, 'tracer', [(i, i ^ flip) for i in range(size)])  7.08 us
    ppermute x2, starting transfers between devices, ring(): return lax.ppermute(x, 'space', [(i, (i + by) % size) for i in range(size)])  5.93 us
    ppermute x3, waiting for transfers between devices, turn(): lax.ppermute(x, 'tracer', [(i, i // 8 * 8 + (i + 2 * by) % 8) for i in ra...  5.74 us
    pallas_call x1, Pallas kernels, inner_update(): pl.pallas_call(inner_kernel, out_shape=(pltpu.VMEM((tracers,) + level, jn...  4.47 us
    ppermute x3, starting transfers between devices, turn(): lax.ppermute(x, 'tracer', [(i, i // 8 * 8 + (i + 2 * by) % 8) for i in ra...  2.73 us
    pallas_call x1, Pallas kernels, edge_update(): pl.pallas_call(edge_kernel, out_shape=jax.ShapeDtypeStruct(sums.shape, jn...  2.52 us
    ppermute x3, waiting for transfers between devices, exchange(): return lax.ppermute(x, 'tracer', [(i, i ^ flip) for i in range(size)])  1.67 us
    pallas_call x1, Pallas kernels, pack(): pl.pallas_call(pack_kernel, out_shape=(packed, packed, pltpu.VMEM((tracer...  1.32 us
  transfers between devices with their start and end apart: 8, of which 6 were waited for; matrix products, arithmetic and copies ran while one was open for 0% of the time, Pallas kernels for 16%

profile of v4, /device:TPU:1, one launch (start us, length us, event | category | flops | bytes accessed | tf_op | source)
XLA Modules:
  0.0 35.3 jit_solution(684412383261281295)
XLA Ops:
  0.0 1.1 %prepare.1 = (f32[224,128]{1,0:T(8,128)S(1)}, f32[224,128]{1,0:T(8,128)S(1)}) custom-call(f32[1,3,32,128]{3,2,1,0:T(8,128)} %refs_0_.1, f32[1,3,32,128]{3,2,1,0:T(8,128)} %refs_1_.1, f32[1,3,32,128]{3,2,1,0:T(8,128)} %refs_2_.1, f32[1,3,32,128]{3,2,1,0:T(8,128)} %refs_3_.1, f32[1,3,32,128]{3,2,1,0:T(8,128)} %refs_4_.1, s32[1,3,32,128]{3,2,1,0:T(8,128)} %refs_5_.1), custom_call_target="tpu_custom_call" | custom-call | tf_op jit(solution)/shard_map/prepare/pallas_call | solution.py:166
  1.1 3.3 %collective-permute-start = (f32[224,128]{1,0:T(8,128)S(1)}, f32[224,128]{1,0:T(8,128)S(1)}, u32[]{:S(2)}, u32[]{:S(2)}) collective-permute-start(f32[224,128]{1,0:T(8,128)S(1)} %get-tuple-element.17), channel_id=1, source_target_pairs={{0,1},{1,0},{2,3},{3,2},{4,5},{5,4},{6,7},{7,6},{8,9},{9,8},{10,11... | collective-permute-start | bytes 344072 | tf_op jit(solution)/shard_map/ppermute | solution.py:495
  5.1 0.3 collective-permute-done
  5.5 1.3 %collective-permute-start.3 = (f32[224,128]{1,0:T(8,128)S(1)}, f32[224,128]{1,0:T(8,128)S(1)}, u32[]{:S(2)}, u32[]{:S(2)}) collective-permute-start(f32[224,128]{1,0:T(8,128)S(1)} %select_select_fusion), channel_id=1, source_target_pairs={{0,4},{1,5},{2,6},{3,7},{4,0},{5,1},{6,2},{7,3},{8,12},{9,13},{10,... | collective-permute-start | bytes 344072 | tf_op jit(solution)/shard_map/ppermute | solution.py:500
  6.7 0.8 %collective-permute-start.2 = (f32[224,128]{1,0:T(8,128)S(1)}, f32[224,128]{1,0:T(8,128)S(1)}, u32[]{:S(2)}, u32[]{:S(2)}) collective-permute-start(f32[224,128]{1,0:T(8,128)S(1)} %select_select_fusion), channel_id=1, source_target_pairs={{0,6},{1,7},{2,0},{3,1},{4,2},{5,3},{6,4},{7,5},{8,14},{9,15},{10,... | collective-permute-start | bytes 344072 | tf_op jit(solution)/shard_map/ppermute | solution.py:500
  7.5 0.7 %collective-permute-start.1 = (f32[224,128]{1,0:T(8,128)S(1)}, f32[224,128]{1,0:T(8,128)S(1)}, u32[]{:S(2)}, u32[]{:S(2)}) collective-permute-start(f32[224,128]{1,0:T(8,128)S(1)} %select_select_fusion), channel_id=1, source_target_pairs={{0,2},{1,3},{2,4},{3,5},{4,6},{5,7},{6,0},{7,1},{8,10},{9,11},{10,... | collective-permute-start | bytes 344072 | tf_op jit(solution)/shard_map/ppermute | solution.py:500
  8.2 3.2 %collective-permute-done.3 = f32[224,128]{1,0:T(8,128)S(1)} collective-permute-done((f32[224,128]{1,0:T(8,128)S(1)}, f32[224,128]{1,0:T(8,128)S(1)}, u32[]{:S(2)}, u32[]{:S(2)}) %collective-permute-start.3) | collective-permute-done | bytes 114720 | tf_op jit(solution)/shard_map/ppermute | solution.py:500
  11.4 1.1 %collective-permute-done.2 = f32[224,128]{1,0:T(8,128)S(1)} collective-permute-done((f32[224,128]{1,0:T(8,128)S(1)}, f32[224,128]{1,0:T(8,128)S(1)}, u32[]{:S(2)}, u32[]{:S(2)}) %collective-permute-start.2) | collective-permute-done | bytes 114720 | tf_op jit(solution)/shard_map/ppermute | solution.py:500
  12.5 1.4 %collective-permute-done.1 = f32[224,128]{1,0:T(8,128)S(1)} collective-permute-done((f32[224,128]{1,0:T(8,128)S(1)}, f32[224,128]{1,0:T(8,128)S(1)}, u32[]{:S(2)}, u32[]{:S(2)}) %collective-permute-start.1) | collective-permute-done | bytes 114720 | tf_op jit(solution)/shard_map/ppermute | solution.py:500
  14.0 1.4 %collective-permute-start.4 = (f32[224,128]{1,0:T(8,128)S(1)}, f32[224,128]{1,0:T(8,128)S(1)}, u32[]{:S(2)}, u32[]{:S(2)}) collective-permute-start(f32[224,128]{1,0:T(8,128)S(1)} %add_add_fusion), channel_id=1, source_target_pairs={{0,8},{1,9},{2,10},{3,11},{4,12},{5,13},{6,14},{7,15},{8,0},{9,1},... | collective-permute-start | bytes 344072 | tf_op jit(solution)/shard_map/ppermute | solution.py:495
  15.3 0.0 copy-start
  15.3 1.2 %copy-done = f32[18,3,32,128]{3,2,1,0:T(8,128)S(1)} copy-done((f32[18,3,32,128]{3,2,1,0:T(8,128)S(1)}, f32[18,3,32,128]{3,2,1,0:T(8,128)}, u32[]{:S(2)}) %copy-start) | copy-done | bytes 884760
  16.5 1.3 %pack.1 = (f32[3,32,128]{2,1,0:T(8,128)S(1)}, f32[3,32,128]{2,1,0:T(8,128)S(1)}, f32[18,3,48,128]{3,2,1,0:T(8,128)S(1)}, f32[3,18,3,32,128]{4,3,2,1,0:T(8,128)S(1)}) custom-call(f32[18,3,32,128]{3,2,1,0:T(8,128)S(1)} %copy-done), custom_call_target="tpu_custom_call" | custom-call | flops 2000000 | bytes 1000000 | tf_op jit(solution)/shard_map/pack/pallas_call | solution.py:206
  17.8 1.4 %collective-permute-done.4 = f32[224,128]{1,0:T(8,128)S(1)} collective-permute-done((f32[224,128]{1,0:T(8,128)S(1)}, f32[224,128]{1,0:T(8,128)S(1)}, u32[]{:S(2)}, u32[]{:S(2)}) %collective-permute-start.4) | collective-permute-done | bytes 114720 | tf_op jit(solution)/shard_map/ppermute | solution.py:495
  19.2 2.4 %collective-permute-start.7 = (f32[192,128]{1,0:T(8,128)S(1)}, f32[192,128]{1,0:T(8,128)S(1)}, u32[]{:S(2)}, u32[]{:S(2)}) collective-permute-start(f32[192,128]{1,0:T(8,128)S(1)} %slice.9.mine), channel_id=1, source_target_pairs={{0,1},{1,0},{2,3},{3,2},{4,5},{5,4},{6,7},{7,6},{8,9},{9,8},{10,11... | collective-permute-start | bytes 294920 | tf_op jit(solution)/shard_map/ppermute | solution.py:495
  21.6 5.9 %collective-permute-start.6 = (f32[128,128]{1,0:T(8,128)S(1)}, f32[128,128]{1,0:T(8,128)S(1)}, u32[]{:S(2)}, u32[]{:S(2)}) collective-permute-start(f32[128,128]{1,0:T(8,128)S(1)} %get-tuple-element.25), channel_id=1, source_target_pairs={{0,240},{16,0},{32,16},{48,32},{64,48},{80,64},{96,80},{112,96},{1... | collective-permute-start | bytes 196616 | tf_op jit(solution)/shard_map/ppermute | solution.py:490
  27.6 0.0 collective-permute-start.5
  27.6 0.0 collective-permute-done.7.other
  27.6 4.5 %inner.1 = (f32[18,3,32,128]{3,2,1,0:T(8,128)S(1)}, f32[11,3,32,128]{3,2,1,0:T(8,128)S(1)}, f32[7,3,32,128]{3,2,1,0:T(8,128)S(1)}, f32[3,32,128]{2,1,0:T(8,128)S(1)}) custom-call(f32[192,128]{1,0:T(8,128)S(1)} %slice.9.mine, f32[192,128]{1,0:T(8,128)S(1)} %collective-permute-done.7.other, f32[18,3,48,128]{3,2,1,0:T(8,128)S(1)} %get-tuple-element.19.padded, ...), custom_call_target="tpu_custom_call" | custom-call | flops 20000000 | bytes 6000000 | tf_op jit(solution)/shard_map/inner/pallas_call | solution.py:374
  32.0 0.0 collective-permute-done.6.east
  32.0 0.7 %collective-permute-done.5.west = f32[128,128]{1,0:T(8,128)S(1)} collective-permute-done((f32[128,128]{1,0:T(8,128)S(1)}, f32[128,128]{1,0:T(8,128)S(1)}, u32[]{:S(2)}, u32[]{:S(2)}) %collective-permute-start.5) | collective-permute-done | bytes 65568 | tf_op jit(solution)/shard_map/ppermute | solution.py:490
  32.8 2.5 %edges.1 = f32[18,3,32,128]{3,2,1,0:T(8,128)} custom-call(f32[128,128]{1,0:T(8,128)S(1)} %collective-permute-done.5.west, f32[128,128]{1,0:T(8,128)S(1)} %collective-permute-done.6.east, f32[96,128]{1,0:T(8,128)S(1)} %bitcast.6, f32[18,3,32,128]{3,2,1,0:T(8,128)S(1)} %get-tuple-element.21.sums, f32[11,3,32,128]{3,2,1,0:T(8,128)S(1)} %get-tuple-element.22.outer_c, ...), custom_call_target="tpu_custom_call" | custom-call | tf_op jit(solution)/shard_map/edges/pallas_call | solution.py:473
  (6 shorter events, 0.1 us)
Async XLA Ops:
  1.1 4.3 %collective-permute-start = (f32[224,128]{1,0:T(8,128)S(1)}, f32[224,128]{1,0:T(8,128)S(1)}, u32[]{:S(2)}, u32[]{:S(2)}) collective-permute-start(f32[224,128]{1,0:T(8,128)S(1)} %get-tuple-element.17), channel_id=1, source_target_pairs={{0,1},{1,0},{2,3},{3,2},{4,5},{5,4},{6,7},{7,6},{8,9},{9,8},{10,11... | collective-permute-start | bytes 344072 | tf_op jit(solution)/shard_map/ppermute | solution.py:495
  5.5 6.0 %collective-permute-start.3 = (f32[224,128]{1,0:T(8,128)S(1)}, f32[224,128]{1,0:T(8,128)S(1)}, u32[]{:S(2)}, u32[]{:S(2)}) collective-permute-start(f32[224,128]{1,0:T(8,128)S(1)} %select_select_fusion), channel_id=1, source_target_pairs={{0,4},{1,5},{2,6},{3,7},{4,0},{5,1},{6,2},{7,3},{8,12},{9,13},{10,... | collective-permute-start | bytes 344072 | tf_op jit(solution)/shard_map/ppermute | solution.py:500
  6.7 5.8 %collective-permute-start.2 = (f32[224,128]{1,0:T(8,128)S(1)}, f32[224,128]{1,0:T(8,128)S(1)}, u32[]{:S(2)}, u32[]{:S(2)}) collective-permute-start(f32[224,128]{1,0:T(8,128)S(1)} %select_select_fusion), channel_id=1, source_target_pairs={{0,6},{1,7},{2,0},{3,1},{4,2},{5,3},{6,4},{7,5},{8,14},{9,15},{10,... | collective-permute-start | bytes 344072 | tf_op jit(solution)/shard_map/ppermute | solution.py:500
  7.5 6.4 %collective-permute-start.1 = (f32[224,128]{1,0:T(8,128)S(1)}, f32[224,128]{1,0:T(8,128)S(1)}, u32[]{:S(2)}, u32[]{:S(2)}) collective-permute-start(f32[224,128]{1,0:T(8,128)S(1)} %select_select_fusion), channel_id=1, source_target_pairs={{0,2},{1,3},{2,4},{3,5},{4,6},{5,7},{6,0},{7,1},{8,10},{9,11},{10,... | collective-permute-start | bytes 344072 | tf_op jit(solution)/shard_map/ppermute | solution.py:500
  14.0 5.2 %collective-permute-start.4 = (f32[224,128]{1,0:T(8,128)S(1)}, f32[224,128]{1,0:T(8,128)S(1)}, u32[]{:S(2)}, u32[]{:S(2)}) collective-permute-start(f32[224,128]{1,0:T(8,128)S(1)} %add_add_fusion), channel_id=1, source_target_pairs={{0,8},{1,9},{2,10},{3,11},{4,12},{5,13},{6,14},{7,15},{8,0},{9,1},... | collective-permute-start | bytes 344072 | tf_op jit(solution)/shard_map/ppermute | solution.py:495
  15.3 1.2 %copy-start = (f32[18,3,32,128]{3,2,1,0:T(8,128)S(1)}, f32[18,3,32,128]{3,2,1,0:T(8,128)}, u32[]{:S(2)}) copy-start(f32[18,3,32,128]{3,2,1,0:T(8,128)} %mass.1) | copy-start | bytes 2654212
  19.2 8.3 %collective-permute-start.7 = (f32[192,128]{1,0:T(8,128)S(1)}, f32[192,128]{1,0:T(8,128)S(1)}, u32[]{:S(2)}, u32[]{:S(2)}) collective-permute-start(f32[192,128]{1,0:T(8,128)S(1)} %slice.9.mine), channel_id=1, source_target_pairs={{0,1},{1,0},{2,3},{3,2},{4,5},{5,4},{6,7},{7,6},{8,9},{9,8},{10,11... | collective-permute-start | bytes 294920 | tf_op jit(solution)/shard_map/ppermute | solution.py:495
  21.6 10.4 %collective-permute-start.6 = (f32[128,128]{1,0:T(8,128)S(1)}, f32[128,128]{1,0:T(8,128)S(1)}, u32[]{:S(2)}, u32[]{:S(2)}) collective-permute-start(f32[128,128]{1,0:T(8,128)S(1)} %get-tuple-element.25), channel_id=1, source_target_pairs={{0,240},{16,0},{32,16},{48,32},{64,48},{80,64},{96,80},{112,96},{1... | collective-permute-start | bytes 196616 | tf_op jit(solution)/shard_map/ppermute | solution.py:490
  27.6 5.2 %collective-permute-start.5 = (f32[128,128]{1,0:T(8,128)S(1)}, f32[128,128]{1,0:T(8,128)S(1)}, u32[]{:S(2)}, u32[]{:S(2)}) collective-permute-start(f32[128,128]{1,0:T(8,128)S(1)} %get-tuple-element.26), channel_id=1, source_target_pairs={{0,16},{16,32},{32,48},{48,64},{64,80},{80,96},{96,112},{112,128},... | collective-permute-start | bytes 196616 | tf_op jit(solution)/shard_map/ppermute | solution.py:490

commit v5 on v4

--- a/solution.py
+++ b/solution.py
@@ -155,14 +155,15 @@
             edges = jnp.where(lane == SEG + k, lanes(value, SEG + k), edges)
         edge_rows = edge_rows + lanes(jnp.where(lane < MET_SEG, edges, 0.0), MET_SEG * l)
     base = 2 * levels * count
-    keep[base : base + count, :] = edge_rows
-    send[base : base + count, :] = edge_rows
+    folded = edge_rows[: count // 2] + lanes(edge_rows[count // 2 :], MET_SEG * levels)
+    keep[base:, :] = folded
+    send[base:, :] = folded
 
 
 def prepare(thick, fe, fn, ce, cn, ne):
     levels, count, width = thick.shape[1:]
     vmem = pl.BlockSpec(memory_space=pltpu.VMEM)
-    half = pltpu.VMEM(((2 * levels + 1) * count, width), jnp.float32)
+    half = pltpu.VMEM((2 * levels * count + count // 2, width), jnp.float32)
     return pl.pallas_call(
         prepare_kernel,
         out_shape=(half, half),
@@ -394,7 +395,7 @@
     )(mine, other, padded, shifted)
 
 
-def edge_kernel(west, east, own, sums, outer_c, edge_c, thickness, out, stage, sems):
+def edge_kernel(west, east, wrapped, own, sums, outer_c, edge_c, thickness, out, stage, sems):
     tracers, levels, count, width = sums.shape
     shape = (count, width)
     lane = lane_index(shape)
@@ -406,8 +407,12 @@
         for shift, q in moved_places(jnp.where(packed_lane, in_segment, -2 * SEG)).items()
     }
     base = levels * count
-    met_east = east[base : base + count, :]
-    met_west = west[base : base + count, :]
+
+    def unfolded(x):
+        return jnp.concatenate([x, lanes(x, -MET_SEG * levels)])
+
+    met_east = unfolded(east[base:, :] + wrapped[base:, :])
+    met_west = unfolded(west[base:, :])
 
     def copy(l):
         return pltpu.make_async_copy(stage.at[:, l], out.at[:, l], sems.at[l])
@@ -440,7 +445,7 @@
             cells = jnp.where(
                 from_west_lane,
                 pick(west[level_rows, :], west_index),
-                pick(east[level_rows, :], east_index),
+                pick(east[level_rows, :] + wrapped[level_rows, :], east_index),
             )
             inner = cells
             own_inner = own_cells
@@ -467,27 +472,26 @@
         copy(l).wait()
 
 
-def edge_update(west, east, own, sums, outer_c, edge_c, thickness):
+def edge_update(west, east, wrapped, own, sums, outer_c, edge_c, thickness):
     tracers, levels, count, width = sums.shape
     vmem = pl.BlockSpec(memory_space=pltpu.VMEM)
     return pl.pallas_call(
         edge_kernel,
         out_shape=jax.ShapeDtypeStruct(sums.shape, jnp.float32),
-        in_specs=[vmem] * 7,
+        in_specs=[vmem] * 8,
         out_specs=pl.BlockSpec(memory_space=pl.ANY),
         scratch_shapes=[pltpu.VMEM(sums.shape, jnp.float32), pltpu.SemaphoreType.DMA((levels,))],
         compiler_params=pltpu.CompilerParams(vmem_limit_bytes=24 * 1024 * 1024),
         name="edges",
-    )(west, east, own, sums, outer_c, edge_c, thickness)
+    )(west, east, wrapped, own, sums, outer_c, edge_c, thickness)
 
 
 def east_group(m):
     return -STEP if m < -1 else (STEP if m > 2 else 0)
 
 
-def ring(x, by):
-    size = lax.axis_size("space")
-    return lax.ppermute(x, "space", [(i, (i + by) % size) for i in range(size)])
+def along(x, pairs):
+    return lax.ppermute(x, "space", pairs)
 
 
 def exchange(x, flip):
@@ -511,10 +515,16 @@
     main = 2 * mass.shape[1] * mass.shape[2]
     mine = total[:main]
     edges = total[main:]
+    size = lax.axis_size("space")
+    to_east = jnp.concatenate([last, edges])
+    to_west = jnp.concatenate([first, edges])
+    west = along(to_east, [(i, (i + 1) % size) for i in range(size)])
     other = exchange(mine, 1)
-    west = ring(jnp.concatenate([last, edges]), 1)
-    east = ring(jnp.concatenate([first, edges]), -1)
-    return edge_update(west, east, last, *inner_update(mine, other, padded, shifted))
+    east = along(to_west, [(i, i - 1) for i in range(1, size)])
+    inner = inner_update(mine, other, padded, shifted)
+    to_west, inner = lax.optimization_barrier((to_west, inner))
+    wrapped = along(to_west, [(0, size - 1)])
+    return edge_update(west, east, wrapped, last, *inner)
 
 
 def solution(mesh):

time: 35.5 us -> 40.7 us (1.15)
  starting transfers between devices: 15.7 us -> 22 us
  waiting for transfers between devices: 8.14 us -> 7 us
    ppermute x2 -> x3, starting transfers between devices: 5.93 us -> 10.4 us  [along(): return lax.ppermute(x, 'space', pairs)]
    ppermute x3, starting transfers between devices: 7.08 us -> 8.86 us  [exchange(): return lax.ppermute(x, 'tracer', [(i, i ^ flip) for i in range(size)])]
    ppermute x3, waiting for transfers between devices: 1.67 us -> 0.73 us  [exchange(): return lax.ppermute(x, 'tracer', [(i, i ^ flip) for i in range(size)])]
    ppermute x3, waiting for transfers between devices: 5.74 us -> 5.06 us  [turn(): lax.ppermute(x, 'tracer', [(i, i // 8 * 8 + (i + 2 * by) % 8) for i in ra...]
    ppermute x2 -> x3, waiting for transfers between devices: 0.74 us -> 1.22 us  [along(): return lax.ppermute(x, 'space', pairs)]
  transfers between devices with their start and end apart: 8 -> 9, of which waited for: 6 -> 6; matrix products, arithmetic and copies ran while one was open for 0% -> 0% of each run, Pallas kernels for 16% -> 14%
where the time goes in v5:
time: 40.7 us; the launch traced here: 40.5 us
  starting transfers between devices  22 us (54%)
  Pallas kernels  9.5 us (23%)
  waiting for transfers between devices  7 us (17%)
  local copies, waits for them, and re-layouts  1.18 us (3%)
  between operations  0.75 us (2%)
    ppermute x3, starting transfers between devices, along(): return lax.ppermute(x, 'space', pairs)  10.4 us
    ppermute x3, starting transfers between devices, exchange(): return lax.ppermute(x, 'tracer', [(i, i ^ flip) for i in range(size)])  8.86 us
    ppermute x3, waiting for transfers between devices, turn(): lax.ppermute(x, 'tracer', [(i, i // 8 * 8 + (i + 2 * by) % 8) for i in ra...  5.06 us
    pallas_call x1, Pallas kernels, inner_update(): pl.pallas_call(inner_kernel, out_shape=(pltpu.VMEM((tracers,) + level, jn...  4.47 us
    ppermute x3, starting transfers between devices, turn(): lax.ppermute(x, 'tracer', [(i, i // 8 * 8 + (i + 2 * by) % 8) for i in ra...  2.75 us
    pallas_call x1, Pallas kernels, edge_update(): pl.pallas_call(edge_kernel, out_shape=jax.ShapeDtypeStruct(sums.shape, jn...  2.51 us
    pallas_call x1, Pallas kernels, pack(): pl.pallas_call(pack_kernel, out_shape=(packed, packed, pltpu.VMEM((tracer...  1.32 us
    ppermute x3, waiting for transfers between devices, along(): return lax.ppermute(x, 'space', pairs)  1.22 us
  transfers between devices with their start and end apart: 9, of which 6 were waited for; matrix products, arithmetic and copies ran while one was open for 0% of the time, Pallas kernels for 14%

profile of v5, /device:TPU:1, one launch (start us, length us, event | category | flops | bytes accessed | tf_op | source)
XLA Modules:
  0.0 40.5 jit_solution(10916625121538542979)
XLA Ops:
  0.0 1.2 %prepare.1 = (f32[208,128]{1,0:T(8,128)S(1)}, f32[208,128]{1,0:T(8,128)S(1)}) custom-call(f32[1,3,32,128]{3,2,1,0:T(8,128)} %refs_0_.1, f32[1,3,32,128]{3,2,1,0:T(8,128)} %refs_1_.1, f32[1,3,32,128]{3,2,1,0:T(8,128)} %refs_2_.1, f32[1,3,32,128]{3,2,1,0:T(8,128)} %refs_3_.1, f32[1,3,32,128]{3,2,1,0:T(8,128)} %refs_4_.1, s32[1,3,32,128]{3,2,1,0:T(8,128)} %refs_5_.1), custom_call_target="tpu_custom_call" | custom-call | tf_op jit(solution)/shard_map/prepare/pallas_call | solution.py:167
  1.2 3.3 %collective-permute-start = (f32[208,128]{1,0:T(8,128)S(1)}, f32[208,128]{1,0:T(8,128)S(1)}, u32[]{:S(2)}, u32[]{:S(2)}) collective-permute-start(f32[208,128]{1,0:T(8,128)S(1)} %get-tuple-element.22), channel_id=1, source_target_pairs={{0,1},{1,0},{2,3},{3,2},{4,5},{5,4},{6,7},{7,6},{8,9},{9,8},{10,11... | collective-permute-start | bytes 319496 | tf_op jit(solution)/shard_map/ppermute | solution.py:499
  5.2 0.3 collective-permute-done
  5.5 0.1 collective-permute-start.1
  5.6 2.7 %collective-permute-start.2 = (f32[208,128]{1,0:T(8,128)S(1)}, f32[208,128]{1,0:T(8,128)S(1)}, u32[]{:S(2)}, u32[]{:S(2)}) collective-permute-start(f32[208,128]{1,0:T(8,128)S(1)} %select_select_fusion), channel_id=1, source_target_pairs={{0,6},{1,7},{2,0},{3,1},{4,2},{5,3},{6,4},{7,5},{8,14},{9,15},{10,... | collective-permute-start | bytes 319496 | tf_op jit(solution)/shard_map/ppermute | solution.py:504
  8.3 0.0 collective-permute-start.3
  8.3 2.7 %collective-permute-done.1 = f32[208,128]{1,0:T(8,128)S(1)} collective-permute-done((f32[208,128]{1,0:T(8,128)S(1)}, f32[208,128]{1,0:T(8,128)S(1)}, u32[]{:S(2)}, u32[]{:S(2)}) %collective-permute-start.1) | collective-permute-done | bytes 106528 | tf_op jit(solution)/shard_map/ppermute | solution.py:504
  11.0 1.5 %collective-permute-done.2 = f32[208,128]{1,0:T(8,128)S(1)} collective-permute-done((f32[208,128]{1,0:T(8,128)S(1)}, f32[208,128]{1,0:T(8,128)S(1)}, u32[]{:S(2)}, u32[]{:S(2)}) %collective-permute-start.2) | collective-permute-done | bytes 106528 | tf_op jit(solution)/shard_map/ppermute | solution.py:504
  12.5 0.8 %collective-permute-done.3 = f32[208,128]{1,0:T(8,128)S(1)} collective-permute-done((f32[208,128]{1,0:T(8,128)S(1)}, f32[208,128]{1,0:T(8,128)S(1)}, u32[]{:S(2)}, u32[]{:S(2)}) %collective-permute-start.3) | collective-permute-done | bytes 106528 | tf_op jit(solution)/shard_map/ppermute | solution.py:504
  13.3 2.2 %collective-permute-start.4 = (f32[208,128]{1,0:T(8,128)S(1)}, f32[208,128]{1,0:T(8,128)S(1)}, u32[]{:S(2)}, u32[]{:S(2)}) collective-permute-start(f32[208,128]{1,0:T(8,128)S(1)} %add_add_fusion), channel_id=1, source_target_pairs={{0,8},{1,9},{2,10},{3,11},{4,12},{5,13},{6,14},{7,15},{8,0},{9,1},... | collective-permute-start | bytes 319496 | tf_op jit(solution)/shard_map/ppermute | solution.py:499
  15.6 0.0 copy-start
  15.6 1.2 %copy-done = f32[18,3,32,128]{3,2,1,0:T(8,128)S(1)} copy-done((f32[18,3,32,128]{3,2,1,0:T(8,128)S(1)}, f32[18,3,32,128]{3,2,1,0:T(8,128)}, u32[]{:S(2)}) %copy-start) | copy-done | bytes 884760
  16.7 1.3 %pack.1 = (f32[3,32,128]{2,1,0:T(8,128)S(1)}, f32[3,32,128]{2,1,0:T(8,128)S(1)}, f32[18,3,48,128]{3,2,1,0:T(8,128)S(1)}, f32[3,18,3,32,128]{4,3,2,1,0:T(8,128)S(1)}) custom-call(f32[18,3,32,128]{3,2,1,0:T(8,128)S(1)} %copy-done), custom_call_target="tpu_custom_call" | custom-call | flops 2000000 | bytes 1000000 | tf_op jit(solution)/shard_map/pack/pallas_call | solution.py:207
  18.1 0.4 %collective-permute-done.4 = f32[208,128]{1,0:T(8,128)S(1)} collective-permute-done((f32[208,128]{1,0:T(8,128)S(1)}, f32[208,128]{1,0:T(8,128)S(1)}, u32[]{:S(2)}, u32[]{:S(2)}) %collective-permute-start.4) | collective-permute-done | bytes 106528 | tf_op jit(solution)/shard_map/ppermute | solution.py:499
  18.5 3.3 %collective-permute-start.7 = (f32[192,128]{1,0:T(8,128)S(1)}, f32[192,128]{1,0:T(8,128)S(1)}, u32[]{:S(2)}, u32[]{:S(2)}) collective-permute-start(f32[192,128]{1,0:T(8,128)S(1)} %slice.9.mine), channel_id=1, source_target_pairs={{0,1},{1,0},{2,3},{3,2},{4,5},{5,4},{6,7},{7,6},{8,9},{9,8},{10,11... | collective-permute-start | bytes 294920 | tf_op jit(solution)/shard_map/ppermute | solution.py:499
  21.8 0.1 collective-permute-start.5
  21.9 1.3 %collective-permute-start.6 = (f32[112,128]{1,0:T(8,128)S(1)}, f32[112,128]{1,0:T(8,128)S(1)}, u32[]{:S(2)}, u32[]{:S(2)}) collective-permute-start(f32[112,128]{1,0:T(8,128)S(1)} %get-tuple-element.30), channel_id=1, source_target_pairs={{16,0},{32,16},{48,32},{64,48},{80,64},{96,80},{112,96},{128,112},... | collective-permute-start | bytes 172040 | tf_op jit(solution)/shard_map/ppermute | solution.py:494
  23.2 0.0 collective-permute-done.7.other
  23.2 4.5 %inner.1 = (f32[18,3,32,128]{3,2,1,0:T(8,128)S(1)}, f32[11,3,32,128]{3,2,1,0:T(8,128)S(1)}, f32[7,3,32,128]{3,2,1,0:T(8,128)S(1)}, f32[3,32,128]{2,1,0:T(8,128)S(1)}) custom-call(f32[192,128]{1,0:T(8,128)S(1)} %slice.9.mine, f32[192,128]{1,0:T(8,128)S(1)} %collective-permute-done.7.other, f32[18,3,48,128]{3,2,1,0:T(8,128)S(1)} %get-tuple-element.24.padded, ...), custom_call_target="tpu_custom_call" | custom-call | flops 20000000 | bytes 6000000 | tf_op jit(solution)/shard_map/inner/pallas_call | solution.py:375
  27.7 9.0 %collective-permute-start.8 = (f32[112,128]{1,0:T(8,128)S(1)}, f32[112,128]{1,0:T(8,128)S(1)}, u32[]{:S(2)}, u32[]{:S(2)}) collective-permute-start(f32[112,128]{1,0:T(8,128)S(1)} %get-tuple-element.30), channel_id=1, source_target_pairs={{0,240},{1,241},{2,242},{3,243},{4,244},{5,245},{6,246},{7,247},{8... | collective-permute-start | bytes 172040 | tf_op jit(solution)/shard_map/ppermute | solution.py:494
  36.8 0.0 collective-permute-done.5.west
  36.8 0.0 collective-permute-done.6.east
  36.8 1.2 %collective-permute-done.8.wrapped = f32[112,128]{1,0:T(8,128)S(1)} collective-permute-done((f32[112,128]{1,0:T(8,128)S(1)}, f32[112,128]{1,0:T(8,128)S(1)}, u32[]{:S(2)}, u32[]{:S(2)}) %collective-permute-start.8) | collective-permute-done | bytes 57376 | tf_op jit(solution)/shard_map/ppermute | solution.py:494
  38.0 2.5 %edges.1 = f32[18,3,32,128]{3,2,1,0:T(8,128)} custom-call(f32[112,128]{1,0:T(8,128)S(1)} %collective-permute-done.5.west, f32[112,128]{1,0:T(8,128)S(1)} %collective-permute-done.6.east, f32[112,128]{1,0:T(8,128)S(1)} %collective-permute-done.8.wrapped, f32[96,128]{1,0:T(8,128)S(1)} %bitcast.6, f32[18,3,32,128]{3,2,1,0:T(8,128)S(1)} %get-tuple-element.31.sums, ...), custom_call_target="tpu_custom_call" | custom-call | tf_op jit(solution)/shard_map/edges/pallas_call | solution.py:478
  (6 shorter events, 0.1 us)
Async XLA Ops:
  1.2 4.3 %collective-permute-start = (f32[208,128]{1,0:T(8,128)S(1)}, f32[208,128]{1,0:T(8,128)S(1)}, u32[]{:S(2)}, u32[]{:S(2)}) collective-permute-start(f32[208,128]{1,0:T(8,128)S(1)} %get-tuple-element.22), channel_id=1, source_target_pairs={{0,1},{1,0},{2,3},{3,2},{4,5},{5,4},{6,7},{7,6},{8,9},{9,8},{10,11... | collective-permute-start | bytes 319496 | tf_op jit(solution)/shard_map/ppermute | solution.py:499
  5.5 5.5 %collective-permute-start.1 = (f32[208,128]{1,0:T(8,128)S(1)}, f32[208,128]{1,0:T(8,128)S(1)}, u32[]{:S(2)}, u32[]{:S(2)}) collective-permute-start(f32[208,128]{1,0:T(8,128)S(1)} %select_select_fusion), channel_id=1, source_target_pairs={{0,2},{1,3},{2,4},{3,5},{4,6},{5,7},{6,0},{7,1},{8,10},{9,11},{10,... | collective-permute-start | bytes 319496 | tf_op jit(solution)/shard_map/ppermute | solution.py:504
  5.6 6.9 %collective-permute-start.2 = (f32[208,128]{1,0:T(8,128)S(1)}, f32[208,128]{1,0:T(8,128)S(1)}, u32[]{:S(2)}, u32[]{:S(2)}) collective-permute-start(f32[208,128]{1,0:T(8,128)S(1)} %select_select_fusion), channel_id=1, source_target_pairs={{0,6},{1,7},{2,0},{3,1},{4,2},{5,3},{6,4},{7,5},{8,14},{9,15},{10,... | collective-permute-start | bytes 319496 | tf_op jit(solution)/shard_map/ppermute | solution.py:504
  8.3 5.1 %collective-permute-start.3 = (f32[208,128]{1,0:T(8,128)S(1)}, f32[208,128]{1,0:T(8,128)S(1)}, u32[]{:S(2)}, u32[]{:S(2)}) collective-permute-start(f32[208,128]{1,0:T(8,128)S(1)} %select_select_fusion), channel_id=1, source_target_pairs={{0,4},{1,5},{2,6},{3,7},{4,0},{5,1},{6,2},{7,3},{8,12},{9,13},{10,... | collective-permute-start | bytes 319496 | tf_op jit(solution)/shard_map/ppermute | solution.py:504
  13.3 5.1 %collective-permute-start.4 = (f32[208,128]{1,0:T(8,128)S(1)}, f32[208,128]{1,0:T(8,128)S(1)}, u32[]{:S(2)}, u32[]{:S(2)}) collective-permute-start(f32[208,128]{1,0:T(8,128)S(1)} %add_add_fusion), channel_id=1, source_target_pairs={{0,8},{1,9},{2,10},{3,11},{4,12},{5,13},{6,14},{7,15},{8,0},{9,1},... | collective-permute-start | bytes 319496 | tf_op jit(solution)/shard_map/ppermute | solution.py:499
  15.6 1.2 %copy-start = (f32[18,3,32,128]{3,2,1,0:T(8,128)S(1)}, f32[18,3,32,128]{3,2,1,0:T(8,128)}, u32[]{:S(2)}) copy-start(f32[18,3,32,128]{3,2,1,0:T(8,128)} %mass.1) | copy-start | bytes 2654212
  18.5 4.7 %collective-permute-start.7 = (f32[192,128]{1,0:T(8,128)S(1)}, f32[192,128]{1,0:T(8,128)S(1)}, u32[]{:S(2)}, u32[]{:S(2)}) collective-permute-start(f32[192,128]{1,0:T(8,128)S(1)} %slice.9.mine), channel_id=1, source_target_pairs={{0,1},{1,0},{2,3},{3,2},{4,5},{5,4},{6,7},{7,6},{8,9},{9,8},{10,11... | collective-permute-start | bytes 294920 | tf_op jit(solution)/shard_map/ppermute | solution.py:499
  21.8 14.9 %collective-permute-start.5 = (f32[112,128]{1,0:T(8,128)S(1)}, f32[112,128]{1,0:T(8,128)S(1)}, u32[]{:S(2)}, u32[]{:S(2)}) collective-permute-start(f32[112,128]{1,0:T(8,128)S(1)} %get-tuple-element.36), channel_id=1, source_target_pairs={{0,16},{16,32},{32,48},{48,64},{64,80},{80,96},{96,112},{112,128},... | collective-permute-start | bytes 172040 | tf_op jit(solution)/shard_map/ppermute | solution.py:494
  21.9 14.8 %collective-permute-start.6 = (f32[112,128]{1,0:T(8,128)S(1)}, f32[112,128]{1,0:T(8,128)S(1)}, u32[]{:S(2)}, u32[]{:S(2)}) collective-permute-start(f32[112,128]{1,0:T(8,128)S(1)} %get-tuple-element.30), channel_id=1, source_target_pairs={{16,0},{32,16},{48,32},{64,48},{80,64},{96,80},{112,96},{128,112},... | collective-permute-start | bytes 172040 | tf_op jit(solution)/shard_map/ppermute | solution.py:494
  27.7 10.3 %collective-permute-start.8 = (f32[112,128]{1,0:T(8,128)S(1)}, f32[112,128]{1,0:T(8,128)S(1)}, u32[]{:S(2)}, u32[]{:S(2)}) collective-permute-start(f32[112,128]{1,0:T(8,128)S(1)} %get-tuple-element.30), channel_id=1, source_target_pairs={{0,240},{1,241},{2,242},{3,243},{4,244},{5,245},{6,246},{7,247},{8... | collective-permute-start | bytes 172040 | tf_op jit(solution)/shard_map/ppermute | solution.py:494

commit v6 on v5

--- a/solution.py
+++ b/solution.py
@@ -1,3 +1,5 @@
+import functools
+
 import jax
 import jax.numpy as jnp
 from jax import lax
@@ -117,6 +119,10 @@
 
 def position():
     return lax.axis_index("tracer")
+
+
+def tile():
+    return lax.axis_index("space")
 
 
 def prepare_kernel(*refs):
@@ -251,7 +257,13 @@
     return {0: x, **{shift: lanes(x, -shift) for shift in NEAR}}
 
 
-def inner_kernel(
+def inner_kernel(tiles, mine, other, padded, shifted, *refs):
+    @pl.when(tiles(tile()))
+    def _():
+        inner_body(mine, other, padded, shifted, *refs)
+
+
+def inner_body(
     mine, other, padded, shifted, sums, outer_c, edge_c, thickness,
     east_c, north_c, inners, middle, partial,
 ):
@@ -368,12 +380,12 @@
     lax.fori_loop(-1, steps + 1, step_of_three, 0)
 
 
-def inner_update(mine, other, padded, shifted):
+def inner_update(tiles, mine, other, padded, shifted):
     tracers, levels, count, width = shifted.shape[1:]
     vmem = pl.BlockSpec(memory_space=pltpu.VMEM)
     level = (levels, count, width)
     return pl.pallas_call(
-        inner_kernel,
+        functools.partial(inner_kernel, tiles),
         out_shape=(
             pltpu.VMEM((tracers,) + level, jnp.float32),
             pltpu.VMEM((2 * EDGE + 1,) + level, jnp.float32),
@@ -395,7 +407,19 @@
     )(mine, other, padded, shifted)
 
 
-def edge_kernel(west, east, wrapped, own, sums, outer_c, edge_c, thickness, out, stage, sems):
+def edge_kernel(early, west, east, own, *refs):
+    before, after, rest = refs[:4], refs[4:8], refs[8:]
+
+    @pl.when(early(tile()))
+    def _():
+        edge_body(west, east, own, *before, *rest)
+
+    @pl.when(jnp.logical_not(early(tile())))
+    def _():
+        edge_body(west, east, own, *after, *rest)
+
+
+def edge_body(west, east, own, sums, outer_c, edge_c, thickness, out, stage, sems):
     tracers, levels, count, width = sums.shape
     shape = (count, width)
     lane = lane_index(shape)
@@ -411,7 +435,7 @@
     def unfolded(x):
         return jnp.concatenate([x, lanes(x, -MET_SEG * levels)])
 
-    met_east = unfolded(east[base:, :] + wrapped[base:, :])
+    met_east = unfolded(east[base:, :])
     met_west = unfolded(west[base:, :])
 
     def copy(l):
@@ -445,7 +469,7 @@
             cells = jnp.where(
                 from_west_lane,
                 pick(west[level_rows, :], west_index),
-                pick(east[level_rows, :] + wrapped[level_rows, :], east_index),
+                pick(east[level_rows, :], east_index),
             )
             inner = cells
             own_inner = own_cells
@@ -472,18 +496,19 @@
         copy(l).wait()
 
 
-def edge_update(west, east, wrapped, own, sums, outer_c, edge_c, thickness):
+def edge_update(early, west, east, own, before, after):
+    sums = before[0]
     tracers, levels, count, width = sums.shape
     vmem = pl.BlockSpec(memory_space=pltpu.VMEM)
     return pl.pallas_call(
-        edge_kernel,
+        functools.partial(edge_kernel, early),
         out_shape=jax.ShapeDtypeStruct(sums.shape, jnp.float32),
-        in_specs=[vmem] * 8,
+        in_specs=[vmem] * 11,
         out_specs=pl.BlockSpec(memory_space=pl.ANY),
         scratch_shapes=[pltpu.VMEM(sums.shape, jnp.float32), pltpu.SemaphoreType.DMA((levels,))],
         compiler_params=pltpu.CompilerParams(vmem_limit_bytes=24 * 1024 * 1024),
         name="edges",
-    )(west, east, wrapped, own, sums, outer_c, edge_c, thickness)
+    )(west, east, own, *before, *after)
 
 
 def east_group(m):
@@ -502,6 +527,10 @@
 def turn(x, by):
     size = lax.axis_size("tracer")
     return lax.ppermute(x, "tracer", [(i, i // 8 * 8 + (i + 2 * by) % 8) for i in range(size)])
+
+
+def early(i):
+    return i == 0
 
 
 def shards(mass, thick, fe, fn, ce, cn, ne, owner):
@@ -520,11 +549,11 @@
     to_west = jnp.concatenate([first, edges])
     west = along(to_east, [(i, (i + 1) % size) for i in range(size)])
     other = exchange(mine, 1)
-    east = along(to_west, [(i, i - 1) for i in range(1, size)])
-    inner = inner_update(mine, other, padded, shifted)
-    to_west, inner = lax.optimization_barrier((to_west, inner))
-    wrapped = along(to_west, [(0, size - 1)])
-    return edge_update(west, east, wrapped, last, *inner)
+    before = inner_update(early, mine, other, padded, shifted)
+    to_west, before = lax.optimization_barrier((to_west, before))
+    east = along(to_west, [(i, (i - 1) % size) for i in range(size)])
+    after = inner_update(lambda i: jnp.logical_not(early(i)), mine, other, padded, shifted)
+    return edge_update(early, west, east, last, before, after)
 
 
 def solution(mesh):

time: 40.7 us -> 33.4 us (0.82)
  the two profiles are of different devices: /device:TPU:1 before, /device:TPU:3 now
where the time goes in v6:
time: 33.4 us; the launch traced here: 33.2 us
  starting transfers between devices  18 us (54%)
  Pallas kernels  9.52 us (29%)
  waiting for transfers between devices  3.76 us (11%)
  local copies, waits for them, and re-layouts  1.18 us (4%)
  between operations  0.72 us (2%)
    ppermute x2, starting transfers between devices, along(): return lax.ppermute(x, 'space', pairs)  7.15 us
    ppermute x3, starting transfers between devices, turn(): lax.ppermute(x, 'tracer', [(i, i // 8 * 8 + (i + 2 * by) % 8) for i in ra...  5.68 us
    ppermute x3, starting transfers between devices, exchange(): return lax.ppermute(x, 'tracer', [(i, i ^ flip) for i in range(size)])  5.14 us
    pallas_call x2, Pallas kernels, inner_update(): pl.pallas_call(functools.partial(inner_kernel, tiles), out_shape=(pltpu.V...  4.47 us
    ppermute x3, waiting for transfers between devices, turn(): lax.ppermute(x, 'tracer', [(i, i // 8 * 8 + (i + 2 * by) % 8) for i in ra...  2.73 us
    pallas_call x1, Pallas kernels, edge_update(): pl.pallas_call(functools.partial(edge_kernel, early), out_shape=jax.Shape...  2.54 us
    pallas_call x1, Pallas kernels, pack(): pl.pallas_call(pack_kernel, out_shape=(packed, packed, pltpu.VMEM((tracer...  1.32 us
    pallas_call x1, Pallas kernels, prepare(): pl.pallas_call(prepare_kernel, out_shape=(half, half), in_specs=[pl.Block...  1.19 us
  transfers between devices with their start and end apart: 8, of which 5 were waited for; matrix products, arithmetic and copies ran while one was open for 0% of the time, Pallas kernels for 17%

profile of v6, /device:TPU:3, one launch (start us, length us, event | category | flops | bytes accessed | tf_op | source)
XLA Modules:
  0.0 33.2 jit_solution(11285162154578010938)
XLA Ops:
  0.0 1.2 %prepare.1 = (f32[208,128]{1,0:T(8,128)S(1)}, f32[208,128]{1,0:T(8,128)S(1)}) custom-call(f32[1,3,32,128]{3,2,1,0:T(8,128)} %refs_0_.1, f32[1,3,32,128]{3,2,1,0:T(8,128)} %refs_1_.1, f32[1,3,32,128]{3,2,1,0:T(8,128)} %refs_2_.1, f32[1,3,32,128]{3,2,1,0:T(8,128)} %refs_3_.1, f32[1,3,32,128]{3,2,1,0:T(8,128)} %refs_4_.1, s32[1,3,32,128]{3,2,1,0:T(8,128)} %refs_5_.1), custom_call_target="tpu_custom_call" | custom-call | tf_op jit(solution)/shard_map/prepare/pallas_call | solution.py:173
  1.2 0.8 %collective-permute-start = (f32[208,128]{1,0:T(8,128)S(1)}, f32[208,128]{1,0:T(8,128)S(1)}, u32[]{:S(2)}, u32[]{:S(2)}) collective-permute-start(f32[208,128]{1,0:T(8,128)S(1)} %get-tuple-element.26), channel_id=1, source_target_pairs={{0,1},{1,0},{2,3},{3,2},{4,5},{5,4},{6,7},{7,6},{8,9},{9,8},{10,11... | collective-permute-start | bytes 319496 | tf_op jit(solution)/shard_map/ppermute | solution.py:524
  2.6 0.3 collective-permute-done
  2.9 3.0 %collective-permute-start.3 = (f32[208,128]{1,0:T(8,128)S(1)}, f32[208,128]{1,0:T(8,128)S(1)}, u32[]{:S(2)}, u32[]{:S(2)}) collective-permute-start(f32[208,128]{1,0:T(8,128)S(1)} %select_select_fusion), channel_id=1, source_target_pairs={{0,4},{1,5},{2,6},{3,7},{4,0},{5,1},{6,2},{7,3},{8,12},{9,13},{10,... | collective-permute-start | bytes 319496 | tf_op jit(solution)/shard_map/ppermute | solution.py:529
  5.9 0.4 %collective-permute-start.1 = (f32[208,128]{1,0:T(8,128)S(1)}, f32[208,128]{1,0:T(8,128)S(1)}, u32[]{:S(2)}, u32[]{:S(2)}) collective-permute-start(f32[208,128]{1,0:T(8,128)S(1)} %select_select_fusion), channel_id=1, source_target_pairs={{0,2},{1,3},{2,4},{3,5},{4,6},{5,7},{6,0},{7,1},{8,10},{9,11},{10,... | collective-permute-start | bytes 319496 | tf_op jit(solution)/shard_map/ppermute | solution.py:529
  6.3 2.3 %collective-permute-start.2 = (f32[208,128]{1,0:T(8,128)S(1)}, f32[208,128]{1,0:T(8,128)S(1)}, u32[]{:S(2)}, u32[]{:S(2)}) collective-permute-start(f32[208,128]{1,0:T(8,128)S(1)} %select_select_fusion), channel_id=1, source_target_pairs={{0,6},{1,7},{2,0},{3,1},{4,2},{5,3},{6,4},{7,5},{8,14},{9,15},{10,... | collective-permute-start | bytes 319496 | tf_op jit(solution)/shard_map/ppermute | solution.py:529
  8.6 0.1 collective-permute-done.3
  8.7 2.3 %collective-permute-done.1 = f32[208,128]{1,0:T(8,128)S(1)} collective-permute-done((f32[208,128]{1,0:T(8,128)S(1)}, f32[208,128]{1,0:T(8,128)S(1)}, u32[]{:S(2)}, u32[]{:S(2)}) %collective-permute-start.1) | collective-permute-done | bytes 106528 | tf_op jit(solution)/shard_map/ppermute | solution.py:529
  11.1 0.3 collective-permute-done.2
  11.4 1.9 %collective-permute-start.4 = (f32[208,128]{1,0:T(8,128)S(1)}, f32[208,128]{1,0:T(8,128)S(1)}, u32[]{:S(2)}, u32[]{:S(2)}) collective-permute-start(f32[208,128]{1,0:T(8,128)S(1)} %add_add_fusion), channel_id=1, source_target_pairs={{0,8},{1,9},{2,10},{3,11},{4,12},{5,13},{6,14},{7,15},{8,0},{9,1},... | collective-permute-start | bytes 319496 | tf_op jit(solution)/shard_map/ppermute | solution.py:524
  13.3 0.0 copy-start
  13.3 1.2 %copy-done = f32[18,3,32,128]{3,2,1,0:T(8,128)S(1)} copy-done((f32[18,3,32,128]{3,2,1,0:T(8,128)S(1)}, f32[18,3,32,128]{3,2,1,0:T(8,128)}, u32[]{:S(2)}) %copy-start) | copy-done | bytes 884760
  14.5 1.3 %pack.1 = (f32[3,32,128]{2,1,0:T(8,128)S(1)}, f32[3,32,128]{2,1,0:T(8,128)S(1)}, f32[18,3,48,128]{3,2,1,0:T(8,128)S(1)}, f32[3,18,3,32,128]{4,3,2,1,0:T(8,128)S(1)}) custom-call(f32[18,3,32,128]{3,2,1,0:T(8,128)S(1)} %copy-done), custom_call_target="tpu_custom_call" | custom-call | flops 2000000 | bytes 1000000 | tf_op jit(solution)/shard_map/pack/pallas_call | solution.py:213
  15.8 0.7 %collective-permute-done.4 = f32[208,128]{1,0:T(8,128)S(1)} collective-permute-done((f32[208,128]{1,0:T(8,128)S(1)}, f32[208,128]{1,0:T(8,128)S(1)}, u32[]{:S(2)}, u32[]{:S(2)}) %collective-permute-start.4) | collective-permute-done | bytes 106528 | tf_op jit(solution)/shard_map/ppermute | solution.py:524
  16.6 2.4 %collective-permute-start.6 = (f32[192,128]{1,0:T(8,128)S(1)}, f32[192,128]{1,0:T(8,128)S(1)}, u32[]{:S(2)}, u32[]{:S(2)}) collective-permute-start(f32[192,128]{1,0:T(8,128)S(1)} %slice.9.mine), channel_id=1, source_target_pairs={{0,1},{1,0},{2,3},{3,2},{4,5},{5,4},{6,7},{7,6},{8,9},{9,8},{10,11... | collective-permute-start | bytes 294920 | tf_op jit(solution)/shard_map/ppermute | solution.py:524
  19.0 1.7 %collective-permute-start.5 = (f32[112,128]{1,0:T(8,128)S(1)}, f32[112,128]{1,0:T(8,128)S(1)}, u32[]{:S(2)}, u32[]{:S(2)}) collective-permute-start(f32[112,128]{1,0:T(8,128)S(1)} %get-tuple-element.44), channel_id=1, source_target_pairs={{0,16},{16,32},{32,48},{48,64},{64,80},{80,96},{96,112},{112,128},... | collective-permute-start | bytes 172040 | tf_op jit(solution)/shard_map/ppermute | solution.py:519
  20.7 0.0 collective-permute-done.6.other
  20.7 5.5 %collective-permute-start.7 = (f32[112,128]{1,0:T(8,128)S(1)}, f32[112,128]{1,0:T(8,128)S(1)}, u32[]{:S(2)}, u32[]{:S(2)}) collective-permute-start(f32[112,128]{1,0:T(8,128)S(1)} %get-tuple-element.34), channel_id=1, source_target_pairs={{0,240},{16,0},{32,16},{48,32},{64,48},{80,64},{96,80},{112,96},{1... | collective-permute-start | bytes 172040 | tf_op jit(solution)/shard_map/ppermute | solution.py:519
  26.2 4.5 %inner.3 = (f32[18,3,32,128]{3,2,1,0:T(8,128)S(1)}, f32[11,3,32,128]{3,2,1,0:T(8,128)S(1)}, f32[7,3,32,128]{3,2,1,0:T(8,128)S(1)}, f32[3,32,128]{2,1,0:T(8,128)S(1)}) custom-call(f32[192,128]{1,0:T(8,128)S(1)} %slice.9.mine, f32[192,128]{1,0:T(8,128)S(1)} %collective-permute-done.6.other, f32[18,3,48,128]{3,2,1,0:T(8,128)S(1)} %get-tuple-element.28.padded, ...), custom_call_target="tpu_custom_call" | custom-call | flops 20000000 | bytes 6000000 | tf_op jit(solution)/shard_map/inner/pallas_call | solution.py:387
  30.7 0.0 collective-permute-done.5.west
  30.7 0.0 collective-permute-done.7.east
  30.7 2.5 %edges.1 = f32[18,3,32,128]{3,2,1,0:T(8,128)} custom-call(f32[112,128]{1,0:T(8,128)S(1)} %collective-permute-done.5.west, f32[112,128]{1,0:T(8,128)S(1)} %collective-permute-done.7.east, f32[96,128]{1,0:T(8,128)S(1)} %bitcast.6, f32[18,3,32,128]{3,2,1,0:T(8,128)S(1)} %get-tuple-element.35.refs_0_, f32[11,3,32,128]{3,2,1,0:T(8,128)S(1)} %get-tuple-element.36.refs_1_, ...), custom_call_target="tpu_custom_call" | custom-call | tf_op jit(solution)/shard_map/edges/pallas_call | solution.py:503
  (7 shorter events, 0.1 us)
Async XLA Ops:
  1.2 1.7 %collective-permute-start = (f32[208,128]{1,0:T(8,128)S(1)}, f32[208,128]{1,0:T(8,128)S(1)}, u32[]{:S(2)}, u32[]{:S(2)}) collective-permute-start(f32[208,128]{1,0:T(8,128)S(1)} %get-tuple-element.26), channel_id=1, source_target_pairs={{0,1},{1,0},{2,3},{3,2},{4,5},{5,4},{6,7},{7,6},{8,9},{9,8},{10,11... | collective-permute-start | bytes 319496 | tf_op jit(solution)/shard_map/ppermute | solution.py:524
  2.9 5.8 %collective-permute-start.3 = (f32[208,128]{1,0:T(8,128)S(1)}, f32[208,128]{1,0:T(8,128)S(1)}, u32[]{:S(2)}, u32[]{:S(2)}) collective-permute-start(f32[208,128]{1,0:T(8,128)S(1)} %select_select_fusion), channel_id=1, source_target_pairs={{0,4},{1,5},{2,6},{3,7},{4,0},{5,1},{6,2},{7,3},{8,12},{9,13},{10,... | collective-permute-start | bytes 319496 | tf_op jit(solution)/shard_map/ppermute | solution.py:529
  5.9 5.1 %collective-permute-start.1 = (f32[208,128]{1,0:T(8,128)S(1)}, f32[208,128]{1,0:T(8,128)S(1)}, u32[]{:S(2)}, u32[]{:S(2)}) collective-permute-start(f32[208,128]{1,0:T(8,128)S(1)} %select_select_fusion), channel_id=1, source_target_pairs={{0,2},{1,3},{2,4},{3,5},{4,6},{5,7},{6,0},{7,1},{8,10},{9,11},{10,... | collective-permute-start | bytes 319496 | tf_op jit(solution)/shard_map/ppermute | solution.py:529
  6.3 5.0 %collective-permute-start.2 = (f32[208,128]{1,0:T(8,128)S(1)}, f32[208,128]{1,0:T(8,128)S(1)}, u32[]{:S(2)}, u32[]{:S(2)}) collective-permute-start(f32[208,128]{1,0:T(8,128)S(1)} %select_select_fusion), channel_id=1, source_target_pairs={{0,6},{1,7},{2,0},{3,1},{4,2},{5,3},{6,4},{7,5},{8,14},{9,15},{10,... | collective-permute-start | bytes 319496 | tf_op jit(solution)/shard_map/ppermute | solution.py:529
  11.4 5.1 %collective-permute-start.4 = (f32[208,128]{1,0:T(8,128)S(1)}, f32[208,128]{1,0:T(8,128)S(1)}, u32[]{:S(2)}, u32[]{:S(2)}) collective-permute-start(f32[208,128]{1,0:T(8,128)S(1)} %add_add_fusion), channel_id=1, source_target_pairs={{0,8},{1,9},{2,10},{3,11},{4,12},{5,13},{6,14},{7,15},{8,0},{9,1},... | collective-permute-start | bytes 319496 | tf_op jit(solution)/shard_map/ppermute | solution.py:524
  13.3 1.2 %copy-start = (f32[18,3,32,128]{3,2,1,0:T(8,128)S(1)}, f32[18,3,32,128]{3,2,1,0:T(8,128)}, u32[]{:S(2)}) copy-start(f32[18,3,32,128]{3,2,1,0:T(8,128)} %mass.1) | copy-start | bytes 2654212
  16.6 4.1 %collective-permute-start.6 = (f32[192,128]{1,0:T(8,128)S(1)}, f32[192,128]{1,0:T(8,128)S(1)}, u32[]{:S(2)}, u32[]{:S(2)}) collective-permute-start(f32[192,128]{1,0:T(8,128)S(1)} %slice.9.mine), channel_id=1, source_target_pairs={{0,1},{1,0},{2,3},{3,2},{4,5},{5,4},{6,7},{7,6},{8,9},{9,8},{10,11... | collective-permute-start | bytes 294920 | tf_op jit(solution)/shard_map/ppermute | solution.py:524
  19.0 11.6 %collective-permute-start.5 = (f32[112,128]{1,0:T(8,128)S(1)}, f32[112,128]{1,0:T(8,128)S(1)}, u32[]{:S(2)}, u32[]{:S(2)}) collective-permute-start(f32[112,128]{1,0:T(8,128)S(1)} %get-tuple-element.44), channel_id=1, source_target_pairs={{0,16},{16,32},{32,48},{48,64},{64,80},{80,96},{96,112},{112,128},... | collective-permute-start | bytes 172040 | tf_op jit(solution)/shard_map/ppermute | solution.py:519
  20.7 10.0 %collective-permute-start.7 = (f32[112,128]{1,0:T(8,128)S(1)}, f32[112,128]{1,0:T(8,128)S(1)}, u32[]{:S(2)}, u32[]{:S(2)}) collective-permute-start(f32[112,128]{1,0:T(8,128)S(1)} %get-tuple-element.34), channel_id=1, source_target_pairs={{0,240},{16,0},{32,16},{48,32},{64,48},{80,64},{96,80},{112,96},{1... | collective-permute-start | bytes 172040 | tf_op jit(solution)/shard_map/ppermute | solution.py:519

commit v7 on v6

--- a/solution.py
+++ b/solution.py
@@ -123,6 +123,10 @@
 
 def tile():
     return lax.axis_index("space")
+
+
+def early_levels(levels):
+    return jnp.clip(levels - tile(), 0, levels - 1)
 
 
 def prepare_kernel(*refs):
@@ -257,14 +261,16 @@
     return {0: x, **{shift: lanes(x, -shift) for shift in NEAR}}
 
 
-def inner_kernel(tiles, mine, other, padded, shifted, *refs):
-    @pl.when(tiles(tile()))
+def inner_kernel(span, mine, other, padded, shifted, *refs):
+    low_level, high_level = span(refs[0].shape[1])
+
+    @pl.when(low_level < high_level)
     def _():
-        inner_body(mine, other, padded, shifted, *refs)
+        inner_body(low_level, high_level, mine, other, padded, shifted, *refs)
 
 
 def inner_body(
-    mine, other, padded, shifted, sums, outer_c, edge_c, thickness,
+    low_level, high_level, mine, other, padded, shifted, sums, outer_c, edge_c, thickness,
     east_c, north_c, inners, middle, partial,
 ):
     tracers, levels, count, width = sums.shape
@@ -313,8 +319,8 @@
             edge_c[m, l] = value
         return carry
 
-    lax.fori_loop(0, levels, level, 0)
-    steps = levels * (tracers // GROUP)
+    lax.fori_loop(low_level, high_level, level, 0)
+    groups = tracers // GROUP
 
     def block(b):
         return slice(b * BLOCK, (b + 1) * BLOCK)
@@ -323,8 +329,8 @@
         return slice(PAD + b * BLOCK + m, PAD + (b + 1) * BLOCK + m)
 
     def place(step):
-        step = jnp.clip(step, 0, steps - 1)
-        return step % levels, (step // levels) * GROUP
+        step = jnp.clip(step, 0, levels * groups - 1)
+        return step // groups, (step % groups) * GROUP
 
     def weights(ref, l, b, reach):
         return {m: ref[m + reach, l, block(b), :] for m in range(-reach, reach + 1)}
@@ -377,15 +383,15 @@
         front(step + 1)
         return carry
 
-    lax.fori_loop(-1, steps + 1, step_of_three, 0)
-
-
-def inner_update(tiles, mine, other, padded, shifted):
+    lax.fori_loop(low_level * groups - 1, high_level * groups + 1, step_of_three, 0)
+
+
+def inner_update(span, mine, other, padded, shifted):
     tracers, levels, count, width = shifted.shape[1:]
     vmem = pl.BlockSpec(memory_space=pltpu.VMEM)
     level = (levels, count, width)
     return pl.pallas_call(
-        functools.partial(inner_kernel, tiles),
+        functools.partial(inner_kernel, span),
         out_shape=(
             pltpu.VMEM((tracers,) + level, jnp.float32),
             pltpu.VMEM((2 * EDGE + 1,) + level, jnp.float32),
@@ -407,20 +413,10 @@
     )(mine, other, padded, shifted)
 
 
-def edge_kernel(early, west, east, own, *refs):
-    before, after, rest = refs[:4], refs[4:8], refs[8:]
-
-    @pl.when(early(tile()))
-    def _():
-        edge_body(west, east, own, *before, *rest)
-
-    @pl.when(jnp.logical_not(early(tile())))
-    def _():
-        edge_body(west, east, own, *after, *rest)
-
-
-def edge_body(west, east, own, sums, outer_c, edge_c, thickness, out, stage, sems):
-    tracers, levels, count, width = sums.shape
+def edge_kernel(west, east, own, *refs):
+    before, after, (out, stage, sems) = refs[:4], refs[4:8], refs[8:]
+    tracers, levels, count, width = stage.shape
+    first_levels = early_levels(levels)
     shape = (count, width)
     lane = lane_index(shape)
     segment, in_segment, packed_lane = segments(shape)
@@ -441,7 +437,7 @@
     def copy(l):
         return pltpu.make_async_copy(stage.at[:, l], out.at[:, l], sems.at[l])
 
-    def level(l, carry):
+    def level(l, sums, outer_c, edge_c, thickness):
         level_rows = pl.ds(pl.multiple_of(l * count, count), count)
         met_lane = jnp.where(packed_lane, in_segment + MET_SEG * l, 0)
         met = jnp.where(lane - MET_SEG * l < EDGE, met_west, met_east)
@@ -489,19 +485,29 @@
                 moved = jnp.where(at_edge, lanes(total, width - EDGE - SEG * k), 0.0)
                 stage[t, l] = (sums[t, l] + moved) * inverse
         copy(l).start()
+
+    def either(l, carry):
+        @pl.when(l < first_levels)
+        def _():
+            level(l, *before)
+
+        @pl.when(l >= first_levels)
+        def _():
+            level(l, *after)
+
         return carry
 
-    lax.fori_loop(0, levels, level, 0)
+    lax.fori_loop(0, levels, either, 0)
     for l in range(levels):
         copy(l).wait()
 
 
-def edge_update(early, west, east, own, before, after):
+def edge_update(west, east, own, before, after):
     sums = before[0]
     tracers, levels, count, width = sums.shape
     vmem = pl.BlockSpec(memory_space=pltpu.VMEM)
     return pl.pallas_call(
-        functools.partial(edge_kernel, early),
+        edge_kernel,
         out_shape=jax.ShapeDtypeStruct(sums.shape, jnp.float32),
         in_specs=[vmem] * 11,
         out_specs=pl.BlockSpec(memory_space=pl.ANY),
@@ -527,10 +533,6 @@
 def turn(x, by):
     size = lax.axis_size("tracer")
     return lax.ppermute(x, "tracer", [(i, i // 8 * 8 + (i + 2 * by) % 8) for i in range(size)])
-
-
-def early(i):
-    return i == 0
 
 
 def shards(mass, thick, fe, fn, ce, cn, ne, owner):
@@ -549,11 +551,11 @@
     to_west = jnp.concatenate([first, edges])
     west = along(to_east, [(i, (i + 1) % size) for i in range(size)])
     other = exchange(mine, 1)
-    before = inner_update(early, mine, other, padded, shifted)
+    before = inner_update(lambda levels: (0, early_levels(levels)), mine, other, padded, shifted)
     to_west, before = lax.optimization_barrier((to_west, before))
     east = along(to_west, [(i, (i - 1) % size) for i in range(size)])
-    after = inner_update(lambda i: jnp.logical_not(early(i)), mine, other, padded, shifted)
-    return edge_update(early, west, east, last, before, after)
+    after = inner_update(lambda levels: (early_levels(levels), levels), mine, other, padded, shifted)
+    return edge_update(west, east, last, before, after)
 
 
 def solution(mesh):

time: 33.4 us -> 32.8 us (0.982)
  the two profiles are of different devices: /device:TPU:3 before, /device:TPU:1 now
where the time goes in v7:
time: 32.8 us; the launch traced here: 32.6 us
  starting transfers between devices  11.7 us (36%)
  Pallas kernels  10.1 us (31%)
  waiting for transfers between devices  8.83 us (27%)
  local copies, waits for them, and re-layouts  1.18 us (4%)
  between operations  0.73 us (2%)
    ppermute x3, starting transfers between devices, exchange(): return lax.ppermute(x, 'tracer', [(i, i ^ flip) for i in range(size)])  5.81 us
    pallas_call x2, Pallas kernels, inner_update(): pl.pallas_call(functools.partial(inner_kernel, span), out_shape=(pltpu.VM...  5 us
    ppermute x3, waiting for transfers between devices, turn(): lax.ppermute(x, 'tracer', [(i, i // 8 * 8 + (i + 2 * by) % 8) for i in ra...  4.68 us
    ppermute x3, starting transfers between devices, turn(): lax.ppermute(x, 'tracer', [(i, i // 8 * 8 + (i + 2 * by) % 8) for i in ra...  3.94 us
    ppermute x3, waiting for transfers between devices, exchange(): return lax.ppermute(x, 'tracer', [(i, i ^ flip) for i in range(size)])  3.23 us
    pallas_call x1, Pallas kernels, edge_update(): pl.pallas_call(edge_kernel, out_shape=jax.ShapeDtypeStruct(sums.shape, jn...  2.54 us
    ppermute x2, starting transfers between devices, along(): return lax.ppermute(x, 'space', pairs)  2 us
    pallas_call x1, Pallas kernels, pack(): pl.pallas_call(pack_kernel, out_shape=(packed, packed, pltpu.VMEM((tracer...  1.32 us
  transfers between devices with their start and end apart: 8, of which 6 were waited for; matrix products, arithmetic and copies ran while one was open for 0% of the time, Pallas kernels for 19%

profile of v7, /device:TPU:1, one launch (start us, length us, event | category | flops | bytes accessed | tf_op | source)
XLA Modules:
  0.0 32.6 jit_solution(8134851115572928481)
XLA Ops:
  0.0 1.2 %prepare.1 = (f32[208,128]{1,0:T(8,128)S(1)}, f32[208,128]{1,0:T(8,128)S(1)}) custom-call(f32[1,3,32,128]{3,2,1,0:T(8,128)} %refs_0_.1, f32[1,3,32,128]{3,2,1,0:T(8,128)} %refs_1_.1, f32[1,3,32,128]{3,2,1,0:T(8,128)} %refs_2_.1, f32[1,3,32,128]{3,2,1,0:T(8,128)} %refs_3_.1, f32[1,3,32,128]{3,2,1,0:T(8,128)} %refs_4_.1, s32[1,3,32,128]{3,2,1,0:T(8,128)} %refs_5_.1), custom_call_target="tpu_custom_call" | custom-call | tf_op jit(solution)/shard_map/prepare/pallas_call | solution.py:177
  1.2 3.3 %collective-permute-start = (f32[208,128]{1,0:T(8,128)S(1)}, f32[208,128]{1,0:T(8,128)S(1)}, u32[]{:S(2)}, u32[]{:S(2)}) collective-permute-start(f32[208,128]{1,0:T(8,128)S(1)} %get-tuple-element.26), channel_id=1, source_target_pairs={{0,1},{1,0},{2,3},{3,2},{4,5},{5,4},{6,7},{7,6},{8,9},{9,8},{10,11... | collective-permute-start | bytes 319496 | tf_op jit(solution)/shard_map/ppermute | solution.py:530
  5.2 0.3 collective-permute-done
  5.5 1.3 %collective-permute-start.3 = (f32[208,128]{1,0:T(8,128)S(1)}, f32[208,128]{1,0:T(8,128)S(1)}, u32[]{:S(2)}, u32[]{:S(2)}) collective-permute-start(f32[208,128]{1,0:T(8,128)S(1)} %select_select_fusion), channel_id=1, source_target_pairs={{0,4},{1,5},{2,6},{3,7},{4,0},{5,1},{6,2},{7,3},{8,12},{9,13},{10,... | collective-permute-start | bytes 319496 | tf_op jit(solution)/shard_map/ppermute | solution.py:535
  6.8 0.4 %collective-permute-start.1 = (f32[208,128]{1,0:T(8,128)S(1)}, f32[208,128]{1,0:T(8,128)S(1)}, u32[]{:S(2)}, u32[]{:S(2)}) collective-permute-start(f32[208,128]{1,0:T(8,128)S(1)} %select_select_fusion), channel_id=1, source_target_pairs={{0,2},{1,3},{2,4},{3,5},{4,6},{5,7},{6,0},{7,1},{8,10},{9,11},{10,... | collective-permute-start | bytes 319496 | tf_op jit(solution)/shard_map/ppermute | solution.py:535
  7.2 2.3 %collective-permute-start.2 = (f32[208,128]{1,0:T(8,128)S(1)}, f32[208,128]{1,0:T(8,128)S(1)}, u32[]{:S(2)}, u32[]{:S(2)}) collective-permute-start(f32[208,128]{1,0:T(8,128)S(1)} %select_select_fusion), channel_id=1, source_target_pairs={{0,6},{1,7},{2,0},{3,1},{4,2},{5,3},{6,4},{7,5},{8,14},{9,15},{10,... | collective-permute-start | bytes 319496 | tf_op jit(solution)/shard_map/ppermute | solution.py:535
  9.4 1.8 %collective-permute-done.3 = f32[208,128]{1,0:T(8,128)S(1)} collective-permute-done((f32[208,128]{1,0:T(8,128)S(1)}, f32[208,128]{1,0:T(8,128)S(1)}, u32[]{:S(2)}, u32[]{:S(2)}) %collective-permute-start.3) | collective-permute-done | bytes 106528 | tf_op jit(solution)/shard_map/ppermute | solution.py:535
  11.3 2.8 %collective-permute-done.1 = f32[208,128]{1,0:T(8,128)S(1)} collective-permute-done((f32[208,128]{1,0:T(8,128)S(1)}, f32[208,128]{1,0:T(8,128)S(1)}, u32[]{:S(2)}, u32[]{:S(2)}) %collective-permute-start.1) | collective-permute-done | bytes 106528 | tf_op jit(solution)/shard_map/ppermute | solution.py:535
  14.1 0.0 collective-permute-done.2
  14.2 0.9 %collective-permute-start.4 = (f32[208,128]{1,0:T(8,128)S(1)}, f32[208,128]{1,0:T(8,128)S(1)}, u32[]{:S(2)}, u32[]{:S(2)}) collective-permute-start(f32[208,128]{1,0:T(8,128)S(1)} %add_add_fusion), channel_id=1, source_target_pairs={{0,8},{1,9},{2,10},{3,11},{4,12},{5,13},{6,14},{7,15},{8,0},{9,1},... | collective-permute-start | bytes 319496 | tf_op jit(solution)/shard_map/ppermute | solution.py:530
  15.0 0.0 copy-start
  15.0 1.2 %copy-done = f32[18,3,32,128]{3,2,1,0:T(8,128)S(1)} copy-done((f32[18,3,32,128]{3,2,1,0:T(8,128)S(1)}, f32[18,3,32,128]{3,2,1,0:T(8,128)}, u32[]{:S(2)}) %copy-start) | copy-done | bytes 884760
  16.2 1.3 %pack.1 = (f32[3,32,128]{2,1,0:T(8,128)S(1)}, f32[3,32,128]{2,1,0:T(8,128)S(1)}, f32[18,3,48,128]{3,2,1,0:T(8,128)S(1)}, f32[3,18,3,32,128]{4,3,2,1,0:T(8,128)S(1)}) custom-call(f32[18,3,32,128]{3,2,1,0:T(8,128)S(1)} %copy-done), custom_call_target="tpu_custom_call" | custom-call | flops 2000000 | bytes 1000000 | tf_op jit(solution)/shard_map/pack/pallas_call | solution.py:217
  17.5 2.1 %collective-permute-done.4 = f32[208,128]{1,0:T(8,128)S(1)} collective-permute-done((f32[208,128]{1,0:T(8,128)S(1)}, f32[208,128]{1,0:T(8,128)S(1)}, u32[]{:S(2)}, u32[]{:S(2)}) %collective-permute-start.4) | collective-permute-done | bytes 106528 | tf_op jit(solution)/shard_map/ppermute | solution.py:530
  19.7 1.6 %collective-permute-start.6 = (f32[192,128]{1,0:T(8,128)S(1)}, f32[192,128]{1,0:T(8,128)S(1)}, u32[]{:S(2)}, u32[]{:S(2)}) collective-permute-start(f32[192,128]{1,0:T(8,128)S(1)} %slice.9.mine), channel_id=1, source_target_pairs={{0,1},{1,0},{2,3},{3,2},{4,5},{5,4},{6,7},{7,6},{8,9},{9,8},{10,11... | collective-permute-start | bytes 294920 | tf_op jit(solution)/shard_map/ppermute | solution.py:530
  21.3 0.1 collective-permute-start.5
  21.4 0.8 %collective-permute-done.6.other = f32[192,128]{1,0:T(8,128)S(1)} collective-permute-done((f32[192,128]{1,0:T(8,128)S(1)}, f32[192,128]{1,0:T(8,128)S(1)}, u32[]{:S(2)}, u32[]{:S(2)}) %collective-permute-start.6) | collective-permute-done | bytes 98336 | tf_op jit(solution)/shard_map/ppermute | solution.py:530
  22.2 3.2 %inner.2 = (f32[18,3,32,128]{3,2,1,0:T(8,128)S(1)}, f32[11,3,32,128]{3,2,1,0:T(8,128)S(1)}, f32[7,3,32,128]{3,2,1,0:T(8,128)S(1)}, f32[3,32,128]{2,1,0:T(8,128)S(1)}) custom-call(f32[192,128]{1,0:T(8,128)S(1)} %slice.9.mine, f32[192,128]{1,0:T(8,128)S(1)} %collective-permute-done.6.other, f32[18,3,48,128]{3,2,1,0:T(8,128)S(1)} %get-tuple-element.28.padded, ...), custom_call_target="tpu_custom_call" | custom-call | flops 20000000 | bytes 6000000 | tf_op jit(solution)/shard_map/inner/pallas_call | solution.py:393
  25.4 1.9 %collective-permute-start.7 = (f32[112,128]{1,0:T(8,128)S(1)}, f32[112,128]{1,0:T(8,128)S(1)}, u32[]{:S(2)}, u32[]{:S(2)}) collective-permute-start(f32[112,128]{1,0:T(8,128)S(1)} %get-tuple-element.34), channel_id=1, source_target_pairs={{0,240},{16,0},{32,16},{48,32},{64,48},{80,64},{96,80},{112,96},{1... | collective-permute-start | bytes 172040 | tf_op jit(solution)/shard_map/ppermute | solution.py:525
  27.3 1.8 %inner.3 = (f32[18,3,32,128]{3,2,1,0:T(8,128)S(1)}, f32[11,3,32,128]{3,2,1,0:T(8,128)S(1)}, f32[7,3,32,128]{3,2,1,0:T(8,128)S(1)}, f32[3,32,128]{2,1,0:T(8,128)S(1)}) custom-call(f32[192,128]{1,0:T(8,128)S(1)} %slice.9.mine, f32[192,128]{1,0:T(8,128)S(1)} %collective-permute-done.6.other, f32[18,3,48,128]{3,2,1,0:T(8,128)S(1)} %get-tuple-element.28.padded, ...), custom_call_target="tpu_custom_call" | custom-call | flops 20000000 | bytes 6000000 | tf_op jit(solution)/shard_map/inner/pallas_call | solution.py:393
  29.1 0.0 collective-permute-done.5.west
  29.1 0.9 %collective-permute-done.7.east = f32[112,128]{1,0:T(8,128)S(1)} collective-permute-done((f32[112,128]{1,0:T(8,128)S(1)}, f32[112,128]{1,0:T(8,128)S(1)}, u32[]{:S(2)}, u32[]{:S(2)}) %collective-permute-start.7) | collective-permute-done | bytes 57376 | tf_op jit(solution)/shard_map/ppermute | solution.py:525
  30.1 2.5 %edges.1 = f32[18,3,32,128]{3,2,1,0:T(8,128)} custom-call(f32[112,128]{1,0:T(8,128)S(1)} %collective-permute-done.5.west, f32[112,128]{1,0:T(8,128)S(1)} %collective-permute-done.7.east, f32[96,128]{1,0:T(8,128)S(1)} %bitcast.6, f32[18,3,32,128]{3,2,1,0:T(8,128)S(1)} %get-tuple-element.35.refs_0_, f32[11,3,32,128]{3,2,1,0:T(8,128)S(1)} %get-tuple-element.36.refs_1_, ...), custom_call_target="tpu_custom_call" | custom-call | tf_op jit(solution)/shard_map/edges/pallas_call | solution.py:509
  (6 shorter events, 0.1 us)
Async XLA Ops:
  1.2 4.3 %collective-permute-start = (f32[208,128]{1,0:T(8,128)S(1)}, f32[208,128]{1,0:T(8,128)S(1)}, u32[]{:S(2)}, u32[]{:S(2)}) collective-permute-start(f32[208,128]{1,0:T(8,128)S(1)} %get-tuple-element.26), channel_id=1, source_target_pairs={{0,1},{1,0},{2,3},{3,2},{4,5},{5,4},{6,7},{7,6},{8,9},{9,8},{10,11... | collective-permute-start | bytes 319496 | tf_op jit(solution)/shard_map/ppermute | solution.py:530
  5.5 5.8 %collective-permute-start.3 = (f32[208,128]{1,0:T(8,128)S(1)}, f32[208,128]{1,0:T(8,128)S(1)}, u32[]{:S(2)}, u32[]{:S(2)}) collective-permute-start(f32[208,128]{1,0:T(8,128)S(1)} %select_select_fusion), channel_id=1, source_target_pairs={{0,4},{1,5},{2,6},{3,7},{4,0},{5,1},{6,2},{7,3},{8,12},{9,13},{10,... | collective-permute-start | bytes 319496 | tf_op jit(solution)/shard_map/ppermute | solution.py:535
  6.8 7.4 %collective-permute-start.1 = (f32[208,128]{1,0:T(8,128)S(1)}, f32[208,128]{1,0:T(8,128)S(1)}, u32[]{:S(2)}, u32[]{:S(2)}) collective-permute-start(f32[208,128]{1,0:T(8,128)S(1)} %select_select_fusion), channel_id=1, source_target_pairs={{0,2},{1,3},{2,4},{3,5},{4,6},{5,7},{6,0},{7,1},{8,10},{9,11},{10,... | collective-permute-start | bytes 319496 | tf_op jit(solution)/shard_map/ppermute | solution.py:535
  7.2 7.0 %collective-permute-start.2 = (f32[208,128]{1,0:T(8,128)S(1)}, f32[208,128]{1,0:T(8,128)S(1)}, u32[]{:S(2)}, u32[]{:S(2)}) collective-permute-start(f32[208,128]{1,0:T(8,128)S(1)} %select_select_fusion), channel_id=1, source_target_pairs={{0,6},{1,7},{2,0},{3,1},{4,2},{5,3},{6,4},{7,5},{8,14},{9,15},{10,... | collective-permute-start | bytes 319496 | tf_op jit(solution)/shard_map/ppermute | solution.py:535
  14.2 5.5 %collective-permute-start.4 = (f32[208,128]{1,0:T(8,128)S(1)}, f32[208,128]{1,0:T(8,128)S(1)}, u32[]{:S(2)}, u32[]{:S(2)}) collective-permute-start(f32[208,128]{1,0:T(8,128)S(1)} %add_add_fusion), channel_id=1, source_target_pairs={{0,8},{1,9},{2,10},{3,11},{4,12},{5,13},{6,14},{7,15},{8,0},{9,1},... | collective-permute-start | bytes 319496 | tf_op jit(solution)/shard_map/ppermute | solution.py:530
  15.0 1.2 %copy-start = (f32[18,3,32,128]{3,2,1,0:T(8,128)S(1)}, f32[18,3,32,128]{3,2,1,0:T(8,128)}, u32[]{:S(2)}) copy-start(f32[18,3,32,128]{3,2,1,0:T(8,128)} %mass.1) | copy-start | bytes 2654212
  19.7 2.5 %collective-permute-start.6 = (f32[192,128]{1,0:T(8,128)S(1)}, f32[192,128]{1,0:T(8,128)S(1)}, u32[]{:S(2)}, u32[]{:S(2)}) collective-permute-start(f32[192,128]{1,0:T(8,128)S(1)} %slice.9.mine), channel_id=1, source_target_pairs={{0,1},{1,0},{2,3},{3,2},{4,5},{5,4},{6,7},{7,6},{8,9},{9,8},{10,11... | collective-permute-start | bytes 294920 | tf_op jit(solution)/shard_map/ppermute | solution.py:530
  21.3 7.9 %collective-permute-start.5 = (f32[112,128]{1,0:T(8,128)S(1)}, f32[112,128]{1,0:T(8,128)S(1)}, u32[]{:S(2)}, u32[]{:S(2)}) collective-permute-start(f32[112,128]{1,0:T(8,128)S(1)} %get-tuple-element.44), channel_id=1, source_target_pairs={{0,16},{16,32},{32,48},{48,64},{64,80},{80,96},{96,112},{112,128},... | collective-permute-start | bytes 172040 | tf_op jit(solution)/shard_map/ppermute | solution.py:525
  25.4 4.7 %collective-permute-start.7 = (f32[112,128]{1,0:T(8,128)S(1)}, f32[112,128]{1,0:T(8,128)S(1)}, u32[]{:S(2)}, u32[]{:S(2)}) collective-permute-start(f32[112,128]{1,0:T(8,128)S(1)} %get-tuple-element.34), channel_id=1, source_target_pairs={{0,240},{16,0},{32,16},{48,32},{64,48},{80,64},{96,80},{112,96},{1... | collective-permute-start | bytes 172040 | tf_op jit(solution)/shard_map/ppermute | solution.py:525

commit v8 on v7

--- a/solution.py
+++ b/solution.py
@@ -185,51 +185,64 @@
     )(thick, fe, fn, ce, cn, ne)
 
 
-def pack_kernel(mass, last, first, padded, moved):
+def pack_kernel(mass, last, first):
     tracers, levels, count, width = mass.shape
     lane = lane_index((count, width))
-    zero_rows = jnp.zeros((PAD, width), jnp.float32)
 
     def level(l, carry):
         a = jnp.zeros((count, width), jnp.float32)
         b = a
         for t in range(tracers):
+            inside = (lane >= EDGE * t) & (lane < EDGE * (t + 1))
+            a = jnp.where(inside, lanes(mass[t, l], EDGE * (t + 1)), a)
+            b = jnp.where(inside, lanes(mass[t, l], EDGE * t), b)
+        place = pl.ds(pl.multiple_of(l * count, count), count)
+        last[place, :] = a
+        first[place, :] = b
+        return carry
+
+    lax.fori_loop(0, levels, level, 0)
+
+
+def copies_kernel(mass, padded, moved):
+    tracers, levels, count, width = mass.shape
+    zero_rows = jnp.zeros((PAD, width), jnp.float32)
+
+    def level(l, carry):
+        for t in range(tracers):
             value = mass[t, l]
-            inside = (lane >= EDGE * t) & (lane < EDGE * (t + 1))
-            a = jnp.where(inside, lanes(value, EDGE * (t + 1)), a)
-            b = jnp.where(inside, lanes(value, EDGE * t), b)
             padded[t, l, :PAD, :] = zero_rows
             padded[t, l, PAD : PAD + count, :] = value
             padded[t, l, PAD + count :, :] = zero_rows
             for k, shift in enumerate(NEAR):
                 moved[k, t, l] = lanes(value, -shift)
-        last[l] = a
-        first[l] = b
         return carry
 
     lax.fori_loop(0, levels, level, 0)
 
 
-def pack(mass):
-    tracers, levels, count, width = mass.shape
+def in_vmem(kernel, name, shapes, *operands):
     vmem = pl.BlockSpec(memory_space=pltpu.VMEM)
-    packed = pltpu.VMEM((levels, count, width), jnp.float32)
-    last, first, padded, moved = pl.pallas_call(
-        pack_kernel,
-        out_shape=(
-            packed,
-            packed,
-            pltpu.VMEM((tracers, levels, count + 2 * PAD, width), jnp.float32),
-            pltpu.VMEM((len(NEAR),) + mass.shape, jnp.float32),
-        ),
-        in_specs=[vmem],
-        out_specs=(vmem,) * 4,
+    return pl.pallas_call(
+        kernel,
+        out_shape=tuple(pltpu.VMEM(shape, jnp.float32) for shape in shapes),
+        in_specs=[vmem] * len(operands),
+        out_specs=(vmem,) * len(shapes),
         compiler_params=pltpu.CompilerParams(vmem_limit_bytes=24 * 1024 * 1024),
         cost_estimate=pl.CostEstimate(flops=2000000, bytes_accessed=1000000, transcendentals=0),
-        name="pack",
-    )(mass)
-    rows_flat = (levels * count, width)
-    return last.reshape(rows_flat), first.reshape(rows_flat), padded, moved
+        name=name,
+    )(*operands)
+
+
+def pack(mass):
+    _, levels, count, width = mass.shape
+    return in_vmem(pack_kernel, "pack", ((levels * count, width),) * 2, mass)
+
+
+def copies(mass):
+    tracers, levels, count, width = mass.shape
+    padded = (tracers, levels, count + 2 * PAD, width)
+    return in_vmem(copies_kernel, "copies", (padded, (len(NEAR),) + mass.shape), mass)
 
 
 def segments(shape):
@@ -341,16 +354,18 @@
         for b in range(count // BLOCK):
             taps = weights(east_c, l, b, EDGE)
             north = weights(north_c, l, b, 3)
+            taps[0] = 1.0 + taps[0]
+            north[0] = 1.0 + north[0]
             for j in range(GROUP):
                 x = padded[t0 + j, l, padded_block(b), :]
-                inner = x + north[0] * x
+                inner = north[0] * x
                 for m in (-3, -2, -1, 1, 2, 3):
                     inner = inner + north[m] * padded[t0 + j, l, padded_block(b, m), :]
                 inners[slot, j, block(b), :] = inner
                 near = {0: x}
                 for k, shift in enumerate(NEAR):
                     near[shift] = shifted[k, t0 + j, l, block(b), :]
-                middle[slot, j, padded_block(b), :] = x + moved_sum(east_parts(taps, near))
+                middle[slot, j, padded_block(b), :] = moved_sum(east_parts(taps, near))
 
     def back(step):
         l, t0 = place(step)
@@ -383,7 +398,9 @@
         front(step + 1)
         return carry
 
-    lax.fori_loop(low_level * groups - 1, high_level * groups + 1, step_of_three, 0)
+    front(low_level * groups)
+    lax.fori_loop(low_level * groups, high_level * groups, step_of_three, 0)
+    finish(high_level * groups - 1)
 
 
 def inner_update(span, mine, other, padded, shifted):
@@ -434,8 +451,9 @@
     met_east = unfolded(east[base:, :])
     met_west = unfolded(west[base:, :])
 
-    def copy(l):
-        return pltpu.make_async_copy(stage.at[:, l], out.at[:, l], sems.at[l])
+    def copy(l, half):
+        place = pl.ds(half * PACK, PACK)
+        return pltpu.make_async_copy(stage.at[place, l], out.at[place, l], sems.at[l, half])
 
     def level(l, sums, outer_c, edge_c, thickness):
         level_rows = pl.ds(pl.multiple_of(l * count, count), count)
@@ -484,7 +502,7 @@
                 t = half * PACK + k
                 moved = jnp.where(at_edge, lanes(total, width - EDGE - SEG * k), 0.0)
                 stage[t, l] = (sums[t, l] + moved) * inverse
-        copy(l).start()
+            copy(l, half).start()
 
     def either(l, carry):
         @pl.when(l < first_levels)
@@ -499,7 +517,8 @@
 
     lax.fori_loop(0, levels, either, 0)
     for l in range(levels):
-        copy(l).wait()
+        for half in range(2):
+            copy(l, half).wait()
 
 
 def edge_update(west, east, own, before, after):
@@ -511,7 +530,7 @@
         out_shape=jax.ShapeDtypeStruct(sums.shape, jnp.float32),
         in_specs=[vmem] * 11,
         out_specs=pl.BlockSpec(memory_space=pl.ANY),
-        scratch_shapes=[pltpu.VMEM(sums.shape, jnp.float32), pltpu.SemaphoreType.DMA((levels,))],
+        scratch_shapes=[pltpu.VMEM(sums.shape, jnp.float32), pltpu.SemaphoreType.DMA((levels, 2))],
         compiler_params=pltpu.CompilerParams(vmem_limit_bytes=24 * 1024 * 1024),
         name="edges",
     )(west, east, own, *before, *after)
@@ -537,12 +556,14 @@
 
 def shards(mass, thick, fe, fn, ce, cn, ne, owner):
     keep, send = prepare(thick, fe, fn, ce, cn, ne)
-    last, first, padded, shifted = pack(mass)
+    last, first = pack(mass)
     me, chosen = position(), owner[0]
     other_core = exchange(send, 1)
     total = jnp.where(chosen == me, keep, jnp.where(chosen == me ^ 1, other_core, 0.0))
     total = total + (turn(total, 1) + turn(total, -1) + turn(total, 2))
+    total, last, first = lax.optimization_barrier((total, last, first))
     total = total + exchange(total, 8)
+    padded, shifted = copies(mass)
     main = 2 * mass.shape[1] * mass.shape[2]
     mine = total[:main]
     edges = total[main:]

time: 32.8 us -> 32.8 us (level)
    ppermute x3, waiting for transfers between devices: 4.68 us -> 2.86 us  [turn(): lax.ppermute(x, 'tracer', [(i, i // 8 * 8 + (i + 2 * by) % 8) for i in ra...]
    ppermute x3, waiting for transfers between devices: 3.23 us -> 4.84 us  [exchange(): return lax.ppermute(x, 'tracer', [(i, i ^ flip) for i in range(size)])]
    pallas_call x2, Pallas kernels: 5 us -> 4.67 us  [inner_update(): pl.pallas_call(functools.partial(inner_kernel, span), out_shape=(pltpu.VM...]
    pallas_call x1 -> x2, Pallas kernels: 1.32 us -> 1.52 us  [in_vmem(): pl.pallas_call(kernel, out_shape=tuple((pltpu.VMEM(shape, jnp.float32) fo...]
  transfers between devices with their start and end apart: 8 -> 8, of which waited for: 6 -> 5; matrix products, arithmetic and copies ran while one was open for 0% -> 0% of each run, Pallas kernels for 19% -> 19%
where the time goes in v8:
time: 32.8 us; the launch traced here: 32.6 us
  starting transfers between devices  11.9 us (36%)
  Pallas kernels  9.93 us (30%)
  waiting for transfers between devices  8.78 us (27%)
  local copies, waits for them, and re-layouts  1.18 us (4%)
  between operations  0.74 us (2%)
    ppermute x3, starting transfers between devices, exchange(): return lax.ppermute(x, 'tracer', [(i, i ^ flip) for i in range(size)])  5.81 us
    ppermute x3, waiting for transfers between devices, exchange(): return lax.ppermute(x, 'tracer', [(i, i ^ flip) for i in range(size)])  4.84 us
    pallas_call x2, Pallas kernels, inner_update(): pl.pallas_call(functools.partial(inner_kernel, span), out_shape=(pltpu.VM...  4.67 us
    ppermute x3, starting transfers between devices, turn(): lax.ppermute(x, 'tracer', [(i, i // 8 * 8 + (i + 2 * by) % 8) for i in ra...  3.94 us
    ppermute x3, waiting for transfers between devices, turn(): lax.ppermute(x, 'tracer', [(i, i // 8 * 8 + (i + 2 * by) % 8) for i in ra...  2.86 us
    pallas_call x1, Pallas kernels, edge_update(): pl.pallas_call(edge_kernel, out_shape=jax.ShapeDtypeStruct(sums.shape, jn...  2.55 us
    ppermute x2, starting transfers between devices, along(): return lax.ppermute(x, 'space', pairs)  2.16 us
    pallas_call x2, Pallas kernels, in_vmem(): pl.pallas_call(kernel, out_shape=tuple((pltpu.VMEM(shape, jnp.float32) fo...  1.52 us
  transfers between devices with their start and end apart: 8, of which 5 were waited for; matrix products, arithmetic and copies ran while one was open for 0% of the time, Pallas kernels for 19%

profile of v8, /device:TPU:1, one launch (start us, length us, event | category | flops | bytes accessed | tf_op | source)
XLA Modules:
  0.0 32.6 jit_solution(9241911755751059032)
XLA Ops:
  0.0 1.2 %prepare.1 = (f32[208,128]{1,0:T(8,128)S(1)}, f32[208,128]{1,0:T(8,128)S(1)}) custom-call(f32[1,3,32,128]{3,2,1,0:T(8,128)} %refs_0_.1, f32[1,3,32,128]{3,2,1,0:T(8,128)} %refs_1_.1, f32[1,3,32,128]{3,2,1,0:T(8,128)} %refs_2_.1, f32[1,3,32,128]{3,2,1,0:T(8,128)} %refs_3_.1, f32[1,3,32,128]{3,2,1,0:T(8,128)} %refs_4_.1, s32[1,3,32,128]{3,2,1,0:T(8,128)} %refs_5_.1), custom_call_target="tpu_custom_call" | custom-call | tf_op jit(solution)/shard_map/prepare/pallas_call | solution.py:177
  1.2 3.3 %collective-permute-start = (f32[208,128]{1,0:T(8,128)S(1)}, f32[208,128]{1,0:T(8,128)S(1)}, u32[]{:S(2)}, u32[]{:S(2)}) collective-permute-start(f32[208,128]{1,0:T(8,128)S(1)} %get-tuple-element.28), channel_id=1, source_target_pairs={{0,1},{1,0},{2,3},{3,2},{4,5},{5,4},{6,7},{7,6},{8,9},{9,8},{10,11... | collective-permute-start | bytes 319496 | tf_op jit(solution)/shard_map/ppermute | solution.py:549
  5.2 0.3 collective-permute-done
  5.5 1.3 %collective-permute-start.3 = (f32[208,128]{1,0:T(8,128)S(1)}, f32[208,128]{1,0:T(8,128)S(1)}, u32[]{:S(2)}, u32[]{:S(2)}) collective-permute-start(f32[208,128]{1,0:T(8,128)S(1)} %select_select_fusion), channel_id=1, source_target_pairs={{0,4},{1,5},{2,6},{3,7},{4,0},{5,1},{6,2},{7,3},{8,12},{9,13},{10,... | collective-permute-start | bytes 319496 | tf_op jit(solution)/shard_map/ppermute | solution.py:554
  6.8 0.4 %collective-permute-start.1 = (f32[208,128]{1,0:T(8,128)S(1)}, f32[208,128]{1,0:T(8,128)S(1)}, u32[]{:S(2)}, u32[]{:S(2)}) collective-permute-start(f32[208,128]{1,0:T(8,128)S(1)} %select_select_fusion), channel_id=1, source_target_pairs={{0,2},{1,3},{2,4},{3,5},{4,6},{5,7},{6,0},{7,1},{8,10},{9,11},{10,... | collective-permute-start | bytes 319496 | tf_op jit(solution)/shard_map/ppermute | solution.py:554
  7.2 2.3 %collective-permute-start.2 = (f32[208,128]{1,0:T(8,128)S(1)}, f32[208,128]{1,0:T(8,128)S(1)}, u32[]{:S(2)}, u32[]{:S(2)}) collective-permute-start(f32[208,128]{1,0:T(8,128)S(1)} %select_select_fusion), channel_id=1, source_target_pairs={{0,6},{1,7},{2,0},{3,1},{4,2},{5,3},{6,4},{7,5},{8,14},{9,15},{10,... | collective-permute-start | bytes 319496 | tf_op jit(solution)/shard_map/ppermute | solution.py:554
  9.4 0.0 copy-start
  9.4 1.2 %copy-done = f32[18,3,32,128]{3,2,1,0:T(8,128)S(1)} copy-done((f32[18,3,32,128]{3,2,1,0:T(8,128)S(1)}, f32[18,3,32,128]{3,2,1,0:T(8,128)}, u32[]{:S(2)}) %copy-start) | copy-done | bytes 884760
  10.6 0.6 %pack.1 = (f32[96,128]{1,0:T(8,128)S(1)}, f32[96,128]{1,0:T(8,128)S(1)}) custom-call(f32[18,3,32,128]{3,2,1,0:T(8,128)S(1)} %copy-done), custom_call_target="tpu_custom_call" | custom-call | flops 2000000 | bytes 1000000 | tf_op jit(solution)/shard_map/pack/pallas_call | solution.py:226
  11.3 0.0 collective-permute-done.3
  11.3 2.8 %collective-permute-done.1 = f32[208,128]{1,0:T(8,128)S(1)} collective-permute-done((f32[208,128]{1,0:T(8,128)S(1)}, f32[208,128]{1,0:T(8,128)S(1)}, u32[]{:S(2)}, u32[]{:S(2)}) %collective-permute-start.1) | collective-permute-done | bytes 106528 | tf_op jit(solution)/shard_map/ppermute | solution.py:554
  14.1 0.0 collective-permute-done.2
  14.2 0.9 %collective-permute-start.4 = (f32[208,128]{1,0:T(8,128)S(1)}, f32[208,128]{1,0:T(8,128)S(1)}, u32[]{:S(2)}, u32[]{:S(2)}) collective-permute-start(f32[208,128]{1,0:T(8,128)S(1)} %add_add_fusion), channel_id=1, source_target_pairs={{0,8},{1,9},{2,10},{3,11},{4,12},{5,13},{6,14},{7,15},{8,0},{9,1},... | collective-permute-start | bytes 319496 | tf_op jit(solution)/shard_map/ppermute | solution.py:549
  15.0 0.9 %copies.1 = (f32[18,3,48,128]{3,2,1,0:T(8,128)S(1)}, f32[3,18,3,32,128]{4,3,2,1,0:T(8,128)S(1)}) custom-call(f32[18,3,32,128]{3,2,1,0:T(8,128)S(1)} %copy-done), custom_call_target="tpu_custom_call" | custom-call | flops 2000000 | bytes 1000000 | tf_op jit(solution)/shard_map/copies/pallas_call | solution.py:226
  15.9 3.7 %collective-permute-done.4 = f32[208,128]{1,0:T(8,128)S(1)} collective-permute-done((f32[208,128]{1,0:T(8,128)S(1)}, f32[208,128]{1,0:T(8,128)S(1)}, u32[]{:S(2)}, u32[]{:S(2)}) %collective-permute-start.4) | collective-permute-done | bytes 106528 | tf_op jit(solution)/shard_map/ppermute | solution.py:549
  19.7 1.6 %collective-permute-start.6 = (f32[192,128]{1,0:T(8,128)S(1)}, f32[192,128]{1,0:T(8,128)S(1)}, u32[]{:S(2)}, u32[]{:S(2)}) collective-permute-start(f32[192,128]{1,0:T(8,128)S(1)} %slice.9.mine), channel_id=1, source_target_pairs={{0,1},{1,0},{2,3},{3,2},{4,5},{5,4},{6,7},{7,6},{8,9},{9,8},{10,11... | collective-permute-start | bytes 294920 | tf_op jit(solution)/shard_map/ppermute | solution.py:549
  21.3 0.1 collective-permute-start.5
  21.4 0.8 %collective-permute-done.6.other = f32[192,128]{1,0:T(8,128)S(1)} collective-permute-done((f32[192,128]{1,0:T(8,128)S(1)}, f32[192,128]{1,0:T(8,128)S(1)}, u32[]{:S(2)}, u32[]{:S(2)}) %collective-permute-start.6) | collective-permute-done | bytes 98336 | tf_op jit(solution)/shard_map/ppermute | solution.py:549
  22.2 3.0 %inner.2 = (f32[18,3,32,128]{3,2,1,0:T(8,128)S(1)}, f32[11,3,32,128]{3,2,1,0:T(8,128)S(1)}, f32[7,3,32,128]{3,2,1,0:T(8,128)S(1)}, f32[3,32,128]{2,1,0:T(8,128)S(1)}) custom-call(f32[192,128]{1,0:T(8,128)S(1)} %slice.9.mine, f32[192,128]{1,0:T(8,128)S(1)} %collective-permute-done.6.other, f32[18,3,48,128]{3,2,1,0:T(8,128)S(1)} %get-tuple-element.34.padded, ...), custom_call_target="tpu_custom_call" | custom-call | flops 20000000 | bytes 6000000 | tf_op jit(solution)/shard_map/inner/pallas_call | solution.py:410
  25.2 2.1 %collective-permute-start.7 = (f32[112,128]{1,0:T(8,128)S(1)}, f32[112,128]{1,0:T(8,128)S(1)}, u32[]{:S(2)}, u32[]{:S(2)}) collective-permute-start(f32[112,128]{1,0:T(8,128)S(1)} %get-tuple-element.40), channel_id=1, source_target_pairs={{0,240},{16,0},{32,16},{48,32},{64,48},{80,64},{96,80},{112,96},{1... | collective-permute-start | bytes 172040 | tf_op jit(solution)/shard_map/ppermute | solution.py:544
  27.3 1.7 %inner.3 = (f32[18,3,32,128]{3,2,1,0:T(8,128)S(1)}, f32[11,3,32,128]{3,2,1,0:T(8,128)S(1)}, f32[7,3,32,128]{3,2,1,0:T(8,128)S(1)}, f32[3,32,128]{2,1,0:T(8,128)S(1)}) custom-call(f32[192,128]{1,0:T(8,128)S(1)} %slice.9.mine, f32[192,128]{1,0:T(8,128)S(1)} %collective-permute-done.6.other, f32[18,3,48,128]{3,2,1,0:T(8,128)S(1)} %get-tuple-element.34.padded, ...), custom_call_target="tpu_custom_call" | custom-call | flops 20000000 | bytes 6000000 | tf_op jit(solution)/shard_map/inner/pallas_call | solution.py:410
  29.0 0.0 collective-permute-done.5.west
  29.0 1.1 %collective-permute-done.7.east = f32[112,128]{1,0:T(8,128)S(1)} collective-permute-done((f32[112,128]{1,0:T(8,128)S(1)}, f32[112,128]{1,0:T(8,128)S(1)}, u32[]{:S(2)}, u32[]{:S(2)}) %collective-permute-start.7) | collective-permute-done | bytes 57376 | tf_op jit(solution)/shard_map/ppermute | solution.py:544
  30.1 2.5 %edges.1 = f32[18,3,32,128]{3,2,1,0:T(8,128)} custom-call(f32[112,128]{1,0:T(8,128)S(1)} %collective-permute-done.5.west, f32[112,128]{1,0:T(8,128)S(1)} %collective-permute-done.7.east, f32[96,128]{1,0:T(8,128)S(1)} %get-tuple-element.31.own, f32[18,3,32,128]{3,2,1,0:T(8,128)S(1)} %get-tuple-element.41.refs_0_, ...), custom_call_target="tpu_custom_call" | custom-call | tf_op jit(solution)/shard_map/edges/pallas_call | solution.py:528
  (6 shorter events, 0.1 us)
Async XLA Ops:
  1.2 4.3 %collective-permute-start = (f32[208,128]{1,0:T(8,128)S(1)}, f32[208,128]{1,0:T(8,128)S(1)}, u32[]{:S(2)}, u32[]{:S(2)}) collective-permute-start(f32[208,128]{1,0:T(8,128)S(1)} %get-tuple-element.28), channel_id=1, source_target_pairs={{0,1},{1,0},{2,3},{3,2},{4,5},{5,4},{6,7},{7,6},{8,9},{9,8},{10,11... | collective-permute-start | bytes 319496 | tf_op jit(solution)/shard_map/ppermute | solution.py:549
  5.5 5.8 %collective-permute-start.3 = (f32[208,128]{1,0:T(8,128)S(1)}, f32[208,128]{1,0:T(8,128)S(1)}, u32[]{:S(2)}, u32[]{:S(2)}) collective-permute-start(f32[208,128]{1,0:T(8,128)S(1)} %select_select_fusion), channel_id=1, source_target_pairs={{0,4},{1,5},{2,6},{3,7},{4,0},{5,1},{6,2},{7,3},{8,12},{9,13},{10,... | collective-permute-start | bytes 319496 | tf_op jit(solution)/shard_map/ppermute | solution.py:554
  6.8 7.4 %collective-permute-start.1 = (f32[208,128]{1,0:T(8,128)S(1)}, f32[208,128]{1,0:T(8,128)S(1)}, u32[]{:S(2)}, u32[]{:S(2)}) collective-permute-start(f32[208,128]{1,0:T(8,128)S(1)} %select_select_fusion), channel_id=1, source_target_pairs={{0,2},{1,3},{2,4},{3,5},{4,6},{5,7},{6,0},{7,1},{8,10},{9,11},{10,... | collective-permute-start | bytes 319496 | tf_op jit(solution)/shard_map/ppermute | solution.py:554
  7.2 7.0 %collective-permute-start.2 = (f32[208,128]{1,0:T(8,128)S(1)}, f32[208,128]{1,0:T(8,128)S(1)}, u32[]{:S(2)}, u32[]{:S(2)}) collective-permute-start(f32[208,128]{1,0:T(8,128)S(1)} %select_select_fusion), channel_id=1, source_target_pairs={{0,6},{1,7},{2,0},{3,1},{4,2},{5,3},{6,4},{7,5},{8,14},{9,15},{10,... | collective-permute-start | bytes 319496 | tf_op jit(solution)/shard_map/ppermute | solution.py:554
  9.4 1.2 %copy-start = (f32[18,3,32,128]{3,2,1,0:T(8,128)S(1)}, f32[18,3,32,128]{3,2,1,0:T(8,128)}, u32[]{:S(2)}) copy-start(f32[18,3,32,128]{3,2,1,0:T(8,128)} %mass.3) | copy-start | bytes 2654212
  14.2 5.5 %collective-permute-start.4 = (f32[208,128]{1,0:T(8,128)S(1)}, f32[208,128]{1,0:T(8,128)S(1)}, u32[]{:S(2)}, u32[]{:S(2)}) collective-permute-start(f32[208,128]{1,0:T(8,128)S(1)} %add_add_fusion), channel_id=1, source_target_pairs={{0,8},{1,9},{2,10},{3,11},{4,12},{5,13},{6,14},{7,15},{8,0},{9,1},... | collective-permute-start | bytes 319496 | tf_op jit(solution)/shard_map/ppermute | solution.py:549
  19.7 2.5 %collective-permute-start.6 = (f32[192,128]{1,0:T(8,128)S(1)}, f32[192,128]{1,0:T(8,128)S(1)}, u32[]{:S(2)}, u32[]{:S(2)}) collective-permute-start(f32[192,128]{1,0:T(8,128)S(1)} %slice.9.mine), channel_id=1, source_target_pairs={{0,1},{1,0},{2,3},{3,2},{4,5},{5,4},{6,7},{7,6},{8,9},{9,8},{10,11... | collective-permute-start | bytes 294920 | tf_op jit(solution)/shard_map/ppermute | solution.py:549
  21.3 7.7 %collective-permute-start.5 = (f32[112,128]{1,0:T(8,128)S(1)}, f32[112,128]{1,0:T(8,128)S(1)}, u32[]{:S(2)}, u32[]{:S(2)}) collective-permute-start(f32[112,128]{1,0:T(8,128)S(1)} %get-tuple-element.50), channel_id=1, source_target_pairs={{0,16},{16,32},{32,48},{48,64},{64,80},{80,96},{96,112},{112,128},... | collective-permute-start | bytes 172040 | tf_op jit(solution)/shard_map/ppermute | solution.py:544
  25.2 4.8 %collective-permute-start.7 = (f32[112,128]{1,0:T(8,128)S(1)}, f32[112,128]{1,0:T(8,128)S(1)}, u32[]{:S(2)}, u32[]{:S(2)}) collective-permute-start(f32[112,128]{1,0:T(8,128)S(1)} %get-tuple-element.40), channel_id=1, source_target_pairs={{0,240},{16,0},{32,16},{48,32},{64,48},{80,64},{96,80},{112,96},{1... | collective-permute-start | bytes 172040 | tf_op jit(solution)/shard_map/ppermute | solution.py:544

commit v9 on v8

--- a/solution.py
+++ b/solution.py
@@ -430,7 +430,7 @@
     )(mine, other, padded, shifted)
 
 
-def edge_kernel(west, east, own, *refs):
+def edge_kernel(west, west_rest, east, own, *refs):
     before, after, (out, stage, sems) = refs[:4], refs[4:8], refs[8:]
     tracers, levels, count, width = stage.shape
     first_levels = early_levels(levels)
@@ -449,7 +449,7 @@
         return jnp.concatenate([x, lanes(x, -MET_SEG * levels)])
 
     met_east = unfolded(east[base:, :])
-    met_west = unfolded(west[base:, :])
+    met_west = unfolded(west[base:, :] + west_rest[:, :])
 
     def copy(l, half):
         place = pl.ds(half * PACK, PACK)
@@ -521,19 +521,19 @@
             copy(l, half).wait()
 
 
-def edge_update(west, east, own, before, after):
+def edge_update(west, west_rest, east, own, before, after):
     sums = before[0]
     tracers, levels, count, width = sums.shape
     vmem = pl.BlockSpec(memory_space=pltpu.VMEM)
     return pl.pallas_call(
         edge_kernel,
         out_shape=jax.ShapeDtypeStruct(sums.shape, jnp.float32),
-        in_specs=[vmem] * 11,
+        in_specs=[vmem] * 12,
         out_specs=pl.BlockSpec(memory_space=pl.ANY),
         scratch_shapes=[pltpu.VMEM(sums.shape, jnp.float32), pltpu.SemaphoreType.DMA((levels, 2))],
         compiler_params=pltpu.CompilerParams(vmem_limit_bytes=24 * 1024 * 1024),
         name="edges",
-    )(west, east, own, *before, *after)
+    )(west, west_rest, east, own, *before, *after)
 
 
 def east_group(m):
@@ -561,22 +561,30 @@
     other_core = exchange(send, 1)
     total = jnp.where(chosen == me, keep, jnp.where(chosen == me ^ 1, other_core, 0.0))
     total = total + (turn(total, 1) + turn(total, -1) + turn(total, 2))
-    total, last, first = lax.optimization_barrier((total, last, first))
+    total, last, first, mass = lax.optimization_barrier((total, last, first, mass))
+    main = 2 * mass.shape[1] * mass.shape[2]
+    size, tracers = lax.axis_size("space"), lax.axis_size("tracer")
+    part = total[main:]
     total = total + exchange(total, 8)
+    west = along(jnp.concatenate([last, part]), [(i, (i + 1) % size) for i in range(size)])
+    west_rest = lax.ppermute(
+        part,
+        ("space", "tracer"),
+        [
+            (i * tracers + t, (i + 1) % size * tracers + (t ^ 8))
+            for i in range(size)
+            for t in range(tracers)
+        ],
+    )
     padded, shifted = copies(mass)
-    main = 2 * mass.shape[1] * mass.shape[2]
     mine = total[:main]
-    edges = total[main:]
-    size = lax.axis_size("space")
-    to_east = jnp.concatenate([last, edges])
-    to_west = jnp.concatenate([first, edges])
-    west = along(to_east, [(i, (i + 1) % size) for i in range(size)])
-    other = exchange(mine, 1)
+    to_west = jnp.concatenate([first, total[main:]])
+    other, west_rest = lax.optimization_barrier((exchange(mine, 1), west_rest))
     before = inner_update(lambda levels: (0, early_levels(levels)), mine, other, padded, shifted)
     to_west, before = lax.optimization_barrier((to_west, before))
     east = along(to_west, [(i, (i - 1) % size) for i in range(size)])
     after = inner_update(lambda levels: (early_levels(levels), levels), mine, other, padded, shifted)
-    return edge_update(west, east, last, before, after)
+    return edge_update(west, west_rest, east, last, before, after)
 
 
 def solution(mesh):

time: 32.8 us -> 33.3 us (1.015)
  the two profiles are of different devices: /device:TPU:1 before, /device:TPU:24 now
where the time goes in v9:
time: 33.3 us; the launch traced here: 33.1 us
  waiting for transfers between devices  11.6 us (35%)
  Pallas kernels  9.94 us (30%)
  starting transfers between devices  9.57 us (29%)
  local copies, waits for them, and re-layouts  1.18 us (4%)
  between operations  0.76 us (2%)
    ppermute x1, waiting for transfers between devices, shards(): lax.ppermute(part, ('space', 'tracer'), [(i * tracers + t, (i + 1) % size...  4.72 us
    pallas_call x2, Pallas kernels, inner_update(): pl.pallas_call(functools.partial(inner_kernel, span), out_shape=(pltpu.VM...  4.67 us
    ppermute x3, waiting for transfers between devices, turn(): lax.ppermute(x, 'tracer', [(i, i // 8 * 8 + (i + 2 * by) % 8) for i in ra...  4.12 us
    ppermute x3, starting transfers between devices, turn(): lax.ppermute(x, 'tracer', [(i, i // 8 * 8 + (i + 2 * by) % 8) for i in ra...  3.51 us
    ppermute x3, starting transfers between devices, exchange(): return lax.ppermute(x, 'tracer', [(i, i ^ flip) for i in range(size)])  3.3 us
    pallas_call x1, Pallas kernels, edge_update(): pl.pallas_call(edge_kernel, out_shape=jax.ShapeDtypeStruct(sums.shape, jn...  2.56 us
    ppermute x2, starting transfers between devices, along(): return lax.ppermute(x, 'space', pairs)  1.62 us
    ppermute x2, waiting for transfers between devices, along(): return lax.ppermute(x, 'space', pairs)  1.62 us
  transfers between devices with their start and end apart: 9, of which 7 were waited for; matrix products, arithmetic and copies ran while one was open for 0% of the time, Pallas kernels for 19%

profile of v9, /device:TPU:24, one launch (start us, length us, event | category | flops | bytes accessed | tf_op | source)
XLA Modules:
  0.0 33.1 jit_solution(4124377041961601843)
XLA Ops:
  0.0 1.2 %prepare.1 = (f32[208,128]{1,0:T(8,128)S(1)}, f32[208,128]{1,0:T(8,128)S(1)}) custom-call(f32[1,3,32,128]{3,2,1,0:T(8,128)} %refs_0_.1, f32[1,3,32,128]{3,2,1,0:T(8,128)} %refs_1_.1, f32[1,3,32,128]{3,2,1,0:T(8,128)} %refs_2_.1, f32[1,3,32,128]{3,2,1,0:T(8,128)} %refs_3_.1, f32[1,3,32,128]{3,2,1,0:T(8,128)} %refs_4_.1, s32[1,3,32,128]{3,2,1,0:T(8,128)} %refs_5_.1), custom_call_target="tpu_custom_call" | custom-call | tf_op jit(solution)/shard_map/prepare/pallas_call | solution.py:177
  1.2 0.1 collective-permute-start
  1.9 0.6 %collective-permute-done = f32[208,128]{1,0:T(8,128)S(1)} collective-permute-done((f32[208,128]{1,0:T(8,128)S(1)}, f32[208,128]{1,0:T(8,128)S(1)}, u32[]{:S(2)}, u32[]{:S(2)}) %collective-permute-start) | collective-permute-done | bytes 106528 | tf_op jit(solution)/shard_map/ppermute | solution.py:549
  2.6 1.3 %collective-permute-start.3 = (f32[208,128]{1,0:T(8,128)S(1)}, f32[208,128]{1,0:T(8,128)S(1)}, u32[]{:S(2)}, u32[]{:S(2)}) collective-permute-start(f32[208,128]{1,0:T(8,128)S(1)} %select_select_fusion), channel_id=1, source_target_pairs={{0,4},{1,5},{2,6},{3,7},{4,0},{5,1},{6,2},{7,3},{8,12},{9,13},{10,... | collective-permute-start | bytes 319496 | tf_op jit(solution)/shard_map/ppermute | solution.py:554
  3.9 2.2 %collective-permute-start.1 = (f32[208,128]{1,0:T(8,128)S(1)}, f32[208,128]{1,0:T(8,128)S(1)}, u32[]{:S(2)}, u32[]{:S(2)}) collective-permute-start(f32[208,128]{1,0:T(8,128)S(1)} %select_select_fusion), channel_id=1, source_target_pairs={{0,2},{1,3},{2,4},{3,5},{4,6},{5,7},{6,0},{7,1},{8,10},{9,11},{10,... | collective-permute-start | bytes 319496 | tf_op jit(solution)/shard_map/ppermute | solution.py:554
  6.1 0.0 collective-permute-start.2
  6.1 0.0 copy-start
  6.1 1.2 %copy-done = f32[18,3,32,128]{3,2,1,0:T(8,128)S(1)} copy-done((f32[18,3,32,128]{3,2,1,0:T(8,128)S(1)}, f32[18,3,32,128]{3,2,1,0:T(8,128)}, u32[]{:S(2)}) %copy-start) | copy-done | bytes 884760
  7.3 0.6 %pack.1 = (f32[96,128]{1,0:T(8,128)S(1)}, f32[96,128]{1,0:T(8,128)S(1)}) custom-call(f32[18,3,32,128]{3,2,1,0:T(8,128)S(1)} %copy-done), custom_call_target="tpu_custom_call" | custom-call | flops 2000000 | bytes 1000000 | tf_op jit(solution)/shard_map/pack/pallas_call | solution.py:226
  7.9 2.1 %collective-permute-done.3 = f32[208,128]{1,0:T(8,128)S(1)} collective-permute-done((f32[208,128]{1,0:T(8,128)S(1)}, f32[208,128]{1,0:T(8,128)S(1)}, u32[]{:S(2)}, u32[]{:S(2)}) %collective-permute-start.3) | collective-permute-done | bytes 106528 | tf_op jit(solution)/shard_map/ppermute | solution.py:554
  10.0 0.8 %collective-permute-done.1 = f32[208,128]{1,0:T(8,128)S(1)} collective-permute-done((f32[208,128]{1,0:T(8,128)S(1)}, f32[208,128]{1,0:T(8,128)S(1)}, u32[]{:S(2)}, u32[]{:S(2)}) %collective-permute-start.1) | collective-permute-done | bytes 106528 | tf_op jit(solution)/shard_map/ppermute | solution.py:554
  10.8 1.3 %collective-permute-done.2 = f32[208,128]{1,0:T(8,128)S(1)} collective-permute-done((f32[208,128]{1,0:T(8,128)S(1)}, f32[208,128]{1,0:T(8,128)S(1)}, u32[]{:S(2)}, u32[]{:S(2)}) %collective-permute-start.2) | collective-permute-done | bytes 106528 | tf_op jit(solution)/shard_map/ppermute | solution.py:554
  12.1 3.1 %collective-permute-start.5 = (f32[208,128]{1,0:T(8,128)S(1)}, f32[208,128]{1,0:T(8,128)S(1)}, u32[]{:S(2)}, u32[]{:S(2)}) collective-permute-start(f32[208,128]{1,0:T(8,128)S(1)} %add_add_fusion), channel_id=1, source_target_pairs={{0,8},{1,9},{2,10},{3,11},{4,12},{5,13},{6,14},{7,15},{8,0},{9,1},... | collective-permute-start | bytes 319496 | tf_op jit(solution)/shard_map/ppermute | solution.py:549
  15.2 1.1 %collective-permute-start.7 = (f32[16,128]{1,0:T(8,128)S(1)}, f32[16,128]{1,0:T(8,128)S(1)}, u32[]{:S(2)}, u32[]{:S(2)}) collective-permute-start(f32[16,128]{1,0:T(8,128)S(1)} %slice.9), channel_id=1, source_target_pairs={{0,24},{1,25},{2,26},{3,27},{4,28},{5,29},{6,30},{7,31},{8,16},{9,... | collective-permute-start | bytes 24584 | tf_op jit(solution)/shard_map/ppermute | solution.py:570
  16.4 0.7 %collective-permute-start.4 = (f32[112,128]{1,0:T(8,128)S(1)}, f32[112,128]{1,0:T(8,128)S(1)}, u32[]{:S(2)}, u32[]{:S(2)}) collective-permute-start(f32[112,128]{1,0:T(8,128)S(1)} %pad_maximum_fusion), channel_id=1, source_target_pairs={{0,16},{16,32},{32,48},{48,64},{64,80},{80,96},{96,112},{112,128},... | collective-permute-start | bytes 172040 | tf_op jit(solution)/shard_map/ppermute | solution.py:544
  17.0 0.9 %copies.1 = (f32[18,3,48,128]{3,2,1,0:T(8,128)S(1)}, f32[3,18,3,32,128]{4,3,2,1,0:T(8,128)S(1)}) custom-call(f32[18,3,32,128]{3,2,1,0:T(8,128)S(1)} %copy-done), custom_call_target="tpu_custom_call" | custom-call | flops 2000000 | bytes 1000000 | tf_op jit(solution)/shard_map/copies/pallas_call | solution.py:226
  17.9 0.5 %collective-permute-done.5 = f32[208,128]{1,0:T(8,128)S(1)} collective-permute-done((f32[208,128]{1,0:T(8,128)S(1)}, f32[208,128]{1,0:T(8,128)S(1)}, u32[]{:S(2)}, u32[]{:S(2)}) %collective-permute-start.5) | collective-permute-done | bytes 106528 | tf_op jit(solution)/shard_map/ppermute | solution.py:549
  18.4 0.1 collective-permute-start.6
  18.5 4.7 %collective-permute-done.7.west_rest = f32[16,128]{1,0:T(8,128)S(1)} collective-permute-done((f32[16,128]{1,0:T(8,128)S(1)}, f32[16,128]{1,0:T(8,128)S(1)}, u32[]{:S(2)}, u32[]{:S(2)}) %collective-permute-start.7) | collective-permute-done | bytes 8224 | tf_op jit(solution)/shard_map/ppermute | solution.py:570
  23.3 0.0 collective-permute-done.6.other
  23.3 3.0 %inner.2 = (f32[18,3,32,128]{3,2,1,0:T(8,128)S(1)}, f32[11,3,32,128]{3,2,1,0:T(8,128)S(1)}, f32[7,3,32,128]{3,2,1,0:T(8,128)S(1)}, f32[3,32,128]{2,1,0:T(8,128)S(1)}) custom-call(f32[192,128]{1,0:T(8,128)S(1)} %slice.12.mine, f32[192,128]{1,0:T(8,128)S(1)} %collective-permute-done.6.other, f32[18,3,48,128]{3,2,1,0:T(8,128)S(1)} %get-tuple-element.40.padded, ...), custom_call_target="tpu_custom_call" | custom-call | flops 20000000 | bytes 6000000 | tf_op jit(solution)/shard_map/inner/pallas_call | solution.py:410
  26.3 0.9 %collective-permute-start.8 = (f32[112,128]{1,0:T(8,128)S(1)}, f32[112,128]{1,0:T(8,128)S(1)}, u32[]{:S(2)}, u32[]{:S(2)}) collective-permute-start(f32[112,128]{1,0:T(8,128)S(1)} %pad_maximum_fusion.1), channel_id=1, source_target_pairs={{0,240},{16,0},{32,16},{48,32},{64,48},{80,64},{96,80},{112,96},{1... | collective-permute-start | bytes 172040 | tf_op jit(solution)/shard_map/ppermute | solution.py:544
  27.2 1.7 %inner.3 = (f32[18,3,32,128]{3,2,1,0:T(8,128)S(1)}, f32[11,3,32,128]{3,2,1,0:T(8,128)S(1)}, f32[7,3,32,128]{3,2,1,0:T(8,128)S(1)}, f32[3,32,128]{2,1,0:T(8,128)S(1)}) custom-call(f32[192,128]{1,0:T(8,128)S(1)} %slice.12.mine, f32[192,128]{1,0:T(8,128)S(1)} %collective-permute-done.6.other, f32[18,3,48,128]{3,2,1,0:T(8,128)S(1)} %get-tuple-element.40.padded, ...), custom_call_target="tpu_custom_call" | custom-call | flops 20000000 | bytes 6000000 | tf_op jit(solution)/shard_map/inner/pallas_call | solution.py:410
  28.9 0.0 collective-permute-done.4.west
  28.9 1.6 %collective-permute-done.8.east = f32[112,128]{1,0:T(8,128)S(1)} collective-permute-done((f32[112,128]{1,0:T(8,128)S(1)}, f32[112,128]{1,0:T(8,128)S(1)}, u32[]{:S(2)}, u32[]{:S(2)}) %collective-permute-start.8) | collective-permute-done | bytes 57376 | tf_op jit(solution)/shard_map/ppermute | solution.py:544
  30.5 2.6 %edges.1 = f32[18,3,32,128]{3,2,1,0:T(8,128)} custom-call(f32[112,128]{1,0:T(8,128)S(1)} %collective-permute-done.4.west, f32[16,128]{1,0:T(8,128)S(1)} %collective-permute-done.7.west_rest, f32[112,128]{1,0:T(8,128)S(1)} %collective-permute-done.8.east, f32[96,128]{1,0:T(8,128)S(1)} %get-tuple-element.34.own, ...), custom_call_target="tpu_custom_call" | custom-call | tf_op jit(solution)/shard_map/edges/pallas_call | solution.py:528
  (8 shorter events, 0.1 us)
Async XLA Ops:
  1.2 1.4 %collective-permute-start = (f32[208,128]{1,0:T(8,128)S(1)}, f32[208,128]{1,0:T(8,128)S(1)}, u32[]{:S(2)}, u32[]{:S(2)}) collective-permute-start(f32[208,128]{1,0:T(8,128)S(1)} %get-tuple-element.31), channel_id=1, source_target_pairs={{0,1},{1,0},{2,3},{3,2},{4,5},{5,4},{6,7},{7,6},{8,9},{9,8},{10,11... | collective-permute-start | bytes 319496 | tf_op jit(solution)/shard_map/ppermute | solution.py:549
  2.6 7.4 %collective-permute-start.3 = (f32[208,128]{1,0:T(8,128)S(1)}, f32[208,128]{1,0:T(8,128)S(1)}, u32[]{:S(2)}, u32[]{:S(2)}) collective-permute-start(f32[208,128]{1,0:T(8,128)S(1)} %select_select_fusion), channel_id=1, source_target_pairs={{0,4},{1,5},{2,6},{3,7},{4,0},{5,1},{6,2},{7,3},{8,12},{9,13},{10,... | collective-permute-start | bytes 319496 | tf_op jit(solution)/shard_map/ppermute | solution.py:554
  3.9 6.9 %collective-permute-start.1 = (f32[208,128]{1,0:T(8,128)S(1)}, f32[208,128]{1,0:T(8,128)S(1)}, u32[]{:S(2)}, u32[]{:S(2)}) collective-permute-start(f32[208,128]{1,0:T(8,128)S(1)} %select_select_fusion), channel_id=1, source_target_pairs={{0,2},{1,3},{2,4},{3,5},{4,6},{5,7},{6,0},{7,1},{8,10},{9,11},{10,... | collective-permute-start | bytes 319496 | tf_op jit(solution)/shard_map/ppermute | solution.py:554
  6.1 5.9 %collective-permute-start.2 = (f32[208,128]{1,0:T(8,128)S(1)}, f32[208,128]{1,0:T(8,128)S(1)}, u32[]{:S(2)}, u32[]{:S(2)}) collective-permute-start(f32[208,128]{1,0:T(8,128)S(1)} %select_select_fusion), channel_id=1, source_target_pairs={{0,6},{1,7},{2,0},{3,1},{4,2},{5,3},{6,4},{7,5},{8,14},{9,15},{10,... | collective-permute-start | bytes 319496 | tf_op jit(solution)/shard_map/ppermute | solution.py:554
  6.1 1.2 %copy-start = (f32[18,3,32,128]{3,2,1,0:T(8,128)S(1)}, f32[18,3,32,128]{3,2,1,0:T(8,128)}, u32[]{:S(2)}) copy-start(f32[18,3,32,128]{3,2,1,0:T(8,128)} %mass.2) | copy-start | bytes 2654212
  12.1 6.3 %collective-permute-start.5 = (f32[208,128]{1,0:T(8,128)S(1)}, f32[208,128]{1,0:T(8,128)S(1)}, u32[]{:S(2)}, u32[]{:S(2)}) collective-permute-start(f32[208,128]{1,0:T(8,128)S(1)} %add_add_fusion), channel_id=1, source_target_pairs={{0,8},{1,9},{2,10},{3,11},{4,12},{5,13},{6,14},{7,15},{8,0},{9,1},... | collective-permute-start | bytes 319496 | tf_op jit(solution)/shard_map/ppermute | solution.py:549
  15.2 8.1 %collective-permute-start.7 = (f32[16,128]{1,0:T(8,128)S(1)}, f32[16,128]{1,0:T(8,128)S(1)}, u32[]{:S(2)}, u32[]{:S(2)}) collective-permute-start(f32[16,128]{1,0:T(8,128)S(1)} %slice.9), channel_id=1, source_target_pairs={{0,24},{1,25},{2,26},{3,27},{4,28},{5,29},{6,30},{7,31},{8,16},{9,... | collective-permute-start | bytes 24584 | tf_op jit(solution)/shard_map/ppermute | solution.py:570
  16.4 12.6 %collective-permute-start.4 = (f32[112,128]{1,0:T(8,128)S(1)}, f32[112,128]{1,0:T(8,128)S(1)}, u32[]{:S(2)}, u32[]{:S(2)}) collective-permute-start(f32[112,128]{1,0:T(8,128)S(1)} %pad_maximum_fusion), channel_id=1, source_target_pairs={{0,16},{16,32},{32,48},{48,64},{64,80},{80,96},{96,112},{112,128},... | collective-permute-start | bytes 172040 | tf_op jit(solution)/shard_map/ppermute | solution.py:544
  18.4 4.8 %collective-permute-start.6 = (f32[192,128]{1,0:T(8,128)S(1)}, f32[192,128]{1,0:T(8,128)S(1)}, u32[]{:S(2)}, u32[]{:S(2)}) collective-permute-start(f32[192,128]{1,0:T(8,128)S(1)} %slice.12.mine), channel_id=1, source_target_pairs={{0,1},{1,0},{2,3},{3,2},{4,5},{5,4},{6,7},{7,6},{8,9},{9,8},{10,11... | collective-permute-start | bytes 294920 | tf_op jit(solution)/shard_map/ppermute | solution.py:549
  26.3 4.3 %collective-permute-start.8 = (f32[112,128]{1,0:T(8,128)S(1)}, f32[112,128]{1,0:T(8,128)S(1)}, u32[]{:S(2)}, u32[]{:S(2)}) collective-permute-start(f32[112,128]{1,0:T(8,128)S(1)} %pad_maximum_fusion.1), channel_id=1, source_target_pairs={{0,240},{16,0},{32,16},{48,32},{64,48},{80,64},{96,80},{112,96},{1... | collective-permute-start | bytes 172040 | tf_op jit(solution)/shard_map/ppermute | solution.py:544

commit v10 on v8

--- a/solution.py
+++ b/solution.py
@@ -144,7 +144,8 @@
     levels, count, width = thick.shape[1:]
     lane = lane_index((count, width))
     row = row_index((count, width))
-    edge_rows = jnp.zeros((count, width), jnp.float32)
+    half_lane = lane_index((count // 2, width))
+    folded = jnp.zeros((count // 2, width), jnp.float32)
     for l in range(levels):
         east_mass = fe[0, l]
         north_mass = jnp.where(row == 0, 0.0, fn[0, l])
@@ -160,12 +161,14 @@
             start = (k * levels + l) * count
             keep[start : start + count, :] = jnp.where(core == 0, first[k], second[k])
             send[start : start + count, :] = jnp.where(core == 0, second[k], first[k])
-        edges = jnp.where(lane < SEG, lanes(cn[0, l], EDGE), 0.0)
-        for k, value in enumerate((ce[0, l], whole, east_mass)):
-            edges = jnp.where(lane == SEG + k, lanes(value, SEG + k), edges)
-        edge_rows = edge_rows + lanes(jnp.where(lane < MET_SEG, edges, 0.0), MET_SEG * l)
+        for part, start in enumerate((MET_SEG * l, MET_SEG * (levels + l))):
+            here = slice(part * count // 2, (part + 1) * count // 2)
+            inside = (half_lane >= start) & (half_lane < start + SEG)
+            folded = jnp.where(inside, lanes(cn[0, l, here, :], start + EDGE), folded)
+            for k, value in enumerate((ce[0, l, here, :], whole[here], east_mass[here])):
+                at = start + SEG + k
+                folded = jnp.where(half_lane == at, lanes(value, at), folded)
     base = 2 * levels * count
-    folded = edge_rows[: count // 2] + lanes(edge_rows[count // 2 :], MET_SEG * levels)
     keep[base:, :] = folded
     send[base:, :] = folded
 
@@ -560,7 +563,7 @@
     me, chosen = position(), owner[0]
     other_core = exchange(send, 1)
     total = jnp.where(chosen == me, keep, jnp.where(chosen == me ^ 1, other_core, 0.0))
-    total = total + (turn(total, 1) + turn(total, -1) + turn(total, 2))
+    total = total + turn(total, 2) + turn(total, -1) + turn(total, 1)
     total, last, first = lax.optimization_barrier((total, last, first))
     total = total + exchange(total, 8)
     padded, shifted = copies(mass)

time: 32.8 us -> 33.3 us (1.015)
  starting transfers between devices: 11.9 us -> 13.8 us
  waiting for transfers between devices: 8.78 us -> 7.49 us
    ppermute x3, starting transfers between devices: 5.81 us -> 8.86 us  [exchange(): return lax.ppermute(x, 'tracer', [(i, i ^ flip) for i in range(size)])]
    ppermute x3, waiting for transfers between devices: 4.84 us -> 3.17 us  [exchange(): return lax.ppermute(x, 'tracer', [(i, i ^ flip) for i in range(size)])]
    ppermute x3, starting transfers between devices: 3.94 us -> 2.75 us  [turn(): lax.ppermute(x, 'tracer', [(i, i // 8 * 8 + (i + 2 * by) % 8) for i in ra...]
    ppermute x3, waiting for transfers between devices: 2.86 us -> 3.24 us  [turn(): lax.ppermute(x, 'tracer', [(i, i // 8 * 8 + (i + 2 * by) % 8) for i in ra...]
  transfers between devices with their start and end apart: 8 -> 8, of which waited for: 5 -> 7; matrix products, arithmetic and copies ran while one was open for 0% -> 0% of each run, Pallas kernels for 19% -> 19%
where the time goes in v10:
time: 33.3 us; the launch traced here: 33.1 us
  starting transfers between devices  13.8 us (41%)
  Pallas kernels  9.84 us (30%)
  waiting for transfers between devices  7.49 us (22%)
  local copies, waits for them, and re-layouts  1.18 us (4%)
  between operations  0.75 us (2%)
    ppermute x3, starting transfers between devices, exchange(): return lax.ppermute(x, 'tracer', [(i, i ^ flip) for i in range(size)])  8.86 us
    pallas_call x2, Pallas kernels, inner_update(): pl.pallas_call(functools.partial(inner_kernel, span), out_shape=(pltpu.VM...  4.67 us
    ppermute x3, waiting for transfers between devices, turn(): lax.ppermute(x, 'tracer', [(i, i // 8 * 8 + (i + 2 * by) % 8) for i in ra...  3.24 us
    ppermute x3, waiting for transfers between devices, exchange(): return lax.ppermute(x, 'tracer', [(i, i ^ flip) for i in range(size)])  3.17 us
    ppermute x3, starting transfers between devices, turn(): lax.ppermute(x, 'tracer', [(i, i // 8 * 8 + (i + 2 * by) % 8) for i in ra...  2.75 us
    pallas_call x1, Pallas kernels, edge_update(): pl.pallas_call(edge_kernel, out_shape=jax.ShapeDtypeStruct(sums.shape, jn...  2.55 us
    ppermute x2, starting transfers between devices, along(): return lax.ppermute(x, 'space', pairs)  2.16 us
    pallas_call x2, Pallas kernels, in_vmem(): pl.pallas_call(kernel, out_shape=tuple((pltpu.VMEM(shape, jnp.float32) fo...  1.52 us
  transfers between devices with their start and end apart: 8, of which 7 were waited for; matrix products, arithmetic and copies ran while one was open for 0% of the time, Pallas kernels for 19%

profile of v10, /device:TPU:1, one launch (start us, length us, event | category | flops | bytes accessed | tf_op | source)
XLA Modules:
  0.0 33.1 jit_solution(563015194515571661)
XLA Ops:
  0.0 1.1 %prepare.1 = (f32[208,128]{1,0:T(8,128)S(1)}, f32[208,128]{1,0:T(8,128)S(1)}) custom-call(f32[1,3,32,128]{3,2,1,0:T(8,128)} %refs_0_.1, f32[1,3,32,128]{3,2,1,0:T(8,128)} %refs_1_.1, f32[1,3,32,128]{3,2,1,0:T(8,128)} %refs_2_.1, f32[1,3,32,128]{3,2,1,0:T(8,128)} %refs_3_.1, f32[1,3,32,128]{3,2,1,0:T(8,128)} %refs_4_.1, s32[1,3,32,128]{3,2,1,0:T(8,128)} %refs_5_.1), custom_call_target="tpu_custom_call" | custom-call | tf_op jit(solution)/shard_map/prepare/pallas_call | solution.py:180
  1.1 3.3 %collective-permute-start = (f32[208,128]{1,0:T(8,128)S(1)}, f32[208,128]{1,0:T(8,128)S(1)}, u32[]{:S(2)}, u32[]{:S(2)}) collective-permute-start(f32[208,128]{1,0:T(8,128)S(1)} %get-tuple-element.28), channel_id=1, source_target_pairs={{0,1},{1,0},{2,3},{3,2},{4,5},{5,4},{6,7},{7,6},{8,9},{9,8},{10,11... | collective-permute-start | bytes 319496 | tf_op jit(solution)/shard_map/ppermute | solution.py:552
  5.1 0.3 collective-permute-done
  5.4 0.1 collective-permute-start.3
  5.5 2.7 %collective-permute-start.2 = (f32[208,128]{1,0:T(8,128)S(1)}, f32[208,128]{1,0:T(8,128)S(1)}, u32[]{:S(2)}, u32[]{:S(2)}) collective-permute-start(f32[208,128]{1,0:T(8,128)S(1)} %select_select_fusion), channel_id=1, source_target_pairs={{0,6},{1,7},{2,0},{3,1},{4,2},{5,3},{6,4},{7,5},{8,14},{9,15},{10,... | collective-permute-start | bytes 319496 | tf_op jit(solution)/shard_map/ppermute | solution.py:557
  8.2 0.0 collective-permute-start.1
  8.2 0.0 copy-start
  8.2 1.2 %copy-done = f32[18,3,32,128]{3,2,1,0:T(8,128)S(1)} copy-done((f32[18,3,32,128]{3,2,1,0:T(8,128)S(1)}, f32[18,3,32,128]{3,2,1,0:T(8,128)}, u32[]{:S(2)}) %copy-start) | copy-done | bytes 884760
  9.3 0.6 %pack.1 = (f32[96,128]{1,0:T(8,128)S(1)}, f32[96,128]{1,0:T(8,128)S(1)}) custom-call(f32[18,3,32,128]{3,2,1,0:T(8,128)S(1)} %copy-done), custom_call_target="tpu_custom_call" | custom-call | flops 2000000 | bytes 1000000 | tf_op jit(solution)/shard_map/pack/pallas_call | solution.py:229
  10.0 0.9 %collective-permute-done.3 = f32[208,128]{1,0:T(8,128)S(1)} collective-permute-done((f32[208,128]{1,0:T(8,128)S(1)}, f32[208,128]{1,0:T(8,128)S(1)}, u32[]{:S(2)}, u32[]{:S(2)}) %collective-permute-start.3) | collective-permute-done | bytes 106528 | tf_op jit(solution)/shard_map/ppermute | solution.py:557
  10.9 1.5 %collective-permute-done.2 = f32[208,128]{1,0:T(8,128)S(1)} collective-permute-done((f32[208,128]{1,0:T(8,128)S(1)}, f32[208,128]{1,0:T(8,128)S(1)}, u32[]{:S(2)}, u32[]{:S(2)}) %collective-permute-start.2) | collective-permute-done | bytes 106528 | tf_op jit(solution)/shard_map/ppermute | solution.py:557
  12.4 0.8 %collective-permute-done.1 = f32[208,128]{1,0:T(8,128)S(1)} collective-permute-done((f32[208,128]{1,0:T(8,128)S(1)}, f32[208,128]{1,0:T(8,128)S(1)}, u32[]{:S(2)}, u32[]{:S(2)}) %collective-permute-start.1) | collective-permute-done | bytes 106528 | tf_op jit(solution)/shard_map/ppermute | solution.py:557
  13.2 2.2 %collective-permute-start.4 = (f32[208,128]{1,0:T(8,128)S(1)}, f32[208,128]{1,0:T(8,128)S(1)}, u32[]{:S(2)}, u32[]{:S(2)}) collective-permute-start(f32[208,128]{1,0:T(8,128)S(1)} %add_add_fusion), channel_id=1, source_target_pairs={{0,8},{1,9},{2,10},{3,11},{4,12},{5,13},{6,14},{7,15},{8,0},{9,1},... | collective-permute-start | bytes 319496 | tf_op jit(solution)/shard_map/ppermute | solution.py:552
  15.5 0.9 %copies.1 = (f32[18,3,48,128]{3,2,1,0:T(8,128)S(1)}, f32[3,18,3,32,128]{4,3,2,1,0:T(8,128)S(1)}) custom-call(f32[18,3,32,128]{3,2,1,0:T(8,128)S(1)} %copy-done), custom_call_target="tpu_custom_call" | custom-call | flops 2000000 | bytes 1000000 | tf_op jit(solution)/shard_map/copies/pallas_call | solution.py:229
  16.4 2.0 %collective-permute-done.4 = f32[208,128]{1,0:T(8,128)S(1)} collective-permute-done((f32[208,128]{1,0:T(8,128)S(1)}, f32[208,128]{1,0:T(8,128)S(1)}, u32[]{:S(2)}, u32[]{:S(2)}) %collective-permute-start.4) | collective-permute-done | bytes 106528 | tf_op jit(solution)/shard_map/ppermute | solution.py:552
  18.4 3.3 %collective-permute-start.6 = (f32[192,128]{1,0:T(8,128)S(1)}, f32[192,128]{1,0:T(8,128)S(1)}, u32[]{:S(2)}, u32[]{:S(2)}) collective-permute-start(f32[192,128]{1,0:T(8,128)S(1)} %slice.9.mine), channel_id=1, source_target_pairs={{0,1},{1,0},{2,3},{3,2},{4,5},{5,4},{6,7},{7,6},{8,9},{9,8},{10,11... | collective-permute-start | bytes 294920 | tf_op jit(solution)/shard_map/ppermute | solution.py:552
  21.8 0.1 collective-permute-start.5
  21.8 0.8 %collective-permute-done.6.other = f32[192,128]{1,0:T(8,128)S(1)} collective-permute-done((f32[192,128]{1,0:T(8,128)S(1)}, f32[192,128]{1,0:T(8,128)S(1)}, u32[]{:S(2)}, u32[]{:S(2)}) %collective-permute-start.6) | collective-permute-done | bytes 98336 | tf_op jit(solution)/shard_map/ppermute | solution.py:552
  22.7 3.0 %inner.2 = (f32[18,3,32,128]{3,2,1,0:T(8,128)S(1)}, f32[11,3,32,128]{3,2,1,0:T(8,128)S(1)}, f32[7,3,32,128]{3,2,1,0:T(8,128)S(1)}, f32[3,32,128]{2,1,0:T(8,128)S(1)}) custom-call(f32[192,128]{1,0:T(8,128)S(1)} %slice.9.mine, f32[192,128]{1,0:T(8,128)S(1)} %collective-permute-done.6.other, f32[18,3,48,128]{3,2,1,0:T(8,128)S(1)} %get-tuple-element.34.padded, ...), custom_call_target="tpu_custom_call" | custom-call | flops 20000000 | bytes 6000000 | tf_op jit(solution)/shard_map/inner/pallas_call | solution.py:413
  25.7 2.1 %collective-permute-start.7 = (f32[112,128]{1,0:T(8,128)S(1)}, f32[112,128]{1,0:T(8,128)S(1)}, u32[]{:S(2)}, u32[]{:S(2)}) collective-permute-start(f32[112,128]{1,0:T(8,128)S(1)} %get-tuple-element.40), channel_id=1, source_target_pairs={{0,240},{16,0},{32,16},{48,32},{64,48},{80,64},{96,80},{112,96},{1... | collective-permute-start | bytes 172040 | tf_op jit(solution)/shard_map/ppermute | solution.py:547
  27.8 1.7 %inner.3 = (f32[18,3,32,128]{3,2,1,0:T(8,128)S(1)}, f32[11,3,32,128]{3,2,1,0:T(8,128)S(1)}, f32[7,3,32,128]{3,2,1,0:T(8,128)S(1)}, f32[3,32,128]{2,1,0:T(8,128)S(1)}) custom-call(f32[192,128]{1,0:T(8,128)S(1)} %slice.9.mine, f32[192,128]{1,0:T(8,128)S(1)} %collective-permute-done.6.other, f32[18,3,48,128]{3,2,1,0:T(8,128)S(1)} %get-tuple-element.34.padded, ...), custom_call_target="tpu_custom_call" | custom-call | flops 20000000 | bytes 6000000 | tf_op jit(solution)/shard_map/inner/pallas_call | solution.py:413
  29.5 0.0 collective-permute-done.5.west
  29.5 1.1 %collective-permute-done.7.east = f32[112,128]{1,0:T(8,128)S(1)} collective-permute-done((f32[112,128]{1,0:T(8,128)S(1)}, f32[112,128]{1,0:T(8,128)S(1)}, u32[]{:S(2)}, u32[]{:S(2)}) %collective-permute-start.7) | collective-permute-done | bytes 57376 | tf_op jit(solution)/shard_map/ppermute | solution.py:547
  30.5 2.5 %edges.1 = f32[18,3,32,128]{3,2,1,0:T(8,128)} custom-call(f32[112,128]{1,0:T(8,128)S(1)} %collective-permute-done.5.west, f32[112,128]{1,0:T(8,128)S(1)} %collective-permute-done.7.east, f32[96,128]{1,0:T(8,128)S(1)} %get-tuple-element.31.own, f32[18,3,32,128]{3,2,1,0:T(8,128)S(1)} %get-tuple-element.41.refs_0_, ...), custom_call_target="tpu_custom_call" | custom-call | tf_op jit(solution)/shard_map/edges/pallas_call | solution.py:531
  (6 shorter events, 0.1 us)
Async XLA Ops:
  1.1 4.3 %collective-permute-start = (f32[208,128]{1,0:T(8,128)S(1)}, f32[208,128]{1,0:T(8,128)S(1)}, u32[]{:S(2)}, u32[]{:S(2)}) collective-permute-start(f32[208,128]{1,0:T(8,128)S(1)} %get-tuple-element.28), channel_id=1, source_target_pairs={{0,1},{1,0},{2,3},{3,2},{4,5},{5,4},{6,7},{7,6},{8,9},{9,8},{10,11... | collective-permute-start | bytes 319496 | tf_op jit(solution)/shard_map/ppermute | solution.py:552
  5.4 5.5 %collective-permute-start.3 = (f32[208,128]{1,0:T(8,128)S(1)}, f32[208,128]{1,0:T(8,128)S(1)}, u32[]{:S(2)}, u32[]{:S(2)}) collective-permute-start(f32[208,128]{1,0:T(8,128)S(1)} %select_select_fusion), channel_id=1, source_target_pairs={{0,2},{1,3},{2,4},{3,5},{4,6},{5,7},{6,0},{7,1},{8,10},{9,11},{10,... | collective-permute-start | bytes 319496 | tf_op jit(solution)/shard_map/ppermute | solution.py:557
  5.5 6.9 %collective-permute-start.2 = (f32[208,128]{1,0:T(8,128)S(1)}, f32[208,128]{1,0:T(8,128)S(1)}, u32[]{:S(2)}, u32[]{:S(2)}) collective-permute-start(f32[208,128]{1,0:T(8,128)S(1)} %select_select_fusion), channel_id=1, source_target_pairs={{0,6},{1,7},{2,0},{3,1},{4,2},{5,3},{6,4},{7,5},{8,14},{9,15},{10,... | collective-permute-start | bytes 319496 | tf_op jit(solution)/shard_map/ppermute | solution.py:557
  8.2 5.1 %collective-permute-start.1 = (f32[208,128]{1,0:T(8,128)S(1)}, f32[208,128]{1,0:T(8,128)S(1)}, u32[]{:S(2)}, u32[]{:S(2)}) collective-permute-start(f32[208,128]{1,0:T(8,128)S(1)} %select_select_fusion), channel_id=1, source_target_pairs={{0,4},{1,5},{2,6},{3,7},{4,0},{5,1},{6,2},{7,3},{8,12},{9,13},{10,... | collective-permute-start | bytes 319496 | tf_op jit(solution)/shard_map/ppermute | solution.py:557
  8.2 1.2 %copy-start = (f32[18,3,32,128]{3,2,1,0:T(8,128)S(1)}, f32[18,3,32,128]{3,2,1,0:T(8,128)}, u32[]{:S(2)}) copy-start(f32[18,3,32,128]{3,2,1,0:T(8,128)} %mass.3) | copy-start | bytes 2654212
  13.2 5.1 %collective-permute-start.4 = (f32[208,128]{1,0:T(8,128)S(1)}, f32[208,128]{1,0:T(8,128)S(1)}, u32[]{:S(2)}, u32[]{:S(2)}) collective-permute-start(f32[208,128]{1,0:T(8,128)S(1)} %add_add_fusion), channel_id=1, source_target_pairs={{0,8},{1,9},{2,10},{3,11},{4,12},{5,13},{6,14},{7,15},{8,0},{9,1},... | collective-permute-start | bytes 319496 | tf_op jit(solution)/shard_map/ppermute | solution.py:552
  18.4 4.2 %collective-permute-start.6 = (f32[192,128]{1,0:T(8,128)S(1)}, f32[192,128]{1,0:T(8,128)S(1)}, u32[]{:S(2)}, u32[]{:S(2)}) collective-permute-start(f32[192,128]{1,0:T(8,128)S(1)} %slice.9.mine), channel_id=1, source_target_pairs={{0,1},{1,0},{2,3},{3,2},{4,5},{5,4},{6,7},{7,6},{8,9},{9,8},{10,11... | collective-permute-start | bytes 294920 | tf_op jit(solution)/shard_map/ppermute | solution.py:552
  21.8 7.7 %collective-permute-start.5 = (f32[112,128]{1,0:T(8,128)S(1)}, f32[112,128]{1,0:T(8,128)S(1)}, u32[]{:S(2)}, u32[]{:S(2)}) collective-permute-start(f32[112,128]{1,0:T(8,128)S(1)} %get-tuple-element.50), channel_id=1, source_target_pairs={{0,16},{16,32},{32,48},{48,64},{64,80},{80,96},{96,112},{112,128},... | collective-permute-start | bytes 172040 | tf_op jit(solution)/shard_map/ppermute | solution.py:547
  25.7 4.8 %collective-permute-start.7 = (f32[112,128]{1,0:T(8,128)S(1)}, f32[112,128]{1,0:T(8,128)S(1)}, u32[]{:S(2)}, u32[]{:S(2)}) collective-permute-start(f32[112,128]{1,0:T(8,128)S(1)} %get-tuple-element.40), channel_id=1, source_target_pairs={{0,240},{16,0},{32,16},{48,32},{64,48},{80,64},{96,80},{112,96},{1... | collective-permute-start | bytes 172040 | tf_op jit(solution)/shard_map/ppermute | solution.py:547

commit v11 on v10

--- a/solution.py
+++ b/solution.py
@@ -125,8 +125,8 @@
     return lax.axis_index("space")
 
 
-def early_levels(levels):
-    return jnp.clip(levels - tile(), 0, levels - 1)
+def early_parts(levels):
+    return jnp.clip(levels + 1 - tile(), 0, levels)
 
 
 def prepare_kernel(*refs):
@@ -278,15 +278,15 @@
 
 
 def inner_kernel(span, mine, other, padded, shifted, *refs):
-    low_level, high_level = span(refs[0].shape[1])
-
-    @pl.when(low_level < high_level)
+    low_part, high_part = span(refs[0].shape[1])
+
+    @pl.when(low_part < high_part)
     def _():
-        inner_body(low_level, high_level, mine, other, padded, shifted, *refs)
+        inner_body(low_part, high_part, mine, other, padded, shifted, *refs)
 
 
 def inner_body(
-    low_level, high_level, mine, other, padded, shifted, sums, outer_c, edge_c, thickness,
+    low_part, high_part, mine, other, padded, shifted, sums, outer_c, edge_c, thickness,
     east_c, north_c, inners, middle, partial,
 ):
     tracers, levels, count, width = sums.shape
@@ -335,8 +335,9 @@
             edge_c[m, l] = value
         return carry
 
-    lax.fori_loop(low_level, high_level, level, 0)
+    lax.fori_loop(low_part // 2, (high_part + 1) // 2, level, 0)
     groups = tracers // GROUP
+    low_step, high_step = low_part * (groups // 2), high_part * (groups // 2)
 
     def block(b):
         return slice(b * BLOCK, (b + 1) * BLOCK)
@@ -401,9 +402,9 @@
         front(step + 1)
         return carry
 
-    front(low_level * groups)
-    lax.fori_loop(low_level * groups, high_level * groups, step_of_three, 0)
-    finish(high_level * groups - 1)
+    front(low_step)
+    lax.fori_loop(low_step, high_step, step_of_three, 0)
+    finish(high_step - 1)
 
 
 def inner_update(span, mine, other, padded, shifted):
@@ -436,7 +437,7 @@
 def edge_kernel(west, east, own, *refs):
     before, after, (out, stage, sems) = refs[:4], refs[4:8], refs[8:]
     tracers, levels, count, width = stage.shape
-    first_levels = early_levels(levels)
+    early = early_parts(levels)
     shape = (count, width)
     lane = lane_index(shape)
     segment, in_segment, packed_lane = segments(shape)
@@ -504,17 +505,21 @@
             for k in range(PACK):
                 t = half * PACK + k
                 moved = jnp.where(at_edge, lanes(total, width - EDGE - SEG * k), 0.0)
-                stage[t, l] = (sums[t, l] + moved) * inverse
+                stage[t, l] = (sums(t, l, half) + moved) * inverse
             copy(l, half).start()
 
+    def sums_after(t, l, half):
+        value = after[0][t, l]
+        return value if half else jnp.where(2 * l < early, before[0][t, l], value)
+
     def either(l, carry):
-        @pl.when(l < first_levels)
+        @pl.when(2 * l + 1 < early)
         def _():
-            level(l, *before)
-
-        @pl.when(l >= first_levels)
+            level(l, lambda t, l, half: before[0][t, l], *before[1:])
+
+        @pl.when(2 * l + 1 >= early)
         def _():
-            level(l, *after)
+            level(l, sums_after, *after[1:])
 
         return carry
 
@@ -563,7 +568,7 @@
     me, chosen = position(), owner[0]
     other_core = exchange(send, 1)
     total = jnp.where(chosen == me, keep, jnp.where(chosen == me ^ 1, other_core, 0.0))
-    total = total + turn(total, 2) + turn(total, -1) + turn(total, 1)
+    total = total + (turn(total, 1) + turn(total, -1) + turn(total, 2))
     total, last, first = lax.optimization_barrier((total, last, first))
     total = total + exchange(total, 8)
     padded, shifted = copies(mass)
@@ -575,10 +580,10 @@
     to_west = jnp.concatenate([first, edges])
     west = along(to_east, [(i, (i + 1) % size) for i in range(size)])
     other = exchange(mine, 1)
-    before = inner_update(lambda levels: (0, early_levels(levels)), mine, other, padded, shifted)
+    before = inner_update(lambda levels: (0, early_parts(levels)), mine, other, padded, shifted)
     to_west, before = lax.optimization_barrier((to_west, before))
     east = along(to_west, [(i, (i - 1) % size) for i in range(size)])
-    after = inner_update(lambda levels: (early_levels(levels), levels), mine, other, padded, shifted)
+    after = inner_update(lambda levels: (early_parts(levels), 2 * levels), mine, other, padded, shifted)
     return edge_update(west, east, last, before, after)
 
 

time: 33.3 us -> 32.4 us (0.973)
  starting transfers between devices: 13.8 us -> 12.5 us
    ppermute x3, starting transfers between devices: 8.86 us -> 5.81 us  [exchange(): return lax.ppermute(x, 'tracer', [(i, i ^ flip) for i in range(size)])]
    ppermute x3, waiting for transfers between devices: 3.17 us -> 4.84 us  [exchange(): return lax.ppermute(x, 'tracer', [(i, i ^ flip) for i in range(size)])]
    ppermute x3, starting transfers between devices: 2.75 us -> 3.94 us  [turn(): lax.ppermute(x, 'tracer', [(i, i // 8 * 8 + (i + 2 * by) % 8) for i in ra...]
    ppermute x2, waiting for transfers between devices: 1.08 us -> 0.01 us  [along(): return lax.ppermute(x, 'space', pairs)]
    ppermute x2, starting transfers between devices: 2.16 us -> 2.71 us  [along(): return lax.ppermute(x, 'space', pairs)]
    ppermute x3, waiting for transfers between devices: 3.24 us -> 2.86 us  [turn(): lax.ppermute(x, 'tracer', [(i, i // 8 * 8 + (i + 2 * by) % 8) for i in ra...]
  transfers between devices with their start and end apart: 8 -> 8, of which waited for: 7 -> 4; matrix products, arithmetic and copies ran while one was open for 0% -> 0% of each run, Pallas kernels for 19% -> 20%
where the time goes in v11:
time: 32.4 us; the launch traced here: 32.2 us
  starting transfers between devices  12.5 us (39%)
  Pallas kernels  10.1 us (31%)
  waiting for transfers between devices  7.7 us (24%)
  local copies, waits for them, and re-layouts  1.18 us (4%)
  between operations  0.75 us (2%)
    ppermute x3, starting transfers between devices, exchange(): return lax.ppermute(x, 'tracer', [(i, i ^ flip) for i in range(size)])  5.81 us
    pallas_call x2, Pallas kernels, inner_update(): pl.pallas_call(functools.partial(inner_kernel, span), out_shape=(pltpu.VM...  4.9 us
    ppermute x3, waiting for transfers between devices, exchange(): return lax.ppermute(x, 'tracer', [(i, i ^ flip) for i in range(size)])  4.84 us
    ppermute x3, starting transfers between devices, turn(): lax.ppermute(x, 'tracer', [(i, i // 8 * 8 + (i + 2 * by) % 8) for i in ra...  3.94 us
    ppermute x3, waiting for transfers between devices, turn(): lax.ppermute(x, 'tracer', [(i, i // 8 * 8 + (i + 2 * by) % 8) for i in ra...  2.86 us
    ppermute x2, starting transfers between devices, along(): return lax.ppermute(x, 'space', pairs)  2.71 us
    pallas_call x1, Pallas kernels, edge_update(): pl.pallas_call(edge_kernel, out_shape=jax.ShapeDtypeStruct(sums.shape, jn...  2.55 us
    pallas_call x2, Pallas kernels, in_vmem(): pl.pallas_call(kernel, out_shape=tuple((pltpu.VMEM(shape, jnp.float32) fo...  1.52 us
  transfers between devices with their start and end apart: 8, of which 4 were waited for; matrix products, arithmetic and copies ran while one was open for 0% of the time, Pallas kernels for 20%

profile of v11, /device:TPU:1, one launch (start us, length us, event | category | flops | bytes accessed | tf_op | source)
XLA Modules:
  0.0 32.2 jit_solution(1419992952202012718)
XLA Ops:
  0.0 1.1 %prepare.1 = (f32[208,128]{1,0:T(8,128)S(1)}, f32[208,128]{1,0:T(8,128)S(1)}) custom-call(f32[1,3,32,128]{3,2,1,0:T(8,128)} %refs_0_.1, f32[1,3,32,128]{3,2,1,0:T(8,128)} %refs_1_.1, f32[1,3,32,128]{3,2,1,0:T(8,128)} %refs_2_.1, f32[1,3,32,128]{3,2,1,0:T(8,128)} %refs_3_.1, f32[1,3,32,128]{3,2,1,0:T(8,128)} %refs_4_.1, s32[1,3,32,128]{3,2,1,0:T(8,128)} %refs_5_.1), custom_call_target="tpu_custom_call" | custom-call | tf_op jit(solution)/shard_map/prepare/pallas_call | solution.py:180
  1.1 3.3 %collective-permute-start = (f32[208,128]{1,0:T(8,128)S(1)}, f32[208,128]{1,0:T(8,128)S(1)}, u32[]{:S(2)}, u32[]{:S(2)}) collective-permute-start(f32[208,128]{1,0:T(8,128)S(1)} %get-tuple-element.28), channel_id=1, source_target_pairs={{0,1},{1,0},{2,3},{3,2},{4,5},{5,4},{6,7},{7,6},{8,9},{9,8},{10,11... | collective-permute-start | bytes 319496 | tf_op jit(solution)/shard_map/ppermute | solution.py:557
  5.1 0.3 collective-permute-done
  5.4 1.3 %collective-permute-start.3 = (f32[208,128]{1,0:T(8,128)S(1)}, f32[208,128]{1,0:T(8,128)S(1)}, u32[]{:S(2)}, u32[]{:S(2)}) collective-permute-start(f32[208,128]{1,0:T(8,128)S(1)} %select_select_fusion), channel_id=1, source_target_pairs={{0,4},{1,5},{2,6},{3,7},{4,0},{5,1},{6,2},{7,3},{8,12},{9,13},{10,... | collective-permute-start | bytes 319496 | tf_op jit(solution)/shard_map/ppermute | solution.py:562
  6.7 0.4 %collective-permute-start.1 = (f32[208,128]{1,0:T(8,128)S(1)}, f32[208,128]{1,0:T(8,128)S(1)}, u32[]{:S(2)}, u32[]{:S(2)}) collective-permute-start(f32[208,128]{1,0:T(8,128)S(1)} %select_select_fusion), channel_id=1, source_target_pairs={{0,2},{1,3},{2,4},{3,5},{4,6},{5,7},{6,0},{7,1},{8,10},{9,11},{10,... | collective-permute-start | bytes 319496 | tf_op jit(solution)/shard_map/ppermute | solution.py:562
  7.1 2.3 %collective-permute-start.2 = (f32[208,128]{1,0:T(8,128)S(1)}, f32[208,128]{1,0:T(8,128)S(1)}, u32[]{:S(2)}, u32[]{:S(2)}) collective-permute-start(f32[208,128]{1,0:T(8,128)S(1)} %select_select_fusion), channel_id=1, source_target_pairs={{0,6},{1,7},{2,0},{3,1},{4,2},{5,3},{6,4},{7,5},{8,14},{9,15},{10,... | collective-permute-start | bytes 319496 | tf_op jit(solution)/shard_map/ppermute | solution.py:562
  9.3 0.0 copy-start
  9.4 1.2 %copy-done = f32[18,3,32,128]{3,2,1,0:T(8,128)S(1)} copy-done((f32[18,3,32,128]{3,2,1,0:T(8,128)S(1)}, f32[18,3,32,128]{3,2,1,0:T(8,128)}, u32[]{:S(2)}) %copy-start) | copy-done | bytes 884760
  10.5 0.6 %pack.1 = (f32[96,128]{1,0:T(8,128)S(1)}, f32[96,128]{1,0:T(8,128)S(1)}) custom-call(f32[18,3,32,128]{3,2,1,0:T(8,128)S(1)} %copy-done), custom_call_target="tpu_custom_call" | custom-call | flops 2000000 | bytes 1000000 | tf_op jit(solution)/shard_map/pack/pallas_call | solution.py:229
  11.2 0.0 collective-permute-done.3
  11.2 2.8 %collective-permute-done.1 = f32[208,128]{1,0:T(8,128)S(1)} collective-permute-done((f32[208,128]{1,0:T(8,128)S(1)}, f32[208,128]{1,0:T(8,128)S(1)}, u32[]{:S(2)}, u32[]{:S(2)}) %collective-permute-start.1) | collective-permute-done | bytes 106528 | tf_op jit(solution)/shard_map/ppermute | solution.py:562
  14.0 0.0 collective-permute-done.2
  14.1 0.9 %collective-permute-start.4 = (f32[208,128]{1,0:T(8,128)S(1)}, f32[208,128]{1,0:T(8,128)S(1)}, u32[]{:S(2)}, u32[]{:S(2)}) collective-permute-start(f32[208,128]{1,0:T(8,128)S(1)} %add_add_fusion), channel_id=1, source_target_pairs={{0,8},{1,9},{2,10},{3,11},{4,12},{5,13},{6,14},{7,15},{8,0},{9,1},... | collective-permute-start | bytes 319496 | tf_op jit(solution)/shard_map/ppermute | solution.py:557
  14.9 0.9 %copies.1 = (f32[18,3,48,128]{3,2,1,0:T(8,128)S(1)}, f32[3,18,3,32,128]{4,3,2,1,0:T(8,128)S(1)}) custom-call(f32[18,3,32,128]{3,2,1,0:T(8,128)S(1)} %copy-done), custom_call_target="tpu_custom_call" | custom-call | flops 2000000 | bytes 1000000 | tf_op jit(solution)/shard_map/copies/pallas_call | solution.py:229
  15.8 3.7 %collective-permute-done.4 = f32[208,128]{1,0:T(8,128)S(1)} collective-permute-done((f32[208,128]{1,0:T(8,128)S(1)}, f32[208,128]{1,0:T(8,128)S(1)}, u32[]{:S(2)}, u32[]{:S(2)}) %collective-permute-start.4) | collective-permute-done | bytes 106528 | tf_op jit(solution)/shard_map/ppermute | solution.py:557
  19.6 1.6 %collective-permute-start.6 = (f32[192,128]{1,0:T(8,128)S(1)}, f32[192,128]{1,0:T(8,128)S(1)}, u32[]{:S(2)}, u32[]{:S(2)}) collective-permute-start(f32[192,128]{1,0:T(8,128)S(1)} %slice.9.mine), channel_id=1, source_target_pairs={{0,1},{1,0},{2,3},{3,2},{4,5},{5,4},{6,7},{7,6},{8,9},{9,8},{10,11... | collective-permute-start | bytes 294920 | tf_op jit(solution)/shard_map/ppermute | solution.py:557
  21.2 0.1 collective-permute-start.5
  21.3 0.8 %collective-permute-done.6.other = f32[192,128]{1,0:T(8,128)S(1)} collective-permute-done((f32[192,128]{1,0:T(8,128)S(1)}, f32[192,128]{1,0:T(8,128)S(1)}, u32[]{:S(2)}, u32[]{:S(2)}) %collective-permute-start.6) | collective-permute-done | bytes 98336 | tf_op jit(solution)/shard_map/ppermute | solution.py:557
  22.1 2.5 %inner.2 = (f32[18,3,32,128]{3,2,1,0:T(8,128)S(1)}, f32[11,3,32,128]{3,2,1,0:T(8,128)S(1)}, f32[7,3,32,128]{3,2,1,0:T(8,128)S(1)}, f32[3,32,128]{2,1,0:T(8,128)S(1)}) custom-call(f32[192,128]{1,0:T(8,128)S(1)} %slice.9.mine, f32[192,128]{1,0:T(8,128)S(1)} %collective-permute-done.6.other, f32[18,3,48,128]{3,2,1,0:T(8,128)S(1)} %get-tuple-element.34.padded, ...), custom_call_target="tpu_custom_call" | custom-call | flops 20000000 | bytes 6000000 | tf_op jit(solution)/shard_map/inner/pallas_call | solution.py:414
  24.6 2.6 %collective-permute-start.7 = (f32[112,128]{1,0:T(8,128)S(1)}, f32[112,128]{1,0:T(8,128)S(1)}, u32[]{:S(2)}, u32[]{:S(2)}) collective-permute-start(f32[112,128]{1,0:T(8,128)S(1)} %get-tuple-element.40), channel_id=1, source_target_pairs={{0,240},{16,0},{32,16},{48,32},{64,48},{80,64},{96,80},{112,96},{1... | collective-permute-start | bytes 172040 | tf_op jit(solution)/shard_map/ppermute | solution.py:552
  27.2 2.5 %inner.3 = (f32[18,3,32,128]{3,2,1,0:T(8,128)S(1)}, f32[11,3,32,128]{3,2,1,0:T(8,128)S(1)}, f32[7,3,32,128]{3,2,1,0:T(8,128)S(1)}, f32[3,32,128]{2,1,0:T(8,128)S(1)}) custom-call(f32[192,128]{1,0:T(8,128)S(1)} %slice.9.mine, f32[192,128]{1,0:T(8,128)S(1)} %collective-permute-done.6.other, f32[18,3,48,128]{3,2,1,0:T(8,128)S(1)} %get-tuple-element.34.padded, ...), custom_call_target="tpu_custom_call" | custom-call | flops 20000000 | bytes 6000000 | tf_op jit(solution)/shard_map/inner/pallas_call | solution.py:414
  29.7 0.0 collective-permute-done.5.west
  29.7 0.0 collective-permute-done.7.east
  29.7 2.6 %edges.1 = f32[18,3,32,128]{3,2,1,0:T(8,128)} custom-call(f32[112,128]{1,0:T(8,128)S(1)} %collective-permute-done.5.west, f32[112,128]{1,0:T(8,128)S(1)} %collective-permute-done.7.east, f32[96,128]{1,0:T(8,128)S(1)} %get-tuple-element.31.own, f32[18,3,32,128]{3,2,1,0:T(8,128)S(1)} %get-tuple-element.41.refs_0_, ...), custom_call_target="tpu_custom_call" | custom-call | tf_op jit(solution)/shard_map/edges/pallas_call | solution.py:536
  (6 shorter events, 0.1 us)
Async XLA Ops:
  1.1 4.3 %collective-permute-start = (f32[208,128]{1,0:T(8,128)S(1)}, f32[208,128]{1,0:T(8,128)S(1)}, u32[]{:S(2)}, u32[]{:S(2)}) collective-permute-start(f32[208,128]{1,0:T(8,128)S(1)} %get-tuple-element.28), channel_id=1, source_target_pairs={{0,1},{1,0},{2,3},{3,2},{4,5},{5,4},{6,7},{7,6},{8,9},{9,8},{10,11... | collective-permute-start | bytes 319496 | tf_op jit(solution)/shard_map/ppermute | solution.py:557
  5.4 5.8 %collective-permute-start.3 = (f32[208,128]{1,0:T(8,128)S(1)}, f32[208,128]{1,0:T(8,128)S(1)}, u32[]{:S(2)}, u32[]{:S(2)}) collective-permute-start(f32[208,128]{1,0:T(8,128)S(1)} %select_select_fusion), channel_id=1, source_target_pairs={{0,4},{1,5},{2,6},{3,7},{4,0},{5,1},{6,2},{7,3},{8,12},{9,13},{10,... | collective-permute-start | bytes 319496 | tf_op jit(solution)/shard_map/ppermute | solution.py:562
  6.7 7.4 %collective-permute-start.1 = (f32[208,128]{1,0:T(8,128)S(1)}, f32[208,128]{1,0:T(8,128)S(1)}, u32[]{:S(2)}, u32[]{:S(2)}) collective-permute-start(f32[208,128]{1,0:T(8,128)S(1)} %select_select_fusion), channel_id=1, source_target_pairs={{0,2},{1,3},{2,4},{3,5},{4,6},{5,7},{6,0},{7,1},{8,10},{9,11},{10,... | collective-permute-start | bytes 319496 | tf_op jit(solution)/shard_map/ppermute | solution.py:562
  7.1 7.0 %collective-permute-start.2 = (f32[208,128]{1,0:T(8,128)S(1)}, f32[208,128]{1,0:T(8,128)S(1)}, u32[]{:S(2)}, u32[]{:S(2)}) collective-permute-start(f32[208,128]{1,0:T(8,128)S(1)} %select_select_fusion), channel_id=1, source_target_pairs={{0,6},{1,7},{2,0},{3,1},{4,2},{5,3},{6,4},{7,5},{8,14},{9,15},{10,... | collective-permute-start | bytes 319496 | tf_op jit(solution)/shard_map/ppermute | solution.py:562
  9.3 1.2 %copy-start = (f32[18,3,32,128]{3,2,1,0:T(8,128)S(1)}, f32[18,3,32,128]{3,2,1,0:T(8,128)}, u32[]{:S(2)}) copy-start(f32[18,3,32,128]{3,2,1,0:T(8,128)} %mass.3) | copy-start | bytes 2654212
  14.1 5.5 %collective-permute-start.4 = (f32[208,128]{1,0:T(8,128)S(1)}, f32[208,128]{1,0:T(8,128)S(1)}, u32[]{:S(2)}, u32[]{:S(2)}) collective-permute-start(f32[208,128]{1,0:T(8,128)S(1)} %add_add_fusion), channel_id=1, source_target_pairs={{0,8},{1,9},{2,10},{3,11},{4,12},{5,13},{6,14},{7,15},{8,0},{9,1},... | collective-permute-start | bytes 319496 | tf_op jit(solution)/shard_map/ppermute | solution.py:557
  19.6 2.5 %collective-permute-start.6 = (f32[192,128]{1,0:T(8,128)S(1)}, f32[192,128]{1,0:T(8,128)S(1)}, u32[]{:S(2)}, u32[]{:S(2)}) collective-permute-start(f32[192,128]{1,0:T(8,128)S(1)} %slice.9.mine), channel_id=1, source_target_pairs={{0,1},{1,0},{2,3},{3,2},{4,5},{5,4},{6,7},{7,6},{8,9},{9,8},{10,11... | collective-permute-start | bytes 294920 | tf_op jit(solution)/shard_map/ppermute | solution.py:557
  21.2 8.5 %collective-permute-start.5 = (f32[112,128]{1,0:T(8,128)S(1)}, f32[112,128]{1,0:T(8,128)S(1)}, u32[]{:S(2)}, u32[]{:S(2)}) collective-permute-start(f32[112,128]{1,0:T(8,128)S(1)} %get-tuple-element.50), channel_id=1, source_target_pairs={{0,16},{16,32},{32,48},{48,64},{64,80},{80,96},{96,112},{112,128},... | collective-permute-start | bytes 172040 | tf_op jit(solution)/shard_map/ppermute | solution.py:552
  24.6 5.1 %collective-permute-start.7 = (f32[112,128]{1,0:T(8,128)S(1)}, f32[112,128]{1,0:T(8,128)S(1)}, u32[]{:S(2)}, u32[]{:S(2)}) collective-permute-start(f32[112,128]{1,0:T(8,128)S(1)} %get-tuple-element.40), channel_id=1, source_target_pairs={{0,240},{16,0},{32,16},{48,32},{64,48},{80,64},{96,80},{112,96},{1... | collective-permute-start | bytes 172040 | tf_op jit(solution)/shard_map/ppermute | solution.py:552

commit v12 on v11

--- a/solution.py
+++ b/solution.py
@@ -568,7 +568,7 @@
     me, chosen = position(), owner[0]
     other_core = exchange(send, 1)
     total = jnp.where(chosen == me, keep, jnp.where(chosen == me ^ 1, other_core, 0.0))
-    total = total + (turn(total, 1) + turn(total, -1) + turn(total, 2))
+    total = total + turn(total, 1) + turn(total, -1) + turn(total, 2)
     total, last, first = lax.optimization_barrier((total, last, first))
     total = total + exchange(total, 8)
     padded, shifted = copies(mass)

time: 32.4 us -> 33.4 us (1.031)
  starting transfers between devices: 12.5 us -> 14.3 us
  waiting for transfers between devices: 7.7 us -> 6.91 us
    ppermute x2, starting transfers between devices: 2.71 us -> 4.39 us  [along(): return lax.ppermute(x, 'space', pairs)]
    ppermute x3, waiting for transfers between devices: 4.84 us -> 3.24 us  [exchange(): return lax.ppermute(x, 'tracer', [(i, i ^ flip) for i in range(size)])]
    ppermute x3, starting transfers between devices: 5.81 us -> 7.13 us  [exchange(): return lax.ppermute(x, 'tracer', [(i, i ^ flip) for i in range(size)])]
    ppermute x3, starting transfers between devices: 3.94 us -> 2.73 us  [turn(): lax.ppermute(x, 'tracer', [(i, i // 8 * 8 + (i + 2 * by) % 8) for i in ra...]
    ppermute x3, waiting for transfers between devices: 2.86 us -> 3.66 us  [turn(): lax.ppermute(x, 'tracer', [(i, i // 8 * 8 + (i + 2 * by) % 8) for i in ra...]
  transfers between devices with their start and end apart: 8 -> 8, of which waited for: 4 -> 6; matrix products, arithmetic and copies ran while one was open for 0% -> 0% of each run, Pallas kernels for 20% -> 19%
where the time goes in v12:
time: 33.4 us; the launch traced here: 33.2 us
  starting transfers between devices  14.3 us (43%)
  Pallas kernels  10.1 us (30%)
  waiting for transfers between devices  6.91 us (21%)
  local copies, waits for them, and re-layouts  1.18 us (4%)
  between operations  0.74 us (2%)
    ppermute x3, starting transfers between devices, exchange(): return lax.ppermute(x, 'tracer', [(i, i ^ flip) for i in range(size)])  7.13 us
    pallas_call x2, Pallas kernels, inner_update(): pl.pallas_call(functools.partial(inner_kernel, span), out_shape=(pltpu.VM...  4.9 us
    ppermute x2, starting transfers between devices, along(): return lax.ppermute(x, 'space', pairs)  4.39 us
    ppermute x3, waiting for transfers between devices, turn(): lax.ppermute(x, 'tracer', [(i, i // 8 * 8 + (i + 2 * by) % 8) for i in ra...  3.66 us
    ppermute x3, waiting for transfers between devices, exchange(): return lax.ppermute(x, 'tracer', [(i, i ^ flip) for i in range(size)])  3.24 us
    ppermute x3, starting transfers between devices, turn(): lax.ppermute(x, 'tracer', [(i, i // 8 * 8 + (i + 2 * by) % 8) for i in ra...  2.73 us
    pallas_call x1, Pallas kernels, edge_update(): pl.pallas_call(edge_kernel, out_shape=jax.ShapeDtypeStruct(sums.shape, jn...  2.55 us
    pallas_call x2, Pallas kernels, in_vmem(): pl.pallas_call(kernel, out_shape=tuple((pltpu.VMEM(shape, jnp.float32) fo...  1.52 us
  transfers between devices with their start and end apart: 8, of which 6 were waited for; matrix products, arithmetic and copies ran while one was open for 0% of the time, Pallas kernels for 19%

profile of v12, /device:TPU:1, one launch (start us, length us, event | category | flops | bytes accessed | tf_op | source)
XLA Modules:
  0.0 33.2 jit_solution(5683841977573315601)
XLA Ops:
  0.0 1.1 %prepare.1 = (f32[208,128]{1,0:T(8,128)S(1)}, f32[208,128]{1,0:T(8,128)S(1)}) custom-call(f32[1,3,32,128]{3,2,1,0:T(8,128)} %refs_0_.1, f32[1,3,32,128]{3,2,1,0:T(8,128)} %refs_1_.1, f32[1,3,32,128]{3,2,1,0:T(8,128)} %refs_2_.1, f32[1,3,32,128]{3,2,1,0:T(8,128)} %refs_3_.1, f32[1,3,32,128]{3,2,1,0:T(8,128)} %refs_4_.1, s32[1,3,32,128]{3,2,1,0:T(8,128)} %refs_5_.1), custom_call_target="tpu_custom_call" | custom-call | tf_op jit(solution)/shard_map/prepare/pallas_call | solution.py:180
  1.1 3.3 %collective-permute-start = (f32[208,128]{1,0:T(8,128)S(1)}, f32[208,128]{1,0:T(8,128)S(1)}, u32[]{:S(2)}, u32[]{:S(2)}) collective-permute-start(f32[208,128]{1,0:T(8,128)S(1)} %get-tuple-element.28), channel_id=1, source_target_pairs={{0,1},{1,0},{2,3},{3,2},{4,5},{5,4},{6,7},{7,6},{8,9},{9,8},{10,11... | collective-permute-start | bytes 319496 | tf_op jit(solution)/shard_map/ppermute | solution.py:557
  5.1 0.3 collective-permute-done
  5.4 1.3 %collective-permute-start.3 = (f32[208,128]{1,0:T(8,128)S(1)}, f32[208,128]{1,0:T(8,128)S(1)}, u32[]{:S(2)}, u32[]{:S(2)}) collective-permute-start(f32[208,128]{1,0:T(8,128)S(1)} %select_select_fusion), channel_id=1, source_target_pairs={{0,4},{1,5},{2,6},{3,7},{4,0},{5,1},{6,2},{7,3},{8,12},{9,13},{10,... | collective-permute-start | bytes 319496 | tf_op jit(solution)/shard_map/ppermute | solution.py:562
  6.7 0.8 %collective-permute-start.2 = (f32[208,128]{1,0:T(8,128)S(1)}, f32[208,128]{1,0:T(8,128)S(1)}, u32[]{:S(2)}, u32[]{:S(2)}) collective-permute-start(f32[208,128]{1,0:T(8,128)S(1)} %select_select_fusion), channel_id=1, source_target_pairs={{0,6},{1,7},{2,0},{3,1},{4,2},{5,3},{6,4},{7,5},{8,14},{9,15},{10,... | collective-permute-start | bytes 319496 | tf_op jit(solution)/shard_map/ppermute | solution.py:562
  7.4 0.7 %collective-permute-start.1 = (f32[208,128]{1,0:T(8,128)S(1)}, f32[208,128]{1,0:T(8,128)S(1)}, u32[]{:S(2)}, u32[]{:S(2)}) collective-permute-start(f32[208,128]{1,0:T(8,128)S(1)} %select_select_fusion), channel_id=1, source_target_pairs={{0,2},{1,3},{2,4},{3,5},{4,6},{5,7},{6,0},{7,1},{8,10},{9,11},{10,... | collective-permute-start | bytes 319496 | tf_op jit(solution)/shard_map/ppermute | solution.py:562
  8.1 0.0 copy-start
  8.1 1.2 %copy-done = f32[18,3,32,128]{3,2,1,0:T(8,128)S(1)} copy-done((f32[18,3,32,128]{3,2,1,0:T(8,128)S(1)}, f32[18,3,32,128]{3,2,1,0:T(8,128)}, u32[]{:S(2)}) %copy-start) | copy-done | bytes 884760
  9.3 0.6 %pack.1 = (f32[96,128]{1,0:T(8,128)S(1)}, f32[96,128]{1,0:T(8,128)S(1)}) custom-call(f32[18,3,32,128]{3,2,1,0:T(8,128)S(1)} %copy-done), custom_call_target="tpu_custom_call" | custom-call | flops 2000000 | bytes 1000000 | tf_op jit(solution)/shard_map/pack/pallas_call | solution.py:229
  10.0 1.2 %collective-permute-done.3 = f32[208,128]{1,0:T(8,128)S(1)} collective-permute-done((f32[208,128]{1,0:T(8,128)S(1)}, f32[208,128]{1,0:T(8,128)S(1)}, u32[]{:S(2)}, u32[]{:S(2)}) %collective-permute-start.3) | collective-permute-done | bytes 106528 | tf_op jit(solution)/shard_map/ppermute | solution.py:562
  11.2 0.9 %collective-permute-done.2 = f32[208,128]{1,0:T(8,128)S(1)} collective-permute-done((f32[208,128]{1,0:T(8,128)S(1)}, f32[208,128]{1,0:T(8,128)S(1)}, u32[]{:S(2)}, u32[]{:S(2)}) %collective-permute-start.2) | collective-permute-done | bytes 106528 | tf_op jit(solution)/shard_map/ppermute | solution.py:562
  12.1 1.5 %collective-permute-done.1 = f32[208,128]{1,0:T(8,128)S(1)} collective-permute-done((f32[208,128]{1,0:T(8,128)S(1)}, f32[208,128]{1,0:T(8,128)S(1)}, u32[]{:S(2)}, u32[]{:S(2)}) %collective-permute-start.1) | collective-permute-done | bytes 106528 | tf_op jit(solution)/shard_map/ppermute | solution.py:562
  13.6 1.4 %collective-permute-start.4 = (f32[208,128]{1,0:T(8,128)S(1)}, f32[208,128]{1,0:T(8,128)S(1)}, u32[]{:S(2)}, u32[]{:S(2)}) collective-permute-start(f32[208,128]{1,0:T(8,128)S(1)} %add_add_fusion), channel_id=1, source_target_pairs={{0,8},{1,9},{2,10},{3,11},{4,12},{5,13},{6,14},{7,15},{8,0},{9,1},... | collective-permute-start | bytes 319496 | tf_op jit(solution)/shard_map/ppermute | solution.py:557
  15.1 0.9 %copies.1 = (f32[18,3,48,128]{3,2,1,0:T(8,128)S(1)}, f32[3,18,3,32,128]{4,3,2,1,0:T(8,128)S(1)}) custom-call(f32[18,3,32,128]{3,2,1,0:T(8,128)S(1)} %copy-done), custom_call_target="tpu_custom_call" | custom-call | flops 2000000 | bytes 1000000 | tf_op jit(solution)/shard_map/copies/pallas_call | solution.py:229
  16.0 2.8 %collective-permute-done.4 = f32[208,128]{1,0:T(8,128)S(1)} collective-permute-done((f32[208,128]{1,0:T(8,128)S(1)}, f32[208,128]{1,0:T(8,128)S(1)}, u32[]{:S(2)}, u32[]{:S(2)}) %collective-permute-start.4) | collective-permute-done | bytes 106528 | tf_op jit(solution)/shard_map/ppermute | solution.py:557
  18.8 2.4 %collective-permute-start.6 = (f32[192,128]{1,0:T(8,128)S(1)}, f32[192,128]{1,0:T(8,128)S(1)}, u32[]{:S(2)}, u32[]{:S(2)}) collective-permute-start(f32[192,128]{1,0:T(8,128)S(1)} %slice.9.mine), channel_id=1, source_target_pairs={{0,1},{1,0},{2,3},{3,2},{4,5},{5,4},{6,7},{7,6},{8,9},{9,8},{10,11... | collective-permute-start | bytes 294920 | tf_op jit(solution)/shard_map/ppermute | solution.py:557
  21.2 0.8 %collective-permute-start.5 = (f32[112,128]{1,0:T(8,128)S(1)}, f32[112,128]{1,0:T(8,128)S(1)}, u32[]{:S(2)}, u32[]{:S(2)}) collective-permute-start(f32[112,128]{1,0:T(8,128)S(1)} %get-tuple-element.50), channel_id=1, source_target_pairs={{0,16},{16,32},{32,48},{48,64},{64,80},{80,96},{96,112},{112,128},... | collective-permute-start | bytes 172040 | tf_op jit(solution)/shard_map/ppermute | solution.py:552
  22.0 0.1 collective-permute-done.6.other
  22.2 2.5 %inner.2 = (f32[18,3,32,128]{3,2,1,0:T(8,128)S(1)}, f32[11,3,32,128]{3,2,1,0:T(8,128)S(1)}, f32[7,3,32,128]{3,2,1,0:T(8,128)S(1)}, f32[3,32,128]{2,1,0:T(8,128)S(1)}) custom-call(f32[192,128]{1,0:T(8,128)S(1)} %slice.9.mine, f32[192,128]{1,0:T(8,128)S(1)} %collective-permute-done.6.other, f32[18,3,48,128]{3,2,1,0:T(8,128)S(1)} %get-tuple-element.34.padded, ...), custom_call_target="tpu_custom_call" | custom-call | flops 20000000 | bytes 6000000 | tf_op jit(solution)/shard_map/inner/pallas_call | solution.py:414
  24.6 3.6 %collective-permute-start.7 = (f32[112,128]{1,0:T(8,128)S(1)}, f32[112,128]{1,0:T(8,128)S(1)}, u32[]{:S(2)}, u32[]{:S(2)}) collective-permute-start(f32[112,128]{1,0:T(8,128)S(1)} %get-tuple-element.40), channel_id=1, source_target_pairs={{0,240},{16,0},{32,16},{48,32},{64,48},{80,64},{96,80},{112,96},{1... | collective-permute-start | bytes 172040 | tf_op jit(solution)/shard_map/ppermute | solution.py:552
  28.2 2.5 %inner.3 = (f32[18,3,32,128]{3,2,1,0:T(8,128)S(1)}, f32[11,3,32,128]{3,2,1,0:T(8,128)S(1)}, f32[7,3,32,128]{3,2,1,0:T(8,128)S(1)}, f32[3,32,128]{2,1,0:T(8,128)S(1)}) custom-call(f32[192,128]{1,0:T(8,128)S(1)} %slice.9.mine, f32[192,128]{1,0:T(8,128)S(1)} %collective-permute-done.6.other, f32[18,3,48,128]{3,2,1,0:T(8,128)S(1)} %get-tuple-element.34.padded, ...), custom_call_target="tpu_custom_call" | custom-call | flops 20000000 | bytes 6000000 | tf_op jit(solution)/shard_map/inner/pallas_call | solution.py:414
  30.6 0.0 collective-permute-done.5.west
  30.7 0.0 collective-permute-done.7.east
  30.7 2.6 %edges.1 = f32[18,3,32,128]{3,2,1,0:T(8,128)} custom-call(f32[112,128]{1,0:T(8,128)S(1)} %collective-permute-done.5.west, f32[112,128]{1,0:T(8,128)S(1)} %collective-permute-done.7.east, f32[96,128]{1,0:T(8,128)S(1)} %get-tuple-element.31.own, f32[18,3,32,128]{3,2,1,0:T(8,128)S(1)} %get-tuple-element.41.refs_0_, ...), custom_call_target="tpu_custom_call" | custom-call | tf_op jit(solution)/shard_map/edges/pallas_call | solution.py:536
  (6 shorter events, 0.1 us)
Async XLA Ops:
  1.1 4.3 %collective-permute-start = (f32[208,128]{1,0:T(8,128)S(1)}, f32[208,128]{1,0:T(8,128)S(1)}, u32[]{:S(2)}, u32[]{:S(2)}) collective-permute-start(f32[208,128]{1,0:T(8,128)S(1)} %get-tuple-element.28), channel_id=1, source_target_pairs={{0,1},{1,0},{2,3},{3,2},{4,5},{5,4},{6,7},{7,6},{8,9},{9,8},{10,11... | collective-permute-start | bytes 319496 | tf_op jit(solution)/shard_map/ppermute | solution.py:557
  5.4 5.8 %collective-permute-start.3 = (f32[208,128]{1,0:T(8,128)S(1)}, f32[208,128]{1,0:T(8,128)S(1)}, u32[]{:S(2)}, u32[]{:S(2)}) collective-permute-start(f32[208,128]{1,0:T(8,128)S(1)} %select_select_fusion), channel_id=1, source_target_pairs={{0,4},{1,5},{2,6},{3,7},{4,0},{5,1},{6,2},{7,3},{8,12},{9,13},{10,... | collective-permute-start | bytes 319496 | tf_op jit(solution)/shard_map/ppermute | solution.py:562
  6.7 5.4 %collective-permute-start.2 = (f32[208,128]{1,0:T(8,128)S(1)}, f32[208,128]{1,0:T(8,128)S(1)}, u32[]{:S(2)}, u32[]{:S(2)}) collective-permute-start(f32[208,128]{1,0:T(8,128)S(1)} %select_select_fusion), channel_id=1, source_target_pairs={{0,6},{1,7},{2,0},{3,1},{4,2},{5,3},{6,4},{7,5},{8,14},{9,15},{10,... | collective-permute-start | bytes 319496 | tf_op jit(solution)/shard_map/ppermute | solution.py:562
  7.4 6.2 %collective-permute-start.1 = (f32[208,128]{1,0:T(8,128)S(1)}, f32[208,128]{1,0:T(8,128)S(1)}, u32[]{:S(2)}, u32[]{:S(2)}) collective-permute-start(f32[208,128]{1,0:T(8,128)S(1)} %select_select_fusion), channel_id=1, source_target_pairs={{0,2},{1,3},{2,4},{3,5},{4,6},{5,7},{6,0},{7,1},{8,10},{9,11},{10,... | collective-permute-start | bytes 319496 | tf_op jit(solution)/shard_map/ppermute | solution.py:562
  8.1 1.2 %copy-start = (f32[18,3,32,128]{3,2,1,0:T(8,128)S(1)}, f32[18,3,32,128]{3,2,1,0:T(8,128)}, u32[]{:S(2)}) copy-start(f32[18,3,32,128]{3,2,1,0:T(8,128)} %mass.3) | copy-start | bytes 2654212
  13.6 5.1 %collective-permute-start.4 = (f32[208,128]{1,0:T(8,128)S(1)}, f32[208,128]{1,0:T(8,128)S(1)}, u32[]{:S(2)}, u32[]{:S(2)}) collective-permute-start(f32[208,128]{1,0:T(8,128)S(1)} %add_add_fusion), channel_id=1, source_target_pairs={{0,8},{1,9},{2,10},{3,11},{4,12},{5,13},{6,14},{7,15},{8,0},{9,1},... | collective-permute-start | bytes 319496 | tf_op jit(solution)/shard_map/ppermute | solution.py:557
  18.8 3.3 %collective-permute-start.6 = (f32[192,128]{1,0:T(8,128)S(1)}, f32[192,128]{1,0:T(8,128)S(1)}, u32[]{:S(2)}, u32[]{:S(2)}) collective-permute-start(f32[192,128]{1,0:T(8,128)S(1)} %slice.9.mine), channel_id=1, source_target_pairs={{0,1},{1,0},{2,3},{3,2},{4,5},{5,4},{6,7},{7,6},{8,9},{9,8},{10,11... | collective-permute-start | bytes 294920 | tf_op jit(solution)/shard_map/ppermute | solution.py:557
  21.2 9.4 %collective-permute-start.5 = (f32[112,128]{1,0:T(8,128)S(1)}, f32[112,128]{1,0:T(8,128)S(1)}, u32[]{:S(2)}, u32[]{:S(2)}) collective-permute-start(f32[112,128]{1,0:T(8,128)S(1)} %get-tuple-element.50), channel_id=1, source_target_pairs={{0,16},{16,32},{32,48},{48,64},{64,80},{80,96},{96,112},{112,128},... | collective-permute-start | bytes 172040 | tf_op jit(solution)/shard_map/ppermute | solution.py:552
  24.6 6.0 %collective-permute-start.7 = (f32[112,128]{1,0:T(8,128)S(1)}, f32[112,128]{1,0:T(8,128)S(1)}, u32[]{:S(2)}, u32[]{:S(2)}) collective-permute-start(f32[112,128]{1,0:T(8,128)S(1)} %get-tuple-element.40), channel_id=1, source_target_pairs={{0,240},{16,0},{32,16},{48,32},{64,48},{80,64},{96,80},{112,96},{1... | collective-permute-start | bytes 172040 | tf_op jit(solution)/shard_map/ppermute | solution.py:552

commit v13 on v12

--- a/solution.py
+++ b/solution.py
@@ -568,9 +568,9 @@
     me, chosen = position(), owner[0]
     other_core = exchange(send, 1)
     total = jnp.where(chosen == me, keep, jnp.where(chosen == me ^ 1, other_core, 0.0))
-    total = total + turn(total, 1) + turn(total, -1) + turn(total, 2)
+    total = total + exchange(total, 8)
     total, last, first = lax.optimization_barrier((total, last, first))
-    total = total + exchange(total, 8)
+    total = total + (turn(total, 1) + turn(total, -1) + turn(total, 2))
     padded, shifted = copies(mass)
     main = 2 * mass.shape[1] * mass.shape[2]
     mine = total[:main]

time: 33.4 us -> 32.7 us (0.979)
  waiting for transfers between devices: 6.91 us -> 5.75 us
  starting transfers between devices: 14.3 us -> 14.7 us
    ppermute x3, waiting for transfers between devices: 3.66 us -> 2.32 us  [turn(): lax.ppermute(x, 'tracer', [(i, i // 8 * 8 + (i + 2 * by) % 8) for i in ra...]
    ppermute x3, starting transfers between devices: 2.73 us -> 3.94 us  [turn(): lax.ppermute(x, 'tracer', [(i, i // 8 * 8 + (i + 2 * by) % 8) for i in ra...]
    ppermute x3, starting transfers between devices: 7.13 us -> 6.62 us  [exchange(): return lax.ppermute(x, 'tracer', [(i, i ^ flip) for i in range(size)])]
  transfers between devices with their start and end apart: 8 -> 8, of which waited for: 6 -> 5; matrix products, arithmetic and copies ran while one was open for 0% -> 0% of each run, Pallas kernels for 19% -> 20%
where the time goes in v13:
time: 32.7 us; the launch traced here: 32.5 us
  starting transfers between devices  14.7 us (45%)
  Pallas kernels  10.1 us (31%)
  waiting for transfers between devices  5.75 us (18%)
  local copies, waits for them, and re-layouts  1.18 us (4%)
  between operations  0.74 us (2%)
    ppermute x3, starting transfers between devices, exchange(): return lax.ppermute(x, 'tracer', [(i, i ^ flip) for i in range(size)])  6.62 us
    pallas_call x2, Pallas kernels, inner_update(): pl.pallas_call(functools.partial(inner_kernel, span), out_shape=(pltpu.VM...  4.9 us
    ppermute x2, starting transfers between devices, along(): return lax.ppermute(x, 'space', pairs)  4.12 us
    ppermute x3, starting transfers between devices, turn(): lax.ppermute(x, 'tracer', [(i, i // 8 * 8 + (i + 2 * by) % 8) for i in ra...  3.94 us
    ppermute x3, waiting for transfers between devices, exchange(): return lax.ppermute(x, 'tracer', [(i, i ^ flip) for i in range(size)])  3.43 us
    pallas_call x1, Pallas kernels, edge_update(): pl.pallas_call(edge_kernel, out_shape=jax.ShapeDtypeStruct(sums.shape, jn...  2.55 us
    ppermute x3, waiting for transfers between devices, turn(): lax.ppermute(x, 'tracer', [(i, i // 8 * 8 + (i + 2 * by) % 8) for i in ra...  2.32 us
    pallas_call x2, Pallas kernels, in_vmem(): pl.pallas_call(kernel, out_shape=tuple((pltpu.VMEM(shape, jnp.float32) fo...  1.52 us
  transfers between devices with their start and end apart: 8, of which 5 were waited for; matrix products, arithmetic and copies ran while one was open for 0% of the time, Pallas kernels for 20%

profile of v13, /device:TPU:1, one launch (start us, length us, event | category | flops | bytes accessed | tf_op | source)
XLA Modules:
  0.0 32.5 jit_solution(14804128264510790626)
XLA Ops:
  0.0 1.1 %prepare.1 = (f32[208,128]{1,0:T(8,128)S(1)}, f32[208,128]{1,0:T(8,128)S(1)}) custom-call(f32[1,3,32,128]{3,2,1,0:T(8,128)} %refs_0_.1, f32[1,3,32,128]{3,2,1,0:T(8,128)} %refs_1_.1, f32[1,3,32,128]{3,2,1,0:T(8,128)} %refs_2_.1, f32[1,3,32,128]{3,2,1,0:T(8,128)} %refs_3_.1, f32[1,3,32,128]{3,2,1,0:T(8,128)} %refs_4_.1, s32[1,3,32,128]{3,2,1,0:T(8,128)} %refs_5_.1), custom_call_target="tpu_custom_call" | custom-call | tf_op jit(solution)/shard_map/prepare/pallas_call | solution.py:180
  1.1 3.3 %collective-permute-start = (f32[208,128]{1,0:T(8,128)S(1)}, f32[208,128]{1,0:T(8,128)S(1)}, u32[]{:S(2)}, u32[]{:S(2)}) collective-permute-start(f32[208,128]{1,0:T(8,128)S(1)} %get-tuple-element.28), channel_id=1, source_target_pairs={{0,1},{1,0},{2,3},{3,2},{4,5},{5,4},{6,7},{7,6},{8,9},{9,8},{10,11... | collective-permute-start | bytes 319496 | tf_op jit(solution)/shard_map/ppermute | solution.py:557
  5.1 0.3 collective-permute-done
  5.4 1.1 %collective-permute-start.1 = (f32[208,128]{1,0:T(8,128)S(1)}, f32[208,128]{1,0:T(8,128)S(1)}, u32[]{:S(2)}, u32[]{:S(2)}) collective-permute-start(f32[208,128]{1,0:T(8,128)S(1)} %select_select_fusion), channel_id=1, source_target_pairs={{0,8},{1,9},{2,10},{3,11},{4,12},{5,13},{6,14},{7,15},{8,0},{9,1},... | collective-permute-start | bytes 319496 | tf_op jit(solution)/shard_map/ppermute | solution.py:557
  6.5 0.0 copy-start
  6.5 1.2 %copy-done = f32[18,3,32,128]{3,2,1,0:T(8,128)S(1)} copy-done((f32[18,3,32,128]{3,2,1,0:T(8,128)S(1)}, f32[18,3,32,128]{3,2,1,0:T(8,128)}, u32[]{:S(2)}) %copy-start) | copy-done | bytes 884760
  7.7 0.6 %pack.1 = (f32[96,128]{1,0:T(8,128)S(1)}, f32[96,128]{1,0:T(8,128)S(1)}) custom-call(f32[18,3,32,128]{3,2,1,0:T(8,128)S(1)} %copy-done), custom_call_target="tpu_custom_call" | custom-call | flops 2000000 | bytes 1000000 | tf_op jit(solution)/shard_map/pack/pallas_call | solution.py:229
  8.3 2.9 %collective-permute-done.1 = f32[208,128]{1,0:T(8,128)S(1)} collective-permute-done((f32[208,128]{1,0:T(8,128)S(1)}, f32[208,128]{1,0:T(8,128)S(1)}, u32[]{:S(2)}, u32[]{:S(2)}) %collective-permute-start.1) | collective-permute-done | bytes 106528 | tf_op jit(solution)/shard_map/ppermute | solution.py:557
  11.2 1.3 %collective-permute-start.4 = (f32[208,128]{1,0:T(8,128)S(1)}, f32[208,128]{1,0:T(8,128)S(1)}, u32[]{:S(2)}, u32[]{:S(2)}) collective-permute-start(f32[208,128]{1,0:T(8,128)S(1)} %add.12), channel_id=1, source_target_pairs={{0,4},{1,5},{2,6},{3,7},{4,0},{5,1},{6,2},{7,3},{8,12},{9,13},{10,... | collective-permute-start | bytes 319496 | tf_op jit(solution)/shard_map/ppermute | solution.py:562
  12.5 0.4 %collective-permute-start.2 = (f32[208,128]{1,0:T(8,128)S(1)}, f32[208,128]{1,0:T(8,128)S(1)}, u32[]{:S(2)}, u32[]{:S(2)}) collective-permute-start(f32[208,128]{1,0:T(8,128)S(1)} %add.12), channel_id=1, source_target_pairs={{0,2},{1,3},{2,4},{3,5},{4,6},{5,7},{6,0},{7,1},{8,10},{9,11},{10,... | collective-permute-start | bytes 319496 | tf_op jit(solution)/shard_map/ppermute | solution.py:562
  12.9 2.3 %collective-permute-start.3 = (f32[208,128]{1,0:T(8,128)S(1)}, f32[208,128]{1,0:T(8,128)S(1)}, u32[]{:S(2)}, u32[]{:S(2)}) collective-permute-start(f32[208,128]{1,0:T(8,128)S(1)} %add.12), channel_id=1, source_target_pairs={{0,6},{1,7},{2,0},{3,1},{4,2},{5,3},{6,4},{7,5},{8,14},{9,15},{10,... | collective-permute-start | bytes 319496 | tf_op jit(solution)/shard_map/ppermute | solution.py:562
  15.2 0.9 %copies.1 = (f32[18,3,48,128]{3,2,1,0:T(8,128)S(1)}, f32[3,18,3,32,128]{4,3,2,1,0:T(8,128)S(1)}) custom-call(f32[18,3,32,128]{3,2,1,0:T(8,128)S(1)} %copy-done), custom_call_target="tpu_custom_call" | custom-call | flops 2000000 | bytes 1000000 | tf_op jit(solution)/shard_map/copies/pallas_call | solution.py:229
  16.0 0.3 %collective-permute-done.4 = f32[208,128]{1,0:T(8,128)S(1)} collective-permute-done((f32[208,128]{1,0:T(8,128)S(1)}, f32[208,128]{1,0:T(8,128)S(1)}, u32[]{:S(2)}, u32[]{:S(2)}) %collective-permute-start.4) | collective-permute-done | bytes 106528 | tf_op jit(solution)/shard_map/ppermute | solution.py:562
  16.4 2.0 %collective-permute-done.2 = f32[208,128]{1,0:T(8,128)S(1)} collective-permute-done((f32[208,128]{1,0:T(8,128)S(1)}, f32[208,128]{1,0:T(8,128)S(1)}, u32[]{:S(2)}, u32[]{:S(2)}) %collective-permute-start.2) | collective-permute-done | bytes 106528 | tf_op jit(solution)/shard_map/ppermute | solution.py:562
  18.4 0.0 collective-permute-done.3
  18.4 2.2 %collective-permute-start.6 = (f32[192,128]{1,0:T(8,128)S(1)}, f32[192,128]{1,0:T(8,128)S(1)}, u32[]{:S(2)}, u32[]{:S(2)}) collective-permute-start(f32[192,128]{1,0:T(8,128)S(1)} %slice.9.mine), channel_id=1, source_target_pairs={{0,1},{1,0},{2,3},{3,2},{4,5},{5,4},{6,7},{7,6},{8,9},{9,8},{10,11... | collective-permute-start | bytes 294920 | tf_op jit(solution)/shard_map/ppermute | solution.py:557
  20.6 0.7 %collective-permute-start.5 = (f32[112,128]{1,0:T(8,128)S(1)}, f32[112,128]{1,0:T(8,128)S(1)}, u32[]{:S(2)}, u32[]{:S(2)}) collective-permute-start(f32[112,128]{1,0:T(8,128)S(1)} %get-tuple-element.50), channel_id=1, source_target_pairs={{0,16},{16,32},{32,48},{48,64},{64,80},{80,96},{96,112},{112,128},... | collective-permute-start | bytes 172040 | tf_op jit(solution)/shard_map/ppermute | solution.py:552
  21.3 0.3 collective-permute-done.6.other
  21.6 2.5 %inner.2 = (f32[18,3,32,128]{3,2,1,0:T(8,128)S(1)}, f32[11,3,32,128]{3,2,1,0:T(8,128)S(1)}, f32[7,3,32,128]{3,2,1,0:T(8,128)S(1)}, f32[3,32,128]{2,1,0:T(8,128)S(1)}) custom-call(f32[192,128]{1,0:T(8,128)S(1)} %slice.9.mine, f32[192,128]{1,0:T(8,128)S(1)} %collective-permute-done.6.other, f32[18,3,48,128]{3,2,1,0:T(8,128)S(1)} %get-tuple-element.34.padded, ...), custom_call_target="tpu_custom_call" | custom-call | flops 20000000 | bytes 6000000 | tf_op jit(solution)/shard_map/inner/pallas_call | solution.py:414
  24.0 3.4 %collective-permute-start.7 = (f32[112,128]{1,0:T(8,128)S(1)}, f32[112,128]{1,0:T(8,128)S(1)}, u32[]{:S(2)}, u32[]{:S(2)}) collective-permute-start(f32[112,128]{1,0:T(8,128)S(1)} %get-tuple-element.40), channel_id=1, source_target_pairs={{0,240},{16,0},{32,16},{48,32},{64,48},{80,64},{96,80},{112,96},{1... | collective-permute-start | bytes 172040 | tf_op jit(solution)/shard_map/ppermute | solution.py:552
  27.5 2.5 %inner.3 = (f32[18,3,32,128]{3,2,1,0:T(8,128)S(1)}, f32[11,3,32,128]{3,2,1,0:T(8,128)S(1)}, f32[7,3,32,128]{3,2,1,0:T(8,128)S(1)}, f32[3,32,128]{2,1,0:T(8,128)S(1)}) custom-call(f32[192,128]{1,0:T(8,128)S(1)} %slice.9.mine, f32[192,128]{1,0:T(8,128)S(1)} %collective-permute-done.6.other, f32[18,3,48,128]{3,2,1,0:T(8,128)S(1)} %get-tuple-element.34.padded, ...), custom_call_target="tpu_custom_call" | custom-call | flops 20000000 | bytes 6000000 | tf_op jit(solution)/shard_map/inner/pallas_call | solution.py:414
  29.9 0.0 collective-permute-done.5.west
  29.9 0.0 collective-permute-done.7.east
  29.9 2.6 %edges.1 = f32[18,3,32,128]{3,2,1,0:T(8,128)} custom-call(f32[112,128]{1,0:T(8,128)S(1)} %collective-permute-done.5.west, f32[112,128]{1,0:T(8,128)S(1)} %collective-permute-done.7.east, f32[96,128]{1,0:T(8,128)S(1)} %get-tuple-element.31.own, f32[18,3,32,128]{3,2,1,0:T(8,128)S(1)} %get-tuple-element.41.refs_0_, ...), custom_call_target="tpu_custom_call" | custom-call | tf_op jit(solution)/shard_map/edges/pallas_call | solution.py:536
  (6 shorter events, 0.1 us)
Async XLA Ops:
  1.1 4.3 %collective-permute-start = (f32[208,128]{1,0:T(8,128)S(1)}, f32[208,128]{1,0:T(8,128)S(1)}, u32[]{:S(2)}, u32[]{:S(2)}) collective-permute-start(f32[208,128]{1,0:T(8,128)S(1)} %get-tuple-element.28), channel_id=1, source_target_pairs={{0,1},{1,0},{2,3},{3,2},{4,5},{5,4},{6,7},{7,6},{8,9},{9,8},{10,11... | collective-permute-start | bytes 319496 | tf_op jit(solution)/shard_map/ppermute | solution.py:557
  5.4 5.8 %collective-permute-start.1 = (f32[208,128]{1,0:T(8,128)S(1)}, f32[208,128]{1,0:T(8,128)S(1)}, u32[]{:S(2)}, u32[]{:S(2)}) collective-permute-start(f32[208,128]{1,0:T(8,128)S(1)} %select_select_fusion), channel_id=1, source_target_pairs={{0,8},{1,9},{2,10},{3,11},{4,12},{5,13},{6,14},{7,15},{8,0},{9,1},... | collective-permute-start | bytes 319496 | tf_op jit(solution)/shard_map/ppermute | solution.py:557
  6.5 1.2 %copy-start = (f32[18,3,32,128]{3,2,1,0:T(8,128)S(1)}, f32[18,3,32,128]{3,2,1,0:T(8,128)}, u32[]{:S(2)}) copy-start(f32[18,3,32,128]{3,2,1,0:T(8,128)} %mass.3) | copy-start | bytes 2654212
  11.2 5.2 %collective-permute-start.4 = (f32[208,128]{1,0:T(8,128)S(1)}, f32[208,128]{1,0:T(8,128)S(1)}, u32[]{:S(2)}, u32[]{:S(2)}) collective-permute-start(f32[208,128]{1,0:T(8,128)S(1)} %add.12), channel_id=1, source_target_pairs={{0,4},{1,5},{2,6},{3,7},{4,0},{5,1},{6,2},{7,3},{8,12},{9,13},{10,... | collective-permute-start | bytes 319496 | tf_op jit(solution)/shard_map/ppermute | solution.py:562
  12.5 5.9 %collective-permute-start.2 = (f32[208,128]{1,0:T(8,128)S(1)}, f32[208,128]{1,0:T(8,128)S(1)}, u32[]{:S(2)}, u32[]{:S(2)}) collective-permute-start(f32[208,128]{1,0:T(8,128)S(1)} %add.12), channel_id=1, source_target_pairs={{0,2},{1,3},{2,4},{3,5},{4,6},{5,7},{6,0},{7,1},{8,10},{9,11},{10,... | collective-permute-start | bytes 319496 | tf_op jit(solution)/shard_map/ppermute | solution.py:562
  12.9 5.5 %collective-permute-start.3 = (f32[208,128]{1,0:T(8,128)S(1)}, f32[208,128]{1,0:T(8,128)S(1)}, u32[]{:S(2)}, u32[]{:S(2)}) collective-permute-start(f32[208,128]{1,0:T(8,128)S(1)} %add.12), channel_id=1, source_target_pairs={{0,6},{1,7},{2,0},{3,1},{4,2},{5,3},{6,4},{7,5},{8,14},{9,15},{10,... | collective-permute-start | bytes 319496 | tf_op jit(solution)/shard_map/ppermute | solution.py:562
  18.4 3.1 %collective-permute-start.6 = (f32[192,128]{1,0:T(8,128)S(1)}, f32[192,128]{1,0:T(8,128)S(1)}, u32[]{:S(2)}, u32[]{:S(2)}) collective-permute-start(f32[192,128]{1,0:T(8,128)S(1)} %slice.9.mine), channel_id=1, source_target_pairs={{0,1},{1,0},{2,3},{3,2},{4,5},{5,4},{6,7},{7,6},{8,9},{9,8},{10,11... | collective-permute-start | bytes 294920 | tf_op jit(solution)/shard_map/ppermute | solution.py:557
  20.6 9.3 %collective-permute-start.5 = (f32[112,128]{1,0:T(8,128)S(1)}, f32[112,128]{1,0:T(8,128)S(1)}, u32[]{:S(2)}, u32[]{:S(2)}) collective-permute-start(f32[112,128]{1,0:T(8,128)S(1)} %get-tuple-element.50), channel_id=1, source_target_pairs={{0,16},{16,32},{32,48},{48,64},{64,80},{80,96},{96,112},{112,128},... | collective-permute-start | bytes 172040 | tf_op jit(solution)/shard_map/ppermute | solution.py:552
  24.0 5.9 %collective-permute-start.7 = (f32[112,128]{1,0:T(8,128)S(1)}, f32[112,128]{1,0:T(8,128)S(1)}, u32[]{:S(2)}, u32[]{:S(2)}) collective-permute-start(f32[112,128]{1,0:T(8,128)S(1)} %get-tuple-element.40), channel_id=1, source_target_pairs={{0,240},{16,0},{32,16},{48,32},{64,48},{80,64},{96,80},{112,96},{1... | collective-permute-start | bytes 172040 | tf_op jit(solution)/shard_map/ppermute | solution.py:552

commit v14 on v11

--- a/solution.py
+++ b/solution.py
@@ -188,9 +188,10 @@
     )(thick, fe, fn, ce, cn, ne)
 
 
-def pack_kernel(mass, last, first):
+def pack_kernel(mass, last, first, own):
     tracers, levels, count, width = mass.shape
     lane = lane_index((count, width))
+    segment, in_segment, packed_lane = segments((count, width))
 
     def level(l, carry):
         a = jnp.zeros((count, width), jnp.float32)
@@ -202,6 +203,12 @@
         place = pl.ds(pl.multiple_of(l * count, count), count)
         last[place, :] = a
         first[place, :] = b
+        for half in range(tracers // PACK):
+            index = EDGE * (segment + PACK * half) + in_segment
+            cells = pick(a, jnp.where(packed_lane & (in_segment < EDGE), index, 0))
+            own[half, 0, l] = cells
+            for k, shift in enumerate(NEAR):
+                own[half, k + 1, l] = lanes(cells, -shift)
         return carry
 
     lax.fori_loop(0, levels, level, 0)
@@ -238,8 +245,9 @@
 
 
 def pack(mass):
-    _, levels, count, width = mass.shape
-    return in_vmem(pack_kernel, "pack", ((levels * count, width),) * 2, mass)
+    tracers, levels, count, width = mass.shape
+    own = (tracers // PACK, 1 + len(NEAR), levels, count, width)
+    return in_vmem(pack_kernel, "pack", ((levels * count, width),) * 2 + (own,), mass)
 
 
 def copies(mass):
@@ -483,7 +491,8 @@
             first_lane = EDGE * (segment + PACK * half) + in_segment
             west_index = jnp.where(packed_lane & from_west_lane, first_lane, 0)
             east_index = jnp.where(packed_lane & ~from_west_lane, first_lane - EDGE, 0)
-            own_cells = pick(own[level_rows, :], west_index)
+            own_cells = own[half, 0, l]
+            own_near = {0: own_cells, **{shift: own[half, k + 1, l] for k, shift in enumerate(NEAR)}}
             cells = jnp.where(
                 from_west_lane,
                 pick(west[level_rows, :], west_index),
@@ -495,7 +504,7 @@
                 inner = inner + packed_taps[m + 3] * rows(cells, -m)
                 own_inner = own_inner + edge_taps[m + 3] * rows(own_cells, -m)
             first = moved_sum(
-                east_parts(inside, near_cells(own_cells), east_parts(outer, near_cells(cells)))
+                east_parts(inside, own_near, east_parts(outer, near_cells(cells)))
             )
             total = moved_sum(
                 east_parts(inside, near_cells(own_inner), east_parts(outer, near_cells(inner)))
@@ -564,12 +573,12 @@
 
 def shards(mass, thick, fe, fn, ce, cn, ne, owner):
     keep, send = prepare(thick, fe, fn, ce, cn, ne)
-    last, first = pack(mass)
+    last, first, own = pack(mass)
     me, chosen = position(), owner[0]
     other_core = exchange(send, 1)
     total = jnp.where(chosen == me, keep, jnp.where(chosen == me ^ 1, other_core, 0.0))
     total = total + (turn(total, 1) + turn(total, -1) + turn(total, 2))
-    total, last, first = lax.optimization_barrier((total, last, first))
+    total, last, first, own = lax.optimization_barrier((total, last, first, own))
     total = total + exchange(total, 8)
     padded, shifted = copies(mass)
     main = 2 * mass.shape[1] * mass.shape[2]
@@ -584,7 +593,7 @@
     to_west, before = lax.optimization_barrier((to_west, before))
     east = along(to_west, [(i, (i - 1) % size) for i in range(size)])
     after = inner_update(lambda levels: (early_parts(levels), 2 * levels), mine, other, padded, shifted)
-    return edge_update(west, east, last, before, after)
+    return edge_update(west, east, own, before, after)
 
 
 def solution(mesh):

time: 32.4 us -> 32.2 us (level)
  waiting for transfers between devices: 7.7 us -> 7.3 us
    ppermute x3, waiting for transfers between devices: 2.86 us -> 2.46 us  [turn(): lax.ppermute(x, 'tracer', [(i, i // 8 * 8 + (i + 2 * by) % 8) for i in ra...]
    pallas_call x2, Pallas kernels: 1.52 us -> 1.92 us  [in_vmem(): pl.pallas_call(kernel, out_shape=tuple((pltpu.VMEM(shape, jnp.float32) fo...]
  transfers between devices with their start and end apart: 8 -> 8, of which waited for: 4 -> 4; matrix products, arithmetic and copies ran while one was open for 0% -> 0% of each run, Pallas kernels for 20% -> 21%
where the time goes in v14:
time: 32.2 us; the launch traced here: 32 us
  starting transfers between devices  12.5 us (39%)
  Pallas kernels  10.2 us (32%)
  waiting for transfers between devices  7.3 us (23%)
  local copies, waits for them, and re-layouts  1.18 us (4%)
  between operations  0.75 us (2%)
    ppermute x3, starting transfers between devices, exchange(): return lax.ppermute(x, 'tracer', [(i, i ^ flip) for i in range(size)])  5.81 us
    pallas_call x2, Pallas kernels, inner_update(): pl.pallas_call(functools.partial(inner_kernel, span), out_shape=(pltpu.VM...  4.9 us
    ppermute x3, waiting for transfers between devices, exchange(): return lax.ppermute(x, 'tracer', [(i, i ^ flip) for i in range(size)])  4.84 us
    ppermute x3, starting transfers between devices, turn(): lax.ppermute(x, 'tracer', [(i, i // 8 * 8 + (i + 2 * by) % 8) for i in ra...  3.94 us
    ppermute x2, starting transfers between devices, along(): return lax.ppermute(x, 'space', pairs)  2.71 us
    ppermute x3, waiting for transfers between devices, turn(): lax.ppermute(x, 'tracer', [(i, i // 8 * 8 + (i + 2 * by) % 8) for i in ra...  2.46 us
    pallas_call x1, Pallas kernels, edge_update(): pl.pallas_call(edge_kernel, out_shape=jax.ShapeDtypeStruct(sums.shape, jn...  2.31 us
    pallas_call x2, Pallas kernels, in_vmem(): pl.pallas_call(kernel, out_shape=tuple((pltpu.VMEM(shape, jnp.float32) fo...  1.92 us
  transfers between devices with their start and end apart: 8, of which 4 were waited for; matrix products, arithmetic and copies ran while one was open for 0% of the time, Pallas kernels for 21%

profile of v14, /device:TPU:1, one launch (start us, length us, event | category | flops | bytes accessed | tf_op | source)
XLA Modules:
  0.0 32.0 jit_solution(12967337348603453649)
XLA Ops:
  0.0 1.1 %prepare.1 = (f32[208,128]{1,0:T(8,128)S(1)}, f32[208,128]{1,0:T(8,128)S(1)}) custom-call(f32[1,3,32,128]{3,2,1,0:T(8,128)} %refs_0_.1, f32[1,3,32,128]{3,2,1,0:T(8,128)} %refs_1_.1, f32[1,3,32,128]{3,2,1,0:T(8,128)} %refs_2_.1, f32[1,3,32,128]{3,2,1,0:T(8,128)} %refs_3_.1, f32[1,3,32,128]{3,2,1,0:T(8,128)} %refs_4_.1, s32[1,3,32,128]{3,2,1,0:T(8,128)} %refs_5_.1), custom_call_target="tpu_custom_call" | custom-call | tf_op jit(solution)/shard_map/prepare/pallas_call | solution.py:180
  1.1 3.3 %collective-permute-start = (f32[208,128]{1,0:T(8,128)S(1)}, f32[208,128]{1,0:T(8,128)S(1)}, u32[]{:S(2)}, u32[]{:S(2)}) collective-permute-start(f32[208,128]{1,0:T(8,128)S(1)} %get-tuple-element.30), channel_id=1, source_target_pairs={{0,1},{1,0},{2,3},{3,2},{4,5},{5,4},{6,7},{7,6},{8,9},{9,8},{10,11... | collective-permute-start | bytes 319496 | tf_op jit(solution)/shard_map/ppermute | solution.py:566
  5.1 0.3 collective-permute-done
  5.4 1.3 %collective-permute-start.3 = (f32[208,128]{1,0:T(8,128)S(1)}, f32[208,128]{1,0:T(8,128)S(1)}, u32[]{:S(2)}, u32[]{:S(2)}) collective-permute-start(f32[208,128]{1,0:T(8,128)S(1)} %select_select_fusion), channel_id=1, source_target_pairs={{0,4},{1,5},{2,6},{3,7},{4,0},{5,1},{6,2},{7,3},{8,12},{9,13},{10,... | collective-permute-start | bytes 319496 | tf_op jit(solution)/shard_map/ppermute | solution.py:571
  6.7 0.4 %collective-permute-start.1 = (f32[208,128]{1,0:T(8,128)S(1)}, f32[208,128]{1,0:T(8,128)S(1)}, u32[]{:S(2)}, u32[]{:S(2)}) collective-permute-start(f32[208,128]{1,0:T(8,128)S(1)} %select_select_fusion), channel_id=1, source_target_pairs={{0,2},{1,3},{2,4},{3,5},{4,6},{5,7},{6,0},{7,1},{8,10},{9,11},{10,... | collective-permute-start | bytes 319496 | tf_op jit(solution)/shard_map/ppermute | solution.py:571
  7.1 2.3 %collective-permute-start.2 = (f32[208,128]{1,0:T(8,128)S(1)}, f32[208,128]{1,0:T(8,128)S(1)}, u32[]{:S(2)}, u32[]{:S(2)}) collective-permute-start(f32[208,128]{1,0:T(8,128)S(1)} %select_select_fusion), channel_id=1, source_target_pairs={{0,6},{1,7},{2,0},{3,1},{4,2},{5,3},{6,4},{7,5},{8,14},{9,15},{10,... | collective-permute-start | bytes 319496 | tf_op jit(solution)/shard_map/ppermute | solution.py:571
  9.3 0.0 copy-start
  9.4 1.2 %copy-done = f32[18,3,32,128]{3,2,1,0:T(8,128)S(1)} copy-done((f32[18,3,32,128]{3,2,1,0:T(8,128)S(1)}, f32[18,3,32,128]{3,2,1,0:T(8,128)}, u32[]{:S(2)}) %copy-start) | copy-done | bytes 884760
  10.5 1.0 %pack.1 = (f32[96,128]{1,0:T(8,128)S(1)}, f32[96,128]{1,0:T(8,128)S(1)}, f32[2,4,3,32,128]{4,3,2,1,0:T(8,128)S(1)}) custom-call(f32[18,3,32,128]{3,2,1,0:T(8,128)S(1)} %copy-done), custom_call_target="tpu_custom_call" | custom-call | flops 2000000 | bytes 1000000 | tf_op jit(solution)/shard_map/pack/pallas_call | solution.py:236
  11.6 0.0 collective-permute-done.3
  11.6 2.5 %collective-permute-done.1 = f32[208,128]{1,0:T(8,128)S(1)} collective-permute-done((f32[208,128]{1,0:T(8,128)S(1)}, f32[208,128]{1,0:T(8,128)S(1)}, u32[]{:S(2)}, u32[]{:S(2)}) %collective-permute-start.1) | collective-permute-done | bytes 106528 | tf_op jit(solution)/shard_map/ppermute | solution.py:571
  14.0 0.0 collective-permute-done.2
  14.1 0.9 %collective-permute-start.4 = (f32[208,128]{1,0:T(8,128)S(1)}, f32[208,128]{1,0:T(8,128)S(1)}, u32[]{:S(2)}, u32[]{:S(2)}) collective-permute-start(f32[208,128]{1,0:T(8,128)S(1)} %add_add_fusion), channel_id=1, source_target_pairs={{0,8},{1,9},{2,10},{3,11},{4,12},{5,13},{6,14},{7,15},{8,0},{9,1},... | collective-permute-start | bytes 319496 | tf_op jit(solution)/shard_map/ppermute | solution.py:566
  14.9 0.9 %copies.1 = (f32[18,3,48,128]{3,2,1,0:T(8,128)S(1)}, f32[3,18,3,32,128]{4,3,2,1,0:T(8,128)S(1)}) custom-call(f32[18,3,32,128]{3,2,1,0:T(8,128)S(1)} %copy-done), custom_call_target="tpu_custom_call" | custom-call | flops 2000000 | bytes 1000000 | tf_op jit(solution)/shard_map/copies/pallas_call | solution.py:236
  15.8 3.7 %collective-permute-done.4 = f32[208,128]{1,0:T(8,128)S(1)} collective-permute-done((f32[208,128]{1,0:T(8,128)S(1)}, f32[208,128]{1,0:T(8,128)S(1)}, u32[]{:S(2)}, u32[]{:S(2)}) %collective-permute-start.4) | collective-permute-done | bytes 106528 | tf_op jit(solution)/shard_map/ppermute | solution.py:566
  19.6 1.6 %collective-permute-start.6 = (f32[192,128]{1,0:T(8,128)S(1)}, f32[192,128]{1,0:T(8,128)S(1)}, u32[]{:S(2)}, u32[]{:S(2)}) collective-permute-start(f32[192,128]{1,0:T(8,128)S(1)} %slice.9.mine), channel_id=1, source_target_pairs={{0,1},{1,0},{2,3},{3,2},{4,5},{5,4},{6,7},{7,6},{8,9},{9,8},{10,11... | collective-permute-start | bytes 294920 | tf_op jit(solution)/shard_map/ppermute | solution.py:566
  21.2 0.1 collective-permute-start.5
  21.3 0.8 %collective-permute-done.6.other = f32[192,128]{1,0:T(8,128)S(1)} collective-permute-done((f32[192,128]{1,0:T(8,128)S(1)}, f32[192,128]{1,0:T(8,128)S(1)}, u32[]{:S(2)}, u32[]{:S(2)}) %collective-permute-start.6) | collective-permute-done | bytes 98336 | tf_op jit(solution)/shard_map/ppermute | solution.py:566
  22.1 2.5 %inner.2 = (f32[18,3,32,128]{3,2,1,0:T(8,128)S(1)}, f32[11,3,32,128]{3,2,1,0:T(8,128)S(1)}, f32[7,3,32,128]{3,2,1,0:T(8,128)S(1)}, f32[3,32,128]{2,1,0:T(8,128)S(1)}) custom-call(f32[192,128]{1,0:T(8,128)S(1)} %slice.9.mine, f32[192,128]{1,0:T(8,128)S(1)} %collective-permute-done.6.other, f32[18,3,48,128]{3,2,1,0:T(8,128)S(1)} %get-tuple-element.37.padded, ...), custom_call_target="tpu_custom_call" | custom-call | flops 20000000 | bytes 6000000 | tf_op jit(solution)/shard_map/inner/pallas_call | solution.py:422
  24.6 2.6 %collective-permute-start.7 = (f32[112,128]{1,0:T(8,128)S(1)}, f32[112,128]{1,0:T(8,128)S(1)}, u32[]{:S(2)}, u32[]{:S(2)}) collective-permute-start(f32[112,128]{1,0:T(8,128)S(1)} %get-tuple-element.43), channel_id=1, source_target_pairs={{0,240},{16,0},{32,16},{48,32},{64,48},{80,64},{96,80},{112,96},{1... | collective-permute-start | bytes 172040 | tf_op jit(solution)/shard_map/ppermute | solution.py:561
  27.2 2.5 %inner.3 = (f32[18,3,32,128]{3,2,1,0:T(8,128)S(1)}, f32[11,3,32,128]{3,2,1,0:T(8,128)S(1)}, f32[7,3,32,128]{3,2,1,0:T(8,128)S(1)}, f32[3,32,128]{2,1,0:T(8,128)S(1)}) custom-call(f32[192,128]{1,0:T(8,128)S(1)} %slice.9.mine, f32[192,128]{1,0:T(8,128)S(1)} %collective-permute-done.6.other, f32[18,3,48,128]{3,2,1,0:T(8,128)S(1)} %get-tuple-element.37.padded, ...), custom_call_target="tpu_custom_call" | custom-call | flops 20000000 | bytes 6000000 | tf_op jit(solution)/shard_map/inner/pallas_call | solution.py:422
  29.7 0.0 collective-permute-done.5.west
  29.7 0.0 collective-permute-done.7.east
  29.7 2.3 %edges.1 = f32[18,3,32,128]{3,2,1,0:T(8,128)} custom-call(f32[112,128]{1,0:T(8,128)S(1)} %collective-permute-done.5.west, f32[112,128]{1,0:T(8,128)S(1)} %collective-permute-done.7.east, f32[2,4,3,32,128]{4,3,2,1,0:T(8,128)S(1)} %get-tuple-element.44.own, f32[18,3,32,128]{3,2,1,0:T(8,128)S(1)} %get-tuple-element.45.refs_0_, ...), custom_call_target="tpu_custom_call" | custom-call | tf_op jit(solution)/shard_map/edges/pallas_call | solution.py:545
  (6 shorter events, 0.1 us)
Async XLA Ops:
  1.1 4.3 %collective-permute-start = (f32[208,128]{1,0:T(8,128)S(1)}, f32[208,128]{1,0:T(8,128)S(1)}, u32[]{:S(2)}, u32[]{:S(2)}) collective-permute-start(f32[208,128]{1,0:T(8,128)S(1)} %get-tuple-element.30), channel_id=1, source_target_pairs={{0,1},{1,0},{2,3},{3,2},{4,5},{5,4},{6,7},{7,6},{8,9},{9,8},{10,11... | collective-permute-start | bytes 319496 | tf_op jit(solution)/shard_map/ppermute | solution.py:566
  5.4 6.2 %collective-permute-start.3 = (f32[208,128]{1,0:T(8,128)S(1)}, f32[208,128]{1,0:T(8,128)S(1)}, u32[]{:S(2)}, u32[]{:S(2)}) collective-permute-start(f32[208,128]{1,0:T(8,128)S(1)} %select_select_fusion), channel_id=1, source_target_pairs={{0,4},{1,5},{2,6},{3,7},{4,0},{5,1},{6,2},{7,3},{8,12},{9,13},{10,... | collective-permute-start | bytes 319496 | tf_op jit(solution)/shard_map/ppermute | solution.py:571
  6.7 7.4 %collective-permute-start.1 = (f32[208,128]{1,0:T(8,128)S(1)}, f32[208,128]{1,0:T(8,128)S(1)}, u32[]{:S(2)}, u32[]{:S(2)}) collective-permute-start(f32[208,128]{1,0:T(8,128)S(1)} %select_select_fusion), channel_id=1, source_target_pairs={{0,2},{1,3},{2,4},{3,5},{4,6},{5,7},{6,0},{7,1},{8,10},{9,11},{10,... | collective-permute-start | bytes 319496 | tf_op jit(solution)/shard_map/ppermute | solution.py:571
  7.1 7.0 %collective-permute-start.2 = (f32[208,128]{1,0:T(8,128)S(1)}, f32[208,128]{1,0:T(8,128)S(1)}, u32[]{:S(2)}, u32[]{:S(2)}) collective-permute-start(f32[208,128]{1,0:T(8,128)S(1)} %select_select_fusion), channel_id=1, source_target_pairs={{0,6},{1,7},{2,0},{3,1},{4,2},{5,3},{6,4},{7,5},{8,14},{9,15},{10,... | collective-permute-start | bytes 319496 | tf_op jit(solution)/shard_map/ppermute | solution.py:571
  9.3 1.2 %copy-start = (f32[18,3,32,128]{3,2,1,0:T(8,128)S(1)}, f32[18,3,32,128]{3,2,1,0:T(8,128)}, u32[]{:S(2)}) copy-start(f32[18,3,32,128]{3,2,1,0:T(8,128)} %mass.3) | copy-start | bytes 2654212
  14.1 5.5 %collective-permute-start.4 = (f32[208,128]{1,0:T(8,128)S(1)}, f32[208,128]{1,0:T(8,128)S(1)}, u32[]{:S(2)}, u32[]{:S(2)}) collective-permute-start(f32[208,128]{1,0:T(8,128)S(1)} %add_add_fusion), channel_id=1, source_target_pairs={{0,8},{1,9},{2,10},{3,11},{4,12},{5,13},{6,14},{7,15},{8,0},{9,1},... | collective-permute-start | bytes 319496 | tf_op jit(solution)/shard_map/ppermute | solution.py:566
  19.6 2.5 %collective-permute-start.6 = (f32[192,128]{1,0:T(8,128)S(1)}, f32[192,128]{1,0:T(8,128)S(1)}, u32[]{:S(2)}, u32[]{:S(2)}) collective-permute-start(f32[192,128]{1,0:T(8,128)S(1)} %slice.9.mine), channel_id=1, source_target_pairs={{0,1},{1,0},{2,3},{3,2},{4,5},{5,4},{6,7},{7,6},{8,9},{9,8},{10,11... | collective-permute-start | bytes 294920 | tf_op jit(solution)/shard_map/ppermute | solution.py:566
  21.2 8.5 %collective-permute-start.5 = (f32[112,128]{1,0:T(8,128)S(1)}, f32[112,128]{1,0:T(8,128)S(1)}, u32[]{:S(2)}, u32[]{:S(2)}) collective-permute-start(f32[112,128]{1,0:T(8,128)S(1)} %get-tuple-element.54), channel_id=1, source_target_pairs={{0,16},{16,32},{32,48},{48,64},{64,80},{80,96},{96,112},{112,128},... | collective-permute-start | bytes 172040 | tf_op jit(solution)/shard_map/ppermute | solution.py:561
  24.6 5.1 %collective-permute-start.7 = (f32[112,128]{1,0:T(8,128)S(1)}, f32[112,128]{1,0:T(8,128)S(1)}, u32[]{:S(2)}, u32[]{:S(2)}) collective-permute-start(f32[112,128]{1,0:T(8,128)S(1)} %get-tuple-element.43), channel_id=1, source_target_pairs={{0,240},{16,0},{32,16},{48,32},{64,48},{80,64},{96,80},{112,96},{1... | collective-permute-start | bytes 172040 | tf_op jit(solution)/shard_map/ppermute | solution.py:561

commit v15 on v14

--- a/solution.py
+++ b/solution.py
@@ -577,7 +577,8 @@
     me, chosen = position(), owner[0]
     other_core = exchange(send, 1)
     total = jnp.where(chosen == me, keep, jnp.where(chosen == me ^ 1, other_core, 0.0))
-    total = total + (turn(total, 1) + turn(total, -1) + turn(total, 2))
+    far = turn(total, 2)
+    total = (total + turn(total, 1)) + (turn(total, -1) + far)
     total, last, first, own = lax.optimization_barrier((total, last, first, own))
     total = total + exchange(total, 8)
     padded, shifted = copies(mass)

time: 32.2 us -> 34.7 us (1.078)
  starting transfers between devices: 12.5 us -> 14.7 us
    ppermute x3, waiting for transfers between devices: 2.46 us -> 5.39 us  [turn(): lax.ppermute(x, 'tracer', [(i, i // 8 * 8 + (i + 2 * by) % 8) for i in ra...]
    ppermute x3, waiting for transfers between devices: 4.84 us -> 2.18 us  [exchange(): return lax.ppermute(x, 'tracer', [(i, i ^ flip) for i in range(size)])]
    ppermute x2, starting transfers between devices: 2.71 us -> 4.97 us  [along(): return lax.ppermute(x, 'space', pairs)]
    ppermute x3, starting transfers between devices: 3.94 us -> 2.12 us  [turn(): lax.ppermute(x, 'tracer', [(i, i // 8 * 8 + (i + 2 * by) % 8) for i in ra...]
    ppermute x3, starting transfers between devices: 5.81 us -> 7.62 us  [exchange(): return lax.ppermute(x, 'tracer', [(i, i ^ flip) for i in range(size)])]
  transfers between devices with their start and end apart: 8 -> 8, of which waited for: 4 -> 4; matrix products, arithmetic and copies ran while one was open for 0% -> 0% of each run, Pallas kernels for 21% -> 20%
where the time goes in v15:
time: 34.7 us; the launch traced here: 34.5 us
  starting transfers between devices  14.7 us (42%)
  Pallas kernels  10.2 us (29%)
  waiting for transfers between devices  7.58 us (22%)
  local copies, waits for them, and re-layouts  1.18 us (3%)
  between operations  0.75 us (2%)
    ppermute x3, starting transfers between devices, exchange(): return lax.ppermute(x, 'tracer', [(i, i ^ flip) for i in range(size)])  7.62 us
    ppermute x3, waiting for transfers between devices, turn(): lax.ppermute(x, 'tracer', [(i, i // 8 * 8 + (i + 2 * by) % 8) for i in ra...  5.39 us
    ppermute x2, starting transfers between devices, along(): return lax.ppermute(x, 'space', pairs)  4.97 us
    pallas_call x2, Pallas kernels, inner_update(): pl.pallas_call(functools.partial(inner_kernel, span), out_shape=(pltpu.VM...  4.9 us
    pallas_call x1, Pallas kernels, edge_update(): pl.pallas_call(edge_kernel, out_shape=jax.ShapeDtypeStruct(sums.shape, jn...  2.31 us
    ppermute x3, waiting for transfers between devices, exchange(): return lax.ppermute(x, 'tracer', [(i, i ^ flip) for i in range(size)])  2.18 us
    ppermute x3, starting transfers between devices, turn(): lax.ppermute(x, 'tracer', [(i, i // 8 * 8 + (i + 2 * by) % 8) for i in ra...  2.12 us
    pallas_call x2, Pallas kernels, in_vmem(): pl.pallas_call(kernel, out_shape=tuple((pltpu.VMEM(shape, jnp.float32) fo...  1.92 us
  transfers between devices with their start and end apart: 8, of which 4 were waited for; matrix products, arithmetic and copies ran while one was open for 0% of the time, Pallas kernels for 20%

profile of v15, /device:TPU:1, one launch (start us, length us, event | category | flops | bytes accessed | tf_op | source)
XLA Modules:
  0.0 34.5 jit_solution(8741935888406965569)
XLA Ops:
  0.0 1.1 %prepare.1 = (f32[208,128]{1,0:T(8,128)S(1)}, f32[208,128]{1,0:T(8,128)S(1)}) custom-call(f32[1,3,32,128]{3,2,1,0:T(8,128)} %refs_0_.1, f32[1,3,32,128]{3,2,1,0:T(8,128)} %refs_1_.1, f32[1,3,32,128]{3,2,1,0:T(8,128)} %refs_2_.1, f32[1,3,32,128]{3,2,1,0:T(8,128)} %refs_3_.1, f32[1,3,32,128]{3,2,1,0:T(8,128)} %refs_4_.1, s32[1,3,32,128]{3,2,1,0:T(8,128)} %refs_5_.1), custom_call_target="tpu_custom_call" | custom-call | tf_op jit(solution)/shard_map/prepare/pallas_call | solution.py:180
  1.1 3.3 %collective-permute-start = (f32[208,128]{1,0:T(8,128)S(1)}, f32[208,128]{1,0:T(8,128)S(1)}, u32[]{:S(2)}, u32[]{:S(2)}) collective-permute-start(f32[208,128]{1,0:T(8,128)S(1)} %get-tuple-element.30), channel_id=1, source_target_pairs={{0,1},{1,0},{2,3},{3,2},{4,5},{5,4},{6,7},{7,6},{8,9},{9,8},{10,11... | collective-permute-start | bytes 319496 | tf_op jit(solution)/shard_map/ppermute | solution.py:566
  5.1 0.3 collective-permute-done
  5.4 1.1 %collective-permute-start.2 = (f32[208,128]{1,0:T(8,128)S(1)}, f32[208,128]{1,0:T(8,128)S(1)}, u32[]{:S(2)}, u32[]{:S(2)}) collective-permute-start(f32[208,128]{1,0:T(8,128)S(1)} %select_select_fusion), channel_id=1, source_target_pairs={{0,6},{1,7},{2,0},{3,1},{4,2},{5,3},{6,4},{7,5},{8,14},{9,15},{10,... | collective-permute-start | bytes 319496 | tf_op jit(solution)/shard_map/ppermute | solution.py:571
  6.5 0.3 %collective-permute-start.3 = (f32[208,128]{1,0:T(8,128)S(1)}, f32[208,128]{1,0:T(8,128)S(1)}, u32[]{:S(2)}, u32[]{:S(2)}) collective-permute-start(f32[208,128]{1,0:T(8,128)S(1)} %select_select_fusion), channel_id=1, source_target_pairs={{0,4},{1,5},{2,6},{3,7},{4,0},{5,1},{6,2},{7,3},{8,12},{9,13},{10,... | collective-permute-start | bytes 319496 | tf_op jit(solution)/shard_map/ppermute | solution.py:571
  6.8 0.7 %collective-permute-start.1 = (f32[208,128]{1,0:T(8,128)S(1)}, f32[208,128]{1,0:T(8,128)S(1)}, u32[]{:S(2)}, u32[]{:S(2)}) collective-permute-start(f32[208,128]{1,0:T(8,128)S(1)} %select_select_fusion), channel_id=1, source_target_pairs={{0,2},{1,3},{2,4},{3,5},{4,6},{5,7},{6,0},{7,1},{8,10},{9,11},{10,... | collective-permute-start | bytes 319496 | tf_op jit(solution)/shard_map/ppermute | solution.py:571
  7.5 0.0 copy-start
  7.5 1.2 %copy-done = f32[18,3,32,128]{3,2,1,0:T(8,128)S(1)} copy-done((f32[18,3,32,128]{3,2,1,0:T(8,128)S(1)}, f32[18,3,32,128]{3,2,1,0:T(8,128)}, u32[]{:S(2)}) %copy-start) | copy-done | bytes 884760
  8.7 1.0 %pack.1 = (f32[96,128]{1,0:T(8,128)S(1)}, f32[96,128]{1,0:T(8,128)S(1)}, f32[2,4,3,32,128]{4,3,2,1,0:T(8,128)S(1)}) custom-call(f32[18,3,32,128]{3,2,1,0:T(8,128)S(1)} %copy-done), custom_call_target="tpu_custom_call" | custom-call | flops 2000000 | bytes 1000000 | tf_op jit(solution)/shard_map/pack/pallas_call | solution.py:236
  9.7 0.0 collective-permute-done.2
  9.7 2.1 %collective-permute-done.3 = f32[208,128]{1,0:T(8,128)S(1)} collective-permute-done((f32[208,128]{1,0:T(8,128)S(1)}, f32[208,128]{1,0:T(8,128)S(1)}, u32[]{:S(2)}, u32[]{:S(2)}) %collective-permute-start.3) | collective-permute-done | bytes 106528 | tf_op jit(solution)/shard_map/ppermute | solution.py:571
  11.9 3.3 %collective-permute-done.1 = f32[208,128]{1,0:T(8,128)S(1)} collective-permute-done((f32[208,128]{1,0:T(8,128)S(1)}, f32[208,128]{1,0:T(8,128)S(1)}, u32[]{:S(2)}, u32[]{:S(2)}) %collective-permute-start.1) | collective-permute-done | bytes 106528 | tf_op jit(solution)/shard_map/ppermute | solution.py:571
  15.2 2.8 %collective-permute-start.4 = (f32[208,128]{1,0:T(8,128)S(1)}, f32[208,128]{1,0:T(8,128)S(1)}, u32[]{:S(2)}, u32[]{:S(2)}) collective-permute-start(f32[208,128]{1,0:T(8,128)S(1)} %add_add_fusion), channel_id=1, source_target_pairs={{0,8},{1,9},{2,10},{3,11},{4,12},{5,13},{6,14},{7,15},{8,0},{9,1},... | collective-permute-start | bytes 319496 | tf_op jit(solution)/shard_map/ppermute | solution.py:566
  18.0 0.9 %copies.1 = (f32[18,3,48,128]{3,2,1,0:T(8,128)S(1)}, f32[3,18,3,32,128]{4,3,2,1,0:T(8,128)S(1)}) custom-call(f32[18,3,32,128]{3,2,1,0:T(8,128)S(1)} %copy-done), custom_call_target="tpu_custom_call" | custom-call | flops 2000000 | bytes 1000000 | tf_op jit(solution)/shard_map/copies/pallas_call | solution.py:236
  18.9 1.9 %collective-permute-done.4 = f32[208,128]{1,0:T(8,128)S(1)} collective-permute-done((f32[208,128]{1,0:T(8,128)S(1)}, f32[208,128]{1,0:T(8,128)S(1)}, u32[]{:S(2)}, u32[]{:S(2)}) %collective-permute-start.4) | collective-permute-done | bytes 106528 | tf_op jit(solution)/shard_map/ppermute | solution.py:566
  20.8 1.5 %collective-permute-start.6 = (f32[192,128]{1,0:T(8,128)S(1)}, f32[192,128]{1,0:T(8,128)S(1)}, u32[]{:S(2)}, u32[]{:S(2)}) collective-permute-start(f32[192,128]{1,0:T(8,128)S(1)} %slice.9.mine), channel_id=1, source_target_pairs={{0,1},{1,0},{2,3},{3,2},{4,5},{5,4},{6,7},{7,6},{8,9},{9,8},{10,11... | collective-permute-start | bytes 294920 | tf_op jit(solution)/shard_map/ppermute | solution.py:566
  22.3 1.3 %collective-permute-start.5 = (f32[112,128]{1,0:T(8,128)S(1)}, f32[112,128]{1,0:T(8,128)S(1)}, u32[]{:S(2)}, u32[]{:S(2)}) collective-permute-start(f32[112,128]{1,0:T(8,128)S(1)} %get-tuple-element.54), channel_id=1, source_target_pairs={{0,16},{16,32},{32,48},{48,64},{64,80},{80,96},{96,112},{112,128},... | collective-permute-start | bytes 172040 | tf_op jit(solution)/shard_map/ppermute | solution.py:561
  23.6 0.0 collective-permute-done.6.other
  23.6 2.5 %inner.2 = (f32[18,3,32,128]{3,2,1,0:T(8,128)S(1)}, f32[11,3,32,128]{3,2,1,0:T(8,128)S(1)}, f32[7,3,32,128]{3,2,1,0:T(8,128)S(1)}, f32[3,32,128]{2,1,0:T(8,128)S(1)}) custom-call(f32[192,128]{1,0:T(8,128)S(1)} %slice.9.mine, f32[192,128]{1,0:T(8,128)S(1)} %collective-permute-done.6.other, f32[18,3,48,128]{3,2,1,0:T(8,128)S(1)} %get-tuple-element.37.padded, ...), custom_call_target="tpu_custom_call" | custom-call | flops 20000000 | bytes 6000000 | tf_op jit(solution)/shard_map/inner/pallas_call | solution.py:422
  26.0 3.7 %collective-permute-start.7 = (f32[112,128]{1,0:T(8,128)S(1)}, f32[112,128]{1,0:T(8,128)S(1)}, u32[]{:S(2)}, u32[]{:S(2)}) collective-permute-start(f32[112,128]{1,0:T(8,128)S(1)} %get-tuple-element.43), channel_id=1, source_target_pairs={{0,240},{16,0},{32,16},{48,32},{64,48},{80,64},{96,80},{112,96},{1... | collective-permute-start | bytes 172040 | tf_op jit(solution)/shard_map/ppermute | solution.py:561
  29.7 2.5 %inner.3 = (f32[18,3,32,128]{3,2,1,0:T(8,128)S(1)}, f32[11,3,32,128]{3,2,1,0:T(8,128)S(1)}, f32[7,3,32,128]{3,2,1,0:T(8,128)S(1)}, f32[3,32,128]{2,1,0:T(8,128)S(1)}) custom-call(f32[192,128]{1,0:T(8,128)S(1)} %slice.9.mine, f32[192,128]{1,0:T(8,128)S(1)} %collective-permute-done.6.other, f32[18,3,48,128]{3,2,1,0:T(8,128)S(1)} %get-tuple-element.37.padded, ...), custom_call_target="tpu_custom_call" | custom-call | flops 20000000 | bytes 6000000 | tf_op jit(solution)/shard_map/inner/pallas_call | solution.py:422
  32.2 0.0 collective-permute-done.5.west
  32.2 0.0 collective-permute-done.7.east
  32.2 2.3 %edges.1 = f32[18,3,32,128]{3,2,1,0:T(8,128)} custom-call(f32[112,128]{1,0:T(8,128)S(1)} %collective-permute-done.5.west, f32[112,128]{1,0:T(8,128)S(1)} %collective-permute-done.7.east, f32[2,4,3,32,128]{4,3,2,1,0:T(8,128)S(1)} %get-tuple-element.44.own, f32[18,3,32,128]{3,2,1,0:T(8,128)S(1)} %get-tuple-element.45.refs_0_, ...), custom_call_target="tpu_custom_call" | custom-call | tf_op jit(solution)/shard_map/edges/pallas_call | solution.py:545
  (6 shorter events, 0.1 us)
Async XLA Ops:
  1.1 4.3 %collective-permute-start = (f32[208,128]{1,0:T(8,128)S(1)}, f32[208,128]{1,0:T(8,128)S(1)}, u32[]{:S(2)}, u32[]{:S(2)}) collective-permute-start(f32[208,128]{1,0:T(8,128)S(1)} %get-tuple-element.30), channel_id=1, source_target_pairs={{0,1},{1,0},{2,3},{3,2},{4,5},{5,4},{6,7},{7,6},{8,9},{9,8},{10,11... | collective-permute-start | bytes 319496 | tf_op jit(solution)/shard_map/ppermute | solution.py:566
  5.4 4.3 %collective-permute-start.2 = (f32[208,128]{1,0:T(8,128)S(1)}, f32[208,128]{1,0:T(8,128)S(1)}, u32[]{:S(2)}, u32[]{:S(2)}) collective-permute-start(f32[208,128]{1,0:T(8,128)S(1)} %select_select_fusion), channel_id=1, source_target_pairs={{0,6},{1,7},{2,0},{3,1},{4,2},{5,3},{6,4},{7,5},{8,14},{9,15},{10,... | collective-permute-start | bytes 319496 | tf_op jit(solution)/shard_map/ppermute | solution.py:571
  6.5 5.4 %collective-permute-start.3 = (f32[208,128]{1,0:T(8,128)S(1)}, f32[208,128]{1,0:T(8,128)S(1)}, u32[]{:S(2)}, u32[]{:S(2)}) collective-permute-start(f32[208,128]{1,0:T(8,128)S(1)} %select_select_fusion), channel_id=1, source_target_pairs={{0,4},{1,5},{2,6},{3,7},{4,0},{5,1},{6,2},{7,3},{8,12},{9,13},{10,... | collective-permute-start | bytes 319496 | tf_op jit(solution)/shard_map/ppermute | solution.py:571
  6.8 8.3 %collective-permute-start.1 = (f32[208,128]{1,0:T(8,128)S(1)}, f32[208,128]{1,0:T(8,128)S(1)}, u32[]{:S(2)}, u32[]{:S(2)}) collective-permute-start(f32[208,128]{1,0:T(8,128)S(1)} %select_select_fusion), channel_id=1, source_target_pairs={{0,2},{1,3},{2,4},{3,5},{4,6},{5,7},{6,0},{7,1},{8,10},{9,11},{10,... | collective-permute-start | bytes 319496 | tf_op jit(solution)/shard_map/ppermute | solution.py:571
  7.5 1.2 %copy-start = (f32[18,3,32,128]{3,2,1,0:T(8,128)S(1)}, f32[18,3,32,128]{3,2,1,0:T(8,128)}, u32[]{:S(2)}) copy-start(f32[18,3,32,128]{3,2,1,0:T(8,128)} %mass.3) | copy-start | bytes 2654212
  15.2 5.6 %collective-permute-start.4 = (f32[208,128]{1,0:T(8,128)S(1)}, f32[208,128]{1,0:T(8,128)S(1)}, u32[]{:S(2)}, u32[]{:S(2)}) collective-permute-start(f32[208,128]{1,0:T(8,128)S(1)} %add_add_fusion), channel_id=1, source_target_pairs={{0,8},{1,9},{2,10},{3,11},{4,12},{5,13},{6,14},{7,15},{8,0},{9,1},... | collective-permute-start | bytes 319496 | tf_op jit(solution)/shard_map/ppermute | solution.py:566
  20.8 2.8 %collective-permute-start.6 = (f32[192,128]{1,0:T(8,128)S(1)}, f32[192,128]{1,0:T(8,128)S(1)}, u32[]{:S(2)}, u32[]{:S(2)}) collective-permute-start(f32[192,128]{1,0:T(8,128)S(1)} %slice.9.mine), channel_id=1, source_target_pairs={{0,1},{1,0},{2,3},{3,2},{4,5},{5,4},{6,7},{7,6},{8,9},{9,8},{10,11... | collective-permute-start | bytes 294920 | tf_op jit(solution)/shard_map/ppermute | solution.py:566
  22.3 9.9 %collective-permute-start.5 = (f32[112,128]{1,0:T(8,128)S(1)}, f32[112,128]{1,0:T(8,128)S(1)}, u32[]{:S(2)}, u32[]{:S(2)}) collective-permute-start(f32[112,128]{1,0:T(8,128)S(1)} %get-tuple-element.54), channel_id=1, source_target_pairs={{0,16},{16,32},{32,48},{48,64},{64,80},{80,96},{96,112},{112,128},... | collective-permute-start | bytes 172040 | tf_op jit(solution)/shard_map/ppermute | solution.py:561
  26.0 6.2 %collective-permute-start.7 = (f32[112,128]{1,0:T(8,128)S(1)}, f32[112,128]{1,0:T(8,128)S(1)}, u32[]{:S(2)}, u32[]{:S(2)}) collective-permute-start(f32[112,128]{1,0:T(8,128)S(1)} %get-tuple-element.43), channel_id=1, source_target_pairs={{0,240},{16,0},{32,16},{48,32},{64,48},{80,64},{96,80},{112,96},{1... | collective-permute-start | bytes 172040 | tf_op jit(solution)/shard_map/ppermute | solution.py:561
